TPU v7x, 32 devices: a whole 2x2x4 slice. The times are simulated.
32 devices in a mesh: gx: 2 (over x), gy: 4 (over y, core), gz: 4 (over z).
Axes of the slice: x: 2, y: 2, z: 4, core: 2. Of those that a mesh axis runs over, the one named last changes fastest.
Arguments:
- left_core: float32 [256, 512, 256], P(None, ('gx', 'gy', 'gz')), may hold values from -4000 to 4000
- right_core: float32 [256, 512, 256], P(None, ('gx', 'gy', 'gz')), may hold values from -0.00036621094 to 0.00036621094
Outputs:
- left_out: float32 [256, 512, 128], P(None, ('gx', 'gy', 'gz'))
- right_out: float32 [128, 512, 256], P(None, ('gx', 'gy', 'gz'))
- next_factor: float32 [256, 256], replicated
All inputs are finite; a program needn't handle non-finite values.
Results may differ from a plain program's by a relative error of at most 0.000075.
Values sent between devices are 32-bit elements; how exact they have to be, the bound alone decides.
No kernel may reach another device: no remote copies, remote signals or barrier semaphores. Data moves between devices by JAX's collectives and lax.ppermute only.
A program may use at most 192 MiB of HBM per device.

v0:
```python
import math

import jax
import jax.numpy as jnp
from jax import lax
from jax.sharding import PartitionSpec as P

RK = 128


def gram_of(matrix_rows):
    return lax.dot_general(
        matrix_rows,
        matrix_rows,
        (((0,), (0,)), ((), ())),
        precision=lax.Precision.HIGHEST,
        preferred_element_type=jnp.float32,
    )


def per_device(left_core, right_core):
    rank_left, points_local, rank_mid = left_core.shape
    rank_right = right_core.shape[2]
    total_points = points_local * lax.axis_size("gx") * lax.axis_size("gy") * lax.axis_size("gz")
    unfold = left_core.reshape(rank_left * points_local, rank_mid)
    lower_one = jnp.linalg.cholesky(lax.psum(gram_of(unfold), ("gx", "gy", "gz")))
    upper_full = lower_one.T
    ortho_cols = lax.linalg.triangular_solve(
        lower_one[:RK, :RK], unfold[:, :RK], left_side=False, lower=True, transpose_a=True
    )
    left_out = (ortho_cols * math.sqrt(rank_left * total_points)).reshape(
        rank_left, points_local, RK
    )
    absorbed = jnp.dot(
        upper_full[:RK, :],
        right_core.reshape(rank_mid, points_local * rank_right),
        precision=lax.Precision.HIGHEST,
        preferred_element_type=jnp.float32,
    )
    summed = lax.psum(gram_of(absorbed.reshape(RK * points_local, rank_right)), ("gx", "gy", "gz"))
    factor = jnp.linalg.cholesky(summed / (RK * total_points)).T
    right_out = absorbed.reshape(RK, points_local, rank_right)
    return (left_out, right_out, factor)


def solution(mesh):
    in_specs = (P(None, ("gx", "gy", "gz"), None), P(None, ("gx", "gy", "gz"), None))
    out_specs = (P(None, ("gx", "gy", "gz"), None), P(None, ("gx", "gy", "gz"), None), P())
    return jax.shard_map(
        per_device, mesh=mesh, in_specs=in_specs, out_specs=out_specs, check_vma=False
    )
```

profile of v0, /device:TPU:0, one launch (start us, length us, event | category | flops | bytes accessed | tf_op | source)
XLA Modules:
  0.0 367.5 jit_solution(17025490143404086426)
XLA Ops:
  7.2 10.9 %convolution_bitcast_fusion = f32[256,256]{0,1:T(8,128)} fusion(f32[256,16,256]{2,1,0:T(8,128)} %param.3), kind=kOutput, calls=%fused_computation.3 | convolution fusion | flops 3221225472 | bytes 4456448 | tf_op jit(solution)/shard_map/dot_general | solution.py:12
  18.3 7.9 %copy.26 = f32[32,8,16,256]{3,1,2,0:T(8,128)} copy(f32[32,8,16,256]{3,2,1,0:T(8,128)} %bitcast.53) | data formatting | bytes 8388608
  26.3 119.6 %all-reduce.4.cloned.1.call-done = f32[256,256]{0,1:T(8,128)} async-done(((f32[256,256]{0,1:T(8,128)}), f32[256,256]{0,1:T(8,128)}) %all-reduce.4.cloned.1.call-update) | async-done | bytes 262160 | tf_op jit(solution)/shard_map/psum | solution.py:26
  145.9 1.1 copy.16
  147.0 1.0 fusion.3
  148.0 11.7 %cholesky.130 = f32[128,128]{1,0:T(8,128)S(1)} custom-call(f32[128,128]{1,0:T(8,128)S(1)} %cholesky.194), custom_call_target="Cholesky" | custom-call | tf_op jit(solution)/shard_map/jit(cholesky)/cholesky | solution.py:26
  159.7 9.8 %custom-call.13 = f32[1,128,128]{1,2,0:T(8,128)S(1)} custom-call(f32[1,128,128]{2,1,0:T(8,128)S(1)} %get-tuple-element.17), custom_call_target="InvertDiagBlocksLowerTriangular" | custom-call | tf_op jit(solution)/shard_map/jit(cholesky)/cholesky | solution.py:26
  170.1 11.9 %cholesky.147 = f32[128,128]{1,0:T(8,128)S(1)} custom-call(f32[128,128]{1,0:T(8,128)S(1)} %convolution_subtract_fusion.1), custom_call_target="Cholesky" | custom-call | tf_op jit(solution)/shard_map/jit(cholesky)/cholesky | solution.py:26
  182.0 0.6 compare_reduce_fusion.2
  184.0 4.5 %fusion.4 = f32[128,4096]{1,0:T(8,128)S(1)} fusion(f32[256,4096]{1,0:T(8,128)} %bitcast.52, f32[256,256]{0,1:T(8,128)S(1)} %fusion.24), kind=kOutput, calls=%fused_computation.13 | convolution fusion | flops 1610612736 | bytes 6422528 | tf_op jit(solution)/shard_map/dot_general | solution.py:34
  188.5 1.5 reshape.39
  190.0 6.4 %fusion.14 = f32[256,256]{0,1:T(8,128)} fusion(f32[2048,256]{1,0:T(8,128)} %reshape.39), kind=kOutput, calls=%fused_computation.41 | convolution fusion | flops 1610612736 | bytes 2359296 | tf_op jit(solution)/shard_map/dot_general | solution.py:12
  196.4 9.8 %custom-call.11 = f32[1,128,128]{1,2,0:T(8,128)S(1)} custom-call(f32[1,128,128]{2,1,0:T(8,128)S(1)} %fusion.8), custom_call_target="InvertDiagBlocksLowerTriangular" | custom-call | tf_op jit(solution)/shard_map/triangular_solve | solution.py:28
  206.2 4.9 %fusion = f32[4096,128]{0,1:T(8,128)} fusion(f32[4096,256]{1,0:T(8,128)} %bitcast.50, f32[1,128,128]{1,2,0:T(8,128)S(1)} %custom-call.11), kind=kOutput, calls=%fused_computation.1 | convolution fusion | flops 805830656 | bytes 4259840 | tf_op jit(solution)/shard_map/triangular_solve | solution.py:28
  211.1 2.0 copy.27
  213.1 3.1 copy.17
  216.2 104.5 %all-reduce.6.cloned.1.call-done = f32[256,256]{0,1:T(8,128)} async-done(((f32[256,256]{0,1:T(8,128)}), f32[256,256]{0,1:T(8,128)}) %all-reduce.6.cloned.1.call-update) | async-done | bytes 262160 | tf_op jit(solution)/shard_map/psum | solution.py:40
  320.7 1.0 broadcast_multiply_fusion
  321.8 1.0 fusion.2
  322.8 11.7 %cholesky.164 = f32[128,128]{1,0:T(8,128)S(1)} custom-call(f32[128,128]{1,0:T(8,128)S(1)} %cholesky.197), custom_call_target="Cholesky" | custom-call | tf_op jit(solution)/shard_map/jit(cholesky)/cholesky | solution.py:41
  334.6 9.8 %custom-call.14 = f32[1,128,128]{1,2,0:T(8,128)S(1)} custom-call(f32[1,128,128]{2,1,0:T(8,128)S(1)} %get-tuple-element.13), custom_call_target="InvertDiagBlocksLowerTriangular" | custom-call | tf_op jit(solution)/shard_map/jit(cholesky)/cholesky | solution.py:41
  344.9 11.7 %cholesky.181 = f32[128,128]{1,0:T(8,128)S(1)} custom-call(f32[128,128]{1,0:T(8,128)S(1)} %convolution_subtract_fusion), custom_call_target="Cholesky" | custom-call | tf_op jit(solution)/shard_map/jit(cholesky)/cholesky | solution.py:41
  356.6 0.7 compare_reduce_fusion
  359.4 0.8 copy.20
  (22 shorter events, 2.3 us)
Async XLA Ops:
  7.2 138.7 %all-reduce.4.cloned.1.call-start = ((), (), s32[]{:S(2)}) async-start(), calls=%async_computation | async-start | bytes 524288 | tf_op jit(solution)/shard_map/psum | solution.py:26
  18.1 302.6 %all-reduce.6.cloned.1.call-start = ((), (), s32[]{:S(2)}) async-start(), calls=%async_computation.1 | async-start | bytes 524288 | tf_op jit(solution)/shard_map/psum | solution.py:40
Sparse Core Ops, SparseCore 0:
  18.2 127.6 all-reduce.3
  196.5 124.1 all-reduce.5
where the time goes:
time: 373 us; the launch traced here: 367 us
  waiting for transfers between devices  224 us (60%)
  other arithmetic  81.6 us (22%)
  matrix products  27.6 us (7%)
  between operations  17.3 us (5%)
  local copies, waits for them, and re-layouts  16.6 us (4%)
    psum x1, waiting for transfers between devices, per_device(): lax.psum(gram_of(unfold), ('gx', 'gy', 'gz'))  120 us
    psum x1, waiting for transfers between devices, per_device(): lax.psum(gram_of(absorbed.reshape(RK * points_local, rank_right)), ('gx',...  104 us
    another operation x7, other arithmetic, per_device(): factor = jnp.linalg.cholesky(summed / (RK * total_points)).T  34.7 us
    another operation x6, other arithmetic, per_device(): jnp.linalg.cholesky(lax.psum(gram_of(unfold), ('gx', 'gy', 'gz')))  34.2 us
    dot_general x2, matrix products, gram_of(): lax.dot_general(matrix_rows, matrix_rows, (((0,), (0,)), ((), ())), preci...  17.3 us
    unnamed x3, local copies, waits for them, and re-layouts  10.7 us
    another operation x2, other arithmetic, per_device(): lax.linalg.triangular_solve(lower_one[:RK, :RK], unfold[:, :RK], left_sid...  9.82 us
  transfers between devices with their start and end apart: 2, of which 2 were waited for; matrix products, arithmetic and copies ran while one was open for 8% of the time, Pallas kernels for 0%

commit v1 on v0

v1 whole, which is shorter than its diff:
```python
import math

import jax
import jax.numpy as jnp
from jax import lax
from jax.sharding import PartitionSpec as P

RK = 128
AXES = ("gx", "gy", "gz")


def gram_of(lhs_rows, matrix_rows):
    return lax.dot_general(
        lhs_rows,
        matrix_rows,
        (((0,), (0,)), ((), ())),
        precision=lax.Precision.HIGHEST,
        preferred_element_type=jnp.float32,
    )


def sum_by_scatter(part, devices):
    rows, columns = part.shape
    tall = jnp.concatenate([part[:, : columns // 2], part[:, columns // 2 :]], axis=0)
    blocks = tall.reshape(devices, 2 * rows // devices, columns // 2)
    mine = jnp.sum(lax.all_to_all(blocks, AXES, 0, 0), axis=0)
    spread = jnp.broadcast_to(mine[None], blocks.shape)
    tall = lax.all_to_all(spread, AXES, 0, 0).reshape(2 * rows, columns // 2)
    return jnp.concatenate([tall[:rows], tall[rows:]], axis=1)


def exchange(value, axis, bit):
    size = lax.axis_size(axis)
    return lax.ppermute(value, axis, [(i, i ^ bit) for i in range(size)])


def sum_by_butterfly(part):
    rows, columns = part.shape
    odd = lax.axis_index("gy") % 2 == 1
    top, bottom = part[: rows // 2], part[rows // 2 :]
    keep = jnp.where(odd, bottom, top)
    total = keep + exchange(jnp.where(odd, top, bottom), "gy", 1)
    for axis in AXES:
        bit = 2 if axis == "gy" else 1
        while bit < lax.axis_size(axis):
            total = total + exchange(total, axis, bit)
            bit *= 2
    other = exchange(total, "gy", 1)
    return jnp.concatenate(
        [jnp.where(odd, other, total), jnp.where(odd, total, other)], axis=0
    )


def per_device(left_core, right_core):
    rank_left, points_local, rank_mid = left_core.shape
    rank_right = right_core.shape[2]
    devices = lax.axis_size("gx") * lax.axis_size("gy") * lax.axis_size("gz")
    total_points = points_local * devices
    unfold = left_core.reshape(rank_left * points_local, rank_mid)
    gram_top = sum_by_scatter(gram_of(unfold[:, :RK], unfold), devices)
    lower_one = jnp.linalg.cholesky(gram_top[:, :RK])
    upper_rest = lax.linalg.triangular_solve(
        lower_one, gram_top[:, RK:], left_side=True, lower=True
    )
    upper_top = jnp.concatenate([lower_one.T, upper_rest], axis=1)
    absorbed = jnp.dot(
        upper_top,
        right_core.reshape(rank_mid, points_local * rank_right),
        precision=lax.Precision.HIGHEST,
        preferred_element_type=jnp.float32,
    )
    rows = absorbed.reshape(RK * points_local, rank_right)
    summed = sum_by_butterfly(gram_of(rows, rows))
    ortho_cols = lax.linalg.triangular_solve(
        lower_one, unfold[:, :RK], left_side=False, lower=True, transpose_a=True
    )
    left_out = (ortho_cols * math.sqrt(rank_left * total_points)).reshape(
        rank_left, points_local, RK
    )
    factor = jnp.linalg.cholesky(summed / (RK * total_points)).T
    right_out = absorbed.reshape(RK, points_local, rank_right)
    return (left_out, right_out, factor)


def solution(mesh):
    in_specs = (P(None, AXES, None), P(None, AXES, None))
    out_specs = (P(None, AXES, None), P(None, AXES, None), P())
    return jax.shard_map(
        per_device, mesh=mesh, in_specs=in_specs, out_specs=out_specs, check_vma=False
    )
```

time: 373 us -> 140 us (0.38); the launches traced: 367 us -> 139 us
  waiting for transfers between devices: 224 us -> 17.6 us
  other arithmetic: 81.6 us -> 57.1 us
  blocking collectives: 0 us -> 15.5 us
  between operations: 17.3 us -> 2.2 us
  starting transfers between devices: 0.25 us -> 9.95 us
  matrix products: 27.6 us -> 21 us
    psum x2 -> x0, waiting for transfers between devices: 224 us -> none  [the longest x1 120 us: per_device(): lax.psum(gram_of(unfold), ('gx', 'gy', 'gz'))]
    another operation x8 -> x4, other arithmetic: 44 us -> 22.2 us  [the longest x3 12.4 us: per_device(): lower_one = jnp.linalg.cholesky(gram_top[:, :RK])]
    ppermute x0 -> x6, waiting for transfers between devices: none -> 17.3 us  [exchange(): return lax.ppermute(value, axis, [(i, i ^ bit) for i in range(size)])]
    all_to_all x0 -> x1, blocking collectives: none -> 15.5 us  [sum_by_scatter(): mine = jnp.sum(lax.all_to_all(blocks, AXES, 0, 0), axis=0)]
    ppermute x0 -> x6, starting transfers between devices: none -> 7.2 us  [exchange(): return lax.ppermute(value, axis, [(i, i ^ bit) for i in range(size)])]
    dot_general x3, matrix products: 21.8 us -> 16.9 us  [the longest x2 12.2 us: gram_of(): lax.dot_general(lhs_rows, matrix_rows, (((0,), (0,)), ((), ())), precisio...]
    another operation x7 -> x6, other arithmetic: 34.7 us -> 34 us  [per_device(): factor = jnp.linalg.cholesky(summed / (RK * total_points)).T]
    unnamed x3 -> x5, local copies, waits for them, and re-layouts: 10.7 us -> 10.7 us
  transfers between devices with their start and end apart: 2 -> 7, of which waited for: 2 -> 6; matrix products, arithmetic and copies ran while one was open for 8% -> 12% of each run, Pallas kernels for 0% -> 0%
where the time goes in v1:
time: 140 us; the launch traced here: 139 us
  other arithmetic  57.1 us (41%)
  matrix products  21 us (15%)
  waiting for transfers between devices  17.6 us (13%)
  local copies, waits for them, and re-layouts  16 us (11%)
  blocking collectives  15.5 us (11%)
  starting transfers between devices  9.95 us (7%)
  between operations  2.2 us (2%)
    another operation x6, other arithmetic, per_device(): factor = jnp.linalg.cholesky(summed / (RK * total_points)).T  34 us
    ppermute x6, waiting for transfers between devices, exchange(): return lax.ppermute(value, axis, [(i, i ^ bit) for i in range(size)])  17.3 us
    all_to_all x1, blocking collectives, sum_by_scatter(): mine = jnp.sum(lax.all_to_all(blocks, AXES, 0, 0), axis=0)  15.5 us
    another operation x3, other arithmetic, per_device(): lower_one = jnp.linalg.cholesky(gram_top[:, :RK])  12.4 us
    dot_general x2, matrix products, gram_of(): lax.dot_general(lhs_rows, matrix_rows, (((0,), (0,)), ((), ())), precisio...  12.2 us
    unnamed x5, local copies, waits for them, and re-layouts  10.7 us
    another operation x1, other arithmetic, per_device(): lax.linalg.triangular_solve(lower_one, unfold[:, :RK], left_side=False, l...  9.81 us
    ppermute x6, starting transfers between devices, exchange(): return lax.ppermute(value, axis, [(i, i ^ bit) for i in range(size)])  7.2 us
  transfers between devices with their start and end apart: 7, of which 6 were waited for; matrix products, arithmetic and copies ran while one was open for 12% of the time, Pallas kernels for 0%

profile of v1, /device:TPU:0, one launch (start us, length us, event | category | flops | bytes accessed | tf_op | source)
XLA Modules:
  0.0 139.4 jit_solution(125047604488553552)
XLA Ops:
  0.6 6.3 %fusion.2 = f32[128,256]{1,0:T(8,128)S(1)} fusion(f32[4096,256]{1,0:T(8,128)} %bitcast.50), kind=kOutput, calls=%fused_computation.3 | convolution fusion | flops 1610612736 | bytes 6422528 | tf_op jit(solution)/shard_map/dot_general | solution.py:13
  7.0 15.5 %all_to_all.10 = f32[32,8,128]{2,1,0:T(8,128)S(1)} all-to-all(f32[32,8,128]{2,1,0:T(8,128)S(1)} %maximum_bitcast_fusion), channel_id=1, replica_groups=mesh['gx'=2,'gy'=4,'gz'=4] {'gx','gy','gz'}, dimensions={0} | all-to-all | bytes 262144 | tf_op jit(solution)/shard_map/all_to_all | solution.py:26
  23.2 2.8 %all-to-all-start.1 = ((f32[32,8,128]{2,1,0:T(8,128)}), f32[32,8,128]{2,1,0:T(8,128)S(1)}, u32[]{:S(2)}, u32[]{:S(2)}) async-start(f32[32,8,128]{2,1,0:T(8,128)} %broadcast_in_dim.4), calls=%async_computation.1 | async-start | bytes 262144 | tf_op jit(solution)/shard_map/all_to_all | solution.py:28
  26.0 7.9 %copy.18 = f32[32,8,16,256]{3,1,2,0:T(8,128)} copy(f32[32,8,16,256]{3,2,1,0:T(8,128)} %bitcast.53) | data formatting | bytes 8388608
  34.3 11.7 %cholesky.52 = f32[128,128]{1,0:T(8,128)S(1)} custom-call(f32[128,128]{1,0:T(8,128)S(1)} %fusion.15), custom_call_target="Cholesky" | custom-call | tf_op jit(solution)/shard_map/jit(cholesky)/cholesky | solution.py:61
  47.4 9.8 %custom-call.19 = f32[1,128,128]{1,2,0:T(8,128)S(1)} custom-call(f32[1,128,128]{2,1,0:T(8,128)S(1)} %get-tuple-element.18), custom_call_target="InvertDiagBlocksLowerTriangular" | custom-call | tf_op jit(solution)/shard_map/triangular_solve | solution.py:74
  57.5 4.7 %fusion.5 = f32[128,4096]{1,0:T(8,128)S(1)} fusion(f32[256,4096]{1,0:T(8,128)} %bitcast.52, f32[128,128]{0,1:T(8,128)S(1)} %fusion.11, f32[128,128]{0,1:T(8,128)S(1)} %get-tuple-element.17), kind=kOutput, calls=%fused_computation.12 | convolution fusion | flops 1610645504 | bytes 6422528 | tf_op jit(solution)/shard_map/dot_general | solution.py:66
  62.2 1.5 %reshape.56 = f32[2048,256]{1,0:T(8,128)} reshape(f32[128,4096]{1,0:T(8,128)S(1)} %fusion.5) | data formatting | bytes 4194304 | tf_op jit(solution)/shard_map/reshape | solution.py:72
  63.7 5.8 %fusion.19 = f32[256,256]{0,1:T(8,128)S(1)} fusion(f32[2048,256]{1,0:T(8,128)} %reshape.56), kind=kOutput, calls=%fused_computation.46 | convolution fusion | flops 1610612736 | bytes 2359296 | tf_op jit(solution)/shard_map/dot_general | solution.py:13
  69.6 1.3 collective-permute-done
  71.0 1.4 %collective-permute-start.1 = (f32[128,256]{0,1:T(8,128)S(1)}, f32[128,256]{0,1:T(8,128)S(1)}, u32[]{:S(2)}, u32[]{:S(2)}) collective-permute-start(f32[128,256]{0,1:T(8,128)S(1)} %select_add_fusion), channel_id=1, source_target_pairs={{0,16},{16,0},{1,17},{17,1},{2,18},{18,2},{3,19},{19,3},{4,20},{20... | collective-permute-start | bytes 393224 | tf_op jit(solution)/shard_map/ppermute | solution.py:34
  72.4 4.2 %collective-permute-done.1 = f32[128,256]{0,1:T(8,128)S(1)} collective-permute-done((f32[128,256]{0,1:T(8,128)S(1)}, f32[128,256]{0,1:T(8,128)S(1)}, u32[]{:S(2)}, u32[]{:S(2)}) %collective-permute-start.1) | collective-permute-done | bytes 131104 | tf_op jit(solution)/shard_map/ppermute | solution.py:34
  76.6 1.4 %collective-permute-start.2 = (f32[128,256]{0,1:T(8,128)S(1)}, f32[128,256]{0,1:T(8,128)S(1)}, u32[]{:S(2)}, u32[]{:S(2)}) collective-permute-start(f32[128,256]{0,1:T(8,128)S(1)} %add.55), channel_id=1, source_target_pairs={{0,8},{4,12},{8,0},{12,4},{1,9},{5,13},{9,1},{13,5},{2,10},{6,14},... | collective-permute-start | bytes 393224 | tf_op jit(solution)/shard_map/ppermute | solution.py:34
  78.1 3.6 %collective-permute-done.2 = f32[128,256]{0,1:T(8,128)S(1)} collective-permute-done((f32[128,256]{0,1:T(8,128)S(1)}, f32[128,256]{0,1:T(8,128)S(1)}, u32[]{:S(2)}, u32[]{:S(2)}) %collective-permute-start.2) | collective-permute-done | bytes 131104 | tf_op jit(solution)/shard_map/ppermute | solution.py:34
  81.7 1.5 %collective-permute-start.3 = (f32[128,256]{0,1:T(8,128)S(1)}, f32[128,256]{0,1:T(8,128)S(1)}, u32[]{:S(2)}, u32[]{:S(2)}) collective-permute-start(f32[128,256]{0,1:T(8,128)S(1)} %add.56), channel_id=1, source_target_pairs={{0,1},{1,0},{2,3},{3,2},{4,5},{5,4},{6,7},{7,6},{8,9},{9,8},{10,11... | collective-permute-start | bytes 393224 | tf_op jit(solution)/shard_map/ppermute | solution.py:34
  83.2 3.6 %collective-permute-done.3 = f32[128,256]{0,1:T(8,128)S(1)} collective-permute-done((f32[128,256]{0,1:T(8,128)S(1)}, f32[128,256]{0,1:T(8,128)S(1)}, u32[]{:S(2)}, u32[]{:S(2)}) %collective-permute-start.3) | collective-permute-done | bytes 131104 | tf_op jit(solution)/shard_map/ppermute | solution.py:34
  86.7 2.8 %collective-permute-start.4 = (f32[128,256]{0,1:T(8,128)S(1)}, f32[128,256]{0,1:T(8,128)S(1)}, u32[]{:S(2)}, u32[]{:S(2)}) collective-permute-start(f32[128,256]{0,1:T(8,128)S(1)} %add.57), channel_id=1, source_target_pairs={{0,2},{1,3},{2,0},{3,1},{4,6},{5,7},{6,4},{7,5},{8,10},{9,11},{10,... | collective-permute-start | bytes 393224 | tf_op jit(solution)/shard_map/ppermute | solution.py:34
  89.5 4.6 %collective-permute-done.4 = f32[128,256]{0,1:T(8,128)S(1)} collective-permute-done((f32[128,256]{0,1:T(8,128)S(1)}, f32[128,256]{0,1:T(8,128)S(1)}, u32[]{:S(2)}, u32[]{:S(2)}) %collective-permute-start.4) | collective-permute-done | bytes 131104 | tf_op jit(solution)/shard_map/ppermute | solution.py:34
  94.2 3.3 %fusion = f32[4096,128]{0,1:T(8,128)} fusion(f32[4096,256]{1,0:T(8,128)S(1)} %bitcast.51, f32[1,128,128]{1,2,0:T(8,128)S(1)} %custom-call.19), kind=kOutput, calls=%fused_computation.1 | convolution fusion | flops 805830656 | bytes 4259840 | tf_op jit(solution)/shard_map/triangular_solve | solution.py:74
  97.5 2.0 %copy.19 = f32[16,8,16,256]{3,2,1,0:T(8,128)} copy(f32[16,8,16,256]{3,1,2,0:T(8,128)S(1)} %bitcast.49) | data formatting | bytes 4194304
  99.5 2.9 %copy.12 = f32[4096,128]{1,0:T(8,128)} copy(f32[4096,128]{0,1:T(8,128)} %fusion) | data formatting | bytes 4194304 | tf_op jit(solution)/shard_map/mul | solution.py:77
  102.6 11.7 %cholesky.104 = f32[128,128]{1,0:T(8,128)S(1)} custom-call(f32[128,128]{1,0:T(8,128)S(1)} %cholesky.130), custom_call_target="Cholesky" | custom-call | tf_op jit(solution)/shard_map/jit(cholesky)/cholesky | solution.py:80
  114.4 9.8 %custom-call.20 = f32[1,128,128]{1,2,0:T(8,128)S(1)} custom-call(f32[1,128,128]{2,1,0:T(8,128)S(1)} %get-tuple-element.16), custom_call_target="InvertDiagBlocksLowerTriangular" | custom-call | tf_op jit(solution)/shard_map/jit(cholesky)/cholesky | solution.py:80
  124.7 11.7 %cholesky.117 = f32[128,128]{1,0:T(8,128)S(1)} custom-call(f32[128,128]{1,0:T(8,128)S(1)} %convolution_subtract_fusion), custom_call_target="Cholesky" | custom-call | tf_op jit(solution)/shard_map/jit(cholesky)/cholesky | solution.py:80
  (36 shorter events, 5.4 us)
Async XLA Ops:
  23.2 11.0 %all-to-all-start.1 = ((f32[32,8,128]{2,1,0:T(8,128)}), f32[32,8,128]{2,1,0:T(8,128)S(1)}, u32[]{:S(2)}, u32[]{:S(2)}) async-start(f32[32,8,128]{2,1,0:T(8,128)} %broadcast_in_dim.4), calls=%async_computation.1 | async-start | bytes 262144 | tf_op jit(solution)/shard_map/all_to_all | solution.py:28
  63.7 30.5 %copy-start = (f32[256,16,256]{2,1,0:T(8,128)S(1)}, f32[256,16,256]{2,1,0:T(8,128)}, u32[]{:S(2)}) copy-start(f32[256,16,256]{2,1,0:T(8,128)} %param.2) | copy-start | bytes 12582916
  69.6 1.4 %collective-permute-start = (f32[128,256]{0,1:T(8,128)S(1)}, f32[128,256]{0,1:T(8,128)S(1)}, u32[]{:S(2)}, u32[]{:S(2)}) collective-permute-start(f32[128,256]{0,1:T(8,128)S(1)} %slice_select_fusion), channel_id=1, source_target_pairs={{0,4},{4,0},{8,12},{12,8},{1,5},{5,1},{9,13},{13,9},{2,6},{6,2},{1... | collective-permute-start | bytes 393224 | tf_op jit(solution)/shard_map/ppermute | solution.py:34
  71.0 5.6 %collective-permute-start.1 = (f32[128,256]{0,1:T(8,128)S(1)}, f32[128,256]{0,1:T(8,128)S(1)}, u32[]{:S(2)}, u32[]{:S(2)}) collective-permute-start(f32[128,256]{0,1:T(8,128)S(1)} %select_add_fusion), channel_id=1, source_target_pairs={{0,16},{16,0},{1,17},{17,1},{2,18},{18,2},{3,19},{19,3},{4,20},{20... | collective-permute-start | bytes 393224 | tf_op jit(solution)/shard_map/ppermute | solution.py:34
  76.6 5.0 %collective-permute-start.2 = (f32[128,256]{0,1:T(8,128)S(1)}, f32[128,256]{0,1:T(8,128)S(1)}, u32[]{:S(2)}, u32[]{:S(2)}) collective-permute-start(f32[128,256]{0,1:T(8,128)S(1)} %add.55), channel_id=1, source_target_pairs={{0,8},{4,12},{8,0},{12,4},{1,9},{5,13},{9,1},{13,5},{2,10},{6,14},... | collective-permute-start | bytes 393224 | tf_op jit(solution)/shard_map/ppermute | solution.py:34
  81.7 5.0 %collective-permute-start.3 = (f32[128,256]{0,1:T(8,128)S(1)}, f32[128,256]{0,1:T(8,128)S(1)}, u32[]{:S(2)}, u32[]{:S(2)}) collective-permute-start(f32[128,256]{0,1:T(8,128)S(1)} %add.56), channel_id=1, source_target_pairs={{0,1},{1,0},{2,3},{3,2},{4,5},{5,4},{6,7},{7,6},{8,9},{9,8},{10,11... | collective-permute-start | bytes 393224 | tf_op jit(solution)/shard_map/ppermute | solution.py:34
  86.7 7.3 %collective-permute-start.4 = (f32[128,256]{0,1:T(8,128)S(1)}, f32[128,256]{0,1:T(8,128)S(1)}, u32[]{:S(2)}, u32[]{:S(2)}) collective-permute-start(f32[128,256]{0,1:T(8,128)S(1)} %add.57), channel_id=1, source_target_pairs={{0,2},{1,3},{2,0},{3,1},{4,6},{5,7},{6,4},{7,5},{8,10},{9,11},{10,... | collective-permute-start | bytes 393224 | tf_op jit(solution)/shard_map/ppermute | solution.py:34
  94.1 8.3 %collective-permute-start.5 = (f32[128,256]{0,1:T(8,128)S(1)}, f32[128,256]{0,1:T(8,128)S(1)}, u32[]{:S(2)}, u32[]{:S(2)}) collective-permute-start(f32[128,256]{0,1:T(8,128)S(1)} %add.58), channel_id=1, source_target_pairs={{0,4},{4,0},{8,12},{12,8},{1,5},{5,1},{9,13},{13,9},{2,6},{6,2},{1... | collective-permute-start | bytes 393224 | tf_op jit(solution)/shard_map/ppermute | solution.py:34

commit v2 on v0

v2 whole, which is shorter than its diff:
```python
import functools
import math

import jax
import jax.numpy as jnp
from jax import lax
from jax.experimental import pallas as pl
from jax.experimental.pallas import tpu as pltpu
from jax.sharding import PartitionSpec as P

RK = 128
AXES = ("gx", "gy", "gz")
LANES = 128
PANEL = 16
SPREAD_ONE = 4
SPREAD_TWO = 2
F32 = jnp.float32
BF16 = jnp.bfloat16
VMEM_LIMIT = 48 * 1024 * 1024


def split(x):
    hi = x.astype(BF16)
    return hi, (x - hi.astype(F32)).astype(BF16)


def dot_tn(a, b):
    return lax.dot_general(a, b, (((0,), (0,)), ((), ())), preferred_element_type=F32)


def dot_nt(a, b):
    return lax.dot_general(a, b, (((1,), (1,)), ((), ())), preferred_element_type=F32)


def dot_nn(a, b):
    return lax.dot_general(a, b, (((1,), (0,)), ((), ())), preferred_element_type=F32)


def stacked_pieces(x):
    one = x.astype(BF16).astype(F32)
    rest = x - one
    two = rest.astype(BF16).astype(F32)
    three = rest - two
    left = jnp.concatenate([one, one, two, two, one, three], axis=0).astype(BF16)
    right = jnp.concatenate([one, two, one, two, three, one], axis=0).astype(BF16)
    return left, right


def factor_rows(w_ref, blocks):
    row_id = lax.broadcasted_iota(jnp.int32, (PANEL, LANES), 0)
    for start in range(0, LANES, PANEL):
        rows = [w_ref[start : start + PANEL, b * LANES : (b + 1) * LANES] for b in range(blocks)]
        columns = [
            jnp.broadcast_to(rows[0][:, start + k : start + k + 1], (PANEL, LANES))
            for k in range(PANEL)
        ]
        scale = jnp.zeros((PANEL, LANES), F32)
        for k in range(PANEL):
            pivot = jnp.broadcast_to(columns[k][k : k + 1, :], (PANEL, LANES))
            inverse = lax.rsqrt(pivot)
            inverse = inverse * (1.5 - 0.5 * pivot * inverse * inverse)
            multiples = columns[k] * inverse
            for m in range(k + 1, PANEL):
                columns[m] = columns[m] - multiples * multiples[m : m + 1, :]
            below = jnp.where(row_id > k, multiples * inverse, 0.0)
            rows = [r - below * r[k : k + 1, :] for r in rows]
            scale = jnp.where(row_id == k, inverse, scale)
        rows = [r * scale for r in rows]
        for b in range(blocks):
            w_ref[start : start + PANEL, b * LANES : (b + 1) * LANES] = rows[b]
        if start + PANEL < LANES:
            both = [stacked_pieces(r) for r in rows]
            left = both[0][0]
            right = jnp.concatenate([b[1] for b in both], axis=1)
            update = dot_tn(left, right)
            w_ref[start + PANEL :, :] = w_ref[start + PANEL :, :] - update[start + PANEL :, :]


def triangle_ids():
    return (
        lax.broadcasted_iota(jnp.int32, (LANES, LANES), 0),
        lax.broadcasted_iota(jnp.int32, (LANES, LANES), 1),
    )


def store_blocks(tall_ref, outs):
    me = lax.rem(lax.axis_index("gy"), len(outs))
    size = outs[0].shape[0]
    for d, out in enumerate(outs):
        out[...] = tall_ref[pl.ds(pl.multiple_of((me ^ d) * size, 8), size), :]


def load_blocks(blocks, tall_ref):
    me = lax.rem(lax.axis_index("gy"), len(blocks))
    size = blocks[0].shape[0]
    for d, block in enumerate(blocks):
        tall_ref[pl.ds(pl.multiple_of((me ^ d) * size, 8), size), :] = block[...]


def gram_kernel(a_ref, *refs):
    outs, tall_ref = refs[:-1], refs[-1]
    step = pl.program_id(0)

    @pl.when(step == 0)
    def _():
        tall_ref[...] = jnp.zeros_like(tall_ref)

    hi, lo = split(a_ref[...])
    both = dot_tn(hi[:, :RK], jnp.concatenate([hi, lo], axis=1))
    top = both[:, :256] + both[:, 256:] + dot_tn(lo[:, :RK], hi)
    tall_ref[:RK, :] += top[:, :RK]
    tall_ref[RK:, :] += top[:, RK:]

    @pl.when(step == pl.num_programs(0) - 1)
    def _():
        store_blocks(tall_ref, outs)


def relay_kernel(points, left_ref, right_ref, hi_ref, lo_ref):
    count = left_ref.shape[0] // points
    for p in range(points):
        for c, half in enumerate((left_ref, right_ref)):
            hi, lo = split(half[pl.ds(p, count, stride=points), :])
            hi_ref[p, :, c * LANES : (c + 1) * LANES] = hi
            lo_ref[p, :, c * LANES : (c + 1) * LANES] = lo


def absorb_kernel(scale, n_in, n_out, *refs):
    blocks = refs[:n_in]
    hi_hbm, lo_hbm = refs[n_in : n_in + 2]
    absorbed_ref, linv_ref = refs[n_in + 2 : n_in + 4]
    outs = refs[n_in + 4 : n_in + 4 + n_out]
    tall_ref, w_ref, hi_ref, lo_ref, pack_ref, sems = refs[n_in + 4 + n_out :]
    copy_hi = pltpu.make_async_copy(hi_hbm, hi_ref, sems.at[0])
    copy_lo = pltpu.make_async_copy(lo_hbm, lo_ref, sems.at[1])
    copy_hi.start()
    copy_lo.start()
    load_blocks(blocks, tall_ref)
    row, col = triangle_ids()
    w_ref[:, :LANES] = tall_ref[:RK, :]
    w_ref[:, LANES : 2 * LANES] = tall_ref[RK:, :]
    w_ref[:, 2 * LANES :] = jnp.where(row == col, 1.0, 0.0).astype(F32)
    factor_rows(w_ref, 3)
    linv_ref[...] = w_ref[:, 2 * LANES :] * scale
    upper = jnp.concatenate(
        [jnp.where(col >= row, w_ref[:, :LANES], 0.0), w_ref[:, LANES : 2 * LANES]], axis=1
    )
    upper_hi, upper_lo = split(upper)
    upper_both = jnp.concatenate([upper_hi, upper_lo], axis=0)
    copy_hi.wait()
    copy_lo.wait()
    points = hi_ref.shape[0]

    def body(p, total):
        high = hi_ref[p]
        first = dot_nn(upper_both, high)
        b = first[:RK, :] + first[RK:, :] + dot_nn(upper_hi, lo_ref[p])
        absorbed_ref[p] = b
        b_hi, b_lo = split(b)
        return total + dot_tn(b_hi, jnp.concatenate([b_hi, b_lo], axis=1))

    total = lax.fori_loop(0, points, body, jnp.zeros((256, 512), F32), unroll=2)
    cross = total[:, 256:]
    gram = total[:, :256] + cross + cross.T
    lower_right = gram[LANES:, LANES:]
    pack_ref[:LANES, :] = jnp.where(col >= row, gram[:LANES, :LANES], lower_right)
    pack_ref[LANES : 2 * LANES, :] = gram[:LANES, LANES:]
    diagonal = jnp.sum(jnp.where(row == col, lower_right, 0.0), axis=0, keepdims=True)
    tail = pack_ref.shape[0] - 2 * LANES
    pack_ref[2 * LANES :, :] = jnp.broadcast_to(diagonal, (tail, LANES))
    store_blocks(pack_ref, outs)


def outputs_kernel(points, a_ref, linv_ref, absorbed_ref, left_ref, right_ref):
    l_hi, l_lo = split(linv_ref[...])
    hi, lo = split(a_ref[...])
    left_ref[...] = dot_nt(hi, l_hi) + dot_nt(hi, l_lo) + dot_nt(lo, l_hi)
    count = absorbed_ref.shape[1]
    for p in range(points):
        right_ref[pl.ds(p, count, stride=points), :] = absorbed_ref[p]


def factor_kernel(scale, n_in, *refs):
    blocks, out_ref = refs[:n_in], refs[n_in]
    pack_ref, w_ref, rest_ref = refs[n_in + 1 :]
    load_blocks(blocks, pack_ref)
    row, col = triangle_ids()
    packed = pack_ref[:LANES, :] * scale
    turned = packed.T
    diagonal = jnp.broadcast_to(pack_ref[2 * LANES : 2 * LANES + 1, :], (LANES, LANES)) * scale
    w_ref[:, :LANES] = jnp.where(col >= row, packed, turned)
    w_ref[:, LANES:] = pack_ref[LANES : 2 * LANES, :] * scale
    rest_ref[...] = jnp.where(row > col, packed, jnp.where(row == col, diagonal, turned))
    factor_rows(w_ref, 2)
    out_ref[:LANES, :LANES] = jnp.where(col >= row, w_ref[:, :LANES], 0.0)
    out_ref[:LANES, LANES:] = w_ref[:, LANES:]
    left, right = stacked_pieces(w_ref[:, LANES:])
    rest_ref[...] = rest_ref[...] - dot_tn(left, right)
    factor_rows(rest_ref, 1)
    out_ref[LANES:, :LANES] = jnp.zeros((LANES, LANES), F32)
    out_ref[LANES:, LANES:] = jnp.where(col >= row, rest_ref[...], 0.0)


def exchange(value, axis, bit):
    size = lax.axis_size(axis)
    return lax.ppermute(value, axis, [(i, i ^ bit) for i in range(size)])


def sum_over_devices(blocks):
    n = len(blocks)
    total = blocks[0]
    for d in range(1, n):
        total = total + exchange(blocks[d], "gy", d)
    for axis in AXES:
        bit = n if axis == "gy" else 1
        while bit < lax.axis_size(axis):
            total = total + exchange(total, axis, bit)
            bit *= 2
    return [total] + [exchange(total, "gy", d) for d in range(1, n)]


def shape(*dims, dtype=F32):
    return jax.ShapeDtypeStruct(dims, dtype)


def params(semantics=None):
    return pltpu.CompilerParams(dimension_semantics=semantics, vmem_limit_bytes=VMEM_LIMIT)


def per_device(left_core, right_core):
    rank_left, points, rank_mid = left_core.shape
    rank_right = right_core.shape[2]
    devices = lax.axis_size("gx") * lax.axis_size("gy") * lax.axis_size("gz")
    total_points = points * devices
    unfold = left_core.reshape(rank_left * points, rank_mid)
    rows_right = right_core.reshape(rank_mid * points, rank_right)
    vmem = pl.BlockSpec(memory_space=pltpu.VMEM)
    anywhere = pl.BlockSpec(memory_space=pl.ANY)

    steps = 8
    chunk = unfold.shape[0] // steps
    size_one = 2 * RK // SPREAD_ONE
    blocks = pl.pallas_call(
        gram_kernel,
        grid=(steps,),
        in_specs=[pl.BlockSpec((chunk, rank_mid), lambda i: (i, 0))],
        out_specs=[pl.BlockSpec((size_one, LANES), lambda i: (0, 0))] * SPREAD_ONE,
        out_shape=[shape(size_one, LANES)] * SPREAD_ONE,
        scratch_shapes=[pltpu.VMEM((2 * RK, LANES), F32)],
        compiler_params=params(("arbitrary",)),
        name="gram_top",
    )(unfold)
    summed = sum_over_devices(blocks)

    ranks = rank_mid // steps
    right_hi, right_lo = pl.pallas_call(
        functools.partial(relay_kernel, points),
        grid=(steps,),
        in_specs=[
            pl.BlockSpec((ranks * points, LANES), lambda i: (i, 0)),
            pl.BlockSpec((ranks * points, LANES), lambda i: (i, 1)),
        ],
        out_specs=[pl.BlockSpec((points, ranks, rank_right), lambda i: (0, i, 0))] * 2,
        out_shape=[shape(points, rank_mid, rank_right, dtype=BF16)] * 2,
        compiler_params=params(("arbitrary",)),
        cost_estimate=pl.CostEstimate(flops=0, bytes_accessed=24 * 2**20, transcendentals=0),
        name="relay_right",
    )(rows_right, rows_right)

    packed_rows = 2 * LANES + 8 * SPREAD_TWO
    size_two = packed_rows // SPREAD_TWO
    absorbed, linv, *blocks = pl.pallas_call(
        functools.partial(
            absorb_kernel, math.sqrt(rank_left * total_points), SPREAD_ONE, SPREAD_TWO
        ),
        in_specs=[vmem] * SPREAD_ONE + [anywhere] * 2,
        out_specs=[vmem] * (2 + SPREAD_TWO),
        out_shape=[shape(points, RK, rank_right), shape(RK, RK)]
        + [shape(size_two, LANES)] * SPREAD_TWO,
        scratch_shapes=[
            pltpu.VMEM((2 * RK, LANES), F32),
            pltpu.VMEM((LANES, 3 * LANES), F32),
            pltpu.VMEM((points, rank_mid, rank_right), BF16),
            pltpu.VMEM((points, rank_mid, rank_right), BF16),
            pltpu.VMEM((packed_rows, LANES), F32),
            pltpu.SemaphoreType.DMA((2,)),
        ],
        compiler_params=params(),
        name="factor_absorb",
    )(*summed, right_hi, right_lo)
    summed = sum_over_devices(blocks)

    ranks = 2 * RK // steps
    left_out, right_out = pl.pallas_call(
        functools.partial(outputs_kernel, points),
        grid=(steps // 2, 2),
        in_specs=[
            pl.BlockSpec((chunk, RK), lambda i, c: (2 * i + c, 0)),
            pl.BlockSpec((RK, RK), lambda i, c: (0, 0)),
            pl.BlockSpec((points, ranks, LANES), lambda i, c: (0, i, c)),
        ],
        out_specs=[
            pl.BlockSpec((chunk, RK), lambda i, c: (2 * i + c, 0)),
            pl.BlockSpec((ranks * points, LANES), lambda i, c: (i, c)),
        ],
        out_shape=[shape(rank_left * points, RK), shape(RK * points, rank_right)],
        compiler_params=params(("arbitrary", "arbitrary")),
        cost_estimate=pl.CostEstimate(flops=0, bytes_accessed=24 * 2**20, transcendentals=0),
        name="outputs",
    )(unfold, linv, absorbed)

    factor = pl.pallas_call(
        functools.partial(factor_kernel, 1.0 / (RK * total_points), SPREAD_TWO),
        in_specs=[vmem] * SPREAD_TWO,
        out_specs=vmem,
        out_shape=shape(rank_right, rank_right),
        scratch_shapes=[
            pltpu.VMEM((packed_rows, LANES), F32),
            pltpu.VMEM((LANES, 2 * LANES), F32),
            pltpu.VMEM((LANES, LANES), F32),
        ],
        compiler_params=params(),
        name="factor_next",
    )(*summed)
    return (
        left_out.reshape(rank_left, points, RK),
        right_out.reshape(RK, points, rank_right),
        factor,
    )


def solution(mesh):
    in_specs = (P(None, AXES, None), P(None, AXES, None))
    out_specs = (P(None, AXES, None), P(None, AXES, None), P())
    return jax.shard_map(
        per_device, mesh=mesh, in_specs=in_specs, out_specs=out_specs, check_vma=False
    )
```

time: 373 us -> 79.6 us (0.21); the launches traced: 367 us -> 79.2 us
  waiting for transfers between devices: 224 us -> 22.9 us
  other arithmetic: 81.6 us -> 0.08 us
  Pallas kernels: 0 us -> 33.8 us
  matrix products: 27.6 us -> 0 us
  starting transfers between devices: 0.25 us -> 18.1 us
  between operations: 17.3 us -> 0.72 us
  local copies, waits for them, and re-layouts: 16.6 us -> 3.5 us
    psum x2 -> x0, waiting for transfers between devices: 224 us -> none  [the longest x1 120 us: per_device(): lax.psum(gram_of(unfold), ('gx', 'gy', 'gz'))]
    another operation x15 -> x0, other arithmetic: 78.6 us -> none  [the longest x7 34.7 us: per_device(): factor = jnp.linalg.cholesky(summed / (RK * total_points)).T]
    pallas_call x0 -> x5, Pallas kernels: none -> 33.8 us  [the longest x1 9.88 us: per_device(): pl.pallas_call(functools.partial(absorb_kernel, math.sqrt(rank_left * tot...]
    ppermute x0 -> x15, waiting for transfers between devices: none -> 22.9 us  [exchange(): return lax.ppermute(value, axis, [(i, i ^ bit) for i in range(size)])]
    dot_general x3 -> x0, matrix products: 21.8 us -> none  [the longest x2 17.3 us: gram_of(): lax.dot_general(matrix_rows, matrix_rows, (((0,), (0,)), ((), ())), preci...]
    ppermute x0 -> x15, starting transfers between devices: none -> 18.1 us  [exchange(): return lax.ppermute(value, axis, [(i, i ^ bit) for i in range(size)])]
    unnamed x3 -> x4, local copies, waits for them, and re-layouts: 10.7 us -> 3.5 us
    another operation x5 -> x0, matrix products: 5.84 us -> none  [the longest x1 4.9 us: per_device(): lax.linalg.triangular_solve(lower_one[:RK, :RK], unfold[:, :RK], left_sid...]
  transfers between devices with their start and end apart: 2 -> 15, of which waited for: 2 -> 10; matrix products, arithmetic and copies ran while one was open for 8% -> 0% of each run, Pallas kernels for 0% -> 16%
where the time goes in v2:
time: 79.6 us; the launch traced here: 79.2 us
  Pallas kernels  33.8 us (42%)
  waiting for transfers between devices  22.9 us (29%)
  starting transfers between devices  18.1 us (23%)
  local copies, waits for them, and re-layouts  3.5 us (4%)
    ppermute x15, waiting for transfers between devices, exchange(): return lax.ppermute(value, axis, [(i, i ^ bit) for i in range(size)])  22.9 us
    ppermute x15, starting transfers between devices, exchange(): return lax.ppermute(value, axis, [(i, i ^ bit) for i in range(size)])  18.1 us
    pallas_call x1, Pallas kernels, per_device(): pl.pallas_call(functools.partial(absorb_kernel, math.sqrt(rank_left * tot...  9.88 us
    pallas_call x1, Pallas kernels, per_device(): pl.pallas_call(functools.partial(factor_kernel, 1.0 / (RK * total_points)...  8.95 us
    pallas_call x1, Pallas kernels, per_device(): pl.pallas_call(functools.partial(outputs_kernel, points), grid=(steps //...  6.82 us
    pallas_call x1, Pallas kernels, per_device(): pl.pallas_call(functools.partial(relay_kernel, points), grid=(steps,), in...  5.47 us
    unnamed x4, local copies, waits for them, and re-layouts  3.5 us
    pallas_call x1, Pallas kernels, per_device(): pl.pallas_call(gram_kernel, grid=(steps,), in_specs=[pl.BlockSpec((chunk,...  2.7 us
  transfers between devices with their start and end apart: 15, of which 10 were waited for; matrix products, arithmetic and copies ran while one was open for 0% of the time, Pallas kernels for 16%

profile of v2, /device:TPU:0, one launch (start us, length us, event | category | flops | bytes accessed | tf_op | source)
XLA Modules:
  0.0 79.2 jit_solution(8658362050893147595)
XLA Ops:
  0.6 2.2 %copy-done = f32[256,16,256]{2,1,0:T(8,128)S(1)} copy-done((f32[256,16,256]{2,1,0:T(8,128)S(1)}, f32[256,16,256]{2,1,0:T(8,128)}, u32[]{:S(2)}) %copy-start) | copy-done | bytes 4194328
  2.8 2.7 %gram_top.1 = (f32[64,128]{1,0:T(8,128)S(1)}, f32[64,128]{1,0:T(8,128)S(1)}, f32[64,128]{1,0:T(8,128)S(1)}, f32[64,128]{1,0:T(8,128)S(1)}) custom-call(f32[4096,256]{1,0:T(8,128)S(1)} %bitcast.5), custom_call_target="tpu_custom_call" | custom-call | tf_op jit(solution)/shard_map/gram_top/pallas_call | solution.py:243
  6.0 2.6 %collective-permute-start.1 = (f32[64,128]{1,0:T(8,128)S(1)}, f32[64,128]{1,0:T(8,128)S(1)}, u32[]{:S(2)}, u32[]{:S(2)}) collective-permute-start(f32[64,128]{1,0:T(8,128)S(1)} %get-tuple-element.17), channel_id=1, source_target_pairs={{0,8},{4,12},{8,0},{12,4},{1,9},{5,13},{9,1},{13,5},{2,10},{6,14},... | collective-permute-start | bytes 98312 | tf_op jit(solution)/shard_map/ppermute | solution.py:206
  8.7 1.9 %collective-permute-done.1 = f32[64,128]{1,0:T(8,128)S(1)} collective-permute-done((f32[64,128]{1,0:T(8,128)S(1)}, f32[64,128]{1,0:T(8,128)S(1)}, u32[]{:S(2)}, u32[]{:S(2)}) %collective-permute-start.1) | collective-permute-done | bytes 32800 | tf_op jit(solution)/shard_map/ppermute | solution.py:206
  10.6 1.4 %collective-permute-done.2 = f32[64,128]{1,0:T(8,128)S(1)} collective-permute-done((f32[64,128]{1,0:T(8,128)S(1)}, f32[64,128]{1,0:T(8,128)S(1)}, u32[]{:S(2)}, u32[]{:S(2)}) %collective-permute-start.2) | collective-permute-done | bytes 32800 | tf_op jit(solution)/shard_map/ppermute | solution.py:206
  12.0 1.6 %collective-permute-start.3 = (f32[64,128]{1,0:T(8,128)S(1)}, f32[64,128]{1,0:T(8,128)S(1)}, u32[]{:S(2)}, u32[]{:S(2)}) collective-permute-start(f32[64,128]{1,0:T(8,128)S(1)} %add_add_fusion), channel_id=1, source_target_pairs={{0,16},{16,0},{1,17},{17,1},{2,18},{18,2},{3,19},{19,3},{4,20},{20... | collective-permute-start | bytes 98312 | tf_op jit(solution)/shard_map/ppermute | solution.py:206
  13.6 2.4 %collective-permute-done.3 = f32[64,128]{1,0:T(8,128)S(1)} collective-permute-done((f32[64,128]{1,0:T(8,128)S(1)}, f32[64,128]{1,0:T(8,128)S(1)}, u32[]{:S(2)}, u32[]{:S(2)}) %collective-permute-start.3) | collective-permute-done | bytes 32800 | tf_op jit(solution)/shard_map/ppermute | solution.py:206
  16.0 1.6 %collective-permute-start.4 = (f32[64,128]{1,0:T(8,128)S(1)}, f32[64,128]{1,0:T(8,128)S(1)}, u32[]{:S(2)}, u32[]{:S(2)}) collective-permute-start(f32[64,128]{1,0:T(8,128)S(1)} %add.36), channel_id=1, source_target_pairs={{0,1},{1,0},{2,3},{3,2},{4,5},{5,4},{6,7},{7,6},{8,9},{9,8},{10,11... | collective-permute-start | bytes 98312 | tf_op jit(solution)/shard_map/ppermute | solution.py:206
  17.6 2.3 %collective-permute-done.4 = f32[64,128]{1,0:T(8,128)S(1)} collective-permute-done((f32[64,128]{1,0:T(8,128)S(1)}, f32[64,128]{1,0:T(8,128)S(1)}, u32[]{:S(2)}, u32[]{:S(2)}) %collective-permute-start.4) | collective-permute-done | bytes 32800 | tf_op jit(solution)/shard_map/ppermute | solution.py:206
  19.9 2.6 %collective-permute-start.5 = (f32[64,128]{1,0:T(8,128)S(1)}, f32[64,128]{1,0:T(8,128)S(1)}, u32[]{:S(2)}, u32[]{:S(2)}) collective-permute-start(f32[64,128]{1,0:T(8,128)S(1)} %add.37), channel_id=1, source_target_pairs={{0,2},{1,3},{2,0},{3,1},{4,6},{5,7},{6,4},{7,5},{8,10},{9,11},{10,... | collective-permute-start | bytes 98312 | tf_op jit(solution)/shard_map/ppermute | solution.py:206
  22.5 2.2 %collective-permute-done.5 = f32[64,128]{1,0:T(8,128)S(1)} collective-permute-done((f32[64,128]{1,0:T(8,128)S(1)}, f32[64,128]{1,0:T(8,128)S(1)}, u32[]{:S(2)}, u32[]{:S(2)}) %collective-permute-start.5) | collective-permute-done | bytes 32800 | tf_op jit(solution)/shard_map/ppermute | solution.py:206
  26.6 5.5 %relay_right.1 = (bf16[16,256,256]{2,1,0:T(8,128)(2,1)S(1)}, bf16[16,256,256]{2,1,0:T(8,128)(2,1)S(1)}) custom-call(f32[4096,256]{1,0:T(8,128)} %bitcast.6, f32[4096,256]{1,0:T(8,128)} %bitcast.7), custom_call_target="tpu_custom_call" | custom-call | bytes 25165824 | tf_op jit(solution)/shard_map/relay_right/pallas_call | solution.py:256
  32.1 1.3 %copy-done.1 = bf16[16,256,256]{2,1,0:T(8,128)(2,1)} copy-done((bf16[16,256,256]{2,1,0:T(8,128)(2,1)}, bf16[16,256,256]{2,1,0:T(8,128)(2,1)S(1)}, u32[]{:S(2)}) %copy-start.1) | copy-done | bytes 2097176
  33.4 9.9 %factor_absorb.1 = (f32[16,128,256]{2,1,0:T(8,128)S(1)}, f32[128,128]{1,0:T(8,128)S(1)}, f32[136,128]{1,0:T(8,128)S(1)}, f32[136,128]{1,0:T(8,128)S(1)}) custom-call(f32[64,128]{1,0:T(8,128)S(1)} %add.38.refs_0_, f32[64,128]{1,0:T(8,128)S(1)} %collective-permute-done.6.refs_1_, f32[64,128]{1,0:T(8,128)S(1)} %collective-permute-done.7.refs_2_, ...), custom_call_target="tpu_custom_call" | custom-call | tf_op jit(solution)/shard_map/factor_absorb/pallas_call | solution.py:272
  43.4 1.2 %collective-permute-done.9 = f32[136,128]{1,0:T(8,128)S(1)} collective-permute-done((f32[136,128]{1,0:T(8,128)S(1)}, f32[136,128]{1,0:T(8,128)S(1)}, u32[]{:S(2)}, u32[]{:S(2)}) %collective-permute-start.9) | collective-permute-done | bytes 69664 | tf_op jit(solution)/shard_map/ppermute | solution.py:206
  44.6 1.6 %collective-permute-start.10 = (f32[136,128]{1,0:T(8,128)S(1)}, f32[136,128]{1,0:T(8,128)S(1)}, u32[]{:S(2)}, u32[]{:S(2)}) collective-permute-start(f32[136,128]{1,0:T(8,128)S(1)} %add.39), channel_id=1, source_target_pairs={{0,16},{16,0},{1,17},{17,1},{2,18},{18,2},{3,19},{19,3},{4,20},{20... | collective-permute-start | bytes 208904 | tf_op jit(solution)/shard_map/ppermute | solution.py:206
  46.2 2.8 %collective-permute-done.10 = f32[136,128]{1,0:T(8,128)S(1)} collective-permute-done((f32[136,128]{1,0:T(8,128)S(1)}, f32[136,128]{1,0:T(8,128)S(1)}, u32[]{:S(2)}, u32[]{:S(2)}) %collective-permute-start.10) | collective-permute-done | bytes 69664 | tf_op jit(solution)/shard_map/ppermute | solution.py:206
  49.8 3.6 %collective-permute-done.11 = f32[136,128]{1,0:T(8,128)S(1)} collective-permute-done((f32[136,128]{1,0:T(8,128)S(1)}, f32[136,128]{1,0:T(8,128)S(1)}, u32[]{:S(2)}, u32[]{:S(2)}) %collective-permute-start.11) | collective-permute-done | bytes 69664 | tf_op jit(solution)/shard_map/ppermute | solution.py:206
  53.4 1.6 %collective-permute-start.12 = (f32[136,128]{1,0:T(8,128)S(1)}, f32[136,128]{1,0:T(8,128)S(1)}, u32[]{:S(2)}, u32[]{:S(2)}) collective-permute-start(f32[136,128]{1,0:T(8,128)S(1)} %add.41), channel_id=1, source_target_pairs={{0,1},{1,0},{2,3},{3,2},{4,5},{5,4},{6,7},{7,6},{8,9},{9,8},{10,11... | collective-permute-start | bytes 208904 | tf_op jit(solution)/shard_map/ppermute | solution.py:206
  55.0 2.7 %collective-permute-done.12 = f32[136,128]{1,0:T(8,128)S(1)} collective-permute-done((f32[136,128]{1,0:T(8,128)S(1)}, f32[136,128]{1,0:T(8,128)S(1)}, u32[]{:S(2)}, u32[]{:S(2)}) %collective-permute-start.12) | collective-permute-done | bytes 69664 | tf_op jit(solution)/shard_map/ppermute | solution.py:206
  57.8 3.2 %collective-permute-start.13 = (f32[136,128]{1,0:T(8,128)S(1)}, f32[136,128]{1,0:T(8,128)S(1)}, u32[]{:S(2)}, u32[]{:S(2)}) collective-permute-start(f32[136,128]{1,0:T(8,128)S(1)} %add.42), channel_id=1, source_target_pairs={{0,2},{1,3},{2,0},{3,1},{4,6},{5,7},{6,4},{7,5},{8,10},{9,11},{10,... | collective-permute-start | bytes 208904 | tf_op jit(solution)/shard_map/ppermute | solution.py:206
  61.0 2.3 %collective-permute-done.13 = f32[136,128]{1,0:T(8,128)S(1)} collective-permute-done((f32[136,128]{1,0:T(8,128)S(1)}, f32[136,128]{1,0:T(8,128)S(1)}, u32[]{:S(2)}, u32[]{:S(2)}) %collective-permute-start.13) | collective-permute-done | bytes 69664 | tf_op jit(solution)/shard_map/ppermute | solution.py:206
  63.4 6.8 %outputs.1 = (f32[4096,128]{1,0:T(8,128)}, f32[2048,256]{1,0:T(8,128)}) custom-call(f32[4096,256]{1,0:T(8,128)} %bitcast.4, f32[128,128]{1,0:T(8,128)S(1)} %get-tuple-element.21.linv_ref, f32[16,128,256]{2,1,0:T(8,128)S(1)} %get-tuple-element.22.absorbed_ref), custom_call_target="tpu_custom_call" | custom-call | bytes 25165824 | tf_op jit(solution)/shard_map/outputs/pallas_call | solution.py:294
  70.2 9.0 %factor_next.1 = f32[256,256]{1,0:T(8,128)} custom-call(f32[136,128]{1,0:T(8,128)S(1)} %add.43.refs_0_, f32[136,128]{1,0:T(8,128)S(1)} %collective-permute-done.14.refs_1_), custom_call_target="tpu_custom_call" | custom-call | tf_op jit(solution)/shard_map/factor_next/pallas_call | solution.py:312
  (24 shorter events, 3.5 us)
Async XLA Ops:
  0.6 2.2 %copy-start = (f32[256,16,256]{2,1,0:T(8,128)S(1)}, f32[256,16,256]{2,1,0:T(8,128)}, u32[]{:S(2)}) copy-start(f32[256,16,256]{2,1,0:T(8,128)} %param.2) | copy-start | bytes 12582916
  5.5 3.2 %collective-permute-start = (f32[64,128]{1,0:T(8,128)S(1)}, f32[64,128]{1,0:T(8,128)S(1)}, u32[]{:S(2)}, u32[]{:S(2)}) collective-permute-start(f32[64,128]{1,0:T(8,128)S(1)} %get-tuple-element.16), channel_id=1, source_target_pairs={{0,4},{4,0},{8,12},{12,8},{1,5},{5,1},{9,13},{13,9},{2,6},{6,2},{1... | collective-permute-start | bytes 98312 | tf_op jit(solution)/shard_map/ppermute | solution.py:206
  6.0 4.6 %collective-permute-start.1 = (f32[64,128]{1,0:T(8,128)S(1)}, f32[64,128]{1,0:T(8,128)S(1)}, u32[]{:S(2)}, u32[]{:S(2)}) collective-permute-start(f32[64,128]{1,0:T(8,128)S(1)} %get-tuple-element.17), channel_id=1, source_target_pairs={{0,8},{4,12},{8,0},{12,4},{1,9},{5,13},{9,1},{13,5},{2,10},{6,14},... | collective-permute-start | bytes 98312 | tf_op jit(solution)/shard_map/ppermute | solution.py:206
  8.6 3.3 %collective-permute-start.2 = (f32[64,128]{1,0:T(8,128)S(1)}, f32[64,128]{1,0:T(8,128)S(1)}, u32[]{:S(2)}, u32[]{:S(2)}) collective-permute-start(f32[64,128]{1,0:T(8,128)S(1)} %get-tuple-element.18), channel_id=1, source_target_pairs={{0,12},{4,8},{8,4},{12,0},{1,13},{5,9},{9,5},{13,1},{2,14},{6,10},... | collective-permute-start | bytes 98312 | tf_op jit(solution)/shard_map/ppermute | solution.py:206
  12.0 4.0 %collective-permute-start.3 = (f32[64,128]{1,0:T(8,128)S(1)}, f32[64,128]{1,0:T(8,128)S(1)}, u32[]{:S(2)}, u32[]{:S(2)}) collective-permute-start(f32[64,128]{1,0:T(8,128)S(1)} %add_add_fusion), channel_id=1, source_target_pairs={{0,16},{16,0},{1,17},{17,1},{2,18},{18,2},{3,19},{19,3},{4,20},{20... | collective-permute-start | bytes 98312 | tf_op jit(solution)/shard_map/ppermute | solution.py:206
  16.0 3.9 %collective-permute-start.4 = (f32[64,128]{1,0:T(8,128)S(1)}, f32[64,128]{1,0:T(8,128)S(1)}, u32[]{:S(2)}, u32[]{:S(2)}) collective-permute-start(f32[64,128]{1,0:T(8,128)S(1)} %add.36), channel_id=1, source_target_pairs={{0,1},{1,0},{2,3},{3,2},{4,5},{5,4},{6,7},{7,6},{8,9},{9,8},{10,11... | collective-permute-start | bytes 98312 | tf_op jit(solution)/shard_map/ppermute | solution.py:206
  19.9 4.8 %collective-permute-start.5 = (f32[64,128]{1,0:T(8,128)S(1)}, f32[64,128]{1,0:T(8,128)S(1)}, u32[]{:S(2)}, u32[]{:S(2)}) collective-permute-start(f32[64,128]{1,0:T(8,128)S(1)} %add.37), channel_id=1, source_target_pairs={{0,2},{1,3},{2,0},{3,1},{4,6},{5,7},{6,4},{7,5},{8,10},{9,11},{10,... | collective-permute-start | bytes 98312 | tf_op jit(solution)/shard_map/ppermute | solution.py:206
  24.7 8.7 %collective-permute-start.8 = (f32[64,128]{1,0:T(8,128)S(1)}, f32[64,128]{1,0:T(8,128)S(1)}, u32[]{:S(2)}, u32[]{:S(2)}) collective-permute-start(f32[64,128]{1,0:T(8,128)S(1)} %add.38.refs_0_), channel_id=1, source_target_pairs={{0,12},{4,8},{8,4},{12,0},{1,13},{5,9},{9,5},{13,1},{2,14},{6,10},... | collective-permute-start | bytes 98312 | tf_op jit(solution)/shard_map/ppermute | solution.py:206
  24.7 8.7 %collective-permute-start.7 = (f32[64,128]{1,0:T(8,128)S(1)}, f32[64,128]{1,0:T(8,128)S(1)}, u32[]{:S(2)}, u32[]{:S(2)}) collective-permute-start(f32[64,128]{1,0:T(8,128)S(1)} %add.38.refs_0_), channel_id=1, source_target_pairs={{0,8},{4,12},{8,0},{12,4},{1,9},{5,13},{9,1},{13,5},{2,10},{6,14},... | collective-permute-start | bytes 98312 | tf_op jit(solution)/shard_map/ppermute | solution.py:206
  25.6 7.8 %collective-permute-start.6 = (f32[64,128]{1,0:T(8,128)S(1)}, f32[64,128]{1,0:T(8,128)S(1)}, u32[]{:S(2)}, u32[]{:S(2)}) collective-permute-start(f32[64,128]{1,0:T(8,128)S(1)} %add.38.refs_0_), channel_id=1, source_target_pairs={{0,4},{4,0},{8,12},{12,8},{1,5},{5,1},{9,13},{13,9},{2,6},{6,2},{1... | collective-permute-start | bytes 98312 | tf_op jit(solution)/shard_map/ppermute | solution.py:206
  32.1 1.3 %copy-start.1 = (bf16[16,256,256]{2,1,0:T(8,128)(2,1)}, bf16[16,256,256]{2,1,0:T(8,128)(2,1)S(1)}, u32[]{:S(2)}) copy-start(bf16[16,256,256]{2,1,0:T(8,128)(2,1)S(1)} %get-tuple-element.20.refs_5_) | copy-start | bytes 6291460
  43.3 1.3 %collective-permute-start.9 = (f32[136,128]{1,0:T(8,128)S(1)}, f32[136,128]{1,0:T(8,128)S(1)}, u32[]{:S(2)}, u32[]{:S(2)}) collective-permute-start(f32[136,128]{1,0:T(8,128)S(1)} %get-tuple-element.26), channel_id=1, source_target_pairs={{0,4},{4,0},{8,12},{12,8},{1,5},{5,1},{9,13},{13,9},{2,6},{6,2},{1... | collective-permute-start | bytes 208904 | tf_op jit(solution)/shard_map/ppermute | solution.py:206
  44.6 4.4 %collective-permute-start.10 = (f32[136,128]{1,0:T(8,128)S(1)}, f32[136,128]{1,0:T(8,128)S(1)}, u32[]{:S(2)}, u32[]{:S(2)}) collective-permute-start(f32[136,128]{1,0:T(8,128)S(1)} %add.39), channel_id=1, source_target_pairs={{0,16},{16,0},{1,17},{17,1},{2,18},{18,2},{3,19},{19,3},{4,20},{20... | collective-permute-start | bytes 208904 | tf_op jit(solution)/shard_map/ppermute | solution.py:206
  49.0 4.4 %collective-permute-start.11 = (f32[136,128]{1,0:T(8,128)S(1)}, f32[136,128]{1,0:T(8,128)S(1)}, u32[]{:S(2)}, u32[]{:S(2)}) collective-permute-start(f32[136,128]{1,0:T(8,128)S(1)} %add.40), channel_id=1, source_target_pairs={{0,8},{4,12},{8,0},{12,4},{1,9},{5,13},{9,1},{13,5},{2,10},{6,14},... | collective-permute-start | bytes 208904 | tf_op jit(solution)/shard_map/ppermute | solution.py:206
  53.4 4.4 %collective-permute-start.12 = (f32[136,128]{1,0:T(8,128)S(1)}, f32[136,128]{1,0:T(8,128)S(1)}, u32[]{:S(2)}, u32[]{:S(2)}) collective-permute-start(f32[136,128]{1,0:T(8,128)S(1)} %add.41), channel_id=1, source_target_pairs={{0,1},{1,0},{2,3},{3,2},{4,5},{5,4},{6,7},{7,6},{8,9},{9,8},{10,11... | collective-permute-start | bytes 208904 | tf_op jit(solution)/shard_map/ppermute | solution.py:206
  57.8 5.5 %collective-permute-start.13 = (f32[136,128]{1,0:T(8,128)S(1)}, f32[136,128]{1,0:T(8,128)S(1)}, u32[]{:S(2)}, u32[]{:S(2)}) collective-permute-start(f32[136,128]{1,0:T(8,128)S(1)} %add.42), channel_id=1, source_target_pairs={{0,2},{1,3},{2,0},{3,1},{4,6},{5,7},{6,4},{7,5},{8,10},{9,11},{10,... | collective-permute-start | bytes 208904 | tf_op jit(solution)/shard_map/ppermute | solution.py:206
  63.3 6.9 %collective-permute-start.14 = (f32[136,128]{1,0:T(8,128)S(1)}, f32[136,128]{1,0:T(8,128)S(1)}, u32[]{:S(2)}, u32[]{:S(2)}) collective-permute-start(f32[136,128]{1,0:T(8,128)S(1)} %add.43.refs_0_), channel_id=1, source_target_pairs={{0,4},{4,0},{8,12},{12,8},{1,5},{5,1},{9,13},{13,9},{2,6},{6,2},{1... | collective-permute-start | bytes 208904 | tf_op jit(solution)/shard_map/ppermute | solution.py:206

commit v3 on v2

v3 whole, which is shorter than its diff:
```python
import functools
import math

import jax
import jax.numpy as jnp
from jax import lax
from jax.experimental import pallas as pl
from jax.experimental.pallas import tpu as pltpu
from jax.sharding import PartitionSpec as P

RK = 128
AXES = ("gx", "gy", "gz")
LANES = 128
PANEL = 16
SCATTER = ("gx", "gy")
RELAYS = 2
F32 = jnp.float32
BF16 = jnp.bfloat16
VMEM_LIMIT = 48 * 1024 * 1024


def split(x):
    hi = x.astype(BF16)
    return hi, (x - hi.astype(F32)).astype(BF16)


def dot_tn(a, b):
    return lax.dot_general(a, b, (((0,), (0,)), ((), ())), preferred_element_type=F32)


def dot_nt(a, b):
    return lax.dot_general(a, b, (((1,), (1,)), ((), ())), preferred_element_type=F32)


def dot_nn(a, b):
    return lax.dot_general(a, b, (((1,), (0,)), ((), ())), preferred_element_type=F32)


def stacked_pieces(x):
    one = x.astype(BF16).astype(F32)
    rest = x - one
    two = rest.astype(BF16).astype(F32)
    three = rest - two
    left = jnp.concatenate([one, one, two, two, one, three], axis=0).astype(BF16)
    right = jnp.concatenate([one, two, one, two, three, one], axis=0).astype(BF16)
    return left, right


def factor_rows(w_ref, blocks):
    row_id = lax.broadcasted_iota(jnp.int32, (PANEL, LANES), 0)
    for start in range(0, LANES, PANEL):
        rows = [w_ref[start : start + PANEL, b * LANES : (b + 1) * LANES] for b in range(blocks)]
        columns = [
            jnp.broadcast_to(rows[0][:, start + k : start + k + 1], (PANEL, LANES))
            for k in range(PANEL)
        ]
        scale = jnp.zeros((PANEL, LANES), F32)
        for k in range(PANEL):
            pivot = jnp.broadcast_to(columns[k][k : k + 1, :], (PANEL, LANES))
            inverse = lax.rsqrt(pivot)
            inverse = inverse * (1.5 - 0.5 * pivot * inverse * inverse)
            multiples = columns[k] * inverse
            for m in range(k + 1, PANEL):
                columns[m] = columns[m] - multiples * multiples[m : m + 1, :]
            below = jnp.where(row_id > k, multiples * inverse, 0.0)
            rows = [r - below * r[k : k + 1, :] for r in rows]
            scale = jnp.where(row_id == k, inverse, scale)
        rows = [r * scale for r in rows]
        for b in range(blocks):
            w_ref[start : start + PANEL, b * LANES : (b + 1) * LANES] = rows[b]
        if start + PANEL < LANES:
            both = [stacked_pieces(r) for r in rows]
            left = both[0][0]
            right = jnp.concatenate([b[1] for b in both], axis=1)
            update = dot_tn(left, right)
            w_ref[start + PANEL :, :] = w_ref[start + PANEL :, :] - update[start + PANEL :, :]


def triangle_ids():
    return (
        lax.broadcasted_iota(jnp.int32, (LANES, LANES), 0),
        lax.broadcasted_iota(jnp.int32, (LANES, LANES), 1),
    )


def gram_kernel(a_ref, tall_ref, token_ref):
    @pl.when(pl.program_id(0) == 0)
    def _():
        tall_ref[...] = jnp.zeros_like(tall_ref)
        token_ref[...] = jnp.zeros_like(token_ref)

    hi, lo = split(a_ref[...])
    both = dot_tn(hi[:, :RK], jnp.concatenate([hi, lo], axis=1))
    top = both[:, :256] + both[:, 256:] + dot_tn(lo[:, :RK], hi)
    tall_ref[:RK, :] += top[:, :RK]
    tall_ref[RK:, :] += top[:, RK:]


def add_kernel(copies, terms_ref, _, out_ref, token_ref):
    total = terms_ref[0]
    for i in range(1, terms_ref.shape[0]):
        total = total + terms_ref[i]
    for i in range(copies):
        out_ref[i] = total
    token_ref[...] = jnp.zeros_like(token_ref)


def relay_kernel(points, left_ref, right_ref, _, hi_ref, lo_ref, token_ref):
    token_ref[...] = jnp.zeros_like(token_ref)
    count = left_ref.shape[0] // points
    for p in range(points):
        for c, half in enumerate((left_ref, right_ref)):
            hi, lo = split(half[pl.ds(p, count, stride=points), :])
            hi_ref[p, :, c * LANES : (c + 1) * LANES] = hi
            lo_ref[p, :, c * LANES : (c + 1) * LANES] = lo


def absorb_kernel(scale, tall_ref, *refs):
    highs, lows = refs[:RELAYS], refs[RELAYS : 2 * RELAYS]
    absorbed_ref, linv_ref, pack_ref, w_ref, total_ref = refs[2 * RELAYS :]
    row, col = triangle_ids()
    w_ref[:, :LANES] = tall_ref[:RK, :]
    w_ref[:, LANES : 2 * LANES] = tall_ref[RK:, :]
    w_ref[:, 2 * LANES :] = jnp.where(row == col, 1.0, 0.0).astype(F32)
    factor_rows(w_ref, 3)
    linv_ref[...] = w_ref[:, 2 * LANES :] * scale
    upper = jnp.concatenate(
        [jnp.where(col >= row, w_ref[:, :LANES], 0.0), w_ref[:, LANES : 2 * LANES]], axis=1
    )
    upper_hi, upper_lo = split(upper)
    upper_both = jnp.concatenate([upper_hi, upper_lo], axis=0)
    points = absorbed_ref.shape[0]
    group = 4
    total_ref[...] = jnp.zeros_like(total_ref)

    def body(step, carry):
        pieces = []
        for i in range(group):
            p = step * group + i
            high = jnp.concatenate([ref[p] for ref in highs], axis=0)
            low = jnp.concatenate([ref[p] for ref in lows], axis=0)
            first = dot_nn(upper_both, high)
            b = first[:RK, :] + first[RK:, :] + dot_nn(upper_hi, low)
            absorbed_ref[p] = b
            pieces.append(split(b))
        b_hi = jnp.concatenate([x[0] for x in pieces], axis=0)
        b_lo = jnp.concatenate([x[1] for x in pieces], axis=0)
        total_ref[...] += dot_tn(b_hi, jnp.concatenate([b_hi, b_lo], axis=1))
        return carry

    lax.fori_loop(0, points // group, body, 0)
    cross = total_ref[:, 256:]
    gram = total_ref[:, :256] + cross + cross.T
    lower_right = gram[LANES:, LANES:]
    pack_ref[:LANES, :] = jnp.where(col >= row, gram[:LANES, :LANES], lower_right)
    pack_ref[LANES : 2 * LANES, :] = gram[:LANES, LANES:]
    diagonal = jnp.sum(jnp.where(row == col, lower_right, 0.0), axis=0, keepdims=True)
    tail = pack_ref.shape[0] - 2 * LANES
    pack_ref[2 * LANES :, :] = jnp.broadcast_to(diagonal, (tail, LANES))


def left_kernel(a_ref, linv_ref, left_ref, token_ref):
    l_hi, l_lo = split(linv_ref[...])
    hi, lo = split(a_ref[...])
    left_ref[...] = dot_nt(hi, l_hi) + dot_nt(hi, l_lo) + dot_nt(lo, l_hi)
    token_ref[...] = jnp.zeros_like(token_ref)


def right_kernel(points, absorbed_ref, _, right_ref, token_ref):
    count = absorbed_ref.shape[1]
    for p in range(points):
        right_ref[pl.ds(p, count, stride=points), :] = absorbed_ref[p]
    token_ref[...] = jnp.zeros_like(token_ref)


def factor_kernel(scale, pack_ref, out_ref, w_ref, rest_ref):
    row, col = triangle_ids()
    packed = pack_ref[:LANES, :] * scale
    turned = packed.T
    diagonal = jnp.broadcast_to(pack_ref[2 * LANES : 2 * LANES + 1, :], (LANES, LANES)) * scale
    w_ref[:, :LANES] = jnp.where(col >= row, packed, turned)
    w_ref[:, LANES:] = pack_ref[LANES : 2 * LANES, :] * scale
    rest_ref[...] = jnp.where(row > col, packed, jnp.where(row == col, diagonal, turned))
    factor_rows(w_ref, 2)
    out_ref[:LANES, :LANES] = jnp.where(col >= row, w_ref[:, :LANES], 0.0)
    out_ref[:LANES, LANES:] = w_ref[:, LANES:]
    left, right = stacked_pieces(w_ref[:, LANES:])
    rest_ref[...] = rest_ref[...] - dot_tn(left, right)
    factor_rows(rest_ref, 1)
    out_ref[LANES:, :LANES] = jnp.zeros((LANES, LANES), F32)
    out_ref[LANES:, LANES:] = jnp.where(col >= row, rest_ref[...], 0.0)


def shape(*dims, dtype=F32):
    return jax.ShapeDtypeStruct(dims, dtype)


TOKEN = shape(8, LANES)


def params(steps=0, limit=VMEM_LIMIT):
    return pltpu.CompilerParams(
        dimension_semantics=("arbitrary",) * steps or None, vmem_limit_bytes=limit
    )


def cost(mebibytes):
    return pl.CostEstimate(flops=0, bytes_accessed=mebibytes * 2**20, transcendentals=0)


def add_terms(terms, token, copies):
    vmem = pl.BlockSpec(memory_space=pltpu.VMEM)
    return pl.pallas_call(
        functools.partial(add_kernel, copies),
        in_specs=[vmem] * 2,
        out_specs=[vmem] * 2,
        out_shape=[shape(copies, *terms.shape[1:]), TOKEN],
        compiler_params=params(limit=8 * 1024 * 1024),
        cost_estimate=cost(1),
        name="add_terms",
    )(terms, token)


def sum_over_devices(tall, token, first_work, second_work):
    spread = lax.axis_size("gx") * lax.axis_size("gy")
    layers = lax.axis_size("gz")
    blocks = tall.reshape(spread, tall.shape[0] // spread, LANES)
    received = lax.all_to_all(blocks, SCATTER, 0, 0)
    first, token = first_work(token)
    copies, token = add_terms(received, token, layers)
    received = lax.all_to_all(copies, "gz", 0, 0)
    second, token = second_work(token)
    copies, _ = add_terms(received, token, spread)
    gathered = lax.all_to_all(copies, SCATTER, 0, 0)
    return gathered.reshape(tall.shape), first, second


def relay_part(rows_right, points, part, token):
    steps = 4
    chunk = rows_right.shape[0] // (RELAYS * steps)
    ranks = chunk // points
    width = rows_right.shape[1]
    high, low, token = pl.pallas_call(
        functools.partial(relay_kernel, points),
        grid=(steps,),
        in_specs=[
            pl.BlockSpec((chunk, LANES), lambda i: (part * steps + i, 0)),
            pl.BlockSpec((chunk, LANES), lambda i: (part * steps + i, 1)),
            pl.BlockSpec((8, LANES), lambda i: (0, 0)),
        ],
        out_specs=[pl.BlockSpec((points, ranks, width), lambda i: (0, i, 0))] * 2
        + [pl.BlockSpec((8, LANES), lambda i: (0, 0))],
        out_shape=[shape(points, steps * ranks, width, dtype=BF16)] * 2 + [TOKEN],
        compiler_params=params(1, 16 * 1024 * 1024),
        cost_estimate=cost(8),
        name="relay_right",
    )(rows_right, rows_right, token)
    return (high, low), token


def left_part(unfold, linv, _):
    steps = 4
    chunk = unfold.shape[0] // steps
    return pl.pallas_call(
        left_kernel,
        grid=(steps,),
        in_specs=[
            pl.BlockSpec((chunk, RK), lambda i: (i, 0)),
            pl.BlockSpec((RK, RK), lambda i: (0, 0)),
        ],
        out_specs=[
            pl.BlockSpec((chunk, RK), lambda i: (i, 0)),
            pl.BlockSpec((8, LANES), lambda i: (0, 0)),
        ],
        out_shape=[shape(unfold.shape[0], RK), TOKEN],
        compiler_params=params(1, 16 * 1024 * 1024),
        cost_estimate=cost(8),
        name="left_out",
    )(unfold, linv)


def right_part(absorbed, token):
    points, ranks, width = absorbed.shape
    steps = 2
    return pl.pallas_call(
        functools.partial(right_kernel, points),
        grid=(steps, 2),
        in_specs=[
            pl.BlockSpec((points, ranks // steps, LANES), lambda i, c: (0, i, c)),
            pl.BlockSpec((8, LANES), lambda i, c: (0, 0)),
        ],
        out_specs=[
            pl.BlockSpec((ranks // steps * points, LANES), lambda i, c: (i, c)),
            pl.BlockSpec((8, LANES), lambda i, c: (0, 0)),
        ],
        out_shape=[shape(ranks * points, width), TOKEN],
        compiler_params=params(2, 16 * 1024 * 1024),
        cost_estimate=cost(8),
        name="right_out",
    )(absorbed, token)


def per_device(left_core, right_core):
    rank_left, points, rank_mid = left_core.shape
    rank_right = right_core.shape[2]
    spread = lax.axis_size("gx") * lax.axis_size("gy")
    total_points = points * spread * lax.axis_size("gz")
    unfold = left_core.reshape(rank_left * points, rank_mid)
    rows_right = right_core.reshape(rank_mid * points, rank_right)
    vmem = pl.BlockSpec(memory_space=pltpu.VMEM)

    steps = 8
    tall, token = pl.pallas_call(
        gram_kernel,
        grid=(steps,),
        in_specs=[pl.BlockSpec((unfold.shape[0] // steps, rank_mid), lambda i: (i, 0))],
        out_specs=[
            pl.BlockSpec((2 * RK, LANES), lambda i: (0, 0)),
            pl.BlockSpec((8, LANES), lambda i: (0, 0)),
        ],
        out_shape=[shape(2 * RK, LANES), TOKEN],
        compiler_params=params(1, 56 * 1024 * 1024),
        name="gram_top",
    )(unfold)
    tall, *relayed = sum_over_devices(
        tall,
        token,
        functools.partial(relay_part, rows_right, points, 0),
        functools.partial(relay_part, rows_right, points, 1),
    )

    block_rows = -(-(2 * LANES + 8) // (8 * spread)) * 8
    absorbed, linv, packed = pl.pallas_call(
        functools.partial(absorb_kernel, math.sqrt(rank_left * total_points)),
        in_specs=[vmem] * (1 + 2 * RELAYS),
        out_specs=[vmem] * 3,
        out_shape=[
            shape(points, RK, rank_right),
            shape(RK, RK),
            shape(block_rows * spread, LANES),
        ],
        scratch_shapes=[
            pltpu.VMEM((LANES, 3 * LANES), F32),
            pltpu.VMEM((rank_right, 2 * rank_right), F32),
        ],
        compiler_params=params(limit=24 * 1024 * 1024),
        name="factor_absorb",
    )(tall, *[r[0] for r in relayed], *[r[1] for r in relayed])
    packed, left_out, right_out = sum_over_devices(
        packed,
        linv,
        functools.partial(left_part, unfold, linv),
        functools.partial(right_part, absorbed),
    )

    factor = pl.pallas_call(
        functools.partial(factor_kernel, 1.0 / (RK * total_points)),
        in_specs=[vmem],
        out_specs=vmem,
        out_shape=shape(rank_right, rank_right),
        scratch_shapes=[
            pltpu.VMEM((LANES, 2 * LANES), F32),
            pltpu.VMEM((LANES, LANES), F32),
        ],
        compiler_params=params(limit=16 * 1024 * 1024),
        name="factor_next",
    )(packed)
    return (
        left_out.reshape(rank_left, points, RK),
        right_out.reshape(RK, points, rank_right),
        factor,
    )


def solution(mesh):
    in_specs = (P(None, AXES, None), P(None, AXES, None))
    out_specs = (P(None, AXES, None), P(None, AXES, None), P())
    return jax.shard_map(
        per_device, mesh=mesh, in_specs=in_specs, out_specs=out_specs, check_vma=False
    )
```

time: 79.6 us -> 88.9 us (1.12)
  waiting for transfers between devices: 22.9 us -> 4.16 us
  blocking collectives: 0 us -> 18 us
  local copies, waits for them, and re-layouts: 3.5 us -> 13.9 us
    ppermute x15 -> x0, waiting for transfers between devices: 22.9 us -> none  [exchange(): return lax.ppermute(value, axis, [(i, i ^ bit) for i in range(size)])]
    all_to_all x0 -> x4, starting transfers between devices: none -> 18.2 us  [the longest x2 9.61 us: sum_over_devices(): received = lax.all_to_all(copies, 'gz', 0, 0)]
    ppermute x15 -> x0, starting transfers between devices: 18.1 us -> none  [exchange(): return lax.ppermute(value, axis, [(i, i ^ bit) for i in range(size)])]
    all_to_all x0 -> x2, blocking collectives: none -> 18 us  [sum_over_devices(): gathered = lax.all_to_all(copies, SCATTER, 0, 0)]
    unnamed x4 -> x20, local copies, waits for them, and re-layouts: 3.5 us -> 13.9 us
    all_to_all x0 -> x4, waiting for transfers between devices: none -> 4.16 us  [the longest x2 3.66 us: sum_over_devices(): received = lax.all_to_all(copies, 'gz', 0, 0)]
    pallas_call x1, Pallas kernels: 9.88 us -> 7.39 us  [per_device(): pl.pallas_call(functools.partial(absorb_kernel, math.sqrt(rank_left * tot...]
    pallas_call x3 -> x9, Pallas kernels: 15 us -> 16.8 us  [the longest x1 6.63 us: per_device(): pl.pallas_call(gram_kernel, grid=(steps,), in_specs=[pl.BlockSpec((unfold...]
  transfers between devices with their start and end apart: 15 -> 4, of which waited for: 10 -> 4; matrix products, arithmetic and copies ran while one was open for 0% -> 0% of each run, Pallas kernels for 16% -> 9%
where the time goes in v3:
time: 88.9 us; the launch traced here: 88 us
  Pallas kernels  33.1 us (37%)
  starting transfers between devices  18.2 us (20%)
  blocking collectives  18 us (20%)
  local copies, waits for them, and re-layouts  13.9 us (16%)
  waiting for transfers between devices  4.16 us (5%)
    all_to_all x2, blocking collectives, sum_over_devices(): gathered = lax.all_to_all(copies, SCATTER, 0, 0)  18 us
    unnamed x20, local copies, waits for them, and re-layouts  13.9 us
    all_to_all x2, starting transfers between devices, sum_over_devices(): received = lax.all_to_all(copies, 'gz', 0, 0)  9.61 us
    pallas_call x1, Pallas kernels, per_device(): pl.pallas_call(functools.partial(factor_kernel, 1.0 / (RK * total_points)...  8.93 us
    all_to_all x2, starting transfers between devices, sum_over_devices(): received = lax.all_to_all(blocks, SCATTER, 0, 0)  8.55 us
    pallas_call x1, Pallas kernels, per_device(): pl.pallas_call(functools.partial(absorb_kernel, math.sqrt(rank_left * tot...  7.39 us
    pallas_call x1, Pallas kernels, per_device(): pl.pallas_call(gram_kernel, grid=(steps,), in_specs=[pl.BlockSpec((unfold...  6.63 us
    all_to_all x2, waiting for transfers between devices, sum_over_devices(): received = lax.all_to_all(copies, 'gz', 0, 0)  3.66 us
  transfers between devices with their start and end apart: 4, of which 4 were waited for; matrix products, arithmetic and copies ran while one was open for 0% of the time, Pallas kernels for 9%

profile of v3, /device:TPU:0, one launch (start us, length us, event | category | flops | bytes accessed | tf_op | source)
XLA Modules:
  0.0 88.0 jit_solution(3998273632056589630)
XLA Ops:
  0.6 6.6 %gram_top.1 = (f32[256,128]{1,0:T(8,128)}, f32[8,128]{1,0:T(8,128)}) custom-call(f32[4096,256]{1,0:T(8,128)} %bitcast.12), custom_call_target="tpu_custom_call" | custom-call | tf_op jit(solution)/shard_map/gram_top/pallas_call | solution.py:313
  7.3 5.2 %all-to-all-start = ((f32[8,32,128]{2,1,0:T(8,128)}), f32[8,32,128]{2,1,0:T(8,128)S(1)}, u32[]{:S(2)}, u32[]{:S(2)}) async-start(f32[8,32,128]{2,1,0:T(8,128)} %bitcast.16), calls=%async_computation | async-start | bytes 262144 | tf_op jit(solution)/shard_map/all_to_all | solution.py:228
  12.4 2.2 %copy-done = f32[256,16,256]{2,1,0:T(8,128)S(1)} copy-done((f32[256,16,256]{2,1,0:T(8,128)S(1)}, f32[256,16,256]{2,1,0:T(8,128)}, u32[]{:S(2)}) %copy-start) | copy-done | bytes 4194328
  14.6 0.7 copy-done.9
  15.3 1.2 %relay_right.2 = (bf16[16,128,256]{2,1,0:T(8,128)(2,1)S(1)}, bf16[16,128,256]{2,1,0:T(8,128)(2,1)S(1)}, f32[8,128]{1,0:T(8,128)S(1)}) custom-call(f32[4096,256]{1,0:T(8,128)S(1)} %bitcast.8, f32[4096,256]{1,0:T(8,128)S(1)} %bitcast.9, f32[8,128]{1,0:T(8,128)S(1)} %copy-done.9), custom_call_target="tpu_custom_call" | custom-call | bytes 8388608 | tf_op jit(solution)/shard_map/relay_right/pallas_call | solution.py:243
  16.5 1.0 %copy-done.3 = bf16[16,128,256]{2,1,0:T(8,128)(2,1)} copy-done((bf16[16,128,256]{2,1,0:T(8,128)(2,1)}, bf16[16,128,256]{2,1,0:T(8,128)(2,1)S(1)}, u32[]{:S(2)}) %copy-start.3) | copy-done | bytes 1048600
  18.3 4.9 %all-to-all-start.1 = ((f32[4,32,128]{2,1,0:T(8,128)}), f32[4,32,128]{2,1,0:T(8,128)S(1)}, u32[]{:S(2)}, u32[]{:S(2)}) async-start(f32[4,32,128]{2,1,0:T(8,128)} %get-tuple-element.27), calls=%async_computation.1 | async-start | bytes 131072 | tf_op jit(solution)/shard_map/all_to_all | solution.py:231
  23.1 2.2 %copy-done.1 = f32[256,16,256]{2,1,0:T(8,128)S(1)} copy-done((f32[256,16,256]{2,1,0:T(8,128)S(1)}, f32[256,16,256]{2,1,0:T(8,128)}, u32[]{:S(2)}) %copy-start.1) | copy-done | bytes 4194328
  25.3 1.2 %relay_right.3 = (bf16[16,128,256]{2,1,0:T(8,128)(2,1)S(1)}, bf16[16,128,256]{2,1,0:T(8,128)(2,1)S(1)}, f32[8,128]{1,0:T(8,128)S(1)}) custom-call(f32[4096,256]{1,0:T(8,128)S(1)} %bitcast.10, f32[4096,256]{1,0:T(8,128)S(1)} %bitcast.11, f32[8,128]{1,0:T(8,128)S(1)} %get-tuple-element.28._), custom_call_target="tpu_custom_call" | custom-call | bytes 8388608 | tf_op jit(solution)/shard_map/relay_right/pallas_call | solution.py:243
  26.5 1.0 %copy-done.5 = bf16[16,128,256]{2,1,0:T(8,128)(2,1)} copy-done((bf16[16,128,256]{2,1,0:T(8,128)(2,1)}, bf16[16,128,256]{2,1,0:T(8,128)(2,1)S(1)}, u32[]{:S(2)}) %copy-start.5) | copy-done | bytes 1048600
  27.5 1.0 %copy-done.7 = bf16[16,128,256]{2,1,0:T(8,128)(2,1)} copy-done((bf16[16,128,256]{2,1,0:T(8,128)(2,1)}, bf16[16,128,256]{2,1,0:T(8,128)(2,1)S(1)}, u32[]{:S(2)}) %copy-start.7) | copy-done | bytes 1048600
  29.5 9.0 %all_to_all.30 = f32[8,32,128]{2,1,0:T(8,128)S(1)} all-to-all(f32[8,32,128]{2,1,0:T(8,128)S(1)} %get-tuple-element.30), channel_id=1, replica_groups=mesh['gx'=2,'gy'=4,'gz'=4] {'gx','gy'}, dimensions={0} | all-to-all | bytes 262144 | tf_op jit(solution)/shard_map/all_to_all | solution.py:234
  38.5 1.2 %copy-done.4 = bf16[16,128,256]{2,1,0:T(8,128)(2,1)S(1)} copy-done((bf16[16,128,256]{2,1,0:T(8,128)(2,1)S(1)}, bf16[16,128,256]{2,1,0:T(8,128)(2,1)}, u32[]{:S(2)}) %copy-start.4) | copy-done | bytes 1048600
  39.7 1.2 %copy-done.6 = bf16[16,128,256]{2,1,0:T(8,128)(2,1)S(1)} copy-done((bf16[16,128,256]{2,1,0:T(8,128)(2,1)S(1)}, bf16[16,128,256]{2,1,0:T(8,128)(2,1)}, u32[]{:S(2)}) %copy-start.6) | copy-done | bytes 1048600
  40.9 1.2 %copy-done.8 = bf16[16,128,256]{2,1,0:T(8,128)(2,1)S(1)} copy-done((bf16[16,128,256]{2,1,0:T(8,128)(2,1)S(1)}, bf16[16,128,256]{2,1,0:T(8,128)(2,1)}, u32[]{:S(2)}) %copy-start.8) | copy-done | bytes 1048600
  42.2 7.4 %factor_absorb.1 = (f32[16,128,256]{2,1,0:T(8,128)S(1)}, f32[128,128]{1,0:T(8,128)S(1)}, f32[320,128]{1,0:T(8,128)}) custom-call(f32[256,128]{1,0:T(8,128)S(1)} %bitcast.15, bf16[16,128,256]{2,1,0:T(8,128)(2,1)S(1)} %get-tuple-element.31.refs_0_, bf16[16,128,256]{2,1,0:T(8,128)(2,1)S(1)} %copy-done.6, bf16[16,128,256]{2,1,0:T(8,128)(2,1)S(1)} %copy-done.4, ...), custom_call_target="tpu_custom_call" | custom-call | tf_op jit(solution)/shard_map/factor_absorb/pallas_call | solution.py:333
  49.5 3.4 %all-to-all-start.3 = ((f32[8,40,128]{2,1,0:T(8,128)}), f32[8,40,128]{2,1,0:T(8,128)S(1)}, u32[]{:S(2)}, u32[]{:S(2)}) async-start(f32[8,40,128]{2,1,0:T(8,128)} %bitcast.5), calls=%async_computation.3 | async-start | bytes 327680 | tf_op jit(solution)/shard_map/all_to_all | solution.py:228
  53.0 2.2 %copy-done.2 = f32[256,16,256]{2,1,0:T(8,128)S(1)} copy-done((f32[256,16,256]{2,1,0:T(8,128)S(1)}, f32[256,16,256]{2,1,0:T(8,128)}, u32[]{:S(2)}) %copy-start.2) | copy-done | bytes 4194328
  55.1 2.8 %left_out.1 = (f32[4096,128]{1,0:T(8,128)}, f32[8,128]{1,0:T(8,128)S(1)}) custom-call(f32[4096,256]{1,0:T(8,128)S(1)} %bitcast.13, f32[128,128]{1,0:T(8,128)S(1)} %get-tuple-element.35.linv_ref), custom_call_target="tpu_custom_call" | custom-call | bytes 8388608 | tf_op jit(solution)/shard_map/left_out/pallas_call | solution.py:264
  59.0 4.7 %all-to-all-start.4 = ((f32[4,40,128]{2,1,0:T(8,128)}), f32[4,40,128]{2,1,0:T(8,128)S(1)}, u32[]{:S(2)}, u32[]{:S(2)}) async-start(f32[4,40,128]{2,1,0:T(8,128)} %get-tuple-element.42), calls=%async_computation.4 | async-start | bytes 163840 | tf_op jit(solution)/shard_map/all_to_all | solution.py:231
  63.7 2.5 %right_out.1 = (f32[2048,256]{1,0:T(8,128)}, f32[8,128]{1,0:T(8,128)S(1)}) custom-call(f32[16,128,256]{2,1,0:T(8,128)S(1)} %get-tuple-element.37.absorbed_ref, f32[8,128]{1,0:T(8,128)S(1)} %get-tuple-element.40._), custom_call_target="tpu_custom_call" | custom-call | bytes 8388608 | tf_op jit(solution)/shard_map/right_out/pallas_call | solution.py:285
  66.2 3.3 %all-to-all-done.4.terms_ref = f32[4,40,128]{2,1,0:T(8,128)S(1)} async-done(((f32[4,40,128]{2,1,0:T(8,128)}), f32[4,40,128]{2,1,0:T(8,128)S(1)}, u32[]{:S(2)}, u32[]{:S(2)}) %all-to-all-start.4) | async-done | bytes 81952 | tf_op jit(solution)/shard_map/all_to_all | solution.py:231
  70.1 9.0 %all_to_all.31 = f32[8,40,128]{2,1,0:T(8,128)S(1)} all-to-all(f32[8,40,128]{2,1,0:T(8,128)S(1)} %get-tuple-element.44), channel_id=1, replica_groups=mesh['gx'=2,'gy'=4,'gz'=4] {'gx','gy'}, dimensions={0} | all-to-all | bytes 327680 | tf_op jit(solution)/shard_map/all_to_all | solution.py:234
  79.1 8.9 %factor_next.1 = f32[256,256]{1,0:T(8,128)} custom-call(f32[320,128]{1,0:T(8,128)S(1)} %bitcast.14), custom_call_target="tpu_custom_call" | custom-call | tf_op jit(solution)/shard_map/factor_next/pallas_call | solution.py:356
  (17 shorter events, 3.4 us)
Async XLA Ops:
  7.3 10.4 %all-to-all-start = ((f32[8,32,128]{2,1,0:T(8,128)}), f32[8,32,128]{2,1,0:T(8,128)S(1)}, u32[]{:S(2)}, u32[]{:S(2)}) async-start(f32[8,32,128]{2,1,0:T(8,128)} %bitcast.16), calls=%async_computation | async-start | bytes 262144 | tf_op jit(solution)/shard_map/all_to_all | solution.py:228
  12.4 2.2 %copy-start = (f32[256,16,256]{2,1,0:T(8,128)S(1)}, f32[256,16,256]{2,1,0:T(8,128)}, u32[]{:S(2)}) copy-start(f32[256,16,256]{2,1,0:T(8,128)} %param.3) | copy-start | bytes 12582916
  14.6 0.7 copy-start.9
  16.5 1.0 %copy-start.3 = (bf16[16,128,256]{2,1,0:T(8,128)(2,1)}, bf16[16,128,256]{2,1,0:T(8,128)(2,1)S(1)}, u32[]{:S(2)}) copy-start(bf16[16,128,256]{2,1,0:T(8,128)(2,1)S(1)} %get-tuple-element.33.refs_2_) | copy-start | bytes 3145732
  18.3 10.6 %all-to-all-start.1 = ((f32[4,32,128]{2,1,0:T(8,128)}), f32[4,32,128]{2,1,0:T(8,128)S(1)}, u32[]{:S(2)}, u32[]{:S(2)}) async-start(f32[4,32,128]{2,1,0:T(8,128)} %get-tuple-element.27), calls=%async_computation.1 | async-start | bytes 131072 | tf_op jit(solution)/shard_map/all_to_all | solution.py:231
  23.1 2.2 %copy-start.1 = (f32[256,16,256]{2,1,0:T(8,128)S(1)}, f32[256,16,256]{2,1,0:T(8,128)}, u32[]{:S(2)}) copy-start(f32[256,16,256]{2,1,0:T(8,128)} %param.3) | copy-start | bytes 12582916
  26.5 1.0 %copy-start.5 = (bf16[16,128,256]{2,1,0:T(8,128)(2,1)}, bf16[16,128,256]{2,1,0:T(8,128)(2,1)S(1)}, u32[]{:S(2)}) copy-start(bf16[16,128,256]{2,1,0:T(8,128)(2,1)S(1)} %get-tuple-element.32.refs_1_) | copy-start | bytes 3145732
  27.5 1.0 %copy-start.7 = (bf16[16,128,256]{2,1,0:T(8,128)(2,1)}, bf16[16,128,256]{2,1,0:T(8,128)(2,1)S(1)}, u32[]{:S(2)}) copy-start(bf16[16,128,256]{2,1,0:T(8,128)(2,1)S(1)} %get-tuple-element.34.refs_3_) | copy-start | bytes 3145732
  38.5 1.2 %copy-start.4 = (bf16[16,128,256]{2,1,0:T(8,128)(2,1)S(1)}, bf16[16,128,256]{2,1,0:T(8,128)(2,1)}, u32[]{:S(2)}) copy-start(bf16[16,128,256]{2,1,0:T(8,128)(2,1)} %copy-done.3) | copy-start | bytes 3145732
  39.7 1.2 %copy-start.6 = (bf16[16,128,256]{2,1,0:T(8,128)(2,1)S(1)}, bf16[16,128,256]{2,1,0:T(8,128)(2,1)}, u32[]{:S(2)}) copy-start(bf16[16,128,256]{2,1,0:T(8,128)(2,1)} %copy-done.5) | copy-start | bytes 3145732
  40.9 1.2 %copy-start.8 = (bf16[16,128,256]{2,1,0:T(8,128)(2,1)S(1)}, bf16[16,128,256]{2,1,0:T(8,128)(2,1)}, u32[]{:S(2)}) copy-start(bf16[16,128,256]{2,1,0:T(8,128)(2,1)} %copy-done.7) | copy-start | bytes 3145732
  49.5 8.8 %all-to-all-start.3 = ((f32[8,40,128]{2,1,0:T(8,128)}), f32[8,40,128]{2,1,0:T(8,128)S(1)}, u32[]{:S(2)}, u32[]{:S(2)}) async-start(f32[8,40,128]{2,1,0:T(8,128)} %bitcast.5), calls=%async_computation.3 | async-start | bytes 327680 | tf_op jit(solution)/shard_map/all_to_all | solution.py:228
  52.9 2.2 %copy-start.2 = (f32[256,16,256]{2,1,0:T(8,128)S(1)}, f32[256,16,256]{2,1,0:T(8,128)}, u32[]{:S(2)}) copy-start(f32[256,16,256]{2,1,0:T(8,128)} %param.2) | copy-start | bytes 12582916
  59.0 10.5 %all-to-all-start.4 = ((f32[4,40,128]{2,1,0:T(8,128)}), f32[4,40,128]{2,1,0:T(8,128)S(1)}, u32[]{:S(2)}, u32[]{:S(2)}) async-start(f32[4,40,128]{2,1,0:T(8,128)} %get-tuple-element.42), calls=%async_computation.4 | async-start | bytes 163840 | tf_op jit(solution)/shard_map/all_to_all | solution.py:231

commit v4 on v3

v4 whole, which is shorter than its diff:
```python
import functools
import math

import jax
import jax.numpy as jnp
from jax import lax
from jax.experimental import pallas as pl
from jax.experimental.pallas import tpu as pltpu
from jax.sharding import PartitionSpec as P

RK = 128
AXES = ("gx", "gy", "gz")
LANES = 128
RELAYS = 2
F32 = jnp.float32
BF16 = jnp.bfloat16
VMEM_LIMIT = 48 * 1024 * 1024


def split(x):
    hi = x.astype(BF16)
    return hi, (x - hi.astype(F32)).astype(BF16)


def dot_tn(a, b):
    return lax.dot_general(a, b, (((0,), (0,)), ((), ())), preferred_element_type=F32)


def dot_nt(a, b):
    return lax.dot_general(a, b, (((1,), (1,)), ((), ())), preferred_element_type=F32)


def dot_nn(a, b):
    return lax.dot_general(a, b, (((1,), (0,)), ((), ())), preferred_element_type=F32)


def stacked_pieces(x):
    one = x.astype(BF16).astype(F32)
    rest = x - one
    two = rest.astype(BF16).astype(F32)
    three = rest - two
    left = jnp.concatenate([one, one, two, two, one, three], axis=0).astype(BF16)
    right = jnp.concatenate([one, two, one, two, three, one], axis=0).astype(BF16)
    return left, right


def spread_row(x, k):
    return jnp.broadcast_to(x[k : k + 1, :], x.shape)


def factor_rows(w_ref, blocks, panel):
    row_id = lax.broadcasted_iota(jnp.int32, (8, LANES), 0)
    groups = panel // 8
    for start in range(0, LANES, panel):
        rows = [
            [
                w_ref[start + 8 * v : start + 8 * v + 8, b * LANES : (b + 1) * LANES]
                for b in range(blocks)
            ]
            for v in range(groups)
        ]
        columns = [
            [
                jnp.broadcast_to(rows[v][0][:, start + k : start + k + 1], (8, LANES))
                for v in range(groups)
            ]
            for k in range(panel)
        ]
        scales = [jnp.zeros((8, LANES), F32)] * groups
        pivot = spread_row(columns[0][0], 0)
        for k in range(panel):
            home, at = k // 8, k % 8
            inverse = pl.reciprocal(pivot, approx=True)
            scales[home] = jnp.where(row_id == at, lax.rsqrt(pivot), scales[home])
            multiples = [columns[k][v] * inverse for v in range(groups)]
            for m in range(k + 1, panel):
                entry = spread_row(columns[k][m // 8], m % 8)
                if m == k + 1:
                    pivot = spread_row(columns[m][m // 8], m % 8) - (entry * inverse) * entry
                for v in range(m // 8, groups):
                    columns[m][v] = columns[m][v] - multiples[v] * entry
            for b in range(blocks):
                source = spread_row(rows[home][b], at)
                for v in range(home, groups):
                    below = multiples[v]
                    if v == home:
                        below = jnp.where(row_id > at, below, 0.0)
                    rows[v][b] = rows[v][b] - below * source
        done = [
            jnp.concatenate([rows[v][b] * scales[v] for v in range(groups)], axis=0)
            for b in range(blocks)
        ]
        for b in range(blocks):
            w_ref[start : start + panel, b * LANES : (b + 1) * LANES] = done[b]
        if start + panel < LANES:
            both = [stacked_pieces(x) for x in done]
            left = both[0][0]
            right = jnp.concatenate([x[1] for x in both], axis=1)
            update = dot_tn(left, right)
            w_ref[start + panel :, :] = w_ref[start + panel :, :] - update[start + panel :, :]


def triangle_ids():
    return (
        lax.broadcasted_iota(jnp.int32, (LANES, LANES), 0),
        lax.broadcasted_iota(jnp.int32, (LANES, LANES), 1),
    )


def store_blocks(tall_ref, outs):
    me = lax.rem(lax.axis_index("gy"), len(outs))
    size = outs[0].shape[0]
    for d, out in enumerate(outs):
        out[...] = tall_ref[pl.ds(pl.multiple_of((me ^ d) * size, 8), size), :]


def load_blocks(blocks, tall_ref):
    me = lax.rem(lax.axis_index("gy"), len(blocks))
    size = blocks[0].shape[0]
    for d, block in enumerate(blocks):
        tall_ref[pl.ds(pl.multiple_of((me ^ d) * size, 8), size), :] = block[...]


def gram_kernel(a_hbm, first_ref, second_ref, a_ref, tall_ref, sems):
    steps = a_ref.shape[0]
    chunk = a_ref.shape[1]

    def copy(i):
        return pltpu.make_async_copy(
            a_hbm.at[pl.ds(i * chunk, chunk), :], a_ref.at[i], sems.at[i]
        )

    for i in range(steps):
        copy(i).start()
    tall_ref[...] = jnp.zeros_like(tall_ref)

    def body(i, carry):
        copy(i).wait()
        hi, lo = split(a_ref[i])
        both = dot_tn(hi[:, :RK], jnp.concatenate([hi, lo], axis=1))
        top = both[:, :256] + both[:, 256:] + dot_tn(lo[:, :RK], hi)
        tall_ref[:RK, :] += top[:, :RK]
        tall_ref[RK:, :] += top[:, RK:]
        return carry

    lax.fori_loop(0, steps, body, 0)
    store_blocks(tall_ref, (first_ref, second_ref))


def relay_kernel(points, left_ref, right_ref, _, hi_ref, lo_ref, token_ref):
    token_ref[...] = jnp.zeros_like(token_ref)
    count = left_ref.shape[0] // points
    for p in range(points):
        for c, half in enumerate((left_ref, right_ref)):
            hi, lo = split(half[pl.ds(p, count, stride=points), :])
            hi_ref[p, :, c * LANES : (c + 1) * LANES] = hi
            lo_ref[p, :, c * LANES : (c + 1) * LANES] = lo


def absorb_kernel(scale, own_ref, other_ref, *refs):
    highs, lows = refs[:RELAYS], refs[RELAYS : 2 * RELAYS]
    absorbed_ref, linv_ref, first_ref, second_ref = refs[2 * RELAYS : 2 * RELAYS + 4]
    tall_ref, pack_ref, w_ref, total_ref = refs[2 * RELAYS + 4 :]
    row, col = triangle_ids()
    load_blocks((own_ref, other_ref), tall_ref)
    w_ref[:, :LANES] = tall_ref[:RK, :]
    w_ref[:, LANES : 2 * LANES] = tall_ref[RK:, :]
    w_ref[:, 2 * LANES :] = jnp.where(row == col, 1.0, 0.0).astype(F32)
    factor_rows(w_ref, 3, 16)
    linv_ref[...] = w_ref[:, 2 * LANES :] * scale
    upper = jnp.concatenate(
        [jnp.where(col >= row, w_ref[:, :LANES], 0.0), w_ref[:, LANES : 2 * LANES]], axis=1
    )
    upper_hi, upper_lo = split(upper)
    upper_both = jnp.concatenate([upper_hi, upper_lo], axis=0)
    points = absorbed_ref.shape[0]
    group = 4
    total_ref[...] = jnp.zeros_like(total_ref)

    def body(step, carry):
        pieces = []
        for i in range(group):
            p = step * group + i
            high = jnp.concatenate([ref[p] for ref in highs], axis=0)
            low = jnp.concatenate([ref[p] for ref in lows], axis=0)
            first = dot_nn(upper_both, high)
            b = first[:RK, :] + first[RK:, :] + dot_nn(upper_hi, low)
            absorbed_ref[p] = b
            pieces.append(split(b))
        b_hi = jnp.concatenate([x[0] for x in pieces], axis=0)
        b_lo = jnp.concatenate([x[1] for x in pieces], axis=0)
        total_ref[...] += dot_tn(b_hi, jnp.concatenate([b_hi, b_lo], axis=1))
        return carry

    lax.fori_loop(0, points // group, body, 0)
    cross = total_ref[:, 256:]
    gram = total_ref[:, :256] + cross + cross.T
    lower_right = gram[LANES:, LANES:]
    pack_ref[:LANES, :] = jnp.where(col >= row, gram[:LANES, :LANES], lower_right)
    pack_ref[LANES : 2 * LANES, :] = gram[:LANES, LANES:]
    diagonal = jnp.sum(jnp.where(row == col, lower_right, 0.0), axis=0, keepdims=True)
    tail = pack_ref.shape[0] - 2 * LANES
    pack_ref[2 * LANES :, :] = jnp.broadcast_to(diagonal, (tail, LANES))
    store_blocks(pack_ref, (first_ref, second_ref))


def left_kernel(a_ref, linv_ref, _, left_ref, token_ref):
    l_hi, l_lo = split(linv_ref[...])
    hi, lo = split(a_ref[...])
    left_ref[...] = dot_nt(hi, l_hi) + dot_nt(hi, l_lo) + dot_nt(lo, l_hi)
    token_ref[...] = jnp.zeros_like(token_ref)


def right_kernel(points, absorbed_ref, _, right_ref, token_ref):
    count = absorbed_ref.shape[1]
    for p in range(points):
        right_ref[pl.ds(p, count, stride=points), :] = absorbed_ref[p]
    token_ref[...] = jnp.zeros_like(token_ref)


def factor_kernel(scale, own_ref, other_ref, out_ref, pack_ref, w_ref, rest_ref):
    load_blocks((own_ref, other_ref), pack_ref)
    row, col = triangle_ids()
    packed = pack_ref[:LANES, :] * scale
    turned = packed.T
    diagonal = jnp.broadcast_to(pack_ref[2 * LANES : 2 * LANES + 1, :], (LANES, LANES)) * scale
    w_ref[:, :LANES] = jnp.where(col >= row, packed, turned)
    w_ref[:, LANES:] = pack_ref[LANES : 2 * LANES, :] * scale
    rest_ref[...] = jnp.where(row > col, packed, jnp.where(row == col, diagonal, turned))
    factor_rows(w_ref, 2, 32)
    out_ref[:LANES, :LANES] = jnp.where(col >= row, w_ref[:, :LANES], 0.0)
    out_ref[:LANES, LANES:] = w_ref[:, LANES:]
    left, right = stacked_pieces(w_ref[:, LANES:])
    rest_ref[...] = rest_ref[...] - dot_tn(left, right)
    factor_rows(rest_ref, 1, 32)
    out_ref[LANES:, :LANES] = jnp.zeros((LANES, LANES), F32)
    out_ref[LANES:, LANES:] = jnp.where(col >= row, rest_ref[...], 0.0)


def shape(*dims, dtype=F32):
    return jax.ShapeDtypeStruct(dims, dtype)


TOKEN = shape(8, LANES)


def params(steps=0, limit=VMEM_LIMIT):
    return pltpu.CompilerParams(
        dimension_semantics=("arbitrary",) * steps or None, vmem_limit_bytes=limit
    )


def cost(mebibytes):
    return pl.CostEstimate(flops=0, bytes_accessed=mebibytes * 2**20, transcendentals=0)


def exchange(value, axis, bit):
    size = lax.axis_size(axis)
    return lax.ppermute(value, axis, [(i, i ^ bit) for i in range(size)])


def sum_over_devices(blocks, works):
    total = blocks[0] + exchange(blocks[1], "gy", 1)
    stages = [
        (axis, 1 << bit)
        for axis in ("gy", "gx", "gz")
        for bit in range(lax.axis_size(axis).bit_length() - 1)
        if (axis, bit) != ("gy", 0)
    ]
    results = []
    for i, (axis, bit) in enumerate(stages):
        received = exchange(total, axis, bit)
        if i in works:
            result, token = works[i](total)
            results.append(result)
            received = received + token[:1, :]
        total = total + received
    return [total, exchange(total, "gy", 1)], results


def relay_part(rows_right, points, part, token):
    steps = 4
    chunk = rows_right.shape[0] // (RELAYS * steps)
    ranks = chunk // points
    width = rows_right.shape[1]
    high, low, token = pl.pallas_call(
        functools.partial(relay_kernel, points),
        grid=(steps,),
        in_specs=[
            pl.BlockSpec((chunk, LANES), lambda i: (part * steps + i, 0)),
            pl.BlockSpec((chunk, LANES), lambda i: (part * steps + i, 1)),
            pl.BlockSpec((8, LANES), lambda i: (0, 0)),
        ],
        out_specs=[pl.BlockSpec((points, ranks, width), lambda i: (0, i, 0))] * 2
        + [pl.BlockSpec((8, LANES), lambda i: (0, 0))],
        out_shape=[shape(points, steps * ranks, width, dtype=BF16)] * 2 + [TOKEN],
        compiler_params=params(1, 16 * 1024 * 1024),
        cost_estimate=cost(8),
        name="relay_right",
    )(rows_right, rows_right, token)
    return (high, low), token


def left_part(unfold, linv, token):
    steps = 4
    chunk = unfold.shape[0] // steps
    return pl.pallas_call(
        left_kernel,
        grid=(steps,),
        in_specs=[
            pl.BlockSpec((chunk, RK), lambda i: (i, 0)),
            pl.BlockSpec((RK, RK), lambda i: (0, 0)),
            pl.BlockSpec((8, LANES), lambda i: (0, 0)),
        ],
        out_specs=[
            pl.BlockSpec((chunk, RK), lambda i: (i, 0)),
            pl.BlockSpec((8, LANES), lambda i: (0, 0)),
        ],
        out_shape=[shape(unfold.shape[0], RK), TOKEN],
        compiler_params=params(1, 16 * 1024 * 1024),
        cost_estimate=cost(8),
        name="left_out",
    )(unfold, linv, token)


def right_part(absorbed, token):
    points, ranks, width = absorbed.shape
    steps = 2
    return pl.pallas_call(
        functools.partial(right_kernel, points),
        grid=(steps, 2),
        in_specs=[
            pl.BlockSpec((points, ranks // steps, LANES), lambda i, c: (0, i, c)),
            pl.BlockSpec((8, LANES), lambda i, c: (0, 0)),
        ],
        out_specs=[
            pl.BlockSpec((ranks // steps * points, LANES), lambda i, c: (i, c)),
            pl.BlockSpec((8, LANES), lambda i, c: (0, 0)),
        ],
        out_shape=[shape(ranks * points, width), TOKEN],
        compiler_params=params(2, 16 * 1024 * 1024),
        cost_estimate=cost(8),
        name="right_out",
    )(absorbed, token)


def per_device(left_core, right_core):
    rank_left, points, rank_mid = left_core.shape
    rank_right = right_core.shape[2]
    total_points = points * lax.axis_size("gx") * lax.axis_size("gy") * lax.axis_size("gz")
    unfold = left_core.reshape(rank_left * points, rank_mid)
    rows_right = right_core.reshape(rank_mid * points, rank_right)
    vmem = pl.BlockSpec(memory_space=pltpu.VMEM)

    steps = 8
    half = RK
    blocks = pl.pallas_call(
        gram_kernel,
        in_specs=[pl.BlockSpec(memory_space=pl.ANY)],
        out_specs=[vmem] * 2,
        out_shape=[shape(half, LANES)] * 2,
        scratch_shapes=[
            pltpu.VMEM((steps, unfold.shape[0] // steps, rank_mid), F32),
            pltpu.VMEM((2 * half, LANES), F32),
            pltpu.SemaphoreType.DMA((steps,)),
        ],
        compiler_params=params(limit=62 * 1024 * 1024),
        name="gram_top",
    )(unfold)
    summed, relayed = sum_over_devices(
        blocks,
        {2 + i: functools.partial(relay_part, rows_right, points, i) for i in range(RELAYS)},
    )

    half = LANES + 8
    absorbed, linv, *blocks = pl.pallas_call(
        functools.partial(absorb_kernel, math.sqrt(rank_left * total_points)),
        in_specs=[vmem] * (2 + 2 * RELAYS),
        out_specs=[vmem] * 4,
        out_shape=[shape(points, RK, rank_right), shape(RK, RK)] + [shape(half, LANES)] * 2,
        scratch_shapes=[
            pltpu.VMEM((2 * RK, LANES), F32),
            pltpu.VMEM((2 * half, LANES), F32),
            pltpu.VMEM((LANES, 3 * LANES), F32),
            pltpu.VMEM((rank_right, 2 * rank_right), F32),
        ],
        compiler_params=params(limit=24 * 1024 * 1024),
        name="factor_absorb",
    )(*summed, *[r[0] for r in relayed], *[r[1] for r in relayed])
    summed, (right_out, left_out) = sum_over_devices(
        blocks,
        {
            2: functools.partial(right_part, absorbed),
            3: functools.partial(left_part, unfold, linv),
        },
    )

    factor = pl.pallas_call(
        functools.partial(factor_kernel, 1.0 / (RK * total_points)),
        in_specs=[vmem] * 2,
        out_specs=vmem,
        out_shape=shape(rank_right, rank_right),
        scratch_shapes=[
            pltpu.VMEM((2 * half, LANES), F32),
            pltpu.VMEM((LANES, 2 * LANES), F32),
            pltpu.VMEM((LANES, LANES), F32),
        ],
        compiler_params=params(limit=16 * 1024 * 1024),
        name="factor_next",
    )(*summed)
    return (
        left_out.reshape(rank_left, points, RK),
        right_out.reshape(RK, points, rank_right),
        factor,
    )


def solution(mesh):
    in_specs = (P(None, AXES, None), P(None, AXES, None))
    out_specs = (P(None, AXES, None), P(None, AXES, None), P())
    return jax.shard_map(
        per_device, mesh=mesh, in_specs=in_specs, out_specs=out_specs, check_vma=False
    )
```

time: 88.9 us -> 65 us (0.73)
  blocking collectives: 18 us -> 0 us
  waiting for transfers between devices: 4.16 us -> 19.3 us
  local copies, waits for them, and re-layouts: 13.9 us -> 2.2 us
  Pallas kernels: 33.1 us -> 25.2 us
  starting transfers between devices: 18.2 us -> 16.5 us
  other arithmetic: 0 us -> 0.95 us
    ppermute x0 -> x12, waiting for transfers between devices: none -> 19.3 us  [exchange(): return lax.ppermute(value, axis, [(i, i ^ bit) for i in range(size)])]
    all_to_all x4 -> x0, starting transfers between devices: 18.2 us -> none  [the longest x2 9.61 us: sum_over_devices(): received = lax.all_to_all(copies, 'gz', 0, 0)]
    all_to_all x2 -> x0, blocking collectives: 18 us -> none  [sum_over_devices(): gathered = lax.all_to_all(copies, SCATTER, 0, 0)]
    ppermute x0 -> x12, starting transfers between devices: none -> 16.5 us  [exchange(): return lax.ppermute(value, axis, [(i, i ^ bit) for i in range(size)])]
    unnamed x20 -> x4, local copies, waits for them, and re-layouts: 13.9 us -> 2.19 us
    pallas_call x5 -> x1, Pallas kernels: 9.12 us -> 4.33 us  [per_device(): pl.pallas_call(gram_kernel, in_specs=[pl.BlockSpec(memory_space=pl.ANY)],...]
    all_to_all x4 -> x0, waiting for transfers between devices: 4.16 us -> none  [the longest x2 3.66 us: sum_over_devices(): received = lax.all_to_all(copies, 'gz', 0, 0)]
    pallas_call x1, Pallas kernels: 8.93 us -> 7.02 us  [per_device(): pl.pallas_call(functools.partial(factor_kernel, 1.0 / (RK * total_points)...]
  transfers between devices with their start and end apart: 4 -> 12, of which waited for: 4 -> 11; matrix products, arithmetic and copies ran while one was open for 0% -> 0% of each run, Pallas kernels for 9% -> 12%
where the time goes in v4:
time: 65 us; the launch traced here: 64.8 us
  Pallas kernels  25.2 us (39%)
  waiting for transfers between devices  19.3 us (30%)
  starting transfers between devices  16.5 us (25%)
  local copies, waits for them, and re-layouts  2.2 us (3%)
  other arithmetic  0.95 us (1%)
  between operations  0.74 us (1%)
    ppermute x12, waiting for transfers between devices, exchange(): return lax.ppermute(value, axis, [(i, i ^ bit) for i in range(size)])  19.3 us
    ppermute x12, starting transfers between devices, exchange(): return lax.ppermute(value, axis, [(i, i ^ bit) for i in range(size)])  16.5 us
    pallas_call x1, Pallas kernels, per_device(): pl.pallas_call(functools.partial(factor_kernel, 1.0 / (RK * total_points)...  7.02 us
    pallas_call x1, Pallas kernels, per_device(): pl.pallas_call(functools.partial(absorb_kernel, math.sqrt(rank_left * tot...  6.15 us
    pallas_call x1, Pallas kernels, per_device(): pl.pallas_call(gram_kernel, in_specs=[pl.BlockSpec(memory_space=pl.ANY)],...  4.33 us
    pallas_call x1, Pallas kernels, left_part(): pl.pallas_call(left_kernel, grid=(steps,), in_specs=[pl.BlockSpec((chunk,...  2.83 us
    pallas_call x1, Pallas kernels, right_part(): pl.pallas_call(functools.partial(right_kernel, points), grid=(steps, 2),...  2.5 us
    pallas_call x2, Pallas kernels, relay_part(): pl.pallas_call(functools.partial(relay_kernel, points), grid=(steps,), in...  2.37 us
  transfers between devices with their start and end apart: 12, of which 11 were waited for; matrix products, arithmetic and copies ran while one was open for 0% of the time, Pallas kernels for 12%

profile of v4, /device:TPU:0, one launch (start us, length us, event | category | flops | bytes accessed | tf_op | source)
XLA Modules:
  0.0 64.8 jit_solution(8148389960345882327)
XLA Ops:
  0.6 4.3 %gram_top.1 = (f32[128,128]{1,0:T(8,128)}, f32[128,128]{1,0:T(8,128)}) custom-call(f32[4096,256]{1,0:T(8,128)} %bitcast.16), custom_call_target="tpu_custom_call" | custom-call | tf_op jit(solution)/shard_map/gram_top/pallas_call | solution.py:357
  5.5 1.1 %collective-permute-done = f32[128,128]{1,0:T(8,128)S(1)} collective-permute-done((f32[128,128]{1,0:T(8,128)}, f32[128,128]{1,0:T(8,128)S(1)}, u32[]{:S(2)}, u32[]{:S(2)}) %collective-permute-start) | collective-permute-done | bytes 65568 | tf_op jit(solution)/shard_map/ppermute | solution.py:259
  7.5 2.9 %collective-permute-start.1 = (f32[128,128]{1,0:T(8,128)S(1)}, f32[128,128]{1,0:T(8,128)S(1)}, u32[]{:S(2)}, u32[]{:S(2)}) collective-permute-start(f32[128,128]{1,0:T(8,128)S(1)} %add.70), channel_id=1, source_target_pairs={{0,8},{4,12},{8,0},{12,4},{1,9},{5,13},{9,1},{13,5},{2,10},{6,14},... | collective-permute-start | bytes 196616 | tf_op jit(solution)/shard_map/ppermute | solution.py:259
  10.4 2.4 %collective-permute-done.1 = f32[128,128]{1,0:T(8,128)S(1)} collective-permute-done((f32[128,128]{1,0:T(8,128)S(1)}, f32[128,128]{1,0:T(8,128)S(1)}, u32[]{:S(2)}, u32[]{:S(2)}) %collective-permute-start.1) | collective-permute-done | bytes 65568 | tf_op jit(solution)/shard_map/ppermute | solution.py:259
  12.8 1.9 %collective-permute-start.2 = (f32[128,128]{1,0:T(8,128)S(1)}, f32[128,128]{1,0:T(8,128)S(1)}, u32[]{:S(2)}, u32[]{:S(2)}) collective-permute-start(f32[128,128]{1,0:T(8,128)S(1)} %add.71), channel_id=1, source_target_pairs={{0,16},{16,0},{1,17},{17,1},{2,18},{18,2},{3,19},{19,3},{4,20},{20... | collective-permute-start | bytes 196616 | tf_op jit(solution)/shard_map/ppermute | solution.py:259
  14.7 2.4 %collective-permute-done.2 = f32[128,128]{1,0:T(8,128)S(1)} collective-permute-done((f32[128,128]{1,0:T(8,128)S(1)}, f32[128,128]{1,0:T(8,128)S(1)}, u32[]{:S(2)}, u32[]{:S(2)}) %collective-permute-start.2) | collective-permute-done | bytes 65568 | tf_op jit(solution)/shard_map/ppermute | solution.py:259
  17.1 2.0 %collective-permute-start.3 = (f32[128,128]{1,0:T(8,128)S(1)}, f32[128,128]{1,0:T(8,128)S(1)}, u32[]{:S(2)}, u32[]{:S(2)}) collective-permute-start(f32[128,128]{1,0:T(8,128)S(1)} %add.72._), channel_id=1, source_target_pairs={{0,1},{1,0},{2,3},{3,2},{4,5},{5,4},{6,7},{7,6},{8,9},{9,8},{10,11... | collective-permute-start | bytes 196616 | tf_op jit(solution)/shard_map/ppermute | solution.py:259
  19.1 2.2 %copy-done = f32[256,16,256]{2,1,0:T(8,128)S(1)} copy-done((f32[256,16,256]{2,1,0:T(8,128)S(1)}, f32[256,16,256]{2,1,0:T(8,128)}, u32[]{:S(2)}) %copy-start) | copy-done | bytes 4194328
  21.3 1.2 %relay_right.2 = (bf16[16,128,256]{2,1,0:T(8,128)(2,1)S(1)}, bf16[16,128,256]{2,1,0:T(8,128)(2,1)S(1)}, f32[8,128]{1,0:T(8,128)S(1)}) custom-call(f32[4096,256]{1,0:T(8,128)S(1)} %bitcast.12, f32[4096,256]{1,0:T(8,128)S(1)} %bitcast.13, f32[128,128]{1,0:T(8,128)S(1)} %add.72._), custom_call_target="tpu_custom_call" | custom-call | bytes 8388608 | tf_op jit(solution)/shard_map/relay_right/pallas_call | solution.py:286
  22.5 2.7 %collective-permute-start.4 = (f32[128,128]{1,0:T(8,128)S(1)}, f32[128,128]{1,0:T(8,128)S(1)}, u32[]{:S(2)}, u32[]{:S(2)}) collective-permute-start(f32[128,128]{1,0:T(8,128)S(1)} %add_add_fusion.3._), channel_id=1, source_target_pairs={{0,2},{1,3},{2,0},{3,1},{4,6},{5,7},{6,4},{7,5},{8,10},{9,11},{10,... | collective-permute-start | bytes 196616 | tf_op jit(solution)/shard_map/ppermute | solution.py:259
  25.2 1.2 %relay_right.3 = (bf16[16,128,256]{2,1,0:T(8,128)(2,1)S(1)}, bf16[16,128,256]{2,1,0:T(8,128)(2,1)S(1)}, f32[8,128]{1,0:T(8,128)S(1)}) custom-call(f32[4096,256]{1,0:T(8,128)S(1)} %bitcast.14, f32[4096,256]{1,0:T(8,128)S(1)} %bitcast.15, f32[128,128]{1,0:T(8,128)S(1)} %add_add_fusion.3._), custom_call_target="tpu_custom_call" | custom-call | bytes 8388608 | tf_op jit(solution)/shard_map/relay_right/pallas_call | solution.py:286
  26.4 2.1 %collective-permute-done.4 = f32[128,128]{1,0:T(8,128)S(1)} collective-permute-done((f32[128,128]{1,0:T(8,128)S(1)}, f32[128,128]{1,0:T(8,128)S(1)}, u32[]{:S(2)}, u32[]{:S(2)}) %collective-permute-start.4) | collective-permute-done | bytes 65568 | tf_op jit(solution)/shard_map/ppermute | solution.py:259
  28.6 1.2 %collective-permute-done.5.other_ref = f32[128,128]{1,0:T(8,128)S(1)} collective-permute-done((f32[128,128]{1,0:T(8,128)S(1)}, f32[128,128]{1,0:T(8,128)S(1)}, u32[]{:S(2)}, u32[]{:S(2)}) %collective-permute-start.5) | collective-permute-done | bytes 65568 | tf_op jit(solution)/shard_map/ppermute | solution.py:259
  29.8 6.2 %factor_absorb.1 = (f32[16,128,256]{2,1,0:T(8,128)S(1)}, f32[128,128]{1,0:T(8,128)S(1)}, f32[136,128]{1,0:T(8,128)S(1)}, f32[136,128]{1,0:T(8,128)S(1)}) custom-call(f32[128,128]{1,0:T(8,128)S(1)} %add_add_fusion.2.own_ref, f32[128,128]{1,0:T(8,128)S(1)} %collective-permute-done.5.other_ref, bf16[16,128,256]{2,1,0:T(8,128)(2,1)S(1)} %get-tuple-element.23.refs_0_, ...), custom_call_target="tpu_custom_call" | custom-call | tf_op jit(solution)/shard_map/factor_absorb/pallas_call | solution.py:376
  37.3 1.6 %collective-permute-start.7 = (f32[136,128]{1,0:T(8,128)S(1)}, f32[136,128]{1,0:T(8,128)S(1)}, u32[]{:S(2)}, u32[]{:S(2)}) collective-permute-start(f32[136,128]{1,0:T(8,128)S(1)} %add.81), channel_id=1, source_target_pairs={{0,8},{4,12},{8,0},{12,4},{1,9},{5,13},{9,1},{13,5},{2,10},{6,14},... | collective-permute-start | bytes 208904 | tf_op jit(solution)/shard_map/ppermute | solution.py:259
  38.9 2.8 %collective-permute-done.7 = f32[136,128]{1,0:T(8,128)S(1)} collective-permute-done((f32[136,128]{1,0:T(8,128)S(1)}, f32[136,128]{1,0:T(8,128)S(1)}, u32[]{:S(2)}, u32[]{:S(2)}) %collective-permute-start.7) | collective-permute-done | bytes 69664 | tf_op jit(solution)/shard_map/ppermute | solution.py:259
  41.7 1.6 %collective-permute-start.8 = (f32[136,128]{1,0:T(8,128)S(1)}, f32[136,128]{1,0:T(8,128)S(1)}, u32[]{:S(2)}, u32[]{:S(2)}) collective-permute-start(f32[136,128]{1,0:T(8,128)S(1)} %add.82), channel_id=1, source_target_pairs={{0,16},{16,0},{1,17},{17,1},{2,18},{18,2},{3,19},{19,3},{4,20},{20... | collective-permute-start | bytes 208904 | tf_op jit(solution)/shard_map/ppermute | solution.py:259
  43.2 2.8 %collective-permute-done.8 = f32[136,128]{1,0:T(8,128)S(1)} collective-permute-done((f32[136,128]{1,0:T(8,128)S(1)}, f32[136,128]{1,0:T(8,128)S(1)}, u32[]{:S(2)}, u32[]{:S(2)}) %collective-permute-start.8) | collective-permute-done | bytes 69664 | tf_op jit(solution)/shard_map/ppermute | solution.py:259
  46.4 2.5 %right_out.1 = (f32[2048,256]{1,0:T(8,128)}, f32[8,128]{1,0:T(8,128)S(1)}) custom-call(f32[16,128,256]{2,1,0:T(8,128)S(1)} %get-tuple-element.30.absorbed_ref, f32[136,128]{1,0:T(8,128)S(1)} %add.83._), custom_call_target="tpu_custom_call" | custom-call | bytes 8388608 | tf_op jit(solution)/shard_map/right_out/pallas_call | solution.py:329
  48.9 1.5 %collective-permute-done.9 = f32[136,128]{1,0:T(8,128)S(1)} collective-permute-done((f32[136,128]{1,0:T(8,128)S(1)}, f32[136,128]{1,0:T(8,128)S(1)}, u32[]{:S(2)}, u32[]{:S(2)}) %collective-permute-start.9) | collective-permute-done | bytes 69664 | tf_op jit(solution)/shard_map/ppermute | solution.py:259
  50.5 2.7 %collective-permute-start.10 = (f32[136,128]{1,0:T(8,128)S(1)}, f32[136,128]{1,0:T(8,128)S(1)}, u32[]{:S(2)}, u32[]{:S(2)}) collective-permute-start(f32[136,128]{1,0:T(8,128)S(1)} %add_add_fusion.1._), channel_id=1, source_target_pairs={{0,2},{1,3},{2,0},{3,1},{4,6},{5,7},{6,4},{7,5},{8,10},{9,11},{10,... | collective-permute-start | bytes 208904 | tf_op jit(solution)/shard_map/ppermute | solution.py:259
  53.1 2.8 %left_out.1 = (f32[4096,128]{1,0:T(8,128)}, f32[8,128]{1,0:T(8,128)S(1)}) custom-call(f32[4096,256]{1,0:T(8,128)S(1)} %bitcast.17, f32[128,128]{1,0:T(8,128)S(1)} %get-tuple-element.27.linv_ref, f32[136,128]{1,0:T(8,128)S(1)} %add_add_fusion.1._), custom_call_target="tpu_custom_call" | custom-call | bytes 8388608 | tf_op jit(solution)/shard_map/left_out/pallas_call | solution.py:307
  56.6 1.2 %collective-permute-done.11.other_ref = f32[136,128]{1,0:T(8,128)S(1)} collective-permute-done((f32[136,128]{1,0:T(8,128)S(1)}, f32[136,128]{1,0:T(8,128)S(1)}, u32[]{:S(2)}, u32[]{:S(2)}) %collective-permute-start.11) | collective-permute-done | bytes 69664 | tf_op jit(solution)/shard_map/ppermute | solution.py:259
  57.8 7.0 %factor_next.1 = f32[256,256]{1,0:T(8,128)} custom-call(f32[136,128]{1,0:T(8,128)S(1)} %add_add_fusion.own_ref, f32[136,128]{1,0:T(8,128)S(1)} %collective-permute-done.11.other_ref), custom_call_target="tpu_custom_call" | custom-call | tf_op jit(solution)/shard_map/factor_next/pallas_call | solution.py:398
  (25 shorter events, 3.8 us)
Async XLA Ops:
  5.0 1.6 %collective-permute-start = (f32[128,128]{1,0:T(8,128)}, f32[128,128]{1,0:T(8,128)S(1)}, u32[]{:S(2)}, u32[]{:S(2)}) collective-permute-start(f32[128,128]{1,0:T(8,128)} %get-tuple-element.20), channel_id=1, source_target_pairs={{0,4},{4,0},{8,12},{12,8},{1,5},{5,1},{9,13},{13,9},{2,6},{6,2},{1... | collective-permute-start | bytes 196616 | tf_op jit(solution)/shard_map/ppermute | solution.py:259
  7.5 5.3 %collective-permute-start.1 = (f32[128,128]{1,0:T(8,128)S(1)}, f32[128,128]{1,0:T(8,128)S(1)}, u32[]{:S(2)}, u32[]{:S(2)}) collective-permute-start(f32[128,128]{1,0:T(8,128)S(1)} %add.70), channel_id=1, source_target_pairs={{0,8},{4,12},{8,0},{12,4},{1,9},{5,13},{9,1},{13,5},{2,10},{6,14},... | collective-permute-start | bytes 196616 | tf_op jit(solution)/shard_map/ppermute | solution.py:259
  12.8 4.3 %collective-permute-start.2 = (f32[128,128]{1,0:T(8,128)S(1)}, f32[128,128]{1,0:T(8,128)S(1)}, u32[]{:S(2)}, u32[]{:S(2)}) collective-permute-start(f32[128,128]{1,0:T(8,128)S(1)} %add.71), channel_id=1, source_target_pairs={{0,16},{16,0},{1,17},{17,1},{2,18},{18,2},{3,19},{19,3},{4,20},{20... | collective-permute-start | bytes 196616 | tf_op jit(solution)/shard_map/ppermute | solution.py:259
  17.1 5.4 %collective-permute-start.3 = (f32[128,128]{1,0:T(8,128)S(1)}, f32[128,128]{1,0:T(8,128)S(1)}, u32[]{:S(2)}, u32[]{:S(2)}) collective-permute-start(f32[128,128]{1,0:T(8,128)S(1)} %add.72._), channel_id=1, source_target_pairs={{0,1},{1,0},{2,3},{3,2},{4,5},{5,4},{6,7},{7,6},{8,9},{9,8},{10,11... | collective-permute-start | bytes 196616 | tf_op jit(solution)/shard_map/ppermute | solution.py:259
  19.1 2.2 %copy-start = (f32[256,16,256]{2,1,0:T(8,128)S(1)}, f32[256,16,256]{2,1,0:T(8,128)}, u32[]{:S(2)}) copy-start(f32[256,16,256]{2,1,0:T(8,128)} %param.3) | copy-start | bytes 12582916
  22.5 5.9 %collective-permute-start.4 = (f32[128,128]{1,0:T(8,128)S(1)}, f32[128,128]{1,0:T(8,128)S(1)}, u32[]{:S(2)}, u32[]{:S(2)}) collective-permute-start(f32[128,128]{1,0:T(8,128)S(1)} %add_add_fusion.3._), channel_id=1, source_target_pairs={{0,2},{1,3},{2,0},{3,1},{4,6},{5,7},{6,4},{7,5},{8,10},{9,11},{10,... | collective-permute-start | bytes 196616 | tf_op jit(solution)/shard_map/ppermute | solution.py:259
  28.5 1.3 %collective-permute-start.5 = (f32[128,128]{1,0:T(8,128)S(1)}, f32[128,128]{1,0:T(8,128)S(1)}, u32[]{:S(2)}, u32[]{:S(2)}) collective-permute-start(f32[128,128]{1,0:T(8,128)S(1)} %add_add_fusion.2.own_ref), channel_id=1, source_target_pairs={{0,4},{4,0},{8,12},{12,8},{1,5},{5,1},{9,13},{13,9},{2,6},{6,2},{1... | collective-permute-start | bytes 196616 | tf_op jit(solution)/shard_map/ppermute | solution.py:259
  29.8 23.3 %copy-start.1 = (f32[256,16,256]{2,1,0:T(8,128)S(1)}, f32[256,16,256]{2,1,0:T(8,128)}, u32[]{:S(2)}) copy-start(f32[256,16,256]{2,1,0:T(8,128)} %param.2) | copy-start | bytes 12582916
  36.0 1.3 %collective-permute-start.6 = (f32[136,128]{1,0:T(8,128)S(1)}, f32[136,128]{1,0:T(8,128)S(1)}, u32[]{:S(2)}, u32[]{:S(2)}) collective-permute-start(f32[136,128]{1,0:T(8,128)S(1)} %get-tuple-element.29), channel_id=1, source_target_pairs={{0,4},{4,0},{8,12},{12,8},{1,5},{5,1},{9,13},{13,9},{2,6},{6,2},{1... | collective-permute-start | bytes 208904 | tf_op jit(solution)/shard_map/ppermute | solution.py:259
  37.3 4.4 %collective-permute-start.7 = (f32[136,128]{1,0:T(8,128)S(1)}, f32[136,128]{1,0:T(8,128)S(1)}, u32[]{:S(2)}, u32[]{:S(2)}) collective-permute-start(f32[136,128]{1,0:T(8,128)S(1)} %add.81), channel_id=1, source_target_pairs={{0,8},{4,12},{8,0},{12,4},{1,9},{5,13},{9,1},{13,5},{2,10},{6,14},... | collective-permute-start | bytes 208904 | tf_op jit(solution)/shard_map/ppermute | solution.py:259
  41.7 4.4 %collective-permute-start.8 = (f32[136,128]{1,0:T(8,128)S(1)}, f32[136,128]{1,0:T(8,128)S(1)}, u32[]{:S(2)}, u32[]{:S(2)}) collective-permute-start(f32[136,128]{1,0:T(8,128)S(1)} %add.82), channel_id=1, source_target_pairs={{0,16},{16,0},{1,17},{17,1},{2,18},{18,2},{3,19},{19,3},{4,20},{20... | collective-permute-start | bytes 208904 | tf_op jit(solution)/shard_map/ppermute | solution.py:259
  46.1 4.4 %collective-permute-start.9 = (f32[136,128]{1,0:T(8,128)S(1)}, f32[136,128]{1,0:T(8,128)S(1)}, u32[]{:S(2)}, u32[]{:S(2)}) collective-permute-start(f32[136,128]{1,0:T(8,128)S(1)} %add.83._), channel_id=1, source_target_pairs={{0,1},{1,0},{2,3},{3,2},{4,5},{5,4},{6,7},{7,6},{8,9},{9,8},{10,11... | collective-permute-start | bytes 208904 | tf_op jit(solution)/shard_map/ppermute | solution.py:259
  50.5 6.0 %collective-permute-start.10 = (f32[136,128]{1,0:T(8,128)S(1)}, f32[136,128]{1,0:T(8,128)S(1)}, u32[]{:S(2)}, u32[]{:S(2)}) collective-permute-start(f32[136,128]{1,0:T(8,128)S(1)} %add_add_fusion.1._), channel_id=1, source_target_pairs={{0,2},{1,3},{2,0},{3,1},{4,6},{5,7},{6,4},{7,5},{8,10},{9,11},{10,... | collective-permute-start | bytes 208904 | tf_op jit(solution)/shard_map/ppermute | solution.py:259
  56.5 1.3 %collective-permute-start.11 = (f32[136,128]{1,0:T(8,128)S(1)}, f32[136,128]{1,0:T(8,128)S(1)}, u32[]{:S(2)}, u32[]{:S(2)}) collective-permute-start(f32[136,128]{1,0:T(8,128)S(1)} %add_add_fusion.own_ref), channel_id=1, source_target_pairs={{0,4},{4,0},{8,12},{12,8},{1,5},{5,1},{9,13},{13,9},{2,6},{6,2},{1... | collective-permute-start | bytes 208904 | tf_op jit(solution)/shard_map/ppermute | solution.py:259

commit v5 on v4

--- a/solution.py
+++ b/solution.py
@@ -11,7 +11,7 @@
 RK = 128
 AXES = ("gx", "gy", "gz")
 LANES = 128
-RELAYS = 2
+PANEL = 16
 F32 = jnp.float32
 BF16 = jnp.bfloat16
 VMEM_LIMIT = 48 * 1024 * 1024
@@ -48,56 +48,75 @@
     return jnp.broadcast_to(x[k : k + 1, :], x.shape)
 
 
-def factor_rows(w_ref, blocks, panel):
+def factor_rows(w_ref, blocks):
     row_id = lax.broadcasted_iota(jnp.int32, (8, LANES), 0)
-    groups = panel // 8
-    for start in range(0, LANES, panel):
-        rows = [
-            [
-                w_ref[start + 8 * v : start + 8 * v + 8, b * LANES : (b + 1) * LANES]
-                for b in range(blocks)
-            ]
-            for v in range(groups)
-        ]
+    groups = PANEL // 8
+    rows = [
+        [w_ref[g : g + 8, b * LANES : (b + 1) * LANES] for b in range(blocks)]
+        for g in range(0, LANES, 8)
+    ]
+    for start in range(0, LANES, PANEL):
+        base = start // 8
+        last = start + PANEL == LANES
         columns = [
             [
-                jnp.broadcast_to(rows[v][0][:, start + k : start + k + 1], (8, LANES))
+                jnp.broadcast_to(rows[base + v][0][:, start + k : start + k + 1], (8, LANES))
                 for v in range(groups)
             ]
-            for k in range(panel)
+            for k in range(PANEL)
         ]
+        ahead_groups = 0 if last else groups
+        if not last:
+            turned = jnp.concatenate([rows[base + v][0] for v in range(groups)], axis=0).T
+            below_rows = [
+                turned[start + PANEL + 8 * v : start + PANEL + 8 * v + 8, :] for v in range(groups)
+            ]
+            ahead = [
+                [jnp.broadcast_to(below_rows[v][:, k : k + 1], (8, LANES)) for v in range(groups)]
+                for k in range(PANEL)
+            ]
         scales = [jnp.zeros((8, LANES), F32)] * groups
         pivot = spread_row(columns[0][0], 0)
-        for k in range(panel):
+        for k in range(PANEL):
             home, at = k // 8, k % 8
             inverse = pl.reciprocal(pivot, approx=True)
             scales[home] = jnp.where(row_id == at, lax.rsqrt(pivot), scales[home])
             multiples = [columns[k][v] * inverse for v in range(groups)]
-            for m in range(k + 1, panel):
+            ahead_multiples = [ahead[k][v] * inverse for v in range(ahead_groups)]
+            for m in range(k + 1, PANEL):
                 entry = spread_row(columns[k][m // 8], m % 8)
                 if m == k + 1:
                     pivot = spread_row(columns[m][m // 8], m % 8) - (entry * inverse) * entry
                 for v in range(m // 8, groups):
                     columns[m][v] = columns[m][v] - multiples[v] * entry
+                for v in range(ahead_groups):
+                    ahead[m][v] = ahead[m][v] - ahead_multiples[v] * entry
             for b in range(blocks):
-                source = spread_row(rows[home][b], at)
+                source = spread_row(rows[base + home][b], at)
                 for v in range(home, groups):
                     below = multiples[v]
                     if v == home:
                         below = jnp.where(row_id > at, below, 0.0)
-                    rows[v][b] = rows[v][b] - below * source
+                    rows[base + v][b] = rows[base + v][b] - below * source
+                for v in range(ahead_groups):
+                    g = base + groups + v
+                    rows[g][b] = rows[g][b] - ahead_multiples[v] * source
         done = [
-            jnp.concatenate([rows[v][b] * scales[v] for v in range(groups)], axis=0)
+            jnp.concatenate([rows[base + v][b] * scales[v] for v in range(groups)], axis=0)
             for b in range(blocks)
         ]
         for b in range(blocks):
-            w_ref[start : start + panel, b * LANES : (b + 1) * LANES] = done[b]
-        if start + panel < LANES:
+            w_ref[start : start + PANEL, b * LANES : (b + 1) * LANES] = done[b]
+        if start + 2 * PANEL < LANES:
             both = [stacked_pieces(x) for x in done]
             left = both[0][0]
             right = jnp.concatenate([x[1] for x in both], axis=1)
             update = dot_tn(left, right)
-            w_ref[start + panel :, :] = w_ref[start + panel :, :] - update[start + panel :, :]
+            for g in range(base + 2 * groups, LANES // 8):
+                for b in range(blocks):
+                    rows[g][b] = (
+                        rows[g][b] - update[8 * g : 8 * g + 8, b * LANES : (b + 1) * LANES]
+                    )
 
 
 def triangle_ids():
@@ -121,52 +140,87 @@
         tall_ref[pl.ds(pl.multiple_of((me ^ d) * size, 8), size), :] = block[...]
 
 
-def gram_kernel(a_hbm, first_ref, second_ref, a_ref, tall_ref, sems):
-    steps = a_ref.shape[0]
-    chunk = a_ref.shape[1]
+def chunk_copies(source, held, sems):
+    steps, chunk = held.shape[:2]
 
     def copy(i):
         return pltpu.make_async_copy(
-            a_hbm.at[pl.ds(i * chunk, chunk), :], a_ref.at[i], sems.at[i]
+            source.at[pl.ds(i * chunk, chunk), :], held.at[i], sems.at[i]
         )
 
     for i in range(steps):
         copy(i).start()
-    tall_ref[...] = jnp.zeros_like(tall_ref)
+    return copy
+
+
+def gram_kernel(a_hbm, first_ref, second_ref, a_ref, total_ref, tall_ref, sems):
+    copy = chunk_copies(a_hbm, a_ref, sems)
+    total_ref[...] = jnp.zeros_like(total_ref)
 
     def body(i, carry):
         copy(i).wait()
         hi, lo = split(a_ref[i])
-        both = dot_tn(hi[:, :RK], jnp.concatenate([hi, lo], axis=1))
-        top = both[:, :256] + both[:, 256:] + dot_tn(lo[:, :RK], hi)
-        tall_ref[:RK, :] += top[:, :RK]
-        tall_ref[RK:, :] += top[:, RK:]
+        total_ref[...] += dot_tn(hi, jnp.concatenate([hi, lo], axis=1))
         return carry
 
+    lax.fori_loop(0, a_ref.shape[0], body, 0)
+    width = a_ref.shape[2]
+    cross = total_ref[:, width : width + RK]
+    tall_ref[:RK, :] = total_ref[:RK, :RK] + total_ref[:RK, width : width + RK] + cross[:RK, :].T
+    tall_ref[RK:, :] = total_ref[:RK, RK:width] + total_ref[:RK, width + RK :] + cross[RK:, :].T
+    store_blocks(tall_ref, (first_ref, second_ref))
+
+
+def relay_kernel(points, r_hbm, _, hi_ref, lo_ref, token_ref, r_ref, sems):
+    token_ref[...] = jnp.zeros_like(token_ref)
+    halves, steps, chunk, _ = r_ref.shape
+    ranks = chunk // points
+
+    def copy(c, i):
+        return pltpu.make_async_copy(
+            r_hbm.at[pl.ds(i * chunk, chunk), pl.ds(c * LANES, LANES)],
+            r_ref.at[c, i],
+            sems.at[c, i],
+        )
+
+    for i in range(steps):
+        for c in range(halves):
+            copy(c, i).start()
+
+    def body(i, carry):
+        for c in range(halves):
+            copy(c, i).wait()
+            for p in range(points):
+                hi, lo = split(r_ref[c, i, pl.ds(p, ranks, stride=points), :])
+                place = pl.ds(pl.multiple_of(i * ranks, ranks), ranks)
+                hi_ref[p, place, c * LANES : (c + 1) * LANES] = hi
+                lo_ref[p, place, c * LANES : (c + 1) * LANES] = lo
+        return carry
+
     lax.fori_loop(0, steps, body, 0)
-    store_blocks(tall_ref, (first_ref, second_ref))
-
-
-def relay_kernel(points, left_ref, right_ref, _, hi_ref, lo_ref, token_ref):
-    token_ref[...] = jnp.zeros_like(token_ref)
-    count = left_ref.shape[0] // points
-    for p in range(points):
-        for c, half in enumerate((left_ref, right_ref)):
-            hi, lo = split(half[pl.ds(p, count, stride=points), :])
-            hi_ref[p, :, c * LANES : (c + 1) * LANES] = hi
-            lo_ref[p, :, c * LANES : (c + 1) * LANES] = lo
-
-
-def absorb_kernel(scale, own_ref, other_ref, *refs):
-    highs, lows = refs[:RELAYS], refs[RELAYS : 2 * RELAYS]
-    absorbed_ref, linv_ref, first_ref, second_ref = refs[2 * RELAYS : 2 * RELAYS + 4]
-    tall_ref, pack_ref, w_ref, total_ref = refs[2 * RELAYS + 4 :]
+
+
+def absorb_kernel(
+    scale,
+    own_ref,
+    other_ref,
+    hi_ref,
+    lo_ref,
+    absorbed_ref,
+    linv_ref,
+    first_ref,
+    second_ref,
+    tall_ref,
+    pack_ref,
+    w_ref,
+    total_ref,
+):
     row, col = triangle_ids()
     load_blocks((own_ref, other_ref), tall_ref)
     w_ref[:, :LANES] = tall_ref[:RK, :]
     w_ref[:, LANES : 2 * LANES] = tall_ref[RK:, :]
     w_ref[:, 2 * LANES :] = jnp.where(row == col, 1.0, 0.0).astype(F32)
-    factor_rows(w_ref, 3, 16)
+    factor_rows(w_ref, 3)
     linv_ref[...] = w_ref[:, 2 * LANES :] * scale
     upper = jnp.concatenate(
         [jnp.where(col >= row, w_ref[:, :LANES], 0.0), w_ref[:, LANES : 2 * LANES]], axis=1
@@ -181,10 +235,8 @@
         pieces = []
         for i in range(group):
             p = step * group + i
-            high = jnp.concatenate([ref[p] for ref in highs], axis=0)
-            low = jnp.concatenate([ref[p] for ref in lows], axis=0)
-            first = dot_nn(upper_both, high)
-            b = first[:RK, :] + first[RK:, :] + dot_nn(upper_hi, low)
+            first = dot_nn(upper_both, hi_ref[p])
+            b = first[:RK, :] + first[RK:, :] + dot_nn(upper_hi, lo_ref[p])
             absorbed_ref[p] = b
             pieces.append(split(b))
         b_hi = jnp.concatenate([x[0] for x in pieces], axis=0)
@@ -227,12 +279,12 @@
     w_ref[:, :LANES] = jnp.where(col >= row, packed, turned)
     w_ref[:, LANES:] = pack_ref[LANES : 2 * LANES, :] * scale
     rest_ref[...] = jnp.where(row > col, packed, jnp.where(row == col, diagonal, turned))
-    factor_rows(w_ref, 2, 32)
+    factor_rows(w_ref, 2)
     out_ref[:LANES, :LANES] = jnp.where(col >= row, w_ref[:, :LANES], 0.0)
     out_ref[:LANES, LANES:] = w_ref[:, LANES:]
     left, right = stacked_pieces(w_ref[:, LANES:])
     rest_ref[...] = rest_ref[...] - dot_tn(left, right)
-    factor_rows(rest_ref, 1, 32)
+    factor_rows(rest_ref, 1)
     out_ref[LANES:, :LANES] = jnp.zeros((LANES, LANES), F32)
     out_ref[LANES:, LANES:] = jnp.where(col >= row, rest_ref[...], 0.0)
 
@@ -278,26 +330,24 @@
     return [total, exchange(total, "gy", 1)], results
 
 
-def relay_part(rows_right, points, part, token):
+def relay_part(rows_right, points, token):
     steps = 4
-    chunk = rows_right.shape[0] // (RELAYS * steps)
-    ranks = chunk // points
-    width = rows_right.shape[1]
+    rows, width = rows_right.shape
+    chunk = rows // steps
+    vmem = pl.BlockSpec(memory_space=pltpu.VMEM)
     high, low, token = pl.pallas_call(
         functools.partial(relay_kernel, points),
-        grid=(steps,),
-        in_specs=[
-            pl.BlockSpec((chunk, LANES), lambda i: (part * steps + i, 0)),
-            pl.BlockSpec((chunk, LANES), lambda i: (part * steps + i, 1)),
-            pl.BlockSpec((8, LANES), lambda i: (0, 0)),
-        ],
-        out_specs=[pl.BlockSpec((points, ranks, width), lambda i: (0, i, 0))] * 2
-        + [pl.BlockSpec((8, LANES), lambda i: (0, 0))],
-        out_shape=[shape(points, steps * ranks, width, dtype=BF16)] * 2 + [TOKEN],
-        compiler_params=params(1, 16 * 1024 * 1024),
+        in_specs=[pl.BlockSpec(memory_space=pl.ANY), vmem],
+        out_specs=[vmem] * 3,
+        out_shape=[shape(points, rows // points, width, dtype=BF16)] * 2 + [TOKEN],
+        scratch_shapes=[
+            pltpu.VMEM((width // LANES, steps, chunk, LANES), F32),
+            pltpu.SemaphoreType.DMA((width // LANES, steps)),
+        ],
+        compiler_params=params(limit=47 * 1024 * 1024),
         cost_estimate=cost(8),
         name="relay_right",
-    )(rows_right, rows_right, token)
+    )(rows_right, token)
     return (high, low), token
 
 
@@ -361,21 +411,22 @@
         out_shape=[shape(half, LANES)] * 2,
         scratch_shapes=[
             pltpu.VMEM((steps, unfold.shape[0] // steps, rank_mid), F32),
+            pltpu.VMEM((rank_mid, 2 * rank_mid), F32),
             pltpu.VMEM((2 * half, LANES), F32),
             pltpu.SemaphoreType.DMA((steps,)),
         ],
-        compiler_params=params(limit=62 * 1024 * 1024),
+        compiler_params=params(limit=53 * 1024 * 1024),
         name="gram_top",
     )(unfold)
-    summed, relayed = sum_over_devices(
+    summed, (relayed,) = sum_over_devices(
         blocks,
-        {2 + i: functools.partial(relay_part, rows_right, points, i) for i in range(RELAYS)},
+        {3: functools.partial(relay_part, rows_right, points)},
     )
 
     half = LANES + 8
     absorbed, linv, *blocks = pl.pallas_call(
         functools.partial(absorb_kernel, math.sqrt(rank_left * total_points)),
-        in_specs=[vmem] * (2 + 2 * RELAYS),
+        in_specs=[vmem] * 4,
         out_specs=[vmem] * 4,
         out_shape=[shape(points, RK, rank_right), shape(RK, RK)] + [shape(half, LANES)] * 2,
         scratch_shapes=[
@@ -386,7 +437,7 @@
         ],
         compiler_params=params(limit=24 * 1024 * 1024),
         name="factor_absorb",
-    )(*summed, *[r[0] for r in relayed], *[r[1] for r in relayed])
+    )(*summed, *relayed)
     summed, (right_out, left_out) = sum_over_devices(
         blocks,
         {

time: 65 us -> 62.5 us (0.962)
  local copies, waits for them, and re-layouts: 2.2 us -> 0.01 us
  starting transfers between devices: 16.5 us -> 18.6 us
  waiting for transfers between devices: 19.3 us -> 18.4 us
  other arithmetic: 0.95 us -> 0.1 us
  Pallas kernels: 25.2 us -> 24.5 us
    unnamed x4 -> x2, local copies, waits for them, and re-layouts: 2.19 us -> 0.01 us
    ppermute x12, starting transfers between devices: 16.5 us -> 18.6 us  [exchange(): return lax.ppermute(value, axis, [(i, i ^ bit) for i in range(size)])]
    ppermute x12, waiting for transfers between devices: 19.3 us -> 18.4 us  [exchange(): return lax.ppermute(value, axis, [(i, i ^ bit) for i in range(size)])]
    add x2, other arithmetic: 0.86 us -> 0.02 us  [sum_over_devices(): total = blocks[0] + exchange(blocks[1], 'gy', 1)]
    pallas_call x2 -> x1, Pallas kernels: 2.37 us -> 2.8 us  [relay_part(): pl.pallas_call(functools.partial(relay_kernel, points), in_specs=[pl.Bloc...]
  transfers between devices with their start and end apart: 12 -> 12, of which waited for: 11 -> 11; matrix products, arithmetic and copies ran while one was open for 0% -> 0% of each run, Pallas kernels for 12% -> 13%
where the time goes in v5:
time: 62.5 us; the launch traced here: 62.3 us
  Pallas kernels  24.5 us (39%)
  starting transfers between devices  18.6 us (30%)
  waiting for transfers between devices  18.4 us (29%)
  between operations  0.73 us (1%)
    ppermute x12, starting transfers between devices, exchange(): return lax.ppermute(value, axis, [(i, i ^ bit) for i in range(size)])  18.6 us
    ppermute x12, waiting for transfers between devices, exchange(): return lax.ppermute(value, axis, [(i, i ^ bit) for i in range(size)])  18.4 us
    pallas_call x1, Pallas kernels, per_device(): pl.pallas_call(functools.partial(factor_kernel, 1.0 / (RK * total_points)...  6.75 us
    pallas_call x1, Pallas kernels, per_device(): pl.pallas_call(functools.partial(absorb_kernel, math.sqrt(rank_left * tot...  5.76 us
    pallas_call x1, Pallas kernels, per_device(): pl.pallas_call(gram_kernel, in_specs=[pl.BlockSpec(memory_space=pl.ANY)],...  3.85 us
    pallas_call x1, Pallas kernels, left_part(): pl.pallas_call(left_kernel, grid=(steps,), in_specs=[pl.BlockSpec((chunk,...  2.83 us
    pallas_call x1, Pallas kernels, relay_part(): pl.pallas_call(functools.partial(relay_kernel, points), in_specs=[pl.Bloc...  2.8 us
    pallas_call x1, Pallas kernels, right_part(): pl.pallas_call(functools.partial(right_kernel, points), grid=(steps, 2),...  2.49 us
  transfers between devices with their start and end apart: 12, of which 11 were waited for; matrix products, arithmetic and copies ran while one was open for 0% of the time, Pallas kernels for 13%

profile of v5, /device:TPU:0, one launch (start us, length us, event | category | flops | bytes accessed | tf_op | source)
XLA Modules:
  0.0 62.3 jit_solution(7111155009745925678)
XLA Ops:
  0.6 3.9 %gram_top.1 = (f32[128,128]{1,0:T(8,128)S(1)}, f32[128,128]{1,0:T(8,128)S(1)}) custom-call(f32[4096,256]{1,0:T(8,128)} %bitcast.10), custom_call_target="tpu_custom_call" | custom-call | tf_op jit(solution)/shard_map/gram_top/pallas_call | solution.py:407
  5.0 0.9 %collective-permute-done = f32[128,128]{1,0:T(8,128)S(1)} collective-permute-done((f32[128,128]{1,0:T(8,128)S(1)}, f32[128,128]{1,0:T(8,128)S(1)}, u32[]{:S(2)}, u32[]{:S(2)}) %collective-permute-start) | collective-permute-done | bytes 65568 | tf_op jit(solution)/shard_map/ppermute | solution.py:311
  5.9 2.9 %collective-permute-start.1 = (f32[128,128]{1,0:T(8,128)S(1)}, f32[128,128]{1,0:T(8,128)S(1)}, u32[]{:S(2)}, u32[]{:S(2)}) collective-permute-start(f32[128,128]{1,0:T(8,128)S(1)} %add.60), channel_id=1, source_target_pairs={{0,8},{4,12},{8,0},{12,4},{1,9},{5,13},{9,1},{13,5},{2,10},{6,14},... | collective-permute-start | bytes 196616 | tf_op jit(solution)/shard_map/ppermute | solution.py:311
  8.9 2.4 %collective-permute-done.1 = f32[128,128]{1,0:T(8,128)S(1)} collective-permute-done((f32[128,128]{1,0:T(8,128)S(1)}, f32[128,128]{1,0:T(8,128)S(1)}, u32[]{:S(2)}, u32[]{:S(2)}) %collective-permute-start.1) | collective-permute-done | bytes 65568 | tf_op jit(solution)/shard_map/ppermute | solution.py:311
  11.3 1.9 %collective-permute-start.2 = (f32[128,128]{1,0:T(8,128)S(1)}, f32[128,128]{1,0:T(8,128)S(1)}, u32[]{:S(2)}, u32[]{:S(2)}) collective-permute-start(f32[128,128]{1,0:T(8,128)S(1)} %add.61), channel_id=1, source_target_pairs={{0,16},{16,0},{1,17},{17,1},{2,18},{18,2},{3,19},{19,3},{4,20},{20... | collective-permute-start | bytes 196616 | tf_op jit(solution)/shard_map/ppermute | solution.py:311
  13.2 2.4 %collective-permute-done.2 = f32[128,128]{1,0:T(8,128)S(1)} collective-permute-done((f32[128,128]{1,0:T(8,128)S(1)}, f32[128,128]{1,0:T(8,128)S(1)}, u32[]{:S(2)}, u32[]{:S(2)}) %collective-permute-start.2) | collective-permute-done | bytes 65568 | tf_op jit(solution)/shard_map/ppermute | solution.py:311
  15.6 2.0 %collective-permute-start.3 = (f32[128,128]{1,0:T(8,128)S(1)}, f32[128,128]{1,0:T(8,128)S(1)}, u32[]{:S(2)}, u32[]{:S(2)}) collective-permute-start(f32[128,128]{1,0:T(8,128)S(1)} %add.62), channel_id=1, source_target_pairs={{0,1},{1,0},{2,3},{3,2},{4,5},{5,4},{6,7},{7,6},{8,9},{9,8},{10,11... | collective-permute-start | bytes 196616 | tf_op jit(solution)/shard_map/ppermute | solution.py:311
  17.6 2.4 %collective-permute-done.3 = f32[128,128]{1,0:T(8,128)S(1)} collective-permute-done((f32[128,128]{1,0:T(8,128)S(1)}, f32[128,128]{1,0:T(8,128)S(1)}, u32[]{:S(2)}, u32[]{:S(2)}) %collective-permute-start.3) | collective-permute-done | bytes 65568 | tf_op jit(solution)/shard_map/ppermute | solution.py:311
  20.0 3.7 %collective-permute-start.4 = (f32[128,128]{1,0:T(8,128)S(1)}, f32[128,128]{1,0:T(8,128)S(1)}, u32[]{:S(2)}, u32[]{:S(2)}) collective-permute-start(f32[128,128]{1,0:T(8,128)S(1)} %add.63._), channel_id=1, source_target_pairs={{0,2},{1,3},{2,0},{3,1},{4,6},{5,7},{6,4},{7,5},{8,10},{9,11},{10,... | collective-permute-start | bytes 196616 | tf_op jit(solution)/shard_map/ppermute | solution.py:311
  23.6 2.8 %relay_right.1 = (bf16[16,256,256]{2,1,0:T(8,128)(2,1)S(1)}, bf16[16,256,256]{2,1,0:T(8,128)(2,1)S(1)}, f32[8,128]{1,0:T(8,128)S(1)}) custom-call(f32[4096,256]{1,0:T(8,128)} %bitcast.12, f32[128,128]{1,0:T(8,128)S(1)} %add.63._), custom_call_target="tpu_custom_call" | custom-call | bytes 8388608 | tf_op jit(solution)/shard_map/relay_right/pallas_call | solution.py:338
  26.6 1.2 %collective-permute-done.5.other_ref = f32[128,128]{1,0:T(8,128)S(1)} collective-permute-done((f32[128,128]{1,0:T(8,128)S(1)}, f32[128,128]{1,0:T(8,128)S(1)}, u32[]{:S(2)}, u32[]{:S(2)}) %collective-permute-start.5) | collective-permute-done | bytes 65568 | tf_op jit(solution)/shard_map/ppermute | solution.py:311
  27.8 5.8 %factor_absorb.1 = (f32[16,128,256]{2,1,0:T(8,128)S(1)}, f32[128,128]{1,0:T(8,128)S(1)}, f32[136,128]{1,0:T(8,128)S(1)}, f32[136,128]{1,0:T(8,128)S(1)}) custom-call(f32[128,128]{1,0:T(8,128)S(1)} %add_add_fusion.2.own_ref, f32[128,128]{1,0:T(8,128)S(1)} %collective-permute-done.5.other_ref, bf16[16,256,256]{2,1,0:T(8,128)(2,1)S(1)} %get-tuple-element.19.hi_ref, ...), custom_call_target="tpu_custom_call" | custom-call | tf_op jit(solution)/shard_map/factor_absorb/pallas_call | solution.py:427
  33.8 1.1 %collective-permute-done.6 = f32[136,128]{1,0:T(8,128)S(1)} collective-permute-done((f32[136,128]{1,0:T(8,128)S(1)}, f32[136,128]{1,0:T(8,128)S(1)}, u32[]{:S(2)}, u32[]{:S(2)}) %collective-permute-start.6) | collective-permute-done | bytes 69664 | tf_op jit(solution)/shard_map/ppermute | solution.py:311
  34.9 1.6 %collective-permute-start.7 = (f32[136,128]{1,0:T(8,128)S(1)}, f32[136,128]{1,0:T(8,128)S(1)}, u32[]{:S(2)}, u32[]{:S(2)}) collective-permute-start(f32[136,128]{1,0:T(8,128)S(1)} %add.68), channel_id=1, source_target_pairs={{0,8},{4,12},{8,0},{12,4},{1,9},{5,13},{9,1},{13,5},{2,10},{6,14},... | collective-permute-start | bytes 208904 | tf_op jit(solution)/shard_map/ppermute | solution.py:311
  36.5 2.8 %collective-permute-done.7 = f32[136,128]{1,0:T(8,128)S(1)} collective-permute-done((f32[136,128]{1,0:T(8,128)S(1)}, f32[136,128]{1,0:T(8,128)S(1)}, u32[]{:S(2)}, u32[]{:S(2)}) %collective-permute-start.7) | collective-permute-done | bytes 69664 | tf_op jit(solution)/shard_map/ppermute | solution.py:311
  39.3 1.6 %collective-permute-start.8 = (f32[136,128]{1,0:T(8,128)S(1)}, f32[136,128]{1,0:T(8,128)S(1)}, u32[]{:S(2)}, u32[]{:S(2)}) collective-permute-start(f32[136,128]{1,0:T(8,128)S(1)} %add.69), channel_id=1, source_target_pairs={{0,16},{16,0},{1,17},{17,1},{2,18},{18,2},{3,19},{19,3},{4,20},{20... | collective-permute-start | bytes 208904 | tf_op jit(solution)/shard_map/ppermute | solution.py:311
  40.8 2.8 %collective-permute-done.8 = f32[136,128]{1,0:T(8,128)S(1)} collective-permute-done((f32[136,128]{1,0:T(8,128)S(1)}, f32[136,128]{1,0:T(8,128)S(1)}, u32[]{:S(2)}, u32[]{:S(2)}) %collective-permute-start.8) | collective-permute-done | bytes 69664 | tf_op jit(solution)/shard_map/ppermute | solution.py:311
  43.7 1.0 %collective-permute-start.9 = (f32[136,128]{1,0:T(8,128)S(1)}, f32[136,128]{1,0:T(8,128)S(1)}, u32[]{:S(2)}, u32[]{:S(2)}) collective-permute-start(f32[136,128]{1,0:T(8,128)S(1)} %add.70._), channel_id=1, source_target_pairs={{0,1},{1,0},{2,3},{3,2},{4,5},{5,4},{6,7},{7,6},{8,9},{9,8},{10,11... | collective-permute-start | bytes 208904 | tf_op jit(solution)/shard_map/ppermute | solution.py:311
  44.6 2.5 %right_out.1 = (f32[2048,256]{1,0:T(8,128)}, f32[8,128]{1,0:T(8,128)S(1)}) custom-call(f32[16,128,256]{2,1,0:T(8,128)S(1)} %get-tuple-element.24.absorbed_ref, f32[136,128]{1,0:T(8,128)S(1)} %add.70._), custom_call_target="tpu_custom_call" | custom-call | bytes 8388608 | tf_op jit(solution)/shard_map/right_out/pallas_call | solution.py:379
  47.1 0.9 %collective-permute-done.9 = f32[136,128]{1,0:T(8,128)S(1)} collective-permute-done((f32[136,128]{1,0:T(8,128)S(1)}, f32[136,128]{1,0:T(8,128)S(1)}, u32[]{:S(2)}, u32[]{:S(2)}) %collective-permute-start.9) | collective-permute-done | bytes 69664 | tf_op jit(solution)/shard_map/ppermute | solution.py:311
  48.1 3.1 %collective-permute-start.10 = (f32[136,128]{1,0:T(8,128)S(1)}, f32[136,128]{1,0:T(8,128)S(1)}, u32[]{:S(2)}, u32[]{:S(2)}) collective-permute-start(f32[136,128]{1,0:T(8,128)S(1)} %add_add_fusion.1._), channel_id=1, source_target_pairs={{0,2},{1,3},{2,0},{3,1},{4,6},{5,7},{6,4},{7,5},{8,10},{9,11},{10,... | collective-permute-start | bytes 208904 | tf_op jit(solution)/shard_map/ppermute | solution.py:311
  51.2 2.8 %left_out.1 = (f32[4096,128]{1,0:T(8,128)}, f32[8,128]{1,0:T(8,128)S(1)}) custom-call(f32[4096,256]{1,0:T(8,128)S(1)} %bitcast.11, f32[128,128]{1,0:T(8,128)S(1)} %get-tuple-element.21.linv_ref, f32[136,128]{1,0:T(8,128)S(1)} %add_add_fusion.1._), custom_call_target="tpu_custom_call" | custom-call | bytes 8388608 | tf_op jit(solution)/shard_map/left_out/pallas_call | solution.py:357
  54.3 1.2 %collective-permute-done.11.other_ref = f32[136,128]{1,0:T(8,128)S(1)} collective-permute-done((f32[136,128]{1,0:T(8,128)S(1)}, f32[136,128]{1,0:T(8,128)S(1)}, u32[]{:S(2)}, u32[]{:S(2)}) %collective-permute-start.11) | collective-permute-done | bytes 69664 | tf_op jit(solution)/shard_map/ppermute | solution.py:311
  55.6 6.8 %factor_next.1 = f32[256,256]{1,0:T(8,128)} custom-call(f32[136,128]{1,0:T(8,128)S(1)} %add_add_fusion.own_ref, f32[136,128]{1,0:T(8,128)S(1)} %collective-permute-done.11.other_ref), custom_call_target="tpu_custom_call" | custom-call | tf_op jit(solution)/shard_map/factor_next/pallas_call | solution.py:449
  (21 shorter events, 1.2 us)
Async XLA Ops:
  4.5 1.4 %collective-permute-start = (f32[128,128]{1,0:T(8,128)S(1)}, f32[128,128]{1,0:T(8,128)S(1)}, u32[]{:S(2)}, u32[]{:S(2)}) collective-permute-start(f32[128,128]{1,0:T(8,128)S(1)} %get-tuple-element.17), channel_id=1, source_target_pairs={{0,4},{4,0},{8,12},{12,8},{1,5},{5,1},{9,13},{13,9},{2,6},{6,2},{1... | collective-permute-start | bytes 196616 | tf_op jit(solution)/shard_map/ppermute | solution.py:311
  5.9 5.3 %collective-permute-start.1 = (f32[128,128]{1,0:T(8,128)S(1)}, f32[128,128]{1,0:T(8,128)S(1)}, u32[]{:S(2)}, u32[]{:S(2)}) collective-permute-start(f32[128,128]{1,0:T(8,128)S(1)} %add.60), channel_id=1, source_target_pairs={{0,8},{4,12},{8,0},{12,4},{1,9},{5,13},{9,1},{13,5},{2,10},{6,14},... | collective-permute-start | bytes 196616 | tf_op jit(solution)/shard_map/ppermute | solution.py:311
  11.3 4.3 %collective-permute-start.2 = (f32[128,128]{1,0:T(8,128)S(1)}, f32[128,128]{1,0:T(8,128)S(1)}, u32[]{:S(2)}, u32[]{:S(2)}) collective-permute-start(f32[128,128]{1,0:T(8,128)S(1)} %add.61), channel_id=1, source_target_pairs={{0,16},{16,0},{1,17},{17,1},{2,18},{18,2},{3,19},{19,3},{4,20},{20... | collective-permute-start | bytes 196616 | tf_op jit(solution)/shard_map/ppermute | solution.py:311
  15.6 4.3 %collective-permute-start.3 = (f32[128,128]{1,0:T(8,128)S(1)}, f32[128,128]{1,0:T(8,128)S(1)}, u32[]{:S(2)}, u32[]{:S(2)}) collective-permute-start(f32[128,128]{1,0:T(8,128)S(1)} %add.62), channel_id=1, source_target_pairs={{0,1},{1,0},{2,3},{3,2},{4,5},{5,4},{6,7},{7,6},{8,9},{9,8},{10,11... | collective-permute-start | bytes 196616 | tf_op jit(solution)/shard_map/ppermute | solution.py:311
  20.0 6.5 %collective-permute-start.4 = (f32[128,128]{1,0:T(8,128)S(1)}, f32[128,128]{1,0:T(8,128)S(1)}, u32[]{:S(2)}, u32[]{:S(2)}) collective-permute-start(f32[128,128]{1,0:T(8,128)S(1)} %add.63._), channel_id=1, source_target_pairs={{0,2},{1,3},{2,0},{3,1},{4,6},{5,7},{6,4},{7,5},{8,10},{9,11},{10,... | collective-permute-start | bytes 196616 | tf_op jit(solution)/shard_map/ppermute | solution.py:311
  26.5 1.3 %collective-permute-start.5 = (f32[128,128]{1,0:T(8,128)S(1)}, f32[128,128]{1,0:T(8,128)S(1)}, u32[]{:S(2)}, u32[]{:S(2)}) collective-permute-start(f32[128,128]{1,0:T(8,128)S(1)} %add_add_fusion.2.own_ref), channel_id=1, source_target_pairs={{0,4},{4,0},{8,12},{12,8},{1,5},{5,1},{9,13},{13,9},{2,6},{6,2},{1... | collective-permute-start | bytes 196616 | tf_op jit(solution)/shard_map/ppermute | solution.py:311
  27.8 23.4 %copy-start = (f32[256,16,256]{2,1,0:T(8,128)S(1)}, f32[256,16,256]{2,1,0:T(8,128)}, u32[]{:S(2)}) copy-start(f32[256,16,256]{2,1,0:T(8,128)} %param.2) | copy-start | bytes 12582916
  33.6 1.3 %collective-permute-start.6 = (f32[136,128]{1,0:T(8,128)S(1)}, f32[136,128]{1,0:T(8,128)S(1)}, u32[]{:S(2)}, u32[]{:S(2)}) collective-permute-start(f32[136,128]{1,0:T(8,128)S(1)} %get-tuple-element.23), channel_id=1, source_target_pairs={{0,4},{4,0},{8,12},{12,8},{1,5},{5,1},{9,13},{13,9},{2,6},{6,2},{1... | collective-permute-start | bytes 208904 | tf_op jit(solution)/shard_map/ppermute | solution.py:311
  34.9 4.4 %collective-permute-start.7 = (f32[136,128]{1,0:T(8,128)S(1)}, f32[136,128]{1,0:T(8,128)S(1)}, u32[]{:S(2)}, u32[]{:S(2)}) collective-permute-start(f32[136,128]{1,0:T(8,128)S(1)} %add.68), channel_id=1, source_target_pairs={{0,8},{4,12},{8,0},{12,4},{1,9},{5,13},{9,1},{13,5},{2,10},{6,14},... | collective-permute-start | bytes 208904 | tf_op jit(solution)/shard_map/ppermute | solution.py:311
  39.3 4.4 %collective-permute-start.8 = (f32[136,128]{1,0:T(8,128)S(1)}, f32[136,128]{1,0:T(8,128)S(1)}, u32[]{:S(2)}, u32[]{:S(2)}) collective-permute-start(f32[136,128]{1,0:T(8,128)S(1)} %add.69), channel_id=1, source_target_pairs={{0,16},{16,0},{1,17},{17,1},{2,18},{18,2},{3,19},{19,3},{4,20},{20... | collective-permute-start | bytes 208904 | tf_op jit(solution)/shard_map/ppermute | solution.py:311
  43.7 4.4 %collective-permute-start.9 = (f32[136,128]{1,0:T(8,128)S(1)}, f32[136,128]{1,0:T(8,128)S(1)}, u32[]{:S(2)}, u32[]{:S(2)}) collective-permute-start(f32[136,128]{1,0:T(8,128)S(1)} %add.70._), channel_id=1, source_target_pairs={{0,1},{1,0},{2,3},{3,2},{4,5},{5,4},{6,7},{7,6},{8,9},{9,8},{10,11... | collective-permute-start | bytes 208904 | tf_op jit(solution)/shard_map/ppermute | solution.py:311
  48.1 6.2 %collective-permute-start.10 = (f32[136,128]{1,0:T(8,128)S(1)}, f32[136,128]{1,0:T(8,128)S(1)}, u32[]{:S(2)}, u32[]{:S(2)}) collective-permute-start(f32[136,128]{1,0:T(8,128)S(1)} %add_add_fusion.1._), channel_id=1, source_target_pairs={{0,2},{1,3},{2,0},{3,1},{4,6},{5,7},{6,4},{7,5},{8,10},{9,11},{10,... | collective-permute-start | bytes 208904 | tf_op jit(solution)/shard_map/ppermute | solution.py:311
  54.3 1.3 %collective-permute-start.11 = (f32[136,128]{1,0:T(8,128)S(1)}, f32[136,128]{1,0:T(8,128)S(1)}, u32[]{:S(2)}, u32[]{:S(2)}) collective-permute-start(f32[136,128]{1,0:T(8,128)S(1)} %add_add_fusion.own_ref), channel_id=1, source_target_pairs={{0,4},{4,0},{8,12},{12,8},{1,5},{5,1},{9,13},{13,9},{2,6},{6,2},{1... | collective-permute-start | bytes 208904 | tf_op jit(solution)/shard_map/ppermute | solution.py:311

commit v6 on v5

--- a/solution.py
+++ b/solution.py
@@ -11,7 +11,10 @@
 RK = 128
 AXES = ("gx", "gy", "gz")
 LANES = 128
-PANEL = 16
+PANEL = 8
+PLANE = ("gx", "gy")
+SPREAD_ONE = 8
+SPREAD_TWO = 2
 F32 = jnp.float32
 BF16 = jnp.bfloat16
 VMEM_LIMIT = 48 * 1024 * 1024
@@ -49,73 +52,59 @@
 
 
 def factor_rows(w_ref, blocks):
-    row_id = lax.broadcasted_iota(jnp.int32, (8, LANES), 0)
-    groups = PANEL // 8
+    size = w_ref.shape[0]
+    row_id = lax.broadcasted_iota(jnp.int32, (PANEL, LANES), 0)
     rows = [
-        [w_ref[g : g + 8, b * LANES : (b + 1) * LANES] for b in range(blocks)]
-        for g in range(0, LANES, 8)
+        [w_ref[g : g + PANEL, b * LANES : (b + 1) * LANES] for b in range(blocks)]
+        for g in range(0, size, PANEL)
     ]
-    for start in range(0, LANES, PANEL):
-        base = start // 8
-        last = start + PANEL == LANES
+    for now in range(len(rows)):
+        own, lane = divmod(now * PANEL, LANES)
+        panel = rows[now]
         columns = [
-            [
-                jnp.broadcast_to(rows[base + v][0][:, start + k : start + k + 1], (8, LANES))
-                for v in range(groups)
-            ]
+            jnp.broadcast_to(panel[own][:, lane + k : lane + k + 1], (PANEL, LANES))
             for k in range(PANEL)
         ]
-        ahead_groups = 0 if last else groups
-        if not last:
-            turned = jnp.concatenate([rows[base + v][0] for v in range(groups)], axis=0).T
-            below_rows = [
-                turned[start + PANEL + 8 * v : start + PANEL + 8 * v + 8, :] for v in range(groups)
-            ]
-            ahead = [
-                [jnp.broadcast_to(below_rows[v][:, k : k + 1], (8, LANES)) for v in range(groups)]
-                for k in range(PANEL)
-            ]
-        scales = [jnp.zeros((8, LANES), F32)] * groups
-        pivot = spread_row(columns[0][0], 0)
+        follows = now + 1 < len(rows)
+        if follows:
+            block, down = divmod((now + 1) * PANEL, LANES)
+            turned = panel[block].T[down : down + PANEL, :]
+            ahead = [jnp.broadcast_to(turned[:, k : k + 1], (PANEL, LANES)) for k in range(PANEL)]
+        scale = jnp.zeros((PANEL, LANES), F32)
+        pivot = spread_row(columns[0], 0)
         for k in range(PANEL):
-            home, at = k // 8, k % 8
             inverse = pl.reciprocal(pivot, approx=True)
-            scales[home] = jnp.where(row_id == at, lax.rsqrt(pivot), scales[home])
-            multiples = [columns[k][v] * inverse for v in range(groups)]
-            ahead_multiples = [ahead[k][v] * inverse for v in range(ahead_groups)]
+            scale = jnp.where(row_id == k, lax.rsqrt(pivot), scale)
+            multiples = columns[k] * inverse
+            if follows:
+                ahead_multiples = ahead[k] * inverse
             for m in range(k + 1, PANEL):
-                entry = spread_row(columns[k][m // 8], m % 8)
+                entry = spread_row(columns[k], m)
                 if m == k + 1:
-                    pivot = spread_row(columns[m][m // 8], m % 8) - (entry * inverse) * entry
-                for v in range(m // 8, groups):
-                    columns[m][v] = columns[m][v] - multiples[v] * entry
-                for v in range(ahead_groups):
-                    ahead[m][v] = ahead[m][v] - ahead_multiples[v] * entry
-            for b in range(blocks):
-                source = spread_row(rows[base + home][b], at)
-                for v in range(home, groups):
-                    below = multiples[v]
-                    if v == home:
-                        below = jnp.where(row_id > at, below, 0.0)
-                    rows[base + v][b] = rows[base + v][b] - below * source
-                for v in range(ahead_groups):
-                    g = base + groups + v
-                    rows[g][b] = rows[g][b] - ahead_multiples[v] * source
-        done = [
-            jnp.concatenate([rows[base + v][b] * scales[v] for v in range(groups)], axis=0)
-            for b in range(blocks)
-        ]
-        for b in range(blocks):
-            w_ref[start : start + PANEL, b * LANES : (b + 1) * LANES] = done[b]
-        if start + 2 * PANEL < LANES:
+                    pivot = spread_row(columns[m], m) - (entry * inverse) * entry
+                columns[m] = columns[m] - multiples * entry
+                if follows:
+                    ahead[m] = ahead[m] - ahead_multiples * entry
+            below = jnp.where(row_id > k, multiples, 0.0)
+            for b in range(own, blocks):
+                source = spread_row(panel[b], k)
+                panel[b] = panel[b] - below * source
+                if follows:
+                    rows[now + 1][b] = rows[now + 1][b] - ahead_multiples * source
+        done = [panel[b] * scale for b in range(own, blocks)]
+        for b in range(own, blocks):
+            w_ref[now * PANEL : (now + 1) * PANEL, b * LANES : (b + 1) * LANES] = done[b - own]
+        if now + 2 < len(rows):
             both = [stacked_pieces(x) for x in done]
-            left = both[0][0]
+            left = jnp.concatenate([x[0] for x in both[: size // LANES - own]], axis=1)
             right = jnp.concatenate([x[1] for x in both], axis=1)
             update = dot_tn(left, right)
-            for g in range(base + 2 * groups, LANES // 8):
-                for b in range(blocks):
+            for g in range(now + 2, len(rows)):
+                top = g * PANEL - own * LANES
+                for b in range(g * PANEL // LANES, blocks):
+                    across = (b - own) * LANES
                     rows[g][b] = (
-                        rows[g][b] - update[8 * g : 8 * g + 8, b * LANES : (b + 1) * LANES]
+                        rows[g][b] - update[top : top + PANEL, across : across + LANES]
                     )
 
 
@@ -127,14 +116,14 @@
 
 
 def store_blocks(tall_ref, outs):
-    me = lax.rem(lax.axis_index("gy"), len(outs))
+    me = lax.rem(lax.axis_index(PLANE), len(outs))
     size = outs[0].shape[0]
     for d, out in enumerate(outs):
         out[...] = tall_ref[pl.ds(pl.multiple_of((me ^ d) * size, 8), size), :]
 
 
 def load_blocks(blocks, tall_ref):
-    me = lax.rem(lax.axis_index("gy"), len(blocks))
+    me = lax.rem(lax.axis_index(PLANE), len(blocks))
     size = blocks[0].shape[0]
     for d, block in enumerate(blocks):
         tall_ref[pl.ds(pl.multiple_of((me ^ d) * size, 8), size), :] = block[...]
@@ -153,7 +142,9 @@
     return copy
 
 
-def gram_kernel(a_hbm, first_ref, second_ref, a_ref, total_ref, tall_ref, sems):
+def gram_kernel(a_hbm, *refs):
+    outs = refs[:SPREAD_ONE]
+    a_ref, total_ref, tall_ref, sems = refs[SPREAD_ONE:]
     copy = chunk_copies(a_hbm, a_ref, sems)
     total_ref[...] = jnp.zeros_like(total_ref)
 
@@ -168,7 +159,7 @@
     cross = total_ref[:, width : width + RK]
     tall_ref[:RK, :] = total_ref[:RK, :RK] + total_ref[:RK, width : width + RK] + cross[:RK, :].T
     tall_ref[RK:, :] = total_ref[:RK, RK:width] + total_ref[:RK, width + RK :] + cross[RK:, :].T
-    store_blocks(tall_ref, (first_ref, second_ref))
+    store_blocks(tall_ref, outs)
 
 
 def relay_kernel(points, r_hbm, _, hi_ref, lo_ref, token_ref, r_ref, sems):
@@ -200,23 +191,13 @@
     lax.fori_loop(0, steps, body, 0)
 
 
-def absorb_kernel(
-    scale,
-    own_ref,
-    other_ref,
-    hi_ref,
-    lo_ref,
-    absorbed_ref,
-    linv_ref,
-    first_ref,
-    second_ref,
-    tall_ref,
-    pack_ref,
-    w_ref,
-    total_ref,
-):
+def absorb_kernel(scale, *refs):
+    blocks, refs = refs[:SPREAD_ONE], refs[SPREAD_ONE:]
+    hi_ref, lo_ref, absorbed_ref, linv_ref = refs[:4]
+    outs = refs[4 : 4 + SPREAD_TWO]
+    tall_ref, pack_ref, w_ref, total_ref = refs[4 + SPREAD_TWO :]
     row, col = triangle_ids()
-    load_blocks((own_ref, other_ref), tall_ref)
+    load_blocks(blocks, tall_ref)
     w_ref[:, :LANES] = tall_ref[:RK, :]
     w_ref[:, LANES : 2 * LANES] = tall_ref[RK:, :]
     w_ref[:, 2 * LANES :] = jnp.where(row == col, 1.0, 0.0).astype(F32)
@@ -253,7 +234,7 @@
     diagonal = jnp.sum(jnp.where(row == col, lower_right, 0.0), axis=0, keepdims=True)
     tail = pack_ref.shape[0] - 2 * LANES
     pack_ref[2 * LANES :, :] = jnp.broadcast_to(diagonal, (tail, LANES))
-    store_blocks(pack_ref, (first_ref, second_ref))
+    store_blocks(pack_ref, outs)
 
 
 def left_kernel(a_ref, linv_ref, _, left_ref, token_ref):
@@ -270,23 +251,22 @@
     token_ref[...] = jnp.zeros_like(token_ref)
 
 
-def factor_kernel(scale, own_ref, other_ref, out_ref, pack_ref, w_ref, rest_ref):
-    load_blocks((own_ref, other_ref), pack_ref)
+def factor_kernel(scale, *refs):
+    blocks, (out_ref, pack_ref, w_ref) = refs[:SPREAD_TWO], refs[SPREAD_TWO:]
+    load_blocks(blocks, pack_ref)
     row, col = triangle_ids()
     packed = pack_ref[:LANES, :] * scale
     turned = packed.T
     diagonal = jnp.broadcast_to(pack_ref[2 * LANES : 2 * LANES + 1, :], (LANES, LANES)) * scale
-    w_ref[:, :LANES] = jnp.where(col >= row, packed, turned)
-    w_ref[:, LANES:] = pack_ref[LANES : 2 * LANES, :] * scale
-    rest_ref[...] = jnp.where(row > col, packed, jnp.where(row == col, diagonal, turned))
+    w_ref[:LANES, :LANES] = jnp.where(col >= row, packed, turned)
+    w_ref[:LANES, LANES:] = pack_ref[LANES : 2 * LANES, :] * scale
+    w_ref[LANES:, :LANES] = jnp.zeros((LANES, LANES), F32)
+    w_ref[LANES:, LANES:] = jnp.where(row > col, packed, jnp.where(row == col, diagonal, turned))
     factor_rows(w_ref, 2)
-    out_ref[:LANES, :LANES] = jnp.where(col >= row, w_ref[:, :LANES], 0.0)
-    out_ref[:LANES, LANES:] = w_ref[:, LANES:]
-    left, right = stacked_pieces(w_ref[:, LANES:])
-    rest_ref[...] = rest_ref[...] - dot_tn(left, right)
-    factor_rows(rest_ref, 1)
+    out_ref[:LANES, :LANES] = jnp.where(col >= row, w_ref[:LANES, :LANES], 0.0)
+    out_ref[:LANES, LANES:] = w_ref[:LANES, LANES:]
     out_ref[LANES:, :LANES] = jnp.zeros((LANES, LANES), F32)
-    out_ref[LANES:, LANES:] = jnp.where(col >= row, rest_ref[...], 0.0)
+    out_ref[LANES:, LANES:] = jnp.where(col >= row, w_ref[LANES:, LANES:], 0.0)
 
 
 def shape(*dims, dtype=F32):
@@ -306,28 +286,51 @@
     return pl.CostEstimate(flops=0, bytes_accessed=mebibytes * 2**20, transcendentals=0)
 
 
-def exchange(value, axis, bit):
-    size = lax.axis_size(axis)
-    return lax.ppermute(value, axis, [(i, i ^ bit) for i in range(size)])
+def swap(value, axes, mask):
+    axes = axes if isinstance(axes, tuple) else (axes,)
+    size = math.prod(lax.axis_size(a) for a in axes)
+    return lax.ppermute(value, axes, [(i, i ^ mask) for i in range(size)])
+
+
+def beside(received, work, start):
+    result, token = work(start)
+    return received + token[:1, :], result
+
+
+def four_sum(total, axes, one, two, work):
+    first = swap(total, axes, one)
+    second = swap(total, axes, two)
+    third = swap(total, axes, one ^ two)
+    third, result = beside(third, work, total)
+    return (total + first) + (second + third), result
+
+
+def rest_sum(total, pairs):
+    for axes, mask in pairs:
+        total = total + swap(total, axes, mask)
+    return total
+
+
+def bits(axis, first):
+    return [1 << i for i in range(first, lax.axis_size(axis).bit_length() - 1)]
 
 
 def sum_over_devices(blocks, works):
-    total = blocks[0] + exchange(blocks[1], "gy", 1)
-    stages = [
-        (axis, 1 << bit)
-        for axis in ("gy", "gx", "gz")
-        for bit in range(lax.axis_size(axis).bit_length() - 1)
-        if (axis, bit) != ("gy", 0)
-    ]
-    results = []
-    for i, (axis, bit) in enumerate(stages):
-        received = exchange(total, axis, bit)
-        if i in works:
-            result, token = works[i](total)
-            results.append(result)
-            received = received + token[:1, :]
+    n = len(blocks)
+    total = blocks[0]
+    for d in range(1, n):
+        total = total + swap(blocks[d], PLANE, d)
+    far = [("gx", m) for m in bits("gx", 1)]
+    if n == 8:
+        total, *results = four_sum(total, "gz", 1, 2, works[0])
+    else:
+        total, first = four_sum(total, PLANE, 2, 4, works[0])
+        total = rest_sum(total, [("gz", 1)])
+        received, second = beside(swap(total, "gz", 2), works[1], total)
         total = total + received
-    return [total, exchange(total, "gy", 1)], results
+        results = [first, second]
+    total = rest_sum(total, far + [("gz", m) for m in bits("gz", 2)])
+    return [total] + [swap(total, PLANE, d) for d in range(1, n)], results
 
 
 def relay_part(rows_right, points, token):
@@ -403,16 +406,16 @@
     vmem = pl.BlockSpec(memory_space=pltpu.VMEM)
 
     steps = 8
-    half = RK
+    block_rows = 2 * RK // SPREAD_ONE
     blocks = pl.pallas_call(
         gram_kernel,
         in_specs=[pl.BlockSpec(memory_space=pl.ANY)],
-        out_specs=[vmem] * 2,
-        out_shape=[shape(half, LANES)] * 2,
+        out_specs=[vmem] * SPREAD_ONE,
+        out_shape=[shape(block_rows, LANES)] * SPREAD_ONE,
         scratch_shapes=[
             pltpu.VMEM((steps, unfold.shape[0] // steps, rank_mid), F32),
             pltpu.VMEM((rank_mid, 2 * rank_mid), F32),
-            pltpu.VMEM((2 * half, LANES), F32),
+            pltpu.VMEM((2 * RK, LANES), F32),
             pltpu.SemaphoreType.DMA((steps,)),
         ],
         compiler_params=params(limit=53 * 1024 * 1024),
@@ -420,18 +423,19 @@
     )(unfold)
     summed, (relayed,) = sum_over_devices(
         blocks,
-        {3: functools.partial(relay_part, rows_right, points)},
-    )
-
-    half = LANES + 8
+        [functools.partial(relay_part, rows_right, points)],
+    )
+
+    block_rows = LANES + 8
+    packed_rows = SPREAD_TWO * block_rows
     absorbed, linv, *blocks = pl.pallas_call(
         functools.partial(absorb_kernel, math.sqrt(rank_left * total_points)),
-        in_specs=[vmem] * 4,
-        out_specs=[vmem] * 4,
-        out_shape=[shape(points, RK, rank_right), shape(RK, RK)] + [shape(half, LANES)] * 2,
+        in_specs=[vmem] * (SPREAD_ONE + 2),
+        out_specs=[vmem] * (2 + SPREAD_TWO),
+        out_shape=[shape(points, RK, rank_right), shape(RK, RK)] + [shape(block_rows, LANES)] * SPREAD_TWO,
         scratch_shapes=[
             pltpu.VMEM((2 * RK, LANES), F32),
-            pltpu.VMEM((2 * half, LANES), F32),
+            pltpu.VMEM((packed_rows, LANES), F32),
             pltpu.VMEM((LANES, 3 * LANES), F32),
             pltpu.VMEM((rank_right, 2 * rank_right), F32),
         ],
@@ -440,21 +444,20 @@
     )(*summed, *relayed)
     summed, (right_out, left_out) = sum_over_devices(
         blocks,
-        {
-            2: functools.partial(right_part, absorbed),
-            3: functools.partial(left_part, unfold, linv),
-        },
+        [
+            functools.partial(right_part, absorbed),
+            functools.partial(left_part, unfold, linv),
+        ],
     )
 
     factor = pl.pallas_call(
         functools.partial(factor_kernel, 1.0 / (RK * total_points)),
-        in_specs=[vmem] * 2,
+        in_specs=[vmem] * SPREAD_TWO,
         out_specs=vmem,
         out_shape=shape(rank_right, rank_right),
         scratch_shapes=[
-            pltpu.VMEM((2 * half, LANES), F32),
-            pltpu.VMEM((LANES, 2 * LANES), F32),
-            pltpu.VMEM((LANES, LANES), F32),
+            pltpu.VMEM((packed_rows, LANES), F32),
+            pltpu.VMEM((2 * LANES, 2 * LANES), F32),
         ],
         compiler_params=params(limit=16 * 1024 * 1024),
         name="factor_next",

time: 62.5 us -> 68 us (1.088)
  starting transfers between devices: 18.6 us -> 24.9 us
  waiting for transfers between devices: 18.4 us -> 14.9 us
  Pallas kernels: 24.5 us -> 27.3 us
    ppermute x12 -> x24, starting transfers between devices: 18.6 us -> 24.9 us  [swap(): return lax.ppermute(value, axes, [(i, i ^ mask) for i in range(size)])]
    ppermute x12 -> x24, waiting for transfers between devices: 18.4 us -> 14.9 us  [swap(): return lax.ppermute(value, axes, [(i, i ^ mask) for i in range(size)])]
    pallas_call x1, Pallas kernels: 6.75 us -> 8.72 us  [per_device(): pl.pallas_call(functools.partial(factor_kernel, 1.0 / (RK * total_points)...]
    pallas_call x1, Pallas kernels: 5.76 us -> 6.65 us  [per_device(): pl.pallas_call(functools.partial(absorb_kernel, math.sqrt(rank_left * tot...]
  transfers between devices with their start and end apart: 12 -> 24, of which waited for: 11 -> 12; matrix products, arithmetic and copies ran while one was open for 0% -> 0% of each run, Pallas kernels for 13% -> 12%
where the time goes in v6:
time: 68 us; the launch traced here: 67.9 us
  Pallas kernels  27.3 us (40%)
  starting transfers between devices  24.9 us (37%)
  waiting for transfers between devices  14.9 us (22%)
  between operations  0.73 us (1%)
    ppermute x24, starting transfers between devices, swap(): return lax.ppermute(value, axes, [(i, i ^ mask) for i in range(size)])  24.9 us
    ppermute x24, waiting for transfers between devices, swap(): return lax.ppermute(value, axes, [(i, i ^ mask) for i in range(size)])  14.9 us
    pallas_call x1, Pallas kernels, per_device(): pl.pallas_call(functools.partial(factor_kernel, 1.0 / (RK * total_points)...  8.72 us
    pallas_call x1, Pallas kernels, per_device(): pl.pallas_call(functools.partial(absorb_kernel, math.sqrt(rank_left * tot...  6.65 us
    pallas_call x1, Pallas kernels, per_device(): pl.pallas_call(gram_kernel, in_specs=[pl.BlockSpec(memory_space=pl.ANY)],...  3.83 us
    pallas_call x1, Pallas kernels, left_part(): pl.pallas_call(left_kernel, grid=(steps,), in_specs=[pl.BlockSpec((chunk,...  2.84 us
    pallas_call x1, Pallas kernels, relay_part(): pl.pallas_call(functools.partial(relay_kernel, points), in_specs=[pl.Bloc...  2.8 us
    pallas_call x1, Pallas kernels, right_part(): pl.pallas_call(functools.partial(right_kernel, points), grid=(steps, 2),...  2.49 us
  transfers between devices with their start and end apart: 24, of which 12 were waited for; matrix products, arithmetic and copies ran while one was open for 0% of the time, Pallas kernels for 12%

profile of v6, /device:TPU:0, one launch (start us, length us, event | category | flops | bytes accessed | tf_op | source)
XLA Modules:
  0.0 67.9 jit_solution(6466080466769957857)
XLA Ops:
  0.6 3.8 %gram_top.1 = (f32[32,128]{1,0:T(8,128)S(1)}, f32[32,128]{1,0:T(8,128)S(1)}, f32[32,128]{1,0:T(8,128)S(1)}, f32[32,128]{1,0:T(8,128)S(1)}, f32[32,128]{1,0:T(8,1...) custom-call(f32[4096,256]{1,0:T(8,128)} %bitcast.10), custom_call_target="tpu_custom_call" | custom-call | tf_op jit(solution)/shard_map/gram_top/pallas_call | solution.py:410
  5.0 2.6 %collective-permute-start.1 = (f32[32,128]{1,0:T(8,128)S(1)}, f32[32,128]{1,0:T(8,128)S(1)}, u32[]{:S(2)}, u32[]{:S(2)}) collective-permute-start(f32[32,128]{1,0:T(8,128)S(1)} %get-tuple-element.24), channel_id=1, source_target_pairs={{0,8},{4,12},{8,0},{12,4},{16,24},{20,28},{24,16},{28,20},{1,9},{5... | collective-permute-start | bytes 49160 | tf_op jit(solution)/shard_map/ppermute | solution.py:292
  7.6 1.7 %collective-permute-start.3 = (f32[32,128]{1,0:T(8,128)S(1)}, f32[32,128]{1,0:T(8,128)S(1)}, u32[]{:S(2)}, u32[]{:S(2)}) collective-permute-start(f32[32,128]{1,0:T(8,128)S(1)} %get-tuple-element.26), channel_id=1, source_target_pairs={{0,16},{4,20},{8,24},{12,28},{16,0},{20,4},{24,8},{28,12},{1,17},{... | collective-permute-start | bytes 49160 | tf_op jit(solution)/shard_map/ppermute | solution.py:292
  9.4 2.6 %collective-permute-start.5 = (f32[32,128]{1,0:T(8,128)S(1)}, f32[32,128]{1,0:T(8,128)S(1)}, u32[]{:S(2)}, u32[]{:S(2)}) collective-permute-start(f32[32,128]{1,0:T(8,128)S(1)} %get-tuple-element.28), channel_id=1, source_target_pairs={{0,24},{4,28},{8,16},{12,20},{16,8},{20,12},{24,0},{28,4},{1,25},{... | collective-permute-start | bytes 49160 | tf_op jit(solution)/shard_map/ppermute | solution.py:292
  12.5 1.5 %collective-permute-done.5 = f32[32,128]{1,0:T(8,128)S(1)} collective-permute-done((f32[32,128]{1,0:T(8,128)S(1)}, f32[32,128]{1,0:T(8,128)S(1)}, u32[]{:S(2)}, u32[]{:S(2)}) %collective-permute-start.5) | collective-permute-done | bytes 16416 | tf_op jit(solution)/shard_map/ppermute | solution.py:292
  14.0 2.1 %collective-permute-done.6 = f32[32,128]{1,0:T(8,128)S(1)} collective-permute-done((f32[32,128]{1,0:T(8,128)S(1)}, f32[32,128]{1,0:T(8,128)S(1)}, u32[]{:S(2)}, u32[]{:S(2)}) %collective-permute-start.6) | collective-permute-done | bytes 16416 | tf_op jit(solution)/shard_map/ppermute | solution.py:292
  16.1 3.7 %collective-permute-start.9 = (f32[32,128]{1,0:T(8,128)S(1)}, f32[32,128]{1,0:T(8,128)S(1)}, u32[]{:S(2)}, u32[]{:S(2)}) collective-permute-start(f32[32,128]{1,0:T(8,128)S(1)} %add_add_fusion.3._), channel_id=1, source_target_pairs={{0,3},{1,2},{2,1},{3,0},{4,7},{5,6},{6,5},{7,4},{8,11},{9,10},{10,... | collective-permute-start | bytes 49160 | tf_op jit(solution)/shard_map/ppermute | solution.py:292
  20.5 2.8 %relay_right.1 = (bf16[16,256,256]{2,1,0:T(8,128)(2,1)S(1)}, bf16[16,256,256]{2,1,0:T(8,128)(2,1)S(1)}, f32[8,128]{1,0:T(8,128)S(1)}) custom-call(f32[4096,256]{1,0:T(8,128)} %bitcast.12, f32[32,128]{1,0:T(8,128)S(1)} %add_add_fusion.3._), custom_call_target="tpu_custom_call" | custom-call | bytes 8388608 | tf_op jit(solution)/shard_map/relay_right/pallas_call | solution.py:341
  23.4 1.0 %collective-permute-done.8 = f32[32,128]{1,0:T(8,128)S(1)} collective-permute-done((f32[32,128]{1,0:T(8,128)S(1)}, f32[32,128]{1,0:T(8,128)S(1)}, u32[]{:S(2)}, u32[]{:S(2)}) %collective-permute-start.8) | collective-permute-done | bytes 16416 | tf_op jit(solution)/shard_map/ppermute | solution.py:292
  24.5 1.3 %collective-permute-start.15 = (f32[32,128]{1,0:T(8,128)S(1)}, f32[32,128]{1,0:T(8,128)S(1)}, u32[]{:S(2)}, u32[]{:S(2)}) collective-permute-start(f32[32,128]{1,0:T(8,128)S(1)} %add_add_fusion.2.refs_0_), channel_id=1, source_target_pairs={{0,24},{4,28},{8,16},{12,20},{16,8},{20,12},{24,0},{28,4},{1,25},{... | collective-permute-start | bytes 49160 | tf_op jit(solution)/shard_map/ppermute | solution.py:292
  25.7 1.6 %collective-permute-start.14 = (f32[32,128]{1,0:T(8,128)S(1)}, f32[32,128]{1,0:T(8,128)S(1)}, u32[]{:S(2)}, u32[]{:S(2)}) collective-permute-start(f32[32,128]{1,0:T(8,128)S(1)} %add_add_fusion.2.refs_0_), channel_id=1, source_target_pairs={{0,20},{4,16},{8,28},{12,24},{16,4},{20,0},{24,12},{28,8},{1,21},{... | collective-permute-start | bytes 49160 | tf_op jit(solution)/shard_map/ppermute | solution.py:292
  27.4 1.5 %collective-permute-start.13 = (f32[32,128]{1,0:T(8,128)S(1)}, f32[32,128]{1,0:T(8,128)S(1)}, u32[]{:S(2)}, u32[]{:S(2)}) collective-permute-start(f32[32,128]{1,0:T(8,128)S(1)} %add_add_fusion.2.refs_0_), channel_id=1, source_target_pairs={{0,16},{4,20},{8,24},{12,28},{16,0},{20,4},{24,8},{28,12},{1,17},{... | collective-permute-start | bytes 49160 | tf_op jit(solution)/shard_map/ppermute | solution.py:292
  29.4 1.3 %collective-permute-start.10 = (f32[32,128]{1,0:T(8,128)S(1)}, f32[32,128]{1,0:T(8,128)S(1)}, u32[]{:S(2)}, u32[]{:S(2)}) collective-permute-start(f32[32,128]{1,0:T(8,128)S(1)} %add_add_fusion.2.refs_0_), channel_id=1, source_target_pairs={{0,4},{4,0},{8,12},{12,8},{16,20},{20,16},{24,28},{28,24},{1,5},{5... | collective-permute-start | bytes 49160 | tf_op jit(solution)/shard_map/ppermute | solution.py:292
  32.6 6.7 %factor_absorb.1 = (f32[16,128,256]{2,1,0:T(8,128)S(1)}, f32[128,128]{1,0:T(8,128)S(1)}, f32[136,128]{1,0:T(8,128)S(1)}, f32[136,128]{1,0:T(8,128)S(1)}) custom-call(f32[32,128]{1,0:T(8,128)S(1)} %add_add_fusion.2.refs_0_, f32[32,128]{1,0:T(8,128)S(1)} %collective-permute-done.10.refs_1_, f32[32,128]{1,0:T(8,128)S(1)} %collective-permute-done.11.refs_2_, ...), custom_call_target="tpu_custom_call" | custom-call | tf_op jit(solution)/shard_map/factor_absorb/pallas_call | solution.py:431
  39.4 1.2 %collective-permute-done.17 = f32[136,128]{1,0:T(8,128)S(1)} collective-permute-done((f32[136,128]{1,0:T(8,128)S(1)}, f32[136,128]{1,0:T(8,128)S(1)}, u32[]{:S(2)}, u32[]{:S(2)}) %collective-permute-start.17) | collective-permute-done | bytes 69664 | tf_op jit(solution)/shard_map/ppermute | solution.py:292
  40.6 1.4 %collective-permute-start.20 = (f32[136,128]{1,0:T(8,128)S(1)}, f32[136,128]{1,0:T(8,128)S(1)}, u32[]{:S(2)}, u32[]{:S(2)}) collective-permute-start(f32[136,128]{1,0:T(8,128)S(1)} %add.91._), channel_id=1, source_target_pairs={{0,24},{4,28},{8,16},{12,20},{16,8},{20,12},{24,0},{28,4},{1,25},{... | collective-permute-start | bytes 208904 | tf_op jit(solution)/shard_map/ppermute | solution.py:292
  42.8 1.4 %collective-permute-start.18 = (f32[136,128]{1,0:T(8,128)S(1)}, f32[136,128]{1,0:T(8,128)S(1)}, u32[]{:S(2)}, u32[]{:S(2)}) collective-permute-start(f32[136,128]{1,0:T(8,128)S(1)} %add.91._), channel_id=1, source_target_pairs={{0,8},{4,12},{8,0},{12,4},{16,24},{20,28},{24,16},{28,20},{1,9},{5... | collective-permute-start | bytes 208904 | tf_op jit(solution)/shard_map/ppermute | solution.py:292
  44.2 2.5 %right_out.1 = (f32[2048,256]{1,0:T(8,128)}, f32[8,128]{1,0:T(8,128)S(1)}) custom-call(f32[16,128,256]{2,1,0:T(8,128)S(1)} %get-tuple-element.36.absorbed_ref, f32[136,128]{1,0:T(8,128)S(1)} %add.91._), custom_call_target="tpu_custom_call" | custom-call | bytes 8388608 | tf_op jit(solution)/shard_map/right_out/pallas_call | solution.py:382
  48.1 3.7 %collective-permute-done.21 = f32[136,128]{1,0:T(8,128)S(1)} collective-permute-done((f32[136,128]{1,0:T(8,128)S(1)}, f32[136,128]{1,0:T(8,128)S(1)}, u32[]{:S(2)}, u32[]{:S(2)}) %collective-permute-start.21) | collective-permute-done | bytes 69664 | tf_op jit(solution)/shard_map/ppermute | solution.py:292
  51.8 2.1 %collective-permute-start.22 = (f32[136,128]{1,0:T(8,128)S(1)}, f32[136,128]{1,0:T(8,128)S(1)}, u32[]{:S(2)}, u32[]{:S(2)}) collective-permute-start(f32[136,128]{1,0:T(8,128)S(1)} %add.98._), channel_id=1, source_target_pairs={{0,2},{1,3},{2,0},{3,1},{4,6},{5,7},{6,4},{7,5},{8,10},{9,11},{10,... | collective-permute-start | bytes 208904 | tf_op jit(solution)/shard_map/ppermute | solution.py:292
  53.9 2.8 %left_out.1 = (f32[4096,128]{1,0:T(8,128)}, f32[8,128]{1,0:T(8,128)S(1)}) custom-call(f32[4096,256]{1,0:T(8,128)S(1)} %bitcast.11, f32[128,128]{1,0:T(8,128)S(1)} %get-tuple-element.33.linv_ref, f32[136,128]{1,0:T(8,128)S(1)} %add.98._), custom_call_target="tpu_custom_call" | custom-call | bytes 8388608 | tf_op jit(solution)/shard_map/left_out/pallas_call | solution.py:360
  56.8 1.1 %collective-permute-done.22 = f32[136,128]{1,0:T(8,128)S(1)} collective-permute-done((f32[136,128]{1,0:T(8,128)S(1)}, f32[136,128]{1,0:T(8,128)S(1)}, u32[]{:S(2)}, u32[]{:S(2)}) %collective-permute-start.22) | collective-permute-done | bytes 69664 | tf_op jit(solution)/shard_map/ppermute | solution.py:292
  57.9 1.2 %collective-permute-done.23.refs_1_ = f32[136,128]{1,0:T(8,128)S(1)} collective-permute-done((f32[136,128]{1,0:T(8,128)S(1)}, f32[136,128]{1,0:T(8,128)S(1)}, u32[]{:S(2)}, u32[]{:S(2)}) %collective-permute-start.23) | collective-permute-done | bytes 69664 | tf_op jit(solution)/shard_map/ppermute | solution.py:292
  59.2 8.7 %factor_next.1 = f32[256,256]{1,0:T(8,128)} custom-call(f32[136,128]{1,0:T(8,128)S(1)} %add_add_fusion.refs_0_, f32[136,128]{1,0:T(8,128)S(1)} %collective-permute-done.23.refs_1_), custom_call_target="tpu_custom_call" | custom-call | tf_op jit(solution)/shard_map/factor_next/pallas_call | solution.py:453
  (41 shorter events, 6.8 us)
Async XLA Ops:
  4.5 4.9 %collective-permute-start = (f32[32,128]{1,0:T(8,128)S(1)}, f32[32,128]{1,0:T(8,128)S(1)}, u32[]{:S(2)}, u32[]{:S(2)}) collective-permute-start(f32[32,128]{1,0:T(8,128)S(1)} %get-tuple-element.23), channel_id=1, source_target_pairs={{0,4},{4,0},{8,12},{12,8},{16,20},{20,16},{24,28},{28,24},{1,5},{5... | collective-permute-start | bytes 49160 | tf_op jit(solution)/shard_map/ppermute | solution.py:292
  5.0 7.0 %collective-permute-start.1 = (f32[32,128]{1,0:T(8,128)S(1)}, f32[32,128]{1,0:T(8,128)S(1)}, u32[]{:S(2)}, u32[]{:S(2)}) collective-permute-start(f32[32,128]{1,0:T(8,128)S(1)} %get-tuple-element.24), channel_id=1, source_target_pairs={{0,8},{4,12},{8,0},{12,4},{16,24},{20,28},{24,16},{28,20},{1,9},{5... | collective-permute-start | bytes 49160 | tf_op jit(solution)/shard_map/ppermute | solution.py:292
  7.6 4.6 %collective-permute-start.2 = (f32[32,128]{1,0:T(8,128)S(1)}, f32[32,128]{1,0:T(8,128)S(1)}, u32[]{:S(2)}, u32[]{:S(2)}) collective-permute-start(f32[32,128]{1,0:T(8,128)S(1)} %get-tuple-element.25), channel_id=1, source_target_pairs={{0,12},{4,8},{8,4},{12,0},{16,28},{20,24},{24,20},{28,16},{1,13},{... | collective-permute-start | bytes 49160 | tf_op jit(solution)/shard_map/ppermute | solution.py:292
  7.6 4.5 %collective-permute-start.3 = (f32[32,128]{1,0:T(8,128)S(1)}, f32[32,128]{1,0:T(8,128)S(1)}, u32[]{:S(2)}, u32[]{:S(2)}) collective-permute-start(f32[32,128]{1,0:T(8,128)S(1)} %get-tuple-element.26), channel_id=1, source_target_pairs={{0,16},{4,20},{8,24},{12,28},{16,0},{20,4},{24,8},{28,12},{1,17},{... | collective-permute-start | bytes 49160 | tf_op jit(solution)/shard_map/ppermute | solution.py:292
  9.4 3.2 %collective-permute-start.4 = (f32[32,128]{1,0:T(8,128)S(1)}, f32[32,128]{1,0:T(8,128)S(1)}, u32[]{:S(2)}, u32[]{:S(2)}) collective-permute-start(f32[32,128]{1,0:T(8,128)S(1)} %get-tuple-element.27), channel_id=1, source_target_pairs={{0,20},{4,16},{8,28},{12,24},{16,4},{20,0},{24,12},{28,8},{1,21},{... | collective-permute-start | bytes 49160 | tf_op jit(solution)/shard_map/ppermute | solution.py:292
  9.4 4.6 %collective-permute-start.5 = (f32[32,128]{1,0:T(8,128)S(1)}, f32[32,128]{1,0:T(8,128)S(1)}, u32[]{:S(2)}, u32[]{:S(2)}) collective-permute-start(f32[32,128]{1,0:T(8,128)S(1)} %get-tuple-element.28), channel_id=1, source_target_pairs={{0,24},{4,28},{8,16},{12,20},{16,8},{20,12},{24,0},{28,4},{1,25},{... | collective-permute-start | bytes 49160 | tf_op jit(solution)/shard_map/ppermute | solution.py:292
  12.0 4.1 %collective-permute-start.6 = (f32[32,128]{1,0:T(8,128)S(1)}, f32[32,128]{1,0:T(8,128)S(1)}, u32[]{:S(2)}, u32[]{:S(2)}) collective-permute-start(f32[32,128]{1,0:T(8,128)S(1)} %get-tuple-element.29), channel_id=1, source_target_pairs={{0,28},{4,24},{8,20},{12,16},{16,12},{20,8},{24,4},{28,0},{1,29},{... | collective-permute-start | bytes 49160 | tf_op jit(solution)/shard_map/ppermute | solution.py:292
  16.1 7.3 %collective-permute-start.9 = (f32[32,128]{1,0:T(8,128)S(1)}, f32[32,128]{1,0:T(8,128)S(1)}, u32[]{:S(2)}, u32[]{:S(2)}) collective-permute-start(f32[32,128]{1,0:T(8,128)S(1)} %add_add_fusion.3._), channel_id=1, source_target_pairs={{0,3},{1,2},{2,1},{3,0},{4,7},{5,6},{6,5},{7,4},{8,11},{9,10},{10,... | collective-permute-start | bytes 49160 | tf_op jit(solution)/shard_map/ppermute | solution.py:292
  19.8 4.6 %collective-permute-start.8 = (f32[32,128]{1,0:T(8,128)S(1)}, f32[32,128]{1,0:T(8,128)S(1)}, u32[]{:S(2)}, u32[]{:S(2)}) collective-permute-start(f32[32,128]{1,0:T(8,128)S(1)} %add_add_fusion.3._), channel_id=1, source_target_pairs={{0,2},{1,3},{2,0},{3,1},{4,6},{5,7},{6,4},{7,5},{8,10},{9,11},{10,... | collective-permute-start | bytes 49160 | tf_op jit(solution)/shard_map/ppermute | solution.py:292
  19.8 4.6 %collective-permute-start.7 = (f32[32,128]{1,0:T(8,128)S(1)}, f32[32,128]{1,0:T(8,128)S(1)}, u32[]{:S(2)}, u32[]{:S(2)}) collective-permute-start(f32[32,128]{1,0:T(8,128)S(1)} %add_add_fusion.3._), channel_id=1, source_target_pairs={{0,1},{1,0},{2,3},{3,2},{4,5},{5,4},{6,7},{7,6},{8,9},{9,8},{10,11... | collective-permute-start | bytes 49160 | tf_op jit(solution)/shard_map/ppermute | solution.py:292
  24.4 4.5 %collective-permute-start.16 = (f32[32,128]{1,0:T(8,128)S(1)}, f32[32,128]{1,0:T(8,128)S(1)}, u32[]{:S(2)}, u32[]{:S(2)}) collective-permute-start(f32[32,128]{1,0:T(8,128)S(1)} %add_add_fusion.2.refs_0_), channel_id=1, source_target_pairs={{0,28},{4,24},{8,20},{12,16},{16,12},{20,8},{24,4},{28,0},{1,29},{... | collective-permute-start | bytes 49160 | tf_op jit(solution)/shard_map/ppermute | solution.py:292
  24.5 4.9 %collective-permute-start.15 = (f32[32,128]{1,0:T(8,128)S(1)}, f32[32,128]{1,0:T(8,128)S(1)}, u32[]{:S(2)}, u32[]{:S(2)}) collective-permute-start(f32[32,128]{1,0:T(8,128)S(1)} %add_add_fusion.2.refs_0_), channel_id=1, source_target_pairs={{0,24},{4,28},{8,16},{12,20},{16,8},{20,12},{24,0},{28,4},{1,25},{... | collective-permute-start | bytes 49160 | tf_op jit(solution)/shard_map/ppermute | solution.py:292
  25.7 5.0 %collective-permute-start.14 = (f32[32,128]{1,0:T(8,128)S(1)}, f32[32,128]{1,0:T(8,128)S(1)}, u32[]{:S(2)}, u32[]{:S(2)}) collective-permute-start(f32[32,128]{1,0:T(8,128)S(1)} %add_add_fusion.2.refs_0_), channel_id=1, source_target_pairs={{0,20},{4,16},{8,28},{12,24},{16,4},{20,0},{24,12},{28,8},{1,21},{... | collective-permute-start | bytes 49160 | tf_op jit(solution)/shard_map/ppermute | solution.py:292
  27.4 3.7 %collective-permute-start.13 = (f32[32,128]{1,0:T(8,128)S(1)}, f32[32,128]{1,0:T(8,128)S(1)}, u32[]{:S(2)}, u32[]{:S(2)}) collective-permute-start(f32[32,128]{1,0:T(8,128)S(1)} %add_add_fusion.2.refs_0_), channel_id=1, source_target_pairs={{0,16},{4,20},{8,24},{12,28},{16,0},{20,4},{24,8},{28,12},{1,17},{... | collective-permute-start | bytes 49160 | tf_op jit(solution)/shard_map/ppermute | solution.py:292
  28.9 3.2 %collective-permute-start.12 = (f32[32,128]{1,0:T(8,128)S(1)}, f32[32,128]{1,0:T(8,128)S(1)}, u32[]{:S(2)}, u32[]{:S(2)}) collective-permute-start(f32[32,128]{1,0:T(8,128)S(1)} %add_add_fusion.2.refs_0_), channel_id=1, source_target_pairs={{0,12},{4,8},{8,4},{12,0},{16,28},{20,24},{24,20},{28,16},{1,13},{... | collective-permute-start | bytes 49160 | tf_op jit(solution)/shard_map/ppermute | solution.py:292
  28.9 3.8 %collective-permute-start.11 = (f32[32,128]{1,0:T(8,128)S(1)}, f32[32,128]{1,0:T(8,128)S(1)}, u32[]{:S(2)}, u32[]{:S(2)}) collective-permute-start(f32[32,128]{1,0:T(8,128)S(1)} %add_add_fusion.2.refs_0_), channel_id=1, source_target_pairs={{0,8},{4,12},{8,0},{12,4},{16,24},{20,28},{24,16},{28,20},{1,9},{5... | collective-permute-start | bytes 49160 | tf_op jit(solution)/shard_map/ppermute | solution.py:292
  29.4 3.2 %collective-permute-start.10 = (f32[32,128]{1,0:T(8,128)S(1)}, f32[32,128]{1,0:T(8,128)S(1)}, u32[]{:S(2)}, u32[]{:S(2)}) collective-permute-start(f32[32,128]{1,0:T(8,128)S(1)} %add_add_fusion.2.refs_0_), channel_id=1, source_target_pairs={{0,4},{4,0},{8,12},{12,8},{16,20},{20,16},{24,28},{28,24},{1,5},{5... | collective-permute-start | bytes 49160 | tf_op jit(solution)/shard_map/ppermute | solution.py:292
  39.3 1.3 %collective-permute-start.17 = (f32[136,128]{1,0:T(8,128)S(1)}, f32[136,128]{1,0:T(8,128)S(1)}, u32[]{:S(2)}, u32[]{:S(2)}) collective-permute-start(f32[136,128]{1,0:T(8,128)S(1)} %get-tuple-element.35), channel_id=1, source_target_pairs={{0,4},{4,0},{8,12},{12,8},{16,20},{20,16},{24,28},{28,24},{1,5},{5... | collective-permute-start | bytes 208904 | tf_op jit(solution)/shard_map/ppermute | solution.py:292
  40.6 6.1 %collective-permute-start.20 = (f32[136,128]{1,0:T(8,128)S(1)}, f32[136,128]{1,0:T(8,128)S(1)}, u32[]{:S(2)}, u32[]{:S(2)}) collective-permute-start(f32[136,128]{1,0:T(8,128)S(1)} %add.91._), channel_id=1, source_target_pairs={{0,24},{4,28},{8,16},{12,20},{16,8},{20,12},{24,0},{28,4},{1,25},{... | collective-permute-start | bytes 208904 | tf_op jit(solution)/shard_map/ppermute | solution.py:292
  42.0 4.7 %collective-permute-start.19 = (f32[136,128]{1,0:T(8,128)S(1)}, f32[136,128]{1,0:T(8,128)S(1)}, u32[]{:S(2)}, u32[]{:S(2)}) collective-permute-start(f32[136,128]{1,0:T(8,128)S(1)} %add.91._), channel_id=1, source_target_pairs={{0,16},{4,20},{8,24},{12,28},{16,0},{20,4},{24,8},{28,12},{1,17},{... | collective-permute-start | bytes 208904 | tf_op jit(solution)/shard_map/ppermute | solution.py:292
  42.8 4.6 %collective-permute-start.18 = (f32[136,128]{1,0:T(8,128)S(1)}, f32[136,128]{1,0:T(8,128)S(1)}, u32[]{:S(2)}, u32[]{:S(2)}) collective-permute-start(f32[136,128]{1,0:T(8,128)S(1)} %add.91._), channel_id=1, source_target_pairs={{0,8},{4,12},{8,0},{12,4},{16,24},{20,28},{24,16},{28,20},{1,9},{5... | collective-permute-start | bytes 208904 | tf_op jit(solution)/shard_map/ppermute | solution.py:292
  47.4 4.4 %collective-permute-start.21 = (f32[136,128]{1,0:T(8,128)S(1)}, f32[136,128]{1,0:T(8,128)S(1)}, u32[]{:S(2)}, u32[]{:S(2)}) collective-permute-start(f32[136,128]{1,0:T(8,128)S(1)} %add_add_fusion.1), channel_id=1, source_target_pairs={{0,1},{1,0},{2,3},{3,2},{4,5},{5,4},{6,7},{7,6},{8,9},{9,8},{10,11... | collective-permute-start | bytes 208904 | tf_op jit(solution)/shard_map/ppermute | solution.py:292
  51.8 6.0 %collective-permute-start.22 = (f32[136,128]{1,0:T(8,128)S(1)}, f32[136,128]{1,0:T(8,128)S(1)}, u32[]{:S(2)}, u32[]{:S(2)}) collective-permute-start(f32[136,128]{1,0:T(8,128)S(1)} %add.98._), channel_id=1, source_target_pairs={{0,2},{1,3},{2,0},{3,1},{4,6},{5,7},{6,4},{7,5},{8,10},{9,11},{10,... | collective-permute-start | bytes 208904 | tf_op jit(solution)/shard_map/ppermute | solution.py:292
  57.9 1.3 %collective-permute-start.23 = (f32[136,128]{1,0:T(8,128)S(1)}, f32[136,128]{1,0:T(8,128)S(1)}, u32[]{:S(2)}, u32[]{:S(2)}) collective-permute-start(f32[136,128]{1,0:T(8,128)S(1)} %add_add_fusion.refs_0_), channel_id=1, source_target_pairs={{0,4},{4,0},{8,12},{12,8},{16,20},{20,16},{24,28},{28,24},{1,5},{5... | collective-permute-start | bytes 208904 | tf_op jit(solution)/shard_map/ppermute | solution.py:292
  (1 other events, 21.3 us)

commit v7 on v6

--- a/solution.py
+++ b/solution.py
@@ -11,9 +11,9 @@
 RK = 128
 AXES = ("gx", "gy", "gz")
 LANES = 128
-PANEL = 8
+PANEL = 16
 PLANE = ("gx", "gy")
-SPREAD_ONE = 8
+SPREAD_ONE = 2
 SPREAD_TWO = 2
 F32 = jnp.float32
 BF16 = jnp.bfloat16
@@ -292,16 +292,14 @@
     return lax.ppermute(value, axes, [(i, i ^ mask) for i in range(size)])
 
 
-def beside(received, work, start):
-    result, token = work(start)
-    return received + token[:1, :], result
-
-
 def four_sum(total, axes, one, two, work):
     first = swap(total, axes, one)
     second = swap(total, axes, two)
     third = swap(total, axes, one ^ two)
-    third, result = beside(third, work, total)
+    result = None
+    if work is not None:
+        result, token = work(total)
+        third = third + token[:1, :]
     return (total + first) + (second + third), result
 
 
@@ -320,17 +318,11 @@
     total = blocks[0]
     for d in range(1, n):
         total = total + swap(blocks[d], PLANE, d)
-    far = [("gx", m) for m in bits("gx", 1)]
-    if n == 8:
-        total, *results = four_sum(total, "gz", 1, 2, works[0])
-    else:
-        total, first = four_sum(total, PLANE, 2, 4, works[0])
-        total = rest_sum(total, [("gz", 1)])
-        received, second = beside(swap(total, "gz", 2), works[1], total)
-        total = total + received
-        results = [first, second]
-    total = rest_sum(total, far + [("gz", m) for m in bits("gz", 2)])
-    return [total] + [swap(total, PLANE, d) for d in range(1, n)], results
+    far = [("gx", m) for m in bits("gx", 1)] + [("gz", m) for m in bits("gz", 2)]
+    total, first = four_sum(total, PLANE, 2, 4, works[0])
+    total, second = four_sum(total, "gz", 1, 2, works[1])
+    total = rest_sum(total, far)
+    return [total] + [swap(total, PLANE, d) for d in range(1, n)], (first, second)
 
 
 def relay_part(rows_right, points, token):
@@ -421,9 +413,9 @@
         compiler_params=params(limit=53 * 1024 * 1024),
         name="gram_top",
     )(unfold)
-    summed, (relayed,) = sum_over_devices(
+    summed, (_, relayed) = sum_over_devices(
         blocks,
-        [functools.partial(relay_part, rows_right, points)],
+        [None, functools.partial(relay_part, rows_right, points)],
     )
 
     block_rows = LANES + 8

time: 68 us -> 56.1 us (0.83)
  starting transfers between devices: 24.9 us -> 17.8 us
  Pallas kernels: 27.3 us -> 24.4 us
  waiting for transfers between devices: 14.9 us -> 12.9 us
    ppermute x24 -> x16, starting transfers between devices: 24.9 us -> 17.8 us  [swap(): return lax.ppermute(value, axes, [(i, i ^ mask) for i in range(size)])]
    pallas_call x1, Pallas kernels: 8.72 us -> 6.69 us  [per_device(): pl.pallas_call(functools.partial(factor_kernel, 1.0 / (RK * total_points)...]
    ppermute x24 -> x16, waiting for transfers between devices: 14.9 us -> 12.9 us  [swap(): return lax.ppermute(value, axes, [(i, i ^ mask) for i in range(size)])]
    pallas_call x1, Pallas kernels: 6.65 us -> 5.76 us  [per_device(): pl.pallas_call(functools.partial(absorb_kernel, math.sqrt(rank_left * tot...]
  transfers between devices with their start and end apart: 24 -> 16, of which waited for: 12 -> 11; matrix products, arithmetic and copies ran while one was open for 0% -> 0% of each run, Pallas kernels for 12% -> 15%
where the time goes in v7:
time: 56.1 us; the launch traced here: 56 us
  Pallas kernels  24.4 us (43%)
  starting transfers between devices  17.8 us (32%)
  waiting for transfers between devices  12.9 us (23%)
  between operations  0.71 us (1%)
    ppermute x16, starting transfers between devices, swap(): return lax.ppermute(value, axes, [(i, i ^ mask) for i in range(size)])  17.8 us
    ppermute x16, waiting for transfers between devices, swap(): return lax.ppermute(value, axes, [(i, i ^ mask) for i in range(size)])  12.9 us
    pallas_call x1, Pallas kernels, per_device(): pl.pallas_call(functools.partial(factor_kernel, 1.0 / (RK * total_points)...  6.69 us
    pallas_call x1, Pallas kernels, per_device(): pl.pallas_call(functools.partial(absorb_kernel, math.sqrt(rank_left * tot...  5.76 us
    pallas_call x1, Pallas kernels, per_device(): pl.pallas_call(gram_kernel, in_specs=[pl.BlockSpec(memory_space=pl.ANY)],...  3.85 us
    pallas_call x1, Pallas kernels, left_part(): pl.pallas_call(left_kernel, grid=(steps,), in_specs=[pl.BlockSpec((chunk,...  2.83 us
    pallas_call x1, Pallas kernels, relay_part(): pl.pallas_call(functools.partial(relay_kernel, points), in_specs=[pl.Bloc...  2.8 us
    pallas_call x1, Pallas kernels, right_part(): pl.pallas_call(functools.partial(right_kernel, points), grid=(steps, 2),...  2.5 us
  transfers between devices with their start and end apart: 16, of which 11 were waited for; matrix products, arithmetic and copies ran while one was open for 0% of the time, Pallas kernels for 15%

profile of v7, /device:TPU:0, one launch (start us, length us, event | category | flops | bytes accessed | tf_op | source)
XLA Modules:
  0.0 56.0 jit_solution(4776983685664211937)
XLA Ops:
  0.6 3.9 %gram_top.1 = (f32[128,128]{1,0:T(8,128)S(1)}, f32[128,128]{1,0:T(8,128)S(1)}) custom-call(f32[4096,256]{1,0:T(8,128)} %bitcast.10), custom_call_target="tpu_custom_call" | custom-call | tf_op jit(solution)/shard_map/gram_top/pallas_call | solution.py:402
  5.0 0.9 %collective-permute-done = f32[128,128]{1,0:T(8,128)S(1)} collective-permute-done((f32[128,128]{1,0:T(8,128)S(1)}, f32[128,128]{1,0:T(8,128)S(1)}, u32[]{:S(2)}, u32[]{:S(2)}) %collective-permute-start) | collective-permute-done | bytes 65568 | tf_op jit(solution)/shard_map/ppermute | solution.py:292
  5.9 3.9 %collective-permute-start.3 = (f32[128,128]{1,0:T(8,128)S(1)}, f32[128,128]{1,0:T(8,128)S(1)}, u32[]{:S(2)}, u32[]{:S(2)}) collective-permute-start(f32[128,128]{1,0:T(8,128)S(1)} %add.72), channel_id=1, source_target_pairs={{0,24},{4,28},{8,16},{12,20},{16,8},{20,12},{24,0},{28,4},{1,25},{... | collective-permute-start | bytes 196616 | tf_op jit(solution)/shard_map/ppermute | solution.py:292
  9.8 0.5 collective-permute-start.2
  10.4 1.8 %collective-permute-done.3 = f32[128,128]{1,0:T(8,128)S(1)} collective-permute-done((f32[128,128]{1,0:T(8,128)S(1)}, f32[128,128]{1,0:T(8,128)S(1)}, u32[]{:S(2)}, u32[]{:S(2)}) %collective-permute-start.3) | collective-permute-done | bytes 65568 | tf_op jit(solution)/shard_map/ppermute | solution.py:292
  12.2 1.9 %collective-permute-done.2 = f32[128,128]{1,0:T(8,128)S(1)} collective-permute-done((f32[128,128]{1,0:T(8,128)S(1)}, f32[128,128]{1,0:T(8,128)S(1)}, u32[]{:S(2)}, u32[]{:S(2)}) %collective-permute-start.2) | collective-permute-done | bytes 65568 | tf_op jit(solution)/shard_map/ppermute | solution.py:292
  14.0 0.5 collective-permute-done.1
  14.6 3.7 %collective-permute-start.6 = (f32[128,128]{1,0:T(8,128)S(1)}, f32[128,128]{1,0:T(8,128)S(1)}, u32[]{:S(2)}, u32[]{:S(2)}) collective-permute-start(f32[128,128]{1,0:T(8,128)S(1)} %add_add_fusion.3._), channel_id=1, source_target_pairs={{0,3},{1,2},{2,1},{3,0},{4,7},{5,6},{6,5},{7,4},{8,11},{9,10},{10,... | collective-permute-start | bytes 196616 | tf_op jit(solution)/shard_map/ppermute | solution.py:292
  18.3 0.8 %collective-permute-start.4 = (f32[128,128]{1,0:T(8,128)S(1)}, f32[128,128]{1,0:T(8,128)S(1)}, u32[]{:S(2)}, u32[]{:S(2)}) collective-permute-start(f32[128,128]{1,0:T(8,128)S(1)} %add_add_fusion.3._), channel_id=1, source_target_pairs={{0,1},{1,0},{2,3},{3,2},{4,5},{5,4},{6,7},{7,6},{8,9},{9,8},{10,11... | collective-permute-start | bytes 196616 | tf_op jit(solution)/shard_map/ppermute | solution.py:292
  19.1 2.8 %relay_right.1 = (bf16[16,256,256]{2,1,0:T(8,128)(2,1)S(1)}, bf16[16,256,256]{2,1,0:T(8,128)(2,1)S(1)}, f32[8,128]{1,0:T(8,128)S(1)}) custom-call(f32[4096,256]{1,0:T(8,128)} %bitcast.12, f32[128,128]{1,0:T(8,128)S(1)} %add_add_fusion.3._), custom_call_target="tpu_custom_call" | custom-call | bytes 8388608 | tf_op jit(solution)/shard_map/relay_right/pallas_call | solution.py:333
  21.9 1.7 %collective-permute-done.5 = f32[128,128]{1,0:T(8,128)S(1)} collective-permute-done((f32[128,128]{1,0:T(8,128)S(1)}, f32[128,128]{1,0:T(8,128)S(1)}, u32[]{:S(2)}, u32[]{:S(2)}) %collective-permute-start.5) | collective-permute-done | bytes 65568 | tf_op jit(solution)/shard_map/ppermute | solution.py:292
  23.7 1.2 %collective-permute-done.7.refs_1_ = f32[128,128]{1,0:T(8,128)S(1)} collective-permute-done((f32[128,128]{1,0:T(8,128)S(1)}, f32[128,128]{1,0:T(8,128)S(1)}, u32[]{:S(2)}, u32[]{:S(2)}) %collective-permute-start.7) | collective-permute-done | bytes 65568 | tf_op jit(solution)/shard_map/ppermute | solution.py:292
  25.0 5.8 %factor_absorb.1 = (f32[16,128,256]{2,1,0:T(8,128)S(1)}, f32[128,128]{1,0:T(8,128)S(1)}, f32[136,128]{1,0:T(8,128)S(1)}, f32[136,128]{1,0:T(8,128)S(1)}) custom-call(f32[128,128]{1,0:T(8,128)S(1)} %add_add_fusion.2.refs_0_, f32[128,128]{1,0:T(8,128)S(1)} %collective-permute-done.7.refs_1_, bf16[16,256,256]{2,1,0:T(8,128)(2,1)S(1)} %get-tuple-element.19.refs_2_, ...), custom_call_target="tpu_custom_call" | custom-call | tf_op jit(solution)/shard_map/factor_absorb/pallas_call | solution.py:423
  31.0 1.1 %collective-permute-done.8 = f32[136,128]{1,0:T(8,128)S(1)} collective-permute-done((f32[136,128]{1,0:T(8,128)S(1)}, f32[136,128]{1,0:T(8,128)S(1)}, u32[]{:S(2)}, u32[]{:S(2)}) %collective-permute-start.8) | collective-permute-done | bytes 69664 | tf_op jit(solution)/shard_map/ppermute | solution.py:292
  32.1 1.7 %collective-permute-start.11 = (f32[136,128]{1,0:T(8,128)S(1)}, f32[136,128]{1,0:T(8,128)S(1)}, u32[]{:S(2)}, u32[]{:S(2)}) collective-permute-start(f32[136,128]{1,0:T(8,128)S(1)} %add.82._), channel_id=1, source_target_pairs={{0,24},{4,28},{8,16},{12,20},{16,8},{20,12},{24,0},{28,4},{1,25},{... | collective-permute-start | bytes 208904 | tf_op jit(solution)/shard_map/ppermute | solution.py:292
  33.8 0.8 %collective-permute-start.10 = (f32[136,128]{1,0:T(8,128)S(1)}, f32[136,128]{1,0:T(8,128)S(1)}, u32[]{:S(2)}, u32[]{:S(2)}) collective-permute-start(f32[136,128]{1,0:T(8,128)S(1)} %add.82._), channel_id=1, source_target_pairs={{0,16},{4,20},{8,24},{12,28},{16,0},{20,4},{24,8},{28,12},{1,17},{... | collective-permute-start | bytes 208904 | tf_op jit(solution)/shard_map/ppermute | solution.py:292
  34.6 1.1 %collective-permute-start.9 = (f32[136,128]{1,0:T(8,128)S(1)}, f32[136,128]{1,0:T(8,128)S(1)}, u32[]{:S(2)}, u32[]{:S(2)}) collective-permute-start(f32[136,128]{1,0:T(8,128)S(1)} %add.82._), channel_id=1, source_target_pairs={{0,8},{4,12},{8,0},{12,4},{16,24},{20,28},{24,16},{28,20},{1,9},{5... | collective-permute-start | bytes 208904 | tf_op jit(solution)/shard_map/ppermute | solution.py:292
  35.6 2.5 %right_out.1 = (f32[2048,256]{1,0:T(8,128)}, f32[8,128]{1,0:T(8,128)S(1)}) custom-call(f32[16,128,256]{2,1,0:T(8,128)S(1)} %get-tuple-element.24.absorbed_ref, f32[136,128]{1,0:T(8,128)S(1)} %add.82._), custom_call_target="tpu_custom_call" | custom-call | bytes 8388608 | tf_op jit(solution)/shard_map/right_out/pallas_call | solution.py:374
  38.9 2.7 %collective-permute-start.14 = (f32[136,128]{1,0:T(8,128)S(1)}, f32[136,128]{1,0:T(8,128)S(1)}, u32[]{:S(2)}, u32[]{:S(2)}) collective-permute-start(f32[136,128]{1,0:T(8,128)S(1)} %add_add_fusion.1._), channel_id=1, source_target_pairs={{0,3},{1,2},{2,1},{3,0},{4,7},{5,6},{6,5},{7,4},{8,11},{9,10},{10,... | collective-permute-start | bytes 208904 | tf_op jit(solution)/shard_map/ppermute | solution.py:292
  41.6 1.8 %collective-permute-start.12 = (f32[136,128]{1,0:T(8,128)S(1)}, f32[136,128]{1,0:T(8,128)S(1)}, u32[]{:S(2)}, u32[]{:S(2)}) collective-permute-start(f32[136,128]{1,0:T(8,128)S(1)} %add_add_fusion.1._), channel_id=1, source_target_pairs={{0,1},{1,0},{2,3},{3,2},{4,5},{5,4},{6,7},{7,6},{8,9},{9,8},{10,11... | collective-permute-start | bytes 208904 | tf_op jit(solution)/shard_map/ppermute | solution.py:292
  43.4 2.8 %left_out.1 = (f32[4096,128]{1,0:T(8,128)}, f32[8,128]{1,0:T(8,128)S(1)}) custom-call(f32[4096,256]{1,0:T(8,128)S(1)} %bitcast.11, f32[128,128]{1,0:T(8,128)S(1)} %get-tuple-element.21.linv_ref, f32[136,128]{1,0:T(8,128)S(1)} %add_add_fusion.1._), custom_call_target="tpu_custom_call" | custom-call | bytes 8388608 | tf_op jit(solution)/shard_map/left_out/pallas_call | solution.py:352
  46.2 1.7 %collective-permute-done.13 = f32[136,128]{1,0:T(8,128)S(1)} collective-permute-done((f32[136,128]{1,0:T(8,128)S(1)}, f32[136,128]{1,0:T(8,128)S(1)}, u32[]{:S(2)}, u32[]{:S(2)}) %collective-permute-start.13) | collective-permute-done | bytes 69664 | tf_op jit(solution)/shard_map/ppermute | solution.py:292
  48.0 1.2 %collective-permute-done.15.refs_1_ = f32[136,128]{1,0:T(8,128)S(1)} collective-permute-done((f32[136,128]{1,0:T(8,128)S(1)}, f32[136,128]{1,0:T(8,128)S(1)}, u32[]{:S(2)}, u32[]{:S(2)}) %collective-permute-start.15) | collective-permute-done | bytes 69664 | tf_op jit(solution)/shard_map/ppermute | solution.py:292
  49.3 6.7 %factor_next.1 = f32[256,256]{1,0:T(8,128)} custom-call(f32[136,128]{1,0:T(8,128)S(1)} %add_add_fusion.refs_0_, f32[136,128]{1,0:T(8,128)S(1)} %collective-permute-done.15.refs_1_), custom_call_target="tpu_custom_call" | custom-call | tf_op jit(solution)/shard_map/factor_next/pallas_call | solution.py:445
  (25 shorter events, 1.9 us)
Async XLA Ops:
  4.5 1.4 %collective-permute-start = (f32[128,128]{1,0:T(8,128)S(1)}, f32[128,128]{1,0:T(8,128)S(1)}, u32[]{:S(2)}, u32[]{:S(2)}) collective-permute-start(f32[128,128]{1,0:T(8,128)S(1)} %get-tuple-element.17), channel_id=1, source_target_pairs={{0,4},{4,0},{8,12},{12,8},{16,20},{20,16},{24,28},{28,24},{1,5},{5... | collective-permute-start | bytes 196616 | tf_op jit(solution)/shard_map/ppermute | solution.py:292
  5.9 6.3 %collective-permute-start.3 = (f32[128,128]{1,0:T(8,128)S(1)}, f32[128,128]{1,0:T(8,128)S(1)}, u32[]{:S(2)}, u32[]{:S(2)}) collective-permute-start(f32[128,128]{1,0:T(8,128)S(1)} %add.72), channel_id=1, source_target_pairs={{0,24},{4,28},{8,16},{12,20},{16,8},{20,12},{24,0},{28,4},{1,25},{... | collective-permute-start | bytes 196616 | tf_op jit(solution)/shard_map/ppermute | solution.py:292
  9.8 4.3 %collective-permute-start.2 = (f32[128,128]{1,0:T(8,128)S(1)}, f32[128,128]{1,0:T(8,128)S(1)}, u32[]{:S(2)}, u32[]{:S(2)}) collective-permute-start(f32[128,128]{1,0:T(8,128)S(1)} %add.72), channel_id=1, source_target_pairs={{0,16},{4,20},{8,24},{12,28},{16,0},{20,4},{24,8},{28,12},{1,17},{... | collective-permute-start | bytes 196616 | tf_op jit(solution)/shard_map/ppermute | solution.py:292
  10.3 4.3 %collective-permute-start.1 = (f32[128,128]{1,0:T(8,128)S(1)}, f32[128,128]{1,0:T(8,128)S(1)}, u32[]{:S(2)}, u32[]{:S(2)}) collective-permute-start(f32[128,128]{1,0:T(8,128)S(1)} %add.72), channel_id=1, source_target_pairs={{0,8},{4,12},{8,0},{12,4},{16,24},{20,28},{24,16},{28,20},{1,9},{5... | collective-permute-start | bytes 196616 | tf_op jit(solution)/shard_map/ppermute | solution.py:292
  14.6 7.3 %collective-permute-start.6 = (f32[128,128]{1,0:T(8,128)S(1)}, f32[128,128]{1,0:T(8,128)S(1)}, u32[]{:S(2)}, u32[]{:S(2)}) collective-permute-start(f32[128,128]{1,0:T(8,128)S(1)} %add_add_fusion.3._), channel_id=1, source_target_pairs={{0,3},{1,2},{2,1},{3,0},{4,7},{5,6},{6,5},{7,4},{8,11},{9,10},{10,... | collective-permute-start | bytes 196616 | tf_op jit(solution)/shard_map/ppermute | solution.py:292
  18.3 5.4 %collective-permute-start.5 = (f32[128,128]{1,0:T(8,128)S(1)}, f32[128,128]{1,0:T(8,128)S(1)}, u32[]{:S(2)}, u32[]{:S(2)}) collective-permute-start(f32[128,128]{1,0:T(8,128)S(1)} %add_add_fusion.3._), channel_id=1, source_target_pairs={{0,2},{1,3},{2,0},{3,1},{4,6},{5,7},{6,4},{7,5},{8,10},{9,11},{10,... | collective-permute-start | bytes 196616 | tf_op jit(solution)/shard_map/ppermute | solution.py:292
  18.3 5.4 %collective-permute-start.4 = (f32[128,128]{1,0:T(8,128)S(1)}, f32[128,128]{1,0:T(8,128)S(1)}, u32[]{:S(2)}, u32[]{:S(2)}) collective-permute-start(f32[128,128]{1,0:T(8,128)S(1)} %add_add_fusion.3._), channel_id=1, source_target_pairs={{0,1},{1,0},{2,3},{3,2},{4,5},{5,4},{6,7},{7,6},{8,9},{9,8},{10,11... | collective-permute-start | bytes 196616 | tf_op jit(solution)/shard_map/ppermute | solution.py:292
  23.7 1.3 %collective-permute-start.7 = (f32[128,128]{1,0:T(8,128)S(1)}, f32[128,128]{1,0:T(8,128)S(1)}, u32[]{:S(2)}, u32[]{:S(2)}) collective-permute-start(f32[128,128]{1,0:T(8,128)S(1)} %add_add_fusion.2.refs_0_), channel_id=1, source_target_pairs={{0,4},{4,0},{8,12},{12,8},{16,20},{20,16},{24,28},{28,24},{1,5},{5... | collective-permute-start | bytes 196616 | tf_op jit(solution)/shard_map/ppermute | solution.py:292
  25.0 18.4 %copy-start = (f32[256,16,256]{2,1,0:T(8,128)S(1)}, f32[256,16,256]{2,1,0:T(8,128)}, u32[]{:S(2)}) copy-start(f32[256,16,256]{2,1,0:T(8,128)} %param.2) | copy-start | bytes 12582916
  30.7 1.3 %collective-permute-start.8 = (f32[136,128]{1,0:T(8,128)S(1)}, f32[136,128]{1,0:T(8,128)S(1)}, u32[]{:S(2)}, u32[]{:S(2)}) collective-permute-start(f32[136,128]{1,0:T(8,128)S(1)} %get-tuple-element.23), channel_id=1, source_target_pairs={{0,4},{4,0},{8,12},{12,8},{16,20},{20,16},{24,28},{28,24},{1,5},{5... | collective-permute-start | bytes 208904 | tf_op jit(solution)/shard_map/ppermute | solution.py:292
  32.1 6.1 %collective-permute-start.11 = (f32[136,128]{1,0:T(8,128)S(1)}, f32[136,128]{1,0:T(8,128)S(1)}, u32[]{:S(2)}, u32[]{:S(2)}) collective-permute-start(f32[136,128]{1,0:T(8,128)S(1)} %add.82._), channel_id=1, source_target_pairs={{0,24},{4,28},{8,16},{12,20},{16,8},{20,12},{24,0},{28,4},{1,25},{... | collective-permute-start | bytes 208904 | tf_op jit(solution)/shard_map/ppermute | solution.py:292
  33.8 4.6 %collective-permute-start.10 = (f32[136,128]{1,0:T(8,128)S(1)}, f32[136,128]{1,0:T(8,128)S(1)}, u32[]{:S(2)}, u32[]{:S(2)}) collective-permute-start(f32[136,128]{1,0:T(8,128)S(1)} %add.82._), channel_id=1, source_target_pairs={{0,16},{4,20},{8,24},{12,28},{16,0},{20,4},{24,8},{28,12},{1,17},{... | collective-permute-start | bytes 208904 | tf_op jit(solution)/shard_map/ppermute | solution.py:292
  34.6 4.3 %collective-permute-start.9 = (f32[136,128]{1,0:T(8,128)S(1)}, f32[136,128]{1,0:T(8,128)S(1)}, u32[]{:S(2)}, u32[]{:S(2)}) collective-permute-start(f32[136,128]{1,0:T(8,128)S(1)} %add.82._), channel_id=1, source_target_pairs={{0,8},{4,12},{8,0},{12,4},{16,24},{20,28},{24,16},{28,20},{1,9},{5... | collective-permute-start | bytes 208904 | tf_op jit(solution)/shard_map/ppermute | solution.py:292
  38.9 7.3 %collective-permute-start.14 = (f32[136,128]{1,0:T(8,128)S(1)}, f32[136,128]{1,0:T(8,128)S(1)}, u32[]{:S(2)}, u32[]{:S(2)}) collective-permute-start(f32[136,128]{1,0:T(8,128)S(1)} %add_add_fusion.1._), channel_id=1, source_target_pairs={{0,3},{1,2},{2,1},{3,0},{4,7},{5,6},{6,5},{7,4},{8,11},{9,10},{10,... | collective-permute-start | bytes 208904 | tf_op jit(solution)/shard_map/ppermute | solution.py:292
  41.6 6.4 %collective-permute-start.13 = (f32[136,128]{1,0:T(8,128)S(1)}, f32[136,128]{1,0:T(8,128)S(1)}, u32[]{:S(2)}, u32[]{:S(2)}) collective-permute-start(f32[136,128]{1,0:T(8,128)S(1)} %add_add_fusion.1._), channel_id=1, source_target_pairs={{0,2},{1,3},{2,0},{3,1},{4,6},{5,7},{6,4},{7,5},{8,10},{9,11},{10,... | collective-permute-start | bytes 208904 | tf_op jit(solution)/shard_map/ppermute | solution.py:292
  41.6 6.4 %collective-permute-start.12 = (f32[136,128]{1,0:T(8,128)S(1)}, f32[136,128]{1,0:T(8,128)S(1)}, u32[]{:S(2)}, u32[]{:S(2)}) collective-permute-start(f32[136,128]{1,0:T(8,128)S(1)} %add_add_fusion.1._), channel_id=1, source_target_pairs={{0,1},{1,0},{2,3},{3,2},{4,5},{5,4},{6,7},{7,6},{8,9},{9,8},{10,11... | collective-permute-start | bytes 208904 | tf_op jit(solution)/shard_map/ppermute | solution.py:292
  48.0 1.3 %collective-permute-start.15 = (f32[136,128]{1,0:T(8,128)S(1)}, f32[136,128]{1,0:T(8,128)S(1)}, u32[]{:S(2)}, u32[]{:S(2)}) collective-permute-start(f32[136,128]{1,0:T(8,128)S(1)} %add_add_fusion.refs_0_), channel_id=1, source_target_pairs={{0,4},{4,0},{8,12},{12,8},{16,20},{20,16},{24,28},{28,24},{1,5},{5... | collective-permute-start | bytes 208904 | tf_op jit(solution)/shard_map/ppermute | solution.py:292

commit v8 on v7

--- a/solution.py
+++ b/solution.py
@@ -157,8 +157,17 @@
     lax.fori_loop(0, a_ref.shape[0], body, 0)
     width = a_ref.shape[2]
     cross = total_ref[:, width : width + RK]
-    tall_ref[:RK, :] = total_ref[:RK, :RK] + total_ref[:RK, width : width + RK] + cross[:RK, :].T
-    tall_ref[RK:, :] = total_ref[:RK, RK:width] + total_ref[:RK, width + RK :] + cross[RK:, :].T
+    first = total_ref[:RK, :RK] + total_ref[:RK, width : width + RK] + cross[:RK, :].T
+    row, col = triangle_ids()
+    half = RK // 2
+    lower = jnp.concatenate([first[half:, half:], first[half:, :half]], axis=1)
+    tall_ref[:half, :] = jnp.where((row >= col)[:half, :], lower, first[:half, :])
+    tall_ref[half : half + RK, :] = (
+        total_ref[:RK, RK:width] + total_ref[:RK, width + RK :] + cross[RK:, :].T
+    )
+    diagonal = jnp.sum(jnp.where(row == col, first, 0.0), axis=0, keepdims=True)
+    tail = tall_ref.shape[0] - half - RK
+    tall_ref[half + RK :, :] = jnp.broadcast_to(diagonal, (tail, LANES))
     store_blocks(tall_ref, outs)
 
 
@@ -198,8 +207,15 @@
     tall_ref, pack_ref, w_ref, total_ref = refs[4 + SPREAD_TWO :]
     row, col = triangle_ids()
     load_blocks(blocks, tall_ref)
-    w_ref[:, :LANES] = tall_ref[:RK, :]
-    w_ref[:, LANES : 2 * LANES] = tall_ref[RK:, :]
+    half = RK // 2
+    top = tall_ref[:half, :]
+    mixed = jnp.concatenate(
+        [top, jnp.concatenate([top[:, half:], top[:, :half]], axis=1)], axis=0
+    )
+    sent = ((row < half) & (col > row)) | ((col >= half) & (row > col))
+    diagonal = jnp.broadcast_to(tall_ref[half + RK : half + RK + 1, :], (LANES, LANES))
+    w_ref[:, :LANES] = jnp.where(sent, mixed, jnp.where(row == col, diagonal, mixed.T))
+    w_ref[:, LANES : 2 * LANES] = tall_ref[half : half + RK, :]
     w_ref[:, 2 * LANES :] = jnp.where(row == col, 1.0, 0.0).astype(F32)
     factor_rows(w_ref, 3)
     linv_ref[...] = w_ref[:, 2 * LANES :] * scale
@@ -210,9 +226,7 @@
     upper_both = jnp.concatenate([upper_hi, upper_lo], axis=0)
     points = absorbed_ref.shape[0]
     group = 4
-    total_ref[...] = jnp.zeros_like(total_ref)
-
-    def body(step, carry):
+    for step in range(points // group):
         pieces = []
         for i in range(group):
             p = step * group + i
@@ -222,10 +236,8 @@
             pieces.append(split(b))
         b_hi = jnp.concatenate([x[0] for x in pieces], axis=0)
         b_lo = jnp.concatenate([x[1] for x in pieces], axis=0)
-        total_ref[...] += dot_tn(b_hi, jnp.concatenate([b_hi, b_lo], axis=1))
-        return carry
-
-    lax.fori_loop(0, points // group, body, 0)
+        part = dot_tn(b_hi, jnp.concatenate([b_hi, b_lo], axis=1))
+        total_ref[...] = part if step == 0 else total_ref[...] + part
     cross = total_ref[:, 256:]
     gram = total_ref[:, :256] + cross + cross.T
     lower_right = gram[LANES:, LANES:]
@@ -398,7 +410,7 @@
     vmem = pl.BlockSpec(memory_space=pltpu.VMEM)
 
     steps = 8
-    block_rows = 2 * RK // SPREAD_ONE
+    block_rows = (RK // 2 + RK + 16) // SPREAD_ONE
     blocks = pl.pallas_call(
         gram_kernel,
         in_specs=[pl.BlockSpec(memory_space=pl.ANY)],
@@ -407,7 +419,7 @@
         scratch_shapes=[
             pltpu.VMEM((steps, unfold.shape[0] // steps, rank_mid), F32),
             pltpu.VMEM((rank_mid, 2 * rank_mid), F32),
-            pltpu.VMEM((2 * RK, LANES), F32),
+            pltpu.VMEM((SPREAD_ONE * block_rows, LANES), F32),
             pltpu.SemaphoreType.DMA((steps,)),
         ],
         compiler_params=params(limit=53 * 1024 * 1024),
@@ -418,6 +430,7 @@
         [None, functools.partial(relay_part, rows_right, points)],
     )
 
+    tall_rows = SPREAD_ONE * block_rows
     block_rows = LANES + 8
     packed_rows = SPREAD_TWO * block_rows
     absorbed, linv, *blocks = pl.pallas_call(
@@ -426,7 +439,7 @@
         out_specs=[vmem] * (2 + SPREAD_TWO),
         out_shape=[shape(points, RK, rank_right), shape(RK, RK)] + [shape(block_rows, LANES)] * SPREAD_TWO,
         scratch_shapes=[
-            pltpu.VMEM((2 * RK, LANES), F32),
+            pltpu.VMEM((tall_rows, LANES), F32),
             pltpu.VMEM((packed_rows, LANES), F32),
             pltpu.VMEM((LANES, 3 * LANES), F32),
             pltpu.VMEM((rank_right, 2 * rank_right), F32),

time: 56.1 us -> 54.9 us (0.979)
  waiting for transfers between devices: 12.9 us -> 12.1 us
    ppermute x16, waiting for transfers between devices: 12.9 us -> 12.1 us  [swap(): return lax.ppermute(value, axes, [(i, i ^ mask) for i in range(size)])]
  transfers between devices with their start and end apart: 16 -> 16, of which waited for: 11 -> 10; matrix products, arithmetic and copies ran while one was open for 0% -> 0% of each run, Pallas kernels for 15% -> 15%
where the time goes in v8:
time: 54.9 us; the launch traced here: 54.8 us
  Pallas kernels  24 us (44%)
  starting transfers between devices  17.9 us (33%)
  waiting for transfers between devices  12.1 us (22%)
  between operations  0.71 us (1%)
    ppermute x16, starting transfers between devices, swap(): return lax.ppermute(value, axes, [(i, i ^ mask) for i in range(size)])  17.9 us
    ppermute x16, waiting for transfers between devices, swap(): return lax.ppermute(value, axes, [(i, i ^ mask) for i in range(size)])  12.1 us
    pallas_call x1, Pallas kernels, per_device(): pl.pallas_call(functools.partial(factor_kernel, 1.0 / (RK * total_points)...  6.69 us
    pallas_call x1, Pallas kernels, per_device(): pl.pallas_call(functools.partial(absorb_kernel, math.sqrt(rank_left * tot...  5.24 us
    pallas_call x1, Pallas kernels, per_device(): pl.pallas_call(gram_kernel, in_specs=[pl.BlockSpec(memory_space=pl.ANY)],...  3.9 us
    pallas_call x1, Pallas kernels, left_part(): pl.pallas_call(left_kernel, grid=(steps,), in_specs=[pl.BlockSpec((chunk,...  2.83 us
    pallas_call x1, Pallas kernels, relay_part(): pl.pallas_call(functools.partial(relay_kernel, points), in_specs=[pl.Bloc...  2.8 us
    pallas_call x1, Pallas kernels, right_part(): pl.pallas_call(functools.partial(right_kernel, points), grid=(steps, 2),...  2.49 us
  transfers between devices with their start and end apart: 16, of which 10 were waited for; matrix products, arithmetic and copies ran while one was open for 0% of the time, Pallas kernels for 15%

profile of v8, /device:TPU:0, one launch (start us, length us, event | category | flops | bytes accessed | tf_op | source)
XLA Modules:
  0.0 54.8 jit_solution(13326205592812675537)
XLA Ops:
  0.6 3.9 %gram_top.1 = (f32[104,128]{1,0:T(8,128)S(1)}, f32[104,128]{1,0:T(8,128)S(1)}) custom-call(f32[4096,256]{1,0:T(8,128)} %bitcast.10), custom_call_target="tpu_custom_call" | custom-call | tf_op jit(solution)/shard_map/gram_top/pallas_call | solution.py:414
  5.1 0.9 %collective-permute-done = f32[104,128]{1,0:T(8,128)S(1)} collective-permute-done((f32[104,128]{1,0:T(8,128)S(1)}, f32[104,128]{1,0:T(8,128)S(1)}, u32[]{:S(2)}, u32[]{:S(2)}) %collective-permute-start) | collective-permute-done | bytes 53280 | tf_op jit(solution)/shard_map/ppermute | solution.py:304
  5.9 3.9 %collective-permute-start.3 = (f32[104,128]{1,0:T(8,128)S(1)}, f32[104,128]{1,0:T(8,128)S(1)}, u32[]{:S(2)}, u32[]{:S(2)}) collective-permute-start(f32[104,128]{1,0:T(8,128)S(1)} %add.72), channel_id=1, source_target_pairs={{0,24},{4,28},{8,16},{12,20},{16,8},{20,12},{24,0},{28,4},{1,25},{... | collective-permute-start | bytes 159752 | tf_op jit(solution)/shard_map/ppermute | solution.py:304
  9.8 0.5 collective-permute-start.2
  10.5 1.5 %collective-permute-done.3 = f32[104,128]{1,0:T(8,128)S(1)} collective-permute-done((f32[104,128]{1,0:T(8,128)S(1)}, f32[104,128]{1,0:T(8,128)S(1)}, u32[]{:S(2)}, u32[]{:S(2)}) %collective-permute-start.3) | collective-permute-done | bytes 53280 | tf_op jit(solution)/shard_map/ppermute | solution.py:304
  11.9 2.0 %collective-permute-done.2 = f32[104,128]{1,0:T(8,128)S(1)} collective-permute-done((f32[104,128]{1,0:T(8,128)S(1)}, f32[104,128]{1,0:T(8,128)S(1)}, u32[]{:S(2)}, u32[]{:S(2)}) %collective-permute-start.2) | collective-permute-done | bytes 53280 | tf_op jit(solution)/shard_map/ppermute | solution.py:304
  13.9 0.5 collective-permute-done.1
  14.5 3.7 %collective-permute-start.6 = (f32[104,128]{1,0:T(8,128)S(1)}, f32[104,128]{1,0:T(8,128)S(1)}, u32[]{:S(2)}, u32[]{:S(2)}) collective-permute-start(f32[104,128]{1,0:T(8,128)S(1)} %add_add_fusion.3._), channel_id=1, source_target_pairs={{0,3},{1,2},{2,1},{3,0},{4,7},{5,6},{6,5},{7,4},{8,11},{9,10},{10,... | collective-permute-start | bytes 159752 | tf_op jit(solution)/shard_map/ppermute | solution.py:304
  18.2 0.8 %collective-permute-start.4 = (f32[104,128]{1,0:T(8,128)S(1)}, f32[104,128]{1,0:T(8,128)S(1)}, u32[]{:S(2)}, u32[]{:S(2)}) collective-permute-start(f32[104,128]{1,0:T(8,128)S(1)} %add_add_fusion.3._), channel_id=1, source_target_pairs={{0,1},{1,0},{2,3},{3,2},{4,5},{5,4},{6,7},{7,6},{8,9},{9,8},{10,11... | collective-permute-start | bytes 159752 | tf_op jit(solution)/shard_map/ppermute | solution.py:304
  19.0 2.8 %relay_right.1 = (bf16[16,256,256]{2,1,0:T(8,128)(2,1)S(1)}, bf16[16,256,256]{2,1,0:T(8,128)(2,1)S(1)}, f32[8,128]{1,0:T(8,128)S(1)}) custom-call(f32[4096,256]{1,0:T(8,128)} %bitcast.12, f32[104,128]{1,0:T(8,128)S(1)} %add_add_fusion.3._), custom_call_target="tpu_custom_call" | custom-call | bytes 8388608 | tf_op jit(solution)/shard_map/relay_right/pallas_call | solution.py:345
  21.8 1.4 %collective-permute-done.5 = f32[104,128]{1,0:T(8,128)S(1)} collective-permute-done((f32[104,128]{1,0:T(8,128)S(1)}, f32[104,128]{1,0:T(8,128)S(1)}, u32[]{:S(2)}, u32[]{:S(2)}) %collective-permute-start.5) | collective-permute-done | bytes 53280 | tf_op jit(solution)/shard_map/ppermute | solution.py:304
  23.3 1.2 %collective-permute-done.7.refs_1_ = f32[104,128]{1,0:T(8,128)S(1)} collective-permute-done((f32[104,128]{1,0:T(8,128)S(1)}, f32[104,128]{1,0:T(8,128)S(1)}, u32[]{:S(2)}, u32[]{:S(2)}) %collective-permute-start.7) | collective-permute-done | bytes 53280 | tf_op jit(solution)/shard_map/ppermute | solution.py:304
  24.5 5.2 %factor_absorb.1 = (f32[16,128,256]{2,1,0:T(8,128)S(1)}, f32[128,128]{1,0:T(8,128)S(1)}, f32[136,128]{1,0:T(8,128)S(1)}, f32[136,128]{1,0:T(8,128)S(1)}) custom-call(f32[104,128]{1,0:T(8,128)S(1)} %add_add_fusion.2.refs_0_, f32[104,128]{1,0:T(8,128)S(1)} %collective-permute-done.7.refs_1_, bf16[16,256,256]{2,1,0:T(8,128)(2,1)S(1)} %get-tuple-element.19.refs_2_, ...), custom_call_target="tpu_custom_call" | custom-call | tf_op jit(solution)/shard_map/factor_absorb/pallas_call | solution.py:436
  30.0 1.1 %collective-permute-done.8 = f32[136,128]{1,0:T(8,128)S(1)} collective-permute-done((f32[136,128]{1,0:T(8,128)S(1)}, f32[136,128]{1,0:T(8,128)S(1)}, u32[]{:S(2)}, u32[]{:S(2)}) %collective-permute-start.8) | collective-permute-done | bytes 69664 | tf_op jit(solution)/shard_map/ppermute | solution.py:304
  31.1 1.6 %collective-permute-start.11 = (f32[136,128]{1,0:T(8,128)S(1)}, f32[136,128]{1,0:T(8,128)S(1)}, u32[]{:S(2)}, u32[]{:S(2)}) collective-permute-start(f32[136,128]{1,0:T(8,128)S(1)} %add.82._), channel_id=1, source_target_pairs={{0,24},{4,28},{8,16},{12,20},{16,8},{20,12},{24,0},{28,4},{1,25},{... | collective-permute-start | bytes 208904 | tf_op jit(solution)/shard_map/ppermute | solution.py:304
  33.1 1.5 %collective-permute-start.9 = (f32[136,128]{1,0:T(8,128)S(1)}, f32[136,128]{1,0:T(8,128)S(1)}, u32[]{:S(2)}, u32[]{:S(2)}) collective-permute-start(f32[136,128]{1,0:T(8,128)S(1)} %add.82._), channel_id=1, source_target_pairs={{0,8},{4,12},{8,0},{12,4},{16,24},{20,28},{24,16},{28,20},{1,9},{5... | collective-permute-start | bytes 208904 | tf_op jit(solution)/shard_map/ppermute | solution.py:304
  34.7 2.5 %right_out.1 = (f32[2048,256]{1,0:T(8,128)}, f32[8,128]{1,0:T(8,128)S(1)}) custom-call(f32[16,128,256]{2,1,0:T(8,128)S(1)} %get-tuple-element.24.absorbed_ref, f32[136,128]{1,0:T(8,128)S(1)} %add.82._), custom_call_target="tpu_custom_call" | custom-call | bytes 8388608 | tf_op jit(solution)/shard_map/right_out/pallas_call | solution.py:386
  37.2 0.6 %collective-permute-done.9 = f32[136,128]{1,0:T(8,128)S(1)} collective-permute-done((f32[136,128]{1,0:T(8,128)S(1)}, f32[136,128]{1,0:T(8,128)S(1)}, u32[]{:S(2)}, u32[]{:S(2)}) %collective-permute-start.9) | collective-permute-done | bytes 69664 | tf_op jit(solution)/shard_map/ppermute | solution.py:304
  37.8 2.3 %collective-permute-start.14 = (f32[136,128]{1,0:T(8,128)S(1)}, f32[136,128]{1,0:T(8,128)S(1)}, u32[]{:S(2)}, u32[]{:S(2)}) collective-permute-start(f32[136,128]{1,0:T(8,128)S(1)} %add_add_fusion.1._), channel_id=1, source_target_pairs={{0,3},{1,2},{2,1},{3,0},{4,7},{5,6},{6,5},{7,4},{8,11},{9,10},{10,... | collective-permute-start | bytes 208904 | tf_op jit(solution)/shard_map/ppermute | solution.py:304
  40.1 2.2 %collective-permute-start.12 = (f32[136,128]{1,0:T(8,128)S(1)}, f32[136,128]{1,0:T(8,128)S(1)}, u32[]{:S(2)}, u32[]{:S(2)}) collective-permute-start(f32[136,128]{1,0:T(8,128)S(1)} %add_add_fusion.1._), channel_id=1, source_target_pairs={{0,1},{1,0},{2,3},{3,2},{4,5},{5,4},{6,7},{7,6},{8,9},{9,8},{10,11... | collective-permute-start | bytes 208904 | tf_op jit(solution)/shard_map/ppermute | solution.py:304
  42.3 2.8 %left_out.1 = (f32[4096,128]{1,0:T(8,128)}, f32[8,128]{1,0:T(8,128)S(1)}) custom-call(f32[4096,256]{1,0:T(8,128)S(1)} %bitcast.11, f32[128,128]{1,0:T(8,128)S(1)} %get-tuple-element.21.linv_ref, f32[136,128]{1,0:T(8,128)S(1)} %add_add_fusion.1._), custom_call_target="tpu_custom_call" | custom-call | bytes 8388608 | tf_op jit(solution)/shard_map/left_out/pallas_call | solution.py:364
  45.1 1.6 %collective-permute-done.13 = f32[136,128]{1,0:T(8,128)S(1)} collective-permute-done((f32[136,128]{1,0:T(8,128)S(1)}, f32[136,128]{1,0:T(8,128)S(1)}, u32[]{:S(2)}, u32[]{:S(2)}) %collective-permute-start.13) | collective-permute-done | bytes 69664 | tf_op jit(solution)/shard_map/ppermute | solution.py:304
  46.9 1.2 %collective-permute-done.15.refs_1_ = f32[136,128]{1,0:T(8,128)S(1)} collective-permute-done((f32[136,128]{1,0:T(8,128)S(1)}, f32[136,128]{1,0:T(8,128)S(1)}, u32[]{:S(2)}, u32[]{:S(2)}) %collective-permute-start.15) | collective-permute-done | bytes 69664 | tf_op jit(solution)/shard_map/ppermute | solution.py:304
  48.1 6.7 %factor_next.1 = f32[256,256]{1,0:T(8,128)} custom-call(f32[136,128]{1,0:T(8,128)S(1)} %add_add_fusion.refs_0_, f32[136,128]{1,0:T(8,128)S(1)} %collective-permute-done.15.refs_1_), custom_call_target="tpu_custom_call" | custom-call | tf_op jit(solution)/shard_map/factor_next/pallas_call | solution.py:458
  (25 shorter events, 1.6 us)
Async XLA Ops:
  4.5 1.4 %collective-permute-start = (f32[104,128]{1,0:T(8,128)S(1)}, f32[104,128]{1,0:T(8,128)S(1)}, u32[]{:S(2)}, u32[]{:S(2)}) collective-permute-start(f32[104,128]{1,0:T(8,128)S(1)} %get-tuple-element.17), channel_id=1, source_target_pairs={{0,4},{4,0},{8,12},{12,8},{16,20},{20,16},{24,28},{28,24},{1,5},{5... | collective-permute-start | bytes 159752 | tf_op jit(solution)/shard_map/ppermute | solution.py:304
  5.9 6.0 %collective-permute-start.3 = (f32[104,128]{1,0:T(8,128)S(1)}, f32[104,128]{1,0:T(8,128)S(1)}, u32[]{:S(2)}, u32[]{:S(2)}) collective-permute-start(f32[104,128]{1,0:T(8,128)S(1)} %add.72), channel_id=1, source_target_pairs={{0,24},{4,28},{8,16},{12,20},{16,8},{20,12},{24,0},{28,4},{1,25},{... | collective-permute-start | bytes 159752 | tf_op jit(solution)/shard_map/ppermute | solution.py:304
  9.8 4.1 %collective-permute-start.2 = (f32[104,128]{1,0:T(8,128)S(1)}, f32[104,128]{1,0:T(8,128)S(1)}, u32[]{:S(2)}, u32[]{:S(2)}) collective-permute-start(f32[104,128]{1,0:T(8,128)S(1)} %add.72), channel_id=1, source_target_pairs={{0,16},{4,20},{8,24},{12,28},{16,0},{20,4},{24,8},{28,12},{1,17},{... | collective-permute-start | bytes 159752 | tf_op jit(solution)/shard_map/ppermute | solution.py:304
  10.3 4.1 %collective-permute-start.1 = (f32[104,128]{1,0:T(8,128)S(1)}, f32[104,128]{1,0:T(8,128)S(1)}, u32[]{:S(2)}, u32[]{:S(2)}) collective-permute-start(f32[104,128]{1,0:T(8,128)S(1)} %add.72), channel_id=1, source_target_pairs={{0,8},{4,12},{8,0},{12,4},{16,24},{20,28},{24,16},{28,20},{1,9},{5... | collective-permute-start | bytes 159752 | tf_op jit(solution)/shard_map/ppermute | solution.py:304
  14.5 7.3 %collective-permute-start.6 = (f32[104,128]{1,0:T(8,128)S(1)}, f32[104,128]{1,0:T(8,128)S(1)}, u32[]{:S(2)}, u32[]{:S(2)}) collective-permute-start(f32[104,128]{1,0:T(8,128)S(1)} %add_add_fusion.3._), channel_id=1, source_target_pairs={{0,3},{1,2},{2,1},{3,0},{4,7},{5,6},{6,5},{7,4},{8,11},{9,10},{10,... | collective-permute-start | bytes 159752 | tf_op jit(solution)/shard_map/ppermute | solution.py:304
  18.2 5.0 %collective-permute-start.5 = (f32[104,128]{1,0:T(8,128)S(1)}, f32[104,128]{1,0:T(8,128)S(1)}, u32[]{:S(2)}, u32[]{:S(2)}) collective-permute-start(f32[104,128]{1,0:T(8,128)S(1)} %add_add_fusion.3._), channel_id=1, source_target_pairs={{0,2},{1,3},{2,0},{3,1},{4,6},{5,7},{6,4},{7,5},{8,10},{9,11},{10,... | collective-permute-start | bytes 159752 | tf_op jit(solution)/shard_map/ppermute | solution.py:304
  18.2 5.0 %collective-permute-start.4 = (f32[104,128]{1,0:T(8,128)S(1)}, f32[104,128]{1,0:T(8,128)S(1)}, u32[]{:S(2)}, u32[]{:S(2)}) collective-permute-start(f32[104,128]{1,0:T(8,128)S(1)} %add_add_fusion.3._), channel_id=1, source_target_pairs={{0,1},{1,0},{2,3},{3,2},{4,5},{5,4},{6,7},{7,6},{8,9},{9,8},{10,11... | collective-permute-start | bytes 159752 | tf_op jit(solution)/shard_map/ppermute | solution.py:304
  23.2 1.3 %collective-permute-start.7 = (f32[104,128]{1,0:T(8,128)S(1)}, f32[104,128]{1,0:T(8,128)S(1)}, u32[]{:S(2)}, u32[]{:S(2)}) collective-permute-start(f32[104,128]{1,0:T(8,128)S(1)} %add_add_fusion.2.refs_0_), channel_id=1, source_target_pairs={{0,4},{4,0},{8,12},{12,8},{16,20},{20,16},{24,28},{28,24},{1,5},{5... | collective-permute-start | bytes 159752 | tf_op jit(solution)/shard_map/ppermute | solution.py:304
  24.5 17.8 %copy-start = (f32[256,16,256]{2,1,0:T(8,128)S(1)}, f32[256,16,256]{2,1,0:T(8,128)}, u32[]{:S(2)}) copy-start(f32[256,16,256]{2,1,0:T(8,128)} %param.2) | copy-start | bytes 12582916
  29.8 1.3 %collective-permute-start.8 = (f32[136,128]{1,0:T(8,128)S(1)}, f32[136,128]{1,0:T(8,128)S(1)}, u32[]{:S(2)}, u32[]{:S(2)}) collective-permute-start(f32[136,128]{1,0:T(8,128)S(1)} %get-tuple-element.23), channel_id=1, source_target_pairs={{0,4},{4,0},{8,12},{12,8},{16,20},{20,16},{24,28},{28,24},{1,5},{5... | collective-permute-start | bytes 208904 | tf_op jit(solution)/shard_map/ppermute | solution.py:304
  31.1 6.1 %collective-permute-start.11 = (f32[136,128]{1,0:T(8,128)S(1)}, f32[136,128]{1,0:T(8,128)S(1)}, u32[]{:S(2)}, u32[]{:S(2)}) collective-permute-start(f32[136,128]{1,0:T(8,128)S(1)} %add.82._), channel_id=1, source_target_pairs={{0,24},{4,28},{8,16},{12,20},{16,8},{20,12},{24,0},{28,4},{1,25},{... | collective-permute-start | bytes 208904 | tf_op jit(solution)/shard_map/ppermute | solution.py:304
  32.7 4.5 %collective-permute-start.10 = (f32[136,128]{1,0:T(8,128)S(1)}, f32[136,128]{1,0:T(8,128)S(1)}, u32[]{:S(2)}, u32[]{:S(2)}) collective-permute-start(f32[136,128]{1,0:T(8,128)S(1)} %add.82._), channel_id=1, source_target_pairs={{0,16},{4,20},{8,24},{12,28},{16,0},{20,4},{24,8},{28,12},{1,17},{... | collective-permute-start | bytes 208904 | tf_op jit(solution)/shard_map/ppermute | solution.py:304
  33.1 4.7 %collective-permute-start.9 = (f32[136,128]{1,0:T(8,128)S(1)}, f32[136,128]{1,0:T(8,128)S(1)}, u32[]{:S(2)}, u32[]{:S(2)}) collective-permute-start(f32[136,128]{1,0:T(8,128)S(1)} %add.82._), channel_id=1, source_target_pairs={{0,8},{4,12},{8,0},{12,4},{16,24},{20,28},{24,16},{28,20},{1,9},{5... | collective-permute-start | bytes 208904 | tf_op jit(solution)/shard_map/ppermute | solution.py:304
  37.8 7.3 %collective-permute-start.14 = (f32[136,128]{1,0:T(8,128)S(1)}, f32[136,128]{1,0:T(8,128)S(1)}, u32[]{:S(2)}, u32[]{:S(2)}) collective-permute-start(f32[136,128]{1,0:T(8,128)S(1)} %add_add_fusion.1._), channel_id=1, source_target_pairs={{0,3},{1,2},{2,1},{3,0},{4,7},{5,6},{6,5},{7,4},{8,11},{9,10},{10,... | collective-permute-start | bytes 208904 | tf_op jit(solution)/shard_map/ppermute | solution.py:304
  40.1 6.6 %collective-permute-start.13 = (f32[136,128]{1,0:T(8,128)S(1)}, f32[136,128]{1,0:T(8,128)S(1)}, u32[]{:S(2)}, u32[]{:S(2)}) collective-permute-start(f32[136,128]{1,0:T(8,128)S(1)} %add_add_fusion.1._), channel_id=1, source_target_pairs={{0,2},{1,3},{2,0},{3,1},{4,6},{5,7},{6,4},{7,5},{8,10},{9,11},{10,... | collective-permute-start | bytes 208904 | tf_op jit(solution)/shard_map/ppermute | solution.py:304
  40.1 6.6 %collective-permute-start.12 = (f32[136,128]{1,0:T(8,128)S(1)}, f32[136,128]{1,0:T(8,128)S(1)}, u32[]{:S(2)}, u32[]{:S(2)}) collective-permute-start(f32[136,128]{1,0:T(8,128)S(1)} %add_add_fusion.1._), channel_id=1, source_target_pairs={{0,1},{1,0},{2,3},{3,2},{4,5},{5,4},{6,7},{7,6},{8,9},{9,8},{10,11... | collective-permute-start | bytes 208904 | tf_op jit(solution)/shard_map/ppermute | solution.py:304
  46.7 1.3 %collective-permute-start.15 = (f32[136,128]{1,0:T(8,128)S(1)}, f32[136,128]{1,0:T(8,128)S(1)}, u32[]{:S(2)}, u32[]{:S(2)}) collective-permute-start(f32[136,128]{1,0:T(8,128)S(1)} %add_add_fusion.refs_0_), channel_id=1, source_target_pairs={{0,4},{4,0},{8,12},{12,8},{16,20},{20,16},{24,28},{28,24},{1,5},{5... | collective-permute-start | bytes 208904 | tf_op jit(solution)/shard_map/ppermute | solution.py:304

commit v9 on v8

--- a/solution.py
+++ b/solution.py
@@ -47,11 +47,25 @@
     return left, right
 
 
+def three_pieces(x):
+    one = x.astype(BF16)
+    rest = x - one.astype(F32)
+    two = rest.astype(BF16)
+    return one, two, (rest - two.astype(F32)).astype(BF16)
+
+
+def turned_product(tall, wide):
+    a, b, c = three_pieces(tall)
+    x, y, z = three_pieces(wide)
+    small = dot_nn(c, x) + dot_nn(a, z) + dot_nn(b, y)
+    return small + (dot_nn(b, x) + dot_nn(a, y)) + dot_nn(a, x)
+
+
 def spread_row(x, k):
     return jnp.broadcast_to(x[k : k + 1, :], x.shape)
 
 
-def factor_rows(w_ref, blocks):
+def factor_rows(w_ref, blocks, stacked):
     size = w_ref.shape[0]
     row_id = lax.broadcasted_iota(jnp.int32, (PANEL, LANES), 0)
     rows = [
@@ -95,10 +109,14 @@
         for b in range(own, blocks):
             w_ref[now * PANEL : (now + 1) * PANEL, b * LANES : (b + 1) * LANES] = done[b - own]
         if now + 2 < len(rows):
-            both = [stacked_pieces(x) for x in done]
-            left = jnp.concatenate([x[0] for x in both[: size // LANES - own]], axis=1)
-            right = jnp.concatenate([x[1] for x in both], axis=1)
-            update = dot_tn(left, right)
+            if stacked:
+                both = [stacked_pieces(x) for x in done]
+                left = jnp.concatenate([x[0] for x in both[: size // LANES - own]], axis=1)
+                right = jnp.concatenate([x[1] for x in both], axis=1)
+                update = dot_tn(left, right)
+            else:
+                tall = jnp.concatenate([x.T for x in done[: size // LANES - own]], axis=0)
+                update = turned_product(tall, jnp.concatenate(done, axis=1))
             for g in range(now + 2, len(rows)):
                 top = g * PANEL - own * LANES
                 for b in range(g * PANEL // LANES, blocks):
@@ -146,15 +164,11 @@
     outs = refs[:SPREAD_ONE]
     a_ref, total_ref, tall_ref, sems = refs[SPREAD_ONE:]
     copy = chunk_copies(a_hbm, a_ref, sems)
-    total_ref[...] = jnp.zeros_like(total_ref)
-
-    def body(i, carry):
+    for i in range(a_ref.shape[0]):
         copy(i).wait()
         hi, lo = split(a_ref[i])
-        total_ref[...] += dot_tn(hi, jnp.concatenate([hi, lo], axis=1))
-        return carry
-
-    lax.fori_loop(0, a_ref.shape[0], body, 0)
+        part = dot_tn(hi, jnp.concatenate([hi, lo], axis=1))
+        total_ref[...] = part if i == 0 else total_ref[...] + part
     width = a_ref.shape[2]
     cross = total_ref[:, width : width + RK]
     first = total_ref[:RK, :RK] + total_ref[:RK, width : width + RK] + cross[:RK, :].T
@@ -217,7 +231,7 @@
     w_ref[:, :LANES] = jnp.where(sent, mixed, jnp.where(row == col, diagonal, mixed.T))
     w_ref[:, LANES : 2 * LANES] = tall_ref[half : half + RK, :]
     w_ref[:, 2 * LANES :] = jnp.where(row == col, 1.0, 0.0).astype(F32)
-    factor_rows(w_ref, 3)
+    factor_rows(w_ref, 3, True)
     linv_ref[...] = w_ref[:, 2 * LANES :] * scale
     upper = jnp.concatenate(
         [jnp.where(col >= row, w_ref[:, :LANES], 0.0), w_ref[:, LANES : 2 * LANES]], axis=1
@@ -274,7 +288,7 @@
     w_ref[:LANES, LANES:] = pack_ref[LANES : 2 * LANES, :] * scale
     w_ref[LANES:, :LANES] = jnp.zeros((LANES, LANES), F32)
     w_ref[LANES:, LANES:] = jnp.where(row > col, packed, jnp.where(row == col, diagonal, turned))
-    factor_rows(w_ref, 2)
+    factor_rows(w_ref, 2, False)
     out_ref[:LANES, :LANES] = jnp.where(col >= row, w_ref[:LANES, :LANES], 0.0)
     out_ref[:LANES, LANES:] = w_ref[:LANES, LANES:]
     out_ref[LANES:, :LANES] = jnp.zeros((LANES, LANES), F32)

time: 54.9 us -> 56.4 us (1.027)
  Pallas kernels: 24 us -> 25.5 us
    pallas_call x1, Pallas kernels: 6.69 us -> 8.29 us  [per_device(): pl.pallas_call(functools.partial(factor_kernel, 1.0 / (RK * total_points)...]
  transfers between devices with their start and end apart: 16 -> 16, of which waited for: 10 -> 10; matrix products, arithmetic and copies ran while one was open for 0% -> 0% of each run, Pallas kernels for 15% -> 14%
where the time goes in v9:
time: 56.4 us; the launch traced here: 56.3 us
  Pallas kernels  25.5 us (45%)
  starting transfers between devices  17.9 us (32%)
  waiting for transfers between devices  12.1 us (21%)
  between operations  0.71 us (1%)
    ppermute x16, starting transfers between devices, swap(): return lax.ppermute(value, axes, [(i, i ^ mask) for i in range(size)])  17.9 us
    ppermute x16, waiting for transfers between devices, swap(): return lax.ppermute(value, axes, [(i, i ^ mask) for i in range(size)])  12.1 us
    pallas_call x1, Pallas kernels, per_device(): pl.pallas_call(functools.partial(factor_kernel, 1.0 / (RK * total_points)...  8.29 us
    pallas_call x1, Pallas kernels, per_device(): pl.pallas_call(functools.partial(absorb_kernel, math.sqrt(rank_left * tot...  5.22 us
    pallas_call x1, Pallas kernels, per_device(): pl.pallas_call(gram_kernel, in_specs=[pl.BlockSpec(memory_space=pl.ANY)],...  3.84 us
    pallas_call x1, Pallas kernels, left_part(): pl.pallas_call(left_kernel, grid=(steps,), in_specs=[pl.BlockSpec((chunk,...  2.83 us
    pallas_call x1, Pallas kernels, relay_part(): pl.pallas_call(functools.partial(relay_kernel, points), in_specs=[pl.Bloc...  2.8 us
    pallas_call x1, Pallas kernels, right_part(): pl.pallas_call(functools.partial(right_kernel, points), grid=(steps, 2),...  2.49 us
  transfers between devices with their start and end apart: 16, of which 10 were waited for; matrix products, arithmetic and copies ran while one was open for 0% of the time, Pallas kernels for 14%

profile of v9, /device:TPU:0, one launch (start us, length us, event | category | flops | bytes accessed | tf_op | source)
XLA Modules:
  0.0 56.3 jit_solution(4964689668518440341)
XLA Ops:
  0.6 3.8 %gram_top.1 = (f32[104,128]{1,0:T(8,128)S(1)}, f32[104,128]{1,0:T(8,128)S(1)}) custom-call(f32[4096,256]{1,0:T(8,128)} %bitcast.10), custom_call_target="tpu_custom_call" | custom-call | tf_op jit(solution)/shard_map/gram_top/pallas_call | solution.py:428
  5.0 0.9 %collective-permute-done = f32[104,128]{1,0:T(8,128)S(1)} collective-permute-done((f32[104,128]{1,0:T(8,128)S(1)}, f32[104,128]{1,0:T(8,128)S(1)}, u32[]{:S(2)}, u32[]{:S(2)}) %collective-permute-start) | collective-permute-done | bytes 53280 | tf_op jit(solution)/shard_map/ppermute | solution.py:318
  5.9 3.9 %collective-permute-start.3 = (f32[104,128]{1,0:T(8,128)S(1)}, f32[104,128]{1,0:T(8,128)S(1)}, u32[]{:S(2)}, u32[]{:S(2)}) collective-permute-start(f32[104,128]{1,0:T(8,128)S(1)} %add.72), channel_id=1, source_target_pairs={{0,24},{4,28},{8,16},{12,20},{16,8},{20,12},{24,0},{28,4},{1,25},{... | collective-permute-start | bytes 159752 | tf_op jit(solution)/shard_map/ppermute | solution.py:318
  9.7 0.5 collective-permute-start.2
  10.4 1.5 %collective-permute-done.3 = f32[104,128]{1,0:T(8,128)S(1)} collective-permute-done((f32[104,128]{1,0:T(8,128)S(1)}, f32[104,128]{1,0:T(8,128)S(1)}, u32[]{:S(2)}, u32[]{:S(2)}) %collective-permute-start.3) | collective-permute-done | bytes 53280 | tf_op jit(solution)/shard_map/ppermute | solution.py:318
  11.9 2.0 %collective-permute-done.2 = f32[104,128]{1,0:T(8,128)S(1)} collective-permute-done((f32[104,128]{1,0:T(8,128)S(1)}, f32[104,128]{1,0:T(8,128)S(1)}, u32[]{:S(2)}, u32[]{:S(2)}) %collective-permute-start.2) | collective-permute-done | bytes 53280 | tf_op jit(solution)/shard_map/ppermute | solution.py:318
  13.9 0.5 collective-permute-done.1
  14.4 3.7 %collective-permute-start.6 = (f32[104,128]{1,0:T(8,128)S(1)}, f32[104,128]{1,0:T(8,128)S(1)}, u32[]{:S(2)}, u32[]{:S(2)}) collective-permute-start(f32[104,128]{1,0:T(8,128)S(1)} %add_add_fusion.3._), channel_id=1, source_target_pairs={{0,3},{1,2},{2,1},{3,0},{4,7},{5,6},{6,5},{7,4},{8,11},{9,10},{10,... | collective-permute-start | bytes 159752 | tf_op jit(solution)/shard_map/ppermute | solution.py:318
  18.1 0.8 %collective-permute-start.4 = (f32[104,128]{1,0:T(8,128)S(1)}, f32[104,128]{1,0:T(8,128)S(1)}, u32[]{:S(2)}, u32[]{:S(2)}) collective-permute-start(f32[104,128]{1,0:T(8,128)S(1)} %add_add_fusion.3._), channel_id=1, source_target_pairs={{0,1},{1,0},{2,3},{3,2},{4,5},{5,4},{6,7},{7,6},{8,9},{9,8},{10,11... | collective-permute-start | bytes 159752 | tf_op jit(solution)/shard_map/ppermute | solution.py:318
  18.9 2.8 %relay_right.1 = (bf16[16,256,256]{2,1,0:T(8,128)(2,1)S(1)}, bf16[16,256,256]{2,1,0:T(8,128)(2,1)S(1)}, f32[8,128]{1,0:T(8,128)S(1)}) custom-call(f32[4096,256]{1,0:T(8,128)} %bitcast.12, f32[104,128]{1,0:T(8,128)S(1)} %add_add_fusion.3._), custom_call_target="tpu_custom_call" | custom-call | bytes 8388608 | tf_op jit(solution)/shard_map/relay_right/pallas_call | solution.py:359
  21.7 1.4 %collective-permute-done.5 = f32[104,128]{1,0:T(8,128)S(1)} collective-permute-done((f32[104,128]{1,0:T(8,128)S(1)}, f32[104,128]{1,0:T(8,128)S(1)}, u32[]{:S(2)}, u32[]{:S(2)}) %collective-permute-start.5) | collective-permute-done | bytes 53280 | tf_op jit(solution)/shard_map/ppermute | solution.py:318
  23.2 1.2 %collective-permute-done.7.refs_1_ = f32[104,128]{1,0:T(8,128)S(1)} collective-permute-done((f32[104,128]{1,0:T(8,128)S(1)}, f32[104,128]{1,0:T(8,128)S(1)}, u32[]{:S(2)}, u32[]{:S(2)}) %collective-permute-start.7) | collective-permute-done | bytes 53280 | tf_op jit(solution)/shard_map/ppermute | solution.py:318
  24.5 5.2 %factor_absorb.1 = (f32[16,128,256]{2,1,0:T(8,128)S(1)}, f32[128,128]{1,0:T(8,128)S(1)}, f32[136,128]{1,0:T(8,128)S(1)}, f32[136,128]{1,0:T(8,128)S(1)}) custom-call(f32[104,128]{1,0:T(8,128)S(1)} %add_add_fusion.2.refs_0_, f32[104,128]{1,0:T(8,128)S(1)} %collective-permute-done.7.refs_1_, bf16[16,256,256]{2,1,0:T(8,128)(2,1)S(1)} %get-tuple-element.19.refs_2_, ...), custom_call_target="tpu_custom_call" | custom-call | tf_op jit(solution)/shard_map/factor_absorb/pallas_call | solution.py:450
  30.0 1.1 %collective-permute-done.8 = f32[136,128]{1,0:T(8,128)S(1)} collective-permute-done((f32[136,128]{1,0:T(8,128)S(1)}, f32[136,128]{1,0:T(8,128)S(1)}, u32[]{:S(2)}, u32[]{:S(2)}) %collective-permute-start.8) | collective-permute-done | bytes 69664 | tf_op jit(solution)/shard_map/ppermute | solution.py:318
  31.0 1.6 %collective-permute-start.11 = (f32[136,128]{1,0:T(8,128)S(1)}, f32[136,128]{1,0:T(8,128)S(1)}, u32[]{:S(2)}, u32[]{:S(2)}) collective-permute-start(f32[136,128]{1,0:T(8,128)S(1)} %add.82._), channel_id=1, source_target_pairs={{0,24},{4,28},{8,16},{12,20},{16,8},{20,12},{24,0},{28,4},{1,25},{... | collective-permute-start | bytes 208904 | tf_op jit(solution)/shard_map/ppermute | solution.py:318
  33.1 1.5 %collective-permute-start.9 = (f32[136,128]{1,0:T(8,128)S(1)}, f32[136,128]{1,0:T(8,128)S(1)}, u32[]{:S(2)}, u32[]{:S(2)}) collective-permute-start(f32[136,128]{1,0:T(8,128)S(1)} %add.82._), channel_id=1, source_target_pairs={{0,8},{4,12},{8,0},{12,4},{16,24},{20,28},{24,16},{28,20},{1,9},{5... | collective-permute-start | bytes 208904 | tf_op jit(solution)/shard_map/ppermute | solution.py:318
  34.6 2.5 %right_out.1 = (f32[2048,256]{1,0:T(8,128)}, f32[8,128]{1,0:T(8,128)S(1)}) custom-call(f32[16,128,256]{2,1,0:T(8,128)S(1)} %get-tuple-element.24.absorbed_ref, f32[136,128]{1,0:T(8,128)S(1)} %add.82._), custom_call_target="tpu_custom_call" | custom-call | bytes 8388608 | tf_op jit(solution)/shard_map/right_out/pallas_call | solution.py:400
  37.1 0.7 %collective-permute-done.9 = f32[136,128]{1,0:T(8,128)S(1)} collective-permute-done((f32[136,128]{1,0:T(8,128)S(1)}, f32[136,128]{1,0:T(8,128)S(1)}, u32[]{:S(2)}, u32[]{:S(2)}) %collective-permute-start.9) | collective-permute-done | bytes 69664 | tf_op jit(solution)/shard_map/ppermute | solution.py:318
  37.8 2.3 %collective-permute-start.14 = (f32[136,128]{1,0:T(8,128)S(1)}, f32[136,128]{1,0:T(8,128)S(1)}, u32[]{:S(2)}, u32[]{:S(2)}) collective-permute-start(f32[136,128]{1,0:T(8,128)S(1)} %add_add_fusion.1._), channel_id=1, source_target_pairs={{0,3},{1,2},{2,1},{3,0},{4,7},{5,6},{6,5},{7,4},{8,11},{9,10},{10,... | collective-permute-start | bytes 208904 | tf_op jit(solution)/shard_map/ppermute | solution.py:318
  40.1 2.2 %collective-permute-start.12 = (f32[136,128]{1,0:T(8,128)S(1)}, f32[136,128]{1,0:T(8,128)S(1)}, u32[]{:S(2)}, u32[]{:S(2)}) collective-permute-start(f32[136,128]{1,0:T(8,128)S(1)} %add_add_fusion.1._), channel_id=1, source_target_pairs={{0,1},{1,0},{2,3},{3,2},{4,5},{5,4},{6,7},{7,6},{8,9},{9,8},{10,11... | collective-permute-start | bytes 208904 | tf_op jit(solution)/shard_map/ppermute | solution.py:318
  42.2 2.8 %left_out.1 = (f32[4096,128]{1,0:T(8,128)}, f32[8,128]{1,0:T(8,128)S(1)}) custom-call(f32[4096,256]{1,0:T(8,128)S(1)} %bitcast.11, f32[128,128]{1,0:T(8,128)S(1)} %get-tuple-element.21.linv_ref, f32[136,128]{1,0:T(8,128)S(1)} %add_add_fusion.1._), custom_call_target="tpu_custom_call" | custom-call | bytes 8388608 | tf_op jit(solution)/shard_map/left_out/pallas_call | solution.py:378
  45.1 1.5 %collective-permute-done.13 = f32[136,128]{1,0:T(8,128)S(1)} collective-permute-done((f32[136,128]{1,0:T(8,128)S(1)}, f32[136,128]{1,0:T(8,128)S(1)}, u32[]{:S(2)}, u32[]{:S(2)}) %collective-permute-start.13) | collective-permute-done | bytes 69664 | tf_op jit(solution)/shard_map/ppermute | solution.py:318
  46.8 1.2 %collective-permute-done.15.refs_1_ = f32[136,128]{1,0:T(8,128)S(1)} collective-permute-done((f32[136,128]{1,0:T(8,128)S(1)}, f32[136,128]{1,0:T(8,128)S(1)}, u32[]{:S(2)}, u32[]{:S(2)}) %collective-permute-start.15) | collective-permute-done | bytes 69664 | tf_op jit(solution)/shard_map/ppermute | solution.py:318
  48.0 8.3 %factor_next.1 = f32[256,256]{1,0:T(8,128)} custom-call(f32[136,128]{1,0:T(8,128)S(1)} %add_add_fusion.refs_0_, f32[136,128]{1,0:T(8,128)S(1)} %collective-permute-done.15.refs_1_), custom_call_target="tpu_custom_call" | custom-call | tf_op jit(solution)/shard_map/factor_next/pallas_call | solution.py:472
  (25 shorter events, 1.7 us)
Async XLA Ops:
  4.5 1.4 %collective-permute-start = (f32[104,128]{1,0:T(8,128)S(1)}, f32[104,128]{1,0:T(8,128)S(1)}, u32[]{:S(2)}, u32[]{:S(2)}) collective-permute-start(f32[104,128]{1,0:T(8,128)S(1)} %get-tuple-element.17), channel_id=1, source_target_pairs={{0,4},{4,0},{8,12},{12,8},{16,20},{20,16},{24,28},{28,24},{1,5},{5... | collective-permute-start | bytes 159752 | tf_op jit(solution)/shard_map/ppermute | solution.py:318
  5.9 6.0 %collective-permute-start.3 = (f32[104,128]{1,0:T(8,128)S(1)}, f32[104,128]{1,0:T(8,128)S(1)}, u32[]{:S(2)}, u32[]{:S(2)}) collective-permute-start(f32[104,128]{1,0:T(8,128)S(1)} %add.72), channel_id=1, source_target_pairs={{0,24},{4,28},{8,16},{12,20},{16,8},{20,12},{24,0},{28,4},{1,25},{... | collective-permute-start | bytes 159752 | tf_op jit(solution)/shard_map/ppermute | solution.py:318
  9.7 4.1 %collective-permute-start.2 = (f32[104,128]{1,0:T(8,128)S(1)}, f32[104,128]{1,0:T(8,128)S(1)}, u32[]{:S(2)}, u32[]{:S(2)}) collective-permute-start(f32[104,128]{1,0:T(8,128)S(1)} %add.72), channel_id=1, source_target_pairs={{0,16},{4,20},{8,24},{12,28},{16,0},{20,4},{24,8},{28,12},{1,17},{... | collective-permute-start | bytes 159752 | tf_op jit(solution)/shard_map/ppermute | solution.py:318
  10.3 4.1 %collective-permute-start.1 = (f32[104,128]{1,0:T(8,128)S(1)}, f32[104,128]{1,0:T(8,128)S(1)}, u32[]{:S(2)}, u32[]{:S(2)}) collective-permute-start(f32[104,128]{1,0:T(8,128)S(1)} %add.72), channel_id=1, source_target_pairs={{0,8},{4,12},{8,0},{12,4},{16,24},{20,28},{24,16},{28,20},{1,9},{5... | collective-permute-start | bytes 159752 | tf_op jit(solution)/shard_map/ppermute | solution.py:318
  14.4 7.3 %collective-permute-start.6 = (f32[104,128]{1,0:T(8,128)S(1)}, f32[104,128]{1,0:T(8,128)S(1)}, u32[]{:S(2)}, u32[]{:S(2)}) collective-permute-start(f32[104,128]{1,0:T(8,128)S(1)} %add_add_fusion.3._), channel_id=1, source_target_pairs={{0,3},{1,2},{2,1},{3,0},{4,7},{5,6},{6,5},{7,4},{8,11},{9,10},{10,... | collective-permute-start | bytes 159752 | tf_op jit(solution)/shard_map/ppermute | solution.py:318
  18.1 5.0 %collective-permute-start.5 = (f32[104,128]{1,0:T(8,128)S(1)}, f32[104,128]{1,0:T(8,128)S(1)}, u32[]{:S(2)}, u32[]{:S(2)}) collective-permute-start(f32[104,128]{1,0:T(8,128)S(1)} %add_add_fusion.3._), channel_id=1, source_target_pairs={{0,2},{1,3},{2,0},{3,1},{4,6},{5,7},{6,4},{7,5},{8,10},{9,11},{10,... | collective-permute-start | bytes 159752 | tf_op jit(solution)/shard_map/ppermute | solution.py:318
  18.1 5.0 %collective-permute-start.4 = (f32[104,128]{1,0:T(8,128)S(1)}, f32[104,128]{1,0:T(8,128)S(1)}, u32[]{:S(2)}, u32[]{:S(2)}) collective-permute-start(f32[104,128]{1,0:T(8,128)S(1)} %add_add_fusion.3._), channel_id=1, source_target_pairs={{0,1},{1,0},{2,3},{3,2},{4,5},{5,4},{6,7},{7,6},{8,9},{9,8},{10,11... | collective-permute-start | bytes 159752 | tf_op jit(solution)/shard_map/ppermute | solution.py:318
  23.2 1.3 %collective-permute-start.7 = (f32[104,128]{1,0:T(8,128)S(1)}, f32[104,128]{1,0:T(8,128)S(1)}, u32[]{:S(2)}, u32[]{:S(2)}) collective-permute-start(f32[104,128]{1,0:T(8,128)S(1)} %add_add_fusion.2.refs_0_), channel_id=1, source_target_pairs={{0,4},{4,0},{8,12},{12,8},{16,20},{20,16},{24,28},{28,24},{1,5},{5... | collective-permute-start | bytes 159752 | tf_op jit(solution)/shard_map/ppermute | solution.py:318
  24.5 17.8 %copy-start = (f32[256,16,256]{2,1,0:T(8,128)S(1)}, f32[256,16,256]{2,1,0:T(8,128)}, u32[]{:S(2)}) copy-start(f32[256,16,256]{2,1,0:T(8,128)} %param.2) | copy-start | bytes 12582916
  29.7 1.3 %collective-permute-start.8 = (f32[136,128]{1,0:T(8,128)S(1)}, f32[136,128]{1,0:T(8,128)S(1)}, u32[]{:S(2)}, u32[]{:S(2)}) collective-permute-start(f32[136,128]{1,0:T(8,128)S(1)} %get-tuple-element.23), channel_id=1, source_target_pairs={{0,4},{4,0},{8,12},{12,8},{16,20},{20,16},{24,28},{28,24},{1,5},{5... | collective-permute-start | bytes 208904 | tf_op jit(solution)/shard_map/ppermute | solution.py:318
  31.0 6.1 %collective-permute-start.11 = (f32[136,128]{1,0:T(8,128)S(1)}, f32[136,128]{1,0:T(8,128)S(1)}, u32[]{:S(2)}, u32[]{:S(2)}) collective-permute-start(f32[136,128]{1,0:T(8,128)S(1)} %add.82._), channel_id=1, source_target_pairs={{0,24},{4,28},{8,16},{12,20},{16,8},{20,12},{24,0},{28,4},{1,25},{... | collective-permute-start | bytes 208904 | tf_op jit(solution)/shard_map/ppermute | solution.py:318
  32.6 4.5 %collective-permute-start.10 = (f32[136,128]{1,0:T(8,128)S(1)}, f32[136,128]{1,0:T(8,128)S(1)}, u32[]{:S(2)}, u32[]{:S(2)}) collective-permute-start(f32[136,128]{1,0:T(8,128)S(1)} %add.82._), channel_id=1, source_target_pairs={{0,16},{4,20},{8,24},{12,28},{16,0},{20,4},{24,8},{28,12},{1,17},{... | collective-permute-start | bytes 208904 | tf_op jit(solution)/shard_map/ppermute | solution.py:318
  33.1 4.7 %collective-permute-start.9 = (f32[136,128]{1,0:T(8,128)S(1)}, f32[136,128]{1,0:T(8,128)S(1)}, u32[]{:S(2)}, u32[]{:S(2)}) collective-permute-start(f32[136,128]{1,0:T(8,128)S(1)} %add.82._), channel_id=1, source_target_pairs={{0,8},{4,12},{8,0},{12,4},{16,24},{20,28},{24,16},{28,20},{1,9},{5... | collective-permute-start | bytes 208904 | tf_op jit(solution)/shard_map/ppermute | solution.py:318
  37.8 7.3 %collective-permute-start.14 = (f32[136,128]{1,0:T(8,128)S(1)}, f32[136,128]{1,0:T(8,128)S(1)}, u32[]{:S(2)}, u32[]{:S(2)}) collective-permute-start(f32[136,128]{1,0:T(8,128)S(1)} %add_add_fusion.1._), channel_id=1, source_target_pairs={{0,3},{1,2},{2,1},{3,0},{4,7},{5,6},{6,5},{7,4},{8,11},{9,10},{10,... | collective-permute-start | bytes 208904 | tf_op jit(solution)/shard_map/ppermute | solution.py:318
  40.1 6.6 %collective-permute-start.13 = (f32[136,128]{1,0:T(8,128)S(1)}, f32[136,128]{1,0:T(8,128)S(1)}, u32[]{:S(2)}, u32[]{:S(2)}) collective-permute-start(f32[136,128]{1,0:T(8,128)S(1)} %add_add_fusion.1._), channel_id=1, source_target_pairs={{0,2},{1,3},{2,0},{3,1},{4,6},{5,7},{6,4},{7,5},{8,10},{9,11},{10,... | collective-permute-start | bytes 208904 | tf_op jit(solution)/shard_map/ppermute | solution.py:318
  40.1 6.6 %collective-permute-start.12 = (f32[136,128]{1,0:T(8,128)S(1)}, f32[136,128]{1,0:T(8,128)S(1)}, u32[]{:S(2)}, u32[]{:S(2)}) collective-permute-start(f32[136,128]{1,0:T(8,128)S(1)} %add_add_fusion.1._), channel_id=1, source_target_pairs={{0,1},{1,0},{2,3},{3,2},{4,5},{5,4},{6,7},{7,6},{8,9},{9,8},{10,11... | collective-permute-start | bytes 208904 | tf_op jit(solution)/shard_map/ppermute | solution.py:318
  46.7 1.3 %collective-permute-start.15 = (f32[136,128]{1,0:T(8,128)S(1)}, f32[136,128]{1,0:T(8,128)S(1)}, u32[]{:S(2)}, u32[]{:S(2)}) collective-permute-start(f32[136,128]{1,0:T(8,128)S(1)} %add_add_fusion.refs_0_), channel_id=1, source_target_pairs={{0,4},{4,0},{8,12},{12,8},{16,20},{20,16},{24,28},{28,24},{1,5},{5... | collective-permute-start | bytes 208904 | tf_op jit(solution)/shard_map/ppermute | solution.py:318

commit v10 on v8

--- a/solution.py
+++ b/solution.py
@@ -72,16 +72,21 @@
             ahead = [jnp.broadcast_to(turned[:, k : k + 1], (PANEL, LANES)) for k in range(PANEL)]
         scale = jnp.zeros((PANEL, LANES), F32)
         pivot = spread_row(columns[0], 0)
+        partial_pivot = spread_row(columns[1], 1)
+        beneath = spread_row(columns[0], 1)
         for k in range(PANEL):
             inverse = pl.reciprocal(pivot, approx=True)
             scale = jnp.where(row_id == k, lax.rsqrt(pivot), scale)
             multiples = columns[k] * inverse
             if follows:
                 ahead_multiples = ahead[k] * inverse
-            for m in range(k + 1, PANEL):
-                entry = spread_row(columns[k], m)
-                if m == k + 1:
-                    pivot = spread_row(columns[m], m) - (entry * inverse) * entry
+            entries = {m: spread_row(columns[k], m) for m in range(k + 1, PANEL)}
+            pivot = partial_pivot - (beneath * inverse) * beneath
+            if k + 2 < PANEL:
+                second = entries[k + 2] * inverse
+                beneath = spread_row(columns[k + 1], k + 2) - second * entries[k + 1]
+                partial_pivot = spread_row(columns[k + 2], k + 2) - second * entries[k + 2]
+            for m, entry in entries.items():
                 columns[m] = columns[m] - multiples * entry
                 if follows:
                     ahead[m] = ahead[m] - ahead_multiples * entry
@@ -138,7 +143,7 @@
         )
 
     for i in range(steps):
-        copy(i).start()
+        copy(i).start(priority=i % 2)
     return copy
 
 
@@ -146,15 +151,11 @@
     outs = refs[:SPREAD_ONE]
     a_ref, total_ref, tall_ref, sems = refs[SPREAD_ONE:]
     copy = chunk_copies(a_hbm, a_ref, sems)
-    total_ref[...] = jnp.zeros_like(total_ref)
-
-    def body(i, carry):
+    for i in range(a_ref.shape[0]):
         copy(i).wait()
         hi, lo = split(a_ref[i])
-        total_ref[...] += dot_tn(hi, jnp.concatenate([hi, lo], axis=1))
-        return carry
-
-    lax.fori_loop(0, a_ref.shape[0], body, 0)
+        part = dot_tn(hi, jnp.concatenate([hi, lo], axis=1))
+        total_ref[...] = part if i == 0 else total_ref[...] + part
     width = a_ref.shape[2]
     cross = total_ref[:, width : width + RK]
     first = total_ref[:RK, :RK] + total_ref[:RK, width : width + RK] + cross[:RK, :].T

time: 54.9 us -> 54.8 us (level)
  no operation moved by 1% of the time
where the time goes in v10:
time: 54.8 us; the launch traced here: 54.6 us
  Pallas kernels  23.9 us (44%)
  starting transfers between devices  17.9 us (33%)
  waiting for transfers between devices  12.1 us (22%)
  between operations  0.71 us (1%)
    ppermute x16, starting transfers between devices, swap(): return lax.ppermute(value, axes, [(i, i ^ mask) for i in range(size)])  17.9 us
    ppermute x16, waiting for transfers between devices, swap(): return lax.ppermute(value, axes, [(i, i ^ mask) for i in range(size)])  12.1 us
    pallas_call x1, Pallas kernels, per_device(): pl.pallas_call(functools.partial(factor_kernel, 1.0 / (RK * total_points)...  6.45 us
    pallas_call x1, Pallas kernels, per_device(): pl.pallas_call(functools.partial(absorb_kernel, math.sqrt(rank_left * tot...  5.14 us
    pallas_call x1, Pallas kernels, per_device(): pl.pallas_call(gram_kernel, in_specs=[pl.BlockSpec(memory_space=pl.ANY)],...  4.14 us
    pallas_call x1, Pallas kernels, left_part(): pl.pallas_call(left_kernel, grid=(steps,), in_specs=[pl.BlockSpec((chunk,...  2.83 us
    pallas_call x1, Pallas kernels, relay_part(): pl.pallas_call(functools.partial(relay_kernel, points), in_specs=[pl.Bloc...  2.8 us
    pallas_call x1, Pallas kernels, right_part(): pl.pallas_call(functools.partial(right_kernel, points), grid=(steps, 2),...  2.49 us
  transfers between devices with their start and end apart: 16, of which 10 were waited for; matrix products, arithmetic and copies ran while one was open for 0% of the time, Pallas kernels for 15%

profile of v10, /device:TPU:0, one launch (start us, length us, event | category | flops | bytes accessed | tf_op | source)
XLA Modules:
  0.0 54.6 jit_solution(7970978663457131827)
XLA Ops:
  0.6 4.1 %gram_top.1 = (f32[104,128]{1,0:T(8,128)S(1)}, f32[104,128]{1,0:T(8,128)S(1)}) custom-call(f32[4096,256]{1,0:T(8,128)} %bitcast.10), custom_call_target="tpu_custom_call" | custom-call | tf_op jit(solution)/shard_map/gram_top/pallas_call | solution.py:415
  5.3 0.9 %collective-permute-done = f32[104,128]{1,0:T(8,128)S(1)} collective-permute-done((f32[104,128]{1,0:T(8,128)S(1)}, f32[104,128]{1,0:T(8,128)S(1)}, u32[]{:S(2)}, u32[]{:S(2)}) %collective-permute-start) | collective-permute-done | bytes 53280 | tf_op jit(solution)/shard_map/ppermute | solution.py:305
  6.2 3.9 %collective-permute-start.3 = (f32[104,128]{1,0:T(8,128)S(1)}, f32[104,128]{1,0:T(8,128)S(1)}, u32[]{:S(2)}, u32[]{:S(2)}) collective-permute-start(f32[104,128]{1,0:T(8,128)S(1)} %add.72), channel_id=1, source_target_pairs={{0,24},{4,28},{8,16},{12,20},{16,8},{20,12},{24,0},{28,4},{1,25},{... | collective-permute-start | bytes 159752 | tf_op jit(solution)/shard_map/ppermute | solution.py:305
  10.1 0.5 collective-permute-start.2
  10.7 1.5 %collective-permute-done.3 = f32[104,128]{1,0:T(8,128)S(1)} collective-permute-done((f32[104,128]{1,0:T(8,128)S(1)}, f32[104,128]{1,0:T(8,128)S(1)}, u32[]{:S(2)}, u32[]{:S(2)}) %collective-permute-start.3) | collective-permute-done | bytes 53280 | tf_op jit(solution)/shard_map/ppermute | solution.py:305
  12.2 2.0 %collective-permute-done.2 = f32[104,128]{1,0:T(8,128)S(1)} collective-permute-done((f32[104,128]{1,0:T(8,128)S(1)}, f32[104,128]{1,0:T(8,128)S(1)}, u32[]{:S(2)}, u32[]{:S(2)}) %collective-permute-start.2) | collective-permute-done | bytes 53280 | tf_op jit(solution)/shard_map/ppermute | solution.py:305
  14.2 0.5 collective-permute-done.1
  14.7 3.7 %collective-permute-start.6 = (f32[104,128]{1,0:T(8,128)S(1)}, f32[104,128]{1,0:T(8,128)S(1)}, u32[]{:S(2)}, u32[]{:S(2)}) collective-permute-start(f32[104,128]{1,0:T(8,128)S(1)} %add_add_fusion.3._), channel_id=1, source_target_pairs={{0,3},{1,2},{2,1},{3,0},{4,7},{5,6},{6,5},{7,4},{8,11},{9,10},{10,... | collective-permute-start | bytes 159752 | tf_op jit(solution)/shard_map/ppermute | solution.py:305
  18.4 0.8 %collective-permute-start.4 = (f32[104,128]{1,0:T(8,128)S(1)}, f32[104,128]{1,0:T(8,128)S(1)}, u32[]{:S(2)}, u32[]{:S(2)}) collective-permute-start(f32[104,128]{1,0:T(8,128)S(1)} %add_add_fusion.3._), channel_id=1, source_target_pairs={{0,1},{1,0},{2,3},{3,2},{4,5},{5,4},{6,7},{7,6},{8,9},{9,8},{10,11... | collective-permute-start | bytes 159752 | tf_op jit(solution)/shard_map/ppermute | solution.py:305
  19.2 2.8 %relay_right.1 = (bf16[16,256,256]{2,1,0:T(8,128)(2,1)S(1)}, bf16[16,256,256]{2,1,0:T(8,128)(2,1)S(1)}, f32[8,128]{1,0:T(8,128)S(1)}) custom-call(f32[4096,256]{1,0:T(8,128)} %bitcast.12, f32[104,128]{1,0:T(8,128)S(1)} %add_add_fusion.3._), custom_call_target="tpu_custom_call" | custom-call | bytes 8388608 | tf_op jit(solution)/shard_map/relay_right/pallas_call | solution.py:346
  22.0 1.4 %collective-permute-done.5 = f32[104,128]{1,0:T(8,128)S(1)} collective-permute-done((f32[104,128]{1,0:T(8,128)S(1)}, f32[104,128]{1,0:T(8,128)S(1)}, u32[]{:S(2)}, u32[]{:S(2)}) %collective-permute-start.5) | collective-permute-done | bytes 53280 | tf_op jit(solution)/shard_map/ppermute | solution.py:305
  23.5 1.2 %collective-permute-done.7.refs_1_ = f32[104,128]{1,0:T(8,128)S(1)} collective-permute-done((f32[104,128]{1,0:T(8,128)S(1)}, f32[104,128]{1,0:T(8,128)S(1)}, u32[]{:S(2)}, u32[]{:S(2)}) %collective-permute-start.7) | collective-permute-done | bytes 53280 | tf_op jit(solution)/shard_map/ppermute | solution.py:305
  24.8 5.1 %factor_absorb.1 = (f32[16,128,256]{2,1,0:T(8,128)S(1)}, f32[128,128]{1,0:T(8,128)S(1)}, f32[136,128]{1,0:T(8,128)S(1)}, f32[136,128]{1,0:T(8,128)S(1)}) custom-call(f32[104,128]{1,0:T(8,128)S(1)} %add_add_fusion.2.refs_0_, f32[104,128]{1,0:T(8,128)S(1)} %collective-permute-done.7.refs_1_, bf16[16,256,256]{2,1,0:T(8,128)(2,1)S(1)} %get-tuple-element.19.refs_2_, ...), custom_call_target="tpu_custom_call" | custom-call | tf_op jit(solution)/shard_map/factor_absorb/pallas_call | solution.py:437
  30.2 1.1 %collective-permute-done.8 = f32[136,128]{1,0:T(8,128)S(1)} collective-permute-done((f32[136,128]{1,0:T(8,128)S(1)}, f32[136,128]{1,0:T(8,128)S(1)}, u32[]{:S(2)}, u32[]{:S(2)}) %collective-permute-start.8) | collective-permute-done | bytes 69664 | tf_op jit(solution)/shard_map/ppermute | solution.py:305
  31.3 1.6 %collective-permute-start.11 = (f32[136,128]{1,0:T(8,128)S(1)}, f32[136,128]{1,0:T(8,128)S(1)}, u32[]{:S(2)}, u32[]{:S(2)}) collective-permute-start(f32[136,128]{1,0:T(8,128)S(1)} %add.82._), channel_id=1, source_target_pairs={{0,24},{4,28},{8,16},{12,20},{16,8},{20,12},{24,0},{28,4},{1,25},{... | collective-permute-start | bytes 208904 | tf_op jit(solution)/shard_map/ppermute | solution.py:305
  33.3 1.5 %collective-permute-start.9 = (f32[136,128]{1,0:T(8,128)S(1)}, f32[136,128]{1,0:T(8,128)S(1)}, u32[]{:S(2)}, u32[]{:S(2)}) collective-permute-start(f32[136,128]{1,0:T(8,128)S(1)} %add.82._), channel_id=1, source_target_pairs={{0,8},{4,12},{8,0},{12,4},{16,24},{20,28},{24,16},{28,20},{1,9},{5... | collective-permute-start | bytes 208904 | tf_op jit(solution)/shard_map/ppermute | solution.py:305
  34.8 2.5 %right_out.1 = (f32[2048,256]{1,0:T(8,128)}, f32[8,128]{1,0:T(8,128)S(1)}) custom-call(f32[16,128,256]{2,1,0:T(8,128)S(1)} %get-tuple-element.24.absorbed_ref, f32[136,128]{1,0:T(8,128)S(1)} %add.82._), custom_call_target="tpu_custom_call" | custom-call | bytes 8388608 | tf_op jit(solution)/shard_map/right_out/pallas_call | solution.py:387
  37.3 0.7 %collective-permute-done.9 = f32[136,128]{1,0:T(8,128)S(1)} collective-permute-done((f32[136,128]{1,0:T(8,128)S(1)}, f32[136,128]{1,0:T(8,128)S(1)}, u32[]{:S(2)}, u32[]{:S(2)}) %collective-permute-start.9) | collective-permute-done | bytes 69664 | tf_op jit(solution)/shard_map/ppermute | solution.py:305
  38.0 2.3 %collective-permute-start.14 = (f32[136,128]{1,0:T(8,128)S(1)}, f32[136,128]{1,0:T(8,128)S(1)}, u32[]{:S(2)}, u32[]{:S(2)}) collective-permute-start(f32[136,128]{1,0:T(8,128)S(1)} %add_add_fusion.1._), channel_id=1, source_target_pairs={{0,3},{1,2},{2,1},{3,0},{4,7},{5,6},{6,5},{7,4},{8,11},{9,10},{10,... | collective-permute-start | bytes 208904 | tf_op jit(solution)/shard_map/ppermute | solution.py:305
  40.3 2.2 %collective-permute-start.12 = (f32[136,128]{1,0:T(8,128)S(1)}, f32[136,128]{1,0:T(8,128)S(1)}, u32[]{:S(2)}, u32[]{:S(2)}) collective-permute-start(f32[136,128]{1,0:T(8,128)S(1)} %add_add_fusion.1._), channel_id=1, source_target_pairs={{0,1},{1,0},{2,3},{3,2},{4,5},{5,4},{6,7},{7,6},{8,9},{9,8},{10,11... | collective-permute-start | bytes 208904 | tf_op jit(solution)/shard_map/ppermute | solution.py:305
  42.4 2.8 %left_out.1 = (f32[4096,128]{1,0:T(8,128)}, f32[8,128]{1,0:T(8,128)S(1)}) custom-call(f32[4096,256]{1,0:T(8,128)S(1)} %bitcast.11, f32[128,128]{1,0:T(8,128)S(1)} %get-tuple-element.21.linv_ref, f32[136,128]{1,0:T(8,128)S(1)} %add_add_fusion.1._), custom_call_target="tpu_custom_call" | custom-call | bytes 8388608 | tf_op jit(solution)/shard_map/left_out/pallas_call | solution.py:365
  45.3 1.6 %collective-permute-done.13 = f32[136,128]{1,0:T(8,128)S(1)} collective-permute-done((f32[136,128]{1,0:T(8,128)S(1)}, f32[136,128]{1,0:T(8,128)S(1)}, u32[]{:S(2)}, u32[]{:S(2)}) %collective-permute-start.13) | collective-permute-done | bytes 69664 | tf_op jit(solution)/shard_map/ppermute | solution.py:305
  47.0 1.2 %collective-permute-done.15.refs_1_ = f32[136,128]{1,0:T(8,128)S(1)} collective-permute-done((f32[136,128]{1,0:T(8,128)S(1)}, f32[136,128]{1,0:T(8,128)S(1)}, u32[]{:S(2)}, u32[]{:S(2)}) %collective-permute-start.15) | collective-permute-done | bytes 69664 | tf_op jit(solution)/shard_map/ppermute | solution.py:305
  48.2 6.4 %factor_next.1 = f32[256,256]{1,0:T(8,128)} custom-call(f32[136,128]{1,0:T(8,128)S(1)} %add_add_fusion.refs_0_, f32[136,128]{1,0:T(8,128)S(1)} %collective-permute-done.15.refs_1_), custom_call_target="tpu_custom_call" | custom-call | tf_op jit(solution)/shard_map/factor_next/pallas_call | solution.py:459
  (25 shorter events, 1.6 us)
Async XLA Ops:
  4.8 1.4 %collective-permute-start = (f32[104,128]{1,0:T(8,128)S(1)}, f32[104,128]{1,0:T(8,128)S(1)}, u32[]{:S(2)}, u32[]{:S(2)}) collective-permute-start(f32[104,128]{1,0:T(8,128)S(1)} %get-tuple-element.17), channel_id=1, source_target_pairs={{0,4},{4,0},{8,12},{12,8},{16,20},{20,16},{24,28},{28,24},{1,5},{5... | collective-permute-start | bytes 159752 | tf_op jit(solution)/shard_map/ppermute | solution.py:305
  6.2 6.0 %collective-permute-start.3 = (f32[104,128]{1,0:T(8,128)S(1)}, f32[104,128]{1,0:T(8,128)S(1)}, u32[]{:S(2)}, u32[]{:S(2)}) collective-permute-start(f32[104,128]{1,0:T(8,128)S(1)} %add.72), channel_id=1, source_target_pairs={{0,24},{4,28},{8,16},{12,20},{16,8},{20,12},{24,0},{28,4},{1,25},{... | collective-permute-start | bytes 159752 | tf_op jit(solution)/shard_map/ppermute | solution.py:305
  10.1 4.1 %collective-permute-start.2 = (f32[104,128]{1,0:T(8,128)S(1)}, f32[104,128]{1,0:T(8,128)S(1)}, u32[]{:S(2)}, u32[]{:S(2)}) collective-permute-start(f32[104,128]{1,0:T(8,128)S(1)} %add.72), channel_id=1, source_target_pairs={{0,16},{4,20},{8,24},{12,28},{16,0},{20,4},{24,8},{28,12},{1,17},{... | collective-permute-start | bytes 159752 | tf_op jit(solution)/shard_map/ppermute | solution.py:305
  10.6 4.1 %collective-permute-start.1 = (f32[104,128]{1,0:T(8,128)S(1)}, f32[104,128]{1,0:T(8,128)S(1)}, u32[]{:S(2)}, u32[]{:S(2)}) collective-permute-start(f32[104,128]{1,0:T(8,128)S(1)} %add.72), channel_id=1, source_target_pairs={{0,8},{4,12},{8,0},{12,4},{16,24},{20,28},{24,16},{28,20},{1,9},{5... | collective-permute-start | bytes 159752 | tf_op jit(solution)/shard_map/ppermute | solution.py:305
  14.7 7.3 %collective-permute-start.6 = (f32[104,128]{1,0:T(8,128)S(1)}, f32[104,128]{1,0:T(8,128)S(1)}, u32[]{:S(2)}, u32[]{:S(2)}) collective-permute-start(f32[104,128]{1,0:T(8,128)S(1)} %add_add_fusion.3._), channel_id=1, source_target_pairs={{0,3},{1,2},{2,1},{3,0},{4,7},{5,6},{6,5},{7,4},{8,11},{9,10},{10,... | collective-permute-start | bytes 159752 | tf_op jit(solution)/shard_map/ppermute | solution.py:305
  18.4 5.0 %collective-permute-start.5 = (f32[104,128]{1,0:T(8,128)S(1)}, f32[104,128]{1,0:T(8,128)S(1)}, u32[]{:S(2)}, u32[]{:S(2)}) collective-permute-start(f32[104,128]{1,0:T(8,128)S(1)} %add_add_fusion.3._), channel_id=1, source_target_pairs={{0,2},{1,3},{2,0},{3,1},{4,6},{5,7},{6,4},{7,5},{8,10},{9,11},{10,... | collective-permute-start | bytes 159752 | tf_op jit(solution)/shard_map/ppermute | solution.py:305
  18.4 5.0 %collective-permute-start.4 = (f32[104,128]{1,0:T(8,128)S(1)}, f32[104,128]{1,0:T(8,128)S(1)}, u32[]{:S(2)}, u32[]{:S(2)}) collective-permute-start(f32[104,128]{1,0:T(8,128)S(1)} %add_add_fusion.3._), channel_id=1, source_target_pairs={{0,1},{1,0},{2,3},{3,2},{4,5},{5,4},{6,7},{7,6},{8,9},{9,8},{10,11... | collective-permute-start | bytes 159752 | tf_op jit(solution)/shard_map/ppermute | solution.py:305
  23.5 1.3 %collective-permute-start.7 = (f32[104,128]{1,0:T(8,128)S(1)}, f32[104,128]{1,0:T(8,128)S(1)}, u32[]{:S(2)}, u32[]{:S(2)}) collective-permute-start(f32[104,128]{1,0:T(8,128)S(1)} %add_add_fusion.2.refs_0_), channel_id=1, source_target_pairs={{0,4},{4,0},{8,12},{12,8},{16,20},{20,16},{24,28},{28,24},{1,5},{5... | collective-permute-start | bytes 159752 | tf_op jit(solution)/shard_map/ppermute | solution.py:305
  24.8 17.7 %copy-start = (f32[256,16,256]{2,1,0:T(8,128)S(1)}, f32[256,16,256]{2,1,0:T(8,128)}, u32[]{:S(2)}) copy-start(f32[256,16,256]{2,1,0:T(8,128)} %param.2) | copy-start | bytes 12582916
  29.9 1.3 %collective-permute-start.8 = (f32[136,128]{1,0:T(8,128)S(1)}, f32[136,128]{1,0:T(8,128)S(1)}, u32[]{:S(2)}, u32[]{:S(2)}) collective-permute-start(f32[136,128]{1,0:T(8,128)S(1)} %get-tuple-element.23), channel_id=1, source_target_pairs={{0,4},{4,0},{8,12},{12,8},{16,20},{20,16},{24,28},{28,24},{1,5},{5... | collective-permute-start | bytes 208904 | tf_op jit(solution)/shard_map/ppermute | solution.py:305
  31.3 6.1 %collective-permute-start.11 = (f32[136,128]{1,0:T(8,128)S(1)}, f32[136,128]{1,0:T(8,128)S(1)}, u32[]{:S(2)}, u32[]{:S(2)}) collective-permute-start(f32[136,128]{1,0:T(8,128)S(1)} %add.82._), channel_id=1, source_target_pairs={{0,24},{4,28},{8,16},{12,20},{16,8},{20,12},{24,0},{28,4},{1,25},{... | collective-permute-start | bytes 208904 | tf_op jit(solution)/shard_map/ppermute | solution.py:305
  32.8 4.5 %collective-permute-start.10 = (f32[136,128]{1,0:T(8,128)S(1)}, f32[136,128]{1,0:T(8,128)S(1)}, u32[]{:S(2)}, u32[]{:S(2)}) collective-permute-start(f32[136,128]{1,0:T(8,128)S(1)} %add.82._), channel_id=1, source_target_pairs={{0,16},{4,20},{8,24},{12,28},{16,0},{20,4},{24,8},{28,12},{1,17},{... | collective-permute-start | bytes 208904 | tf_op jit(solution)/shard_map/ppermute | solution.py:305
  33.3 4.7 %collective-permute-start.9 = (f32[136,128]{1,0:T(8,128)S(1)}, f32[136,128]{1,0:T(8,128)S(1)}, u32[]{:S(2)}, u32[]{:S(2)}) collective-permute-start(f32[136,128]{1,0:T(8,128)S(1)} %add.82._), channel_id=1, source_target_pairs={{0,8},{4,12},{8,0},{12,4},{16,24},{20,28},{24,16},{28,20},{1,9},{5... | collective-permute-start | bytes 208904 | tf_op jit(solution)/shard_map/ppermute | solution.py:305
  38.0 7.3 %collective-permute-start.14 = (f32[136,128]{1,0:T(8,128)S(1)}, f32[136,128]{1,0:T(8,128)S(1)}, u32[]{:S(2)}, u32[]{:S(2)}) collective-permute-start(f32[136,128]{1,0:T(8,128)S(1)} %add_add_fusion.1._), channel_id=1, source_target_pairs={{0,3},{1,2},{2,1},{3,0},{4,7},{5,6},{6,5},{7,4},{8,11},{9,10},{10,... | collective-permute-start | bytes 208904 | tf_op jit(solution)/shard_map/ppermute | solution.py:305
  40.3 6.6 %collective-permute-start.13 = (f32[136,128]{1,0:T(8,128)S(1)}, f32[136,128]{1,0:T(8,128)S(1)}, u32[]{:S(2)}, u32[]{:S(2)}) collective-permute-start(f32[136,128]{1,0:T(8,128)S(1)} %add_add_fusion.1._), channel_id=1, source_target_pairs={{0,2},{1,3},{2,0},{3,1},{4,6},{5,7},{6,4},{7,5},{8,10},{9,11},{10,... | collective-permute-start | bytes 208904 | tf_op jit(solution)/shard_map/ppermute | solution.py:305
  40.3 6.6 %collective-permute-start.12 = (f32[136,128]{1,0:T(8,128)S(1)}, f32[136,128]{1,0:T(8,128)S(1)}, u32[]{:S(2)}, u32[]{:S(2)}) collective-permute-start(f32[136,128]{1,0:T(8,128)S(1)} %add_add_fusion.1._), channel_id=1, source_target_pairs={{0,1},{1,0},{2,3},{3,2},{4,5},{5,4},{6,7},{7,6},{8,9},{9,8},{10,11... | collective-permute-start | bytes 208904 | tf_op jit(solution)/shard_map/ppermute | solution.py:305
  46.9 1.3 %collective-permute-start.15 = (f32[136,128]{1,0:T(8,128)S(1)}, f32[136,128]{1,0:T(8,128)S(1)}, u32[]{:S(2)}, u32[]{:S(2)}) collective-permute-start(f32[136,128]{1,0:T(8,128)S(1)} %add_add_fusion.refs_0_), channel_id=1, source_target_pairs={{0,4},{4,0},{8,12},{12,8},{16,20},{20,16},{24,28},{28,24},{1,5},{5... | collective-permute-start | bytes 208904 | tf_op jit(solution)/shard_map/ppermute | solution.py:305

commit v11 on v10

--- a/solution.py
+++ b/solution.py
@@ -13,8 +13,8 @@
 LANES = 128
 PANEL = 16
 PLANE = ("gx", "gy")
-SPREAD_ONE = 2
-SPREAD_TWO = 2
+QUARTERS = 4
+SENT = 3
 F32 = jnp.float32
 BF16 = jnp.bfloat16
 VMEM_LIMIT = 48 * 1024 * 1024
@@ -120,11 +120,11 @@
     )
 
 
-def store_blocks(tall_ref, outs):
-    me = lax.rem(lax.axis_index(PLANE), len(outs))
-    size = outs[0].shape[0]
-    for d, out in enumerate(outs):
-        out[...] = tall_ref[pl.ds(pl.multiple_of((me ^ d) * size, 8), size), :]
+def store_blocks(tall_ref, own, across, pair):
+    me = lax.rem(lax.axis_index(PLANE), QUARTERS)
+    size = own.shape[0]
+    for d, out, at in ((0, own, 0), (2, across, 0), (1, pair, 0), (3, pair, size)):
+        out[at : at + size, :] = tall_ref[pl.ds(pl.multiple_of((me ^ d) * size, 8), size), :]
 
 
 def load_blocks(blocks, tall_ref):
@@ -143,13 +143,13 @@
         )
 
     for i in range(steps):
-        copy(i).start(priority=i % 2)
+        copy(i).start()
     return copy
 
 
 def gram_kernel(a_hbm, *refs):
-    outs = refs[:SPREAD_ONE]
-    a_ref, total_ref, tall_ref, sems = refs[SPREAD_ONE:]
+    outs = refs[:SENT]
+    a_ref, total_ref, tall_ref, sems = refs[SENT:]
     copy = chunk_copies(a_hbm, a_ref, sems)
     for i in range(a_ref.shape[0]):
         copy(i).wait()
@@ -169,7 +169,7 @@
     diagonal = jnp.sum(jnp.where(row == col, first, 0.0), axis=0, keepdims=True)
     tail = tall_ref.shape[0] - half - RK
     tall_ref[half + RK :, :] = jnp.broadcast_to(diagonal, (tail, LANES))
-    store_blocks(tall_ref, outs)
+    store_blocks(tall_ref, *outs)
 
 
 def relay_kernel(points, r_hbm, _, hi_ref, lo_ref, token_ref, r_ref, sems):
@@ -202,10 +202,10 @@
 
 
 def absorb_kernel(scale, *refs):
-    blocks, refs = refs[:SPREAD_ONE], refs[SPREAD_ONE:]
+    blocks, refs = refs[:QUARTERS], refs[QUARTERS:]
     hi_ref, lo_ref, absorbed_ref, linv_ref = refs[:4]
-    outs = refs[4 : 4 + SPREAD_TWO]
-    tall_ref, pack_ref, w_ref, total_ref = refs[4 + SPREAD_TWO :]
+    outs = refs[4 : 4 + SENT]
+    tall_ref, pack_ref, w_ref, total_ref = refs[4 + SENT :]
     row, col = triangle_ids()
     load_blocks(blocks, tall_ref)
     half = RK // 2
@@ -247,7 +247,7 @@
     diagonal = jnp.sum(jnp.where(row == col, lower_right, 0.0), axis=0, keepdims=True)
     tail = pack_ref.shape[0] - 2 * LANES
     pack_ref[2 * LANES :, :] = jnp.broadcast_to(diagonal, (tail, LANES))
-    store_blocks(pack_ref, outs)
+    store_blocks(pack_ref, *outs)
 
 
 def left_kernel(a_ref, linv_ref, _, left_ref, token_ref):
@@ -265,7 +265,7 @@
 
 
 def factor_kernel(scale, *refs):
-    blocks, (out_ref, pack_ref, w_ref) = refs[:SPREAD_TWO], refs[SPREAD_TWO:]
+    blocks, (out_ref, pack_ref, w_ref) = refs[:QUARTERS], refs[QUARTERS:]
     load_blocks(blocks, pack_ref)
     row, col = triangle_ids()
     packed = pack_ref[:LANES, :] * scale
@@ -286,6 +286,10 @@
     return jax.ShapeDtypeStruct(dims, dtype)
 
 
+def quarter_shapes(rows):
+    return [shape(rows, LANES), shape(rows, LANES), shape(2 * rows, LANES)]
+
+
 TOKEN = shape(8, LANES)
 
 
@@ -305,10 +309,8 @@
     return lax.ppermute(value, axes, [(i, i ^ mask) for i in range(size)])
 
 
-def four_sum(total, axes, one, two, work):
-    first = swap(total, axes, one)
-    second = swap(total, axes, two)
-    third = swap(total, axes, one ^ two)
+def four_sum(total, moves, work):
+    first, second, third = [swap(*move) for move in moves]
     result = None
     if work is not None:
         result, token = work(total)
@@ -326,16 +328,18 @@
     return [1 << i for i in range(first, lax.axis_size(axis).bit_length() - 1)]
 
 
-def sum_over_devices(blocks, works):
-    n = len(blocks)
-    total = blocks[0]
-    for d in range(1, n):
-        total = total + swap(blocks[d], PLANE, d)
-    far = [("gx", m) for m in bits("gx", 1)] + [("gz", m) for m in bits("gz", 2)]
-    total, first = four_sum(total, PLANE, 2, 4, works[0])
-    total, second = four_sum(total, "gz", 1, 2, works[1])
-    total = rest_sum(total, far)
-    return [total] + [swap(total, PLANE, d) for d in range(1, n)], (first, second)
+def sum_over_devices(parts, works):
+    own, across, pair = parts
+    size = own.shape[0]
+    received = swap(pair, PLANE, 1)
+    own, across = own + received[:size], across + received[size:]
+    moves = [(across, PLANE, 2), (own, PLANE, 4), (across, PLANE, 6)]
+    total, first = four_sum(own, moves, works[0])
+    total, second = four_sum(total, [(total, "gz", m) for m in (1, 2, 3)], works[1])
+    total = rest_sum(
+        total, [("gx", m) for m in bits("gx", 1)] + [("gz", m) for m in bits("gz", 2)]
+    )
+    return [total] + [swap(total, PLANE, d) for d in range(1, QUARTERS)], (first, second)
 
 
 def relay_part(rows_right, points, token):
@@ -411,16 +415,16 @@
     vmem = pl.BlockSpec(memory_space=pltpu.VMEM)
 
     steps = 8
-    block_rows = (RK // 2 + RK + 16) // SPREAD_ONE
+    block_rows = (RK // 2 + RK + 32) // QUARTERS
     blocks = pl.pallas_call(
         gram_kernel,
         in_specs=[pl.BlockSpec(memory_space=pl.ANY)],
-        out_specs=[vmem] * SPREAD_ONE,
-        out_shape=[shape(block_rows, LANES)] * SPREAD_ONE,
+        out_specs=[vmem] * SENT,
+        out_shape=quarter_shapes(block_rows),
         scratch_shapes=[
             pltpu.VMEM((steps, unfold.shape[0] // steps, rank_mid), F32),
             pltpu.VMEM((rank_mid, 2 * rank_mid), F32),
-            pltpu.VMEM((SPREAD_ONE * block_rows, LANES), F32),
+            pltpu.VMEM((QUARTERS * block_rows, LANES), F32),
             pltpu.SemaphoreType.DMA((steps,)),
         ],
         compiler_params=params(limit=53 * 1024 * 1024),
@@ -431,14 +435,14 @@
         [None, functools.partial(relay_part, rows_right, points)],
     )
 
-    tall_rows = SPREAD_ONE * block_rows
-    block_rows = LANES + 8
-    packed_rows = SPREAD_TWO * block_rows
+    tall_rows = QUARTERS * block_rows
+    block_rows = (2 * LANES + 32) // QUARTERS
+    packed_rows = QUARTERS * block_rows
     absorbed, linv, *blocks = pl.pallas_call(
         functools.partial(absorb_kernel, math.sqrt(rank_left * total_points)),
-        in_specs=[vmem] * (SPREAD_ONE + 2),
-        out_specs=[vmem] * (2 + SPREAD_TWO),
-        out_shape=[shape(points, RK, rank_right), shape(RK, RK)] + [shape(block_rows, LANES)] * SPREAD_TWO,
+        in_specs=[vmem] * (QUARTERS + 2),
+        out_specs=[vmem] * (2 + SENT),
+        out_shape=[shape(points, RK, rank_right), shape(RK, RK)] + quarter_shapes(block_rows),
         scratch_shapes=[
             pltpu.VMEM((tall_rows, LANES), F32),
             pltpu.VMEM((packed_rows, LANES), F32),
@@ -458,7 +462,7 @@
 
     factor = pl.pallas_call(
         functools.partial(factor_kernel, 1.0 / (RK * total_points)),
-        in_specs=[vmem] * SPREAD_TWO,
+        in_specs=[vmem] * QUARTERS,
         out_specs=vmem,
         out_shape=shape(rank_right, rank_right),
         scratch_shapes=[

time: 54.8 us -> 57.7 us (1.053)
  starting transfers between devices: 17.9 us -> 21.8 us
  waiting for transfers between devices: 12.1 us -> 11.4 us
    ppermute x16 -> x20, starting transfers between devices: 17.9 us -> 21.8 us  [swap(): return lax.ppermute(value, axes, [(i, i ^ mask) for i in range(size)])]
    ppermute x16 -> x20, waiting for transfers between devices: 12.1 us -> 11.4 us  [swap(): return lax.ppermute(value, axes, [(i, i ^ mask) for i in range(size)])]
  transfers between devices with their start and end apart: 16 -> 20, of which waited for: 10 -> 11; matrix products, arithmetic and copies ran while one was open for 0% -> 0% of each run, Pallas kernels for 15% -> 14%
where the time goes in v11:
time: 57.7 us; the launch traced here: 57.6 us
  Pallas kernels  23.6 us (41%)
  starting transfers between devices  21.8 us (38%)
  waiting for transfers between devices  11.4 us (20%)
  between operations  0.73 us (1%)
    ppermute x20, starting transfers between devices, swap(): return lax.ppermute(value, axes, [(i, i ^ mask) for i in range(size)])  21.8 us
    ppermute x20, waiting for transfers between devices, swap(): return lax.ppermute(value, axes, [(i, i ^ mask) for i in range(size)])  11.4 us
    pallas_call x1, Pallas kernels, per_device(): pl.pallas_call(functools.partial(factor_kernel, 1.0 / (RK * total_points)...  6.45 us
    pallas_call x1, Pallas kernels, per_device(): pl.pallas_call(functools.partial(absorb_kernel, math.sqrt(rank_left * tot...  5.14 us
    pallas_call x1, Pallas kernels, per_device(): pl.pallas_call(gram_kernel, in_specs=[pl.BlockSpec(memory_space=pl.ANY)],...  3.84 us
    pallas_call x1, Pallas kernels, left_part(): pl.pallas_call(left_kernel, grid=(steps,), in_specs=[pl.BlockSpec((chunk,...  2.83 us
    pallas_call x1, Pallas kernels, relay_part(): pl.pallas_call(functools.partial(relay_kernel, points), in_specs=[pl.Bloc...  2.8 us
    pallas_call x1, Pallas kernels, right_part(): pl.pallas_call(functools.partial(right_kernel, points), grid=(steps, 2),...  2.49 us
  transfers between devices with their start and end apart: 20, of which 11 were waited for; matrix products, arithmetic and copies ran while one was open for 0% of the time, Pallas kernels for 14%

profile of v11, /device:TPU:0, one launch (start us, length us, event | category | flops | bytes accessed | tf_op | source)
XLA Modules:
  0.0 57.6 jit_solution(11477162593885293651)
XLA Ops:
  0.6 3.8 %gram_top.1 = (f32[56,128]{1,0:T(8,128)S(1)}, f32[56,128]{1,0:T(8,128)S(1)}, f32[112,128]{1,0:T(8,128)S(1)}) custom-call(f32[4096,256]{1,0:T(8,128)} %bitcast.10), custom_call_target="tpu_custom_call" | custom-call | tf_op jit(solution)/shard_map/gram_top/pallas_call | solution.py:419
  5.0 0.9 %collective-permute-done = f32[112,128]{1,0:T(8,128)S(1)} collective-permute-done((f32[112,128]{1,0:T(8,128)S(1)}, f32[112,128]{1,0:T(8,128)S(1)}, u32[]{:S(2)}, u32[]{:S(2)}) %collective-permute-start) | collective-permute-done | bytes 57376 | tf_op jit(solution)/shard_map/ppermute | solution.py:309
  5.9 3.9 %collective-permute-start.3 = (f32[56,128]{1,0:T(8,128)S(1)}, f32[56,128]{1,0:T(8,128)S(1)}, u32[]{:S(2)}, u32[]{:S(2)}) collective-permute-start(f32[56,128]{1,0:T(8,128)S(1)} %get-tuple-element.35), channel_id=1, source_target_pairs={{0,24},{4,28},{8,16},{12,20},{16,8},{20,12},{24,0},{28,4},{1,25},{... | collective-permute-start | bytes 86024 | tf_op jit(solution)/shard_map/ppermute | solution.py:309
  9.7 0.5 collective-permute-start.1
  10.4 1.2 %collective-permute-done.3 = f32[56,128]{1,0:T(8,128)S(1)} collective-permute-done((f32[56,128]{1,0:T(8,128)S(1)}, f32[56,128]{1,0:T(8,128)S(1)}, u32[]{:S(2)}, u32[]{:S(2)}) %collective-permute-start.3) | collective-permute-done | bytes 28704 | tf_op jit(solution)/shard_map/ppermute | solution.py:309
  11.6 2.0 %collective-permute-done.1 = f32[56,128]{1,0:T(8,128)S(1)} collective-permute-done((f32[56,128]{1,0:T(8,128)S(1)}, f32[56,128]{1,0:T(8,128)S(1)}, u32[]{:S(2)}, u32[]{:S(2)}) %collective-permute-start.1) | collective-permute-done | bytes 28704 | tf_op jit(solution)/shard_map/ppermute | solution.py:309
  14.1 3.7 %collective-permute-start.6 = (f32[56,128]{1,0:T(8,128)S(1)}, f32[56,128]{1,0:T(8,128)S(1)}, u32[]{:S(2)}, u32[]{:S(2)}) collective-permute-start(f32[56,128]{1,0:T(8,128)S(1)} %add_add_fusion.3._), channel_id=1, source_target_pairs={{0,3},{1,2},{2,1},{3,0},{4,7},{5,6},{6,5},{7,4},{8,11},{9,10},{10,... | collective-permute-start | bytes 86024 | tf_op jit(solution)/shard_map/ppermute | solution.py:309
  17.8 0.8 %collective-permute-start.4 = (f32[56,128]{1,0:T(8,128)S(1)}, f32[56,128]{1,0:T(8,128)S(1)}, u32[]{:S(2)}, u32[]{:S(2)}) collective-permute-start(f32[56,128]{1,0:T(8,128)S(1)} %add_add_fusion.3._), channel_id=1, source_target_pairs={{0,1},{1,0},{2,3},{3,2},{4,5},{5,4},{6,7},{7,6},{8,9},{9,8},{10,11... | collective-permute-start | bytes 86024 | tf_op jit(solution)/shard_map/ppermute | solution.py:309
  18.6 2.8 %relay_right.1 = (bf16[16,256,256]{2,1,0:T(8,128)(2,1)S(1)}, bf16[16,256,256]{2,1,0:T(8,128)(2,1)S(1)}, f32[8,128]{1,0:T(8,128)S(1)}) custom-call(f32[4096,256]{1,0:T(8,128)} %bitcast.12, f32[56,128]{1,0:T(8,128)S(1)} %add_add_fusion.3._), custom_call_target="tpu_custom_call" | custom-call | bytes 8388608 | tf_op jit(solution)/shard_map/relay_right/pallas_call | solution.py:350
  21.4 1.1 %collective-permute-done.5 = f32[56,128]{1,0:T(8,128)S(1)} collective-permute-done((f32[56,128]{1,0:T(8,128)S(1)}, f32[56,128]{1,0:T(8,128)S(1)}, u32[]{:S(2)}, u32[]{:S(2)}) %collective-permute-start.5) | collective-permute-done | bytes 28704 | tf_op jit(solution)/shard_map/ppermute | solution.py:309
  22.7 1.6 %collective-permute-start.8 = (f32[56,128]{1,0:T(8,128)S(1)}, f32[56,128]{1,0:T(8,128)S(1)}, u32[]{:S(2)}, u32[]{:S(2)}) collective-permute-start(f32[56,128]{1,0:T(8,128)S(1)} %add_add_fusion.2.refs_0_), channel_id=1, source_target_pairs={{0,8},{4,12},{8,0},{12,4},{16,24},{20,28},{24,16},{28,20},{1,9},{5... | collective-permute-start | bytes 86024 | tf_op jit(solution)/shard_map/ppermute | solution.py:309
  24.5 1.7 %collective-permute-done.9.refs_3_ = f32[56,128]{1,0:T(8,128)S(1)} collective-permute-done((f32[56,128]{1,0:T(8,128)S(1)}, f32[56,128]{1,0:T(8,128)S(1)}, u32[]{:S(2)}, u32[]{:S(2)}) %collective-permute-start.9) | collective-permute-done | bytes 28704 | tf_op jit(solution)/shard_map/ppermute | solution.py:309
  26.6 5.1 %factor_absorb.1 = (f32[16,128,256]{2,1,0:T(8,128)S(1)}, f32[128,128]{1,0:T(8,128)S(1)}, f32[72,128]{1,0:T(8,128)S(1)}, f32[72,128]{1,0:T(8,128)S(1)}, f32[144,128]{1,0:T(8,128)S(1)}) custom-call(f32[56,128]{1,0:T(8,128)S(1)} %add_add_fusion.2.refs_0_, f32[56,128]{1,0:T(8,128)S(1)} %collective-permute-done.7.refs_1_, ...), custom_call_target="tpu_custom_call" | custom-call | tf_op jit(solution)/shard_map/factor_absorb/pallas_call | solution.py:441
  32.2 0.9 %collective-permute-done.10 = f32[144,128]{1,0:T(8,128)S(1)} collective-permute-done((f32[144,128]{1,0:T(8,128)S(1)}, f32[144,128]{1,0:T(8,128)S(1)}, u32[]{:S(2)}, u32[]{:S(2)}) %collective-permute-start.10) | collective-permute-done | bytes 73760 | tf_op jit(solution)/shard_map/ppermute | solution.py:309
  33.2 1.5 %collective-permute-start.13 = (f32[72,128]{1,0:T(8,128)S(1)}, f32[72,128]{1,0:T(8,128)S(1)}, u32[]{:S(2)}, u32[]{:S(2)}) collective-permute-start(f32[72,128]{1,0:T(8,128)S(1)} %get-tuple-element.33), channel_id=1, source_target_pairs={{0,24},{4,28},{8,16},{12,20},{16,8},{20,12},{24,0},{28,4},{1,25},{... | collective-permute-start | bytes 110600 | tf_op jit(solution)/shard_map/ppermute | solution.py:309
  34.7 0.5 collective-permute-start.11
  35.2 1.5 %collective-permute-start.12 = (f32[72,128]{1,0:T(8,128)S(1)}, f32[72,128]{1,0:T(8,128)S(1)}, u32[]{:S(2)}, u32[]{:S(2)}) collective-permute-start(f32[72,128]{1,0:T(8,128)S(1)} %get-tuple-element.34._), channel_id=1, source_target_pairs={{0,16},{4,20},{8,24},{12,28},{16,0},{20,4},{24,8},{28,12},{1,17},{... | collective-permute-start | bytes 110600 | tf_op jit(solution)/shard_map/ppermute | solution.py:309
  36.7 2.5 %right_out.1 = (f32[2048,256]{1,0:T(8,128)}, f32[8,128]{1,0:T(8,128)S(1)}) custom-call(f32[16,128,256]{2,1,0:T(8,128)S(1)} %get-tuple-element.28.absorbed_ref, f32[72,128]{1,0:T(8,128)S(1)} %get-tuple-element.34._), custom_call_target="tpu_custom_call" | custom-call | bytes 8388608 | tf_op jit(solution)/shard_map/right_out/pallas_call | solution.py:391
  39.2 2.5 %collective-permute-start.16 = (f32[72,128]{1,0:T(8,128)S(1)}, f32[72,128]{1,0:T(8,128)S(1)}, u32[]{:S(2)}, u32[]{:S(2)}) collective-permute-start(f32[72,128]{1,0:T(8,128)S(1)} %add_add_fusion.1._), channel_id=1, source_target_pairs={{0,3},{1,2},{2,1},{3,0},{4,7},{5,6},{6,5},{7,4},{8,11},{9,10},{10,... | collective-permute-start | bytes 110600 | tf_op jit(solution)/shard_map/ppermute | solution.py:309
  41.8 1.9 %collective-permute-start.14 = (f32[72,128]{1,0:T(8,128)S(1)}, f32[72,128]{1,0:T(8,128)S(1)}, u32[]{:S(2)}, u32[]{:S(2)}) collective-permute-start(f32[72,128]{1,0:T(8,128)S(1)} %add_add_fusion.1._), channel_id=1, source_target_pairs={{0,1},{1,0},{2,3},{3,2},{4,5},{5,4},{6,7},{7,6},{8,9},{9,8},{10,11... | collective-permute-start | bytes 110600 | tf_op jit(solution)/shard_map/ppermute | solution.py:309
  43.7 2.8 %left_out.1 = (f32[4096,128]{1,0:T(8,128)}, f32[8,128]{1,0:T(8,128)S(1)}) custom-call(f32[4096,256]{1,0:T(8,128)S(1)} %bitcast.11, f32[128,128]{1,0:T(8,128)S(1)} %get-tuple-element.24.linv_ref, f32[72,128]{1,0:T(8,128)S(1)} %add_add_fusion.1._), custom_call_target="tpu_custom_call" | custom-call | bytes 8388608 | tf_op jit(solution)/shard_map/left_out/pallas_call | solution.py:369
  46.9 1.4 %collective-permute-start.18 = (f32[72,128]{1,0:T(8,128)S(1)}, f32[72,128]{1,0:T(8,128)S(1)}, u32[]{:S(2)}, u32[]{:S(2)}) collective-permute-start(f32[72,128]{1,0:T(8,128)S(1)} %add_add_fusion.refs_0_), channel_id=1, source_target_pairs={{0,8},{4,12},{8,0},{12,4},{16,24},{20,28},{24,16},{28,20},{1,9},{5... | collective-permute-start | bytes 110600 | tf_op jit(solution)/shard_map/ppermute | solution.py:309
  48.8 1.9 %collective-permute-done.19.refs_3_ = f32[72,128]{1,0:T(8,128)S(1)} collective-permute-done((f32[72,128]{1,0:T(8,128)S(1)}, f32[72,128]{1,0:T(8,128)S(1)}, u32[]{:S(2)}, u32[]{:S(2)}) %collective-permute-start.19) | collective-permute-done | bytes 36896 | tf_op jit(solution)/shard_map/ppermute | solution.py:309
  51.1 6.5 %factor_next.1 = f32[256,256]{1,0:T(8,128)} custom-call(f32[72,128]{1,0:T(8,128)S(1)} %add_add_fusion.refs_0_, f32[72,128]{1,0:T(8,128)S(1)} %collective-permute-done.17.refs_1_, f32[72,128]{1,0:T(8,128)S(1)} %collective-permute-done.18.refs_2_, f32[72,128]{1,0:T(8,128)S(1)} %collective-permute-done.19.refs_3_), custom_call_target="tpu_custom_call" | custom-call | tf_op jit(solution)/shard_map/factor_next/pallas_call | solution.py:463
  (33 shorter events, 3.7 us)
Async XLA Ops:
  4.5 1.4 %collective-permute-start = (f32[112,128]{1,0:T(8,128)S(1)}, f32[112,128]{1,0:T(8,128)S(1)}, u32[]{:S(2)}, u32[]{:S(2)}) collective-permute-start(f32[112,128]{1,0:T(8,128)S(1)} %get-tuple-element.19), channel_id=1, source_target_pairs={{0,4},{4,0},{8,12},{12,8},{16,20},{20,16},{24,28},{28,24},{1,5},{5... | collective-permute-start | bytes 172040 | tf_op jit(solution)/shard_map/ppermute | solution.py:309
  5.9 5.7 %collective-permute-start.3 = (f32[56,128]{1,0:T(8,128)S(1)}, f32[56,128]{1,0:T(8,128)S(1)}, u32[]{:S(2)}, u32[]{:S(2)}) collective-permute-start(f32[56,128]{1,0:T(8,128)S(1)} %get-tuple-element.35), channel_id=1, source_target_pairs={{0,24},{4,28},{8,16},{12,20},{16,8},{20,12},{24,0},{28,4},{1,25},{... | collective-permute-start | bytes 86024 | tf_op jit(solution)/shard_map/ppermute | solution.py:309
  9.7 3.9 %collective-permute-start.1 = (f32[56,128]{1,0:T(8,128)S(1)}, f32[56,128]{1,0:T(8,128)S(1)}, u32[]{:S(2)}, u32[]{:S(2)}) collective-permute-start(f32[56,128]{1,0:T(8,128)S(1)} %get-tuple-element.35), channel_id=1, source_target_pairs={{0,8},{4,12},{8,0},{12,4},{16,24},{20,28},{24,16},{28,20},{1,9},{5... | collective-permute-start | bytes 86024 | tf_op jit(solution)/shard_map/ppermute | solution.py:309
  10.3 3.9 %collective-permute-start.2 = (f32[56,128]{1,0:T(8,128)S(1)}, f32[56,128]{1,0:T(8,128)S(1)}, u32[]{:S(2)}, u32[]{:S(2)}) collective-permute-start(f32[56,128]{1,0:T(8,128)S(1)} %get-tuple-element.36), channel_id=1, source_target_pairs={{0,16},{4,20},{8,24},{12,28},{16,0},{20,4},{24,8},{28,12},{1,17},{... | collective-permute-start | bytes 86024 | tf_op jit(solution)/shard_map/ppermute | solution.py:309
  14.1 7.3 %collective-permute-start.6 = (f32[56,128]{1,0:T(8,128)S(1)}, f32[56,128]{1,0:T(8,128)S(1)}, u32[]{:S(2)}, u32[]{:S(2)}) collective-permute-start(f32[56,128]{1,0:T(8,128)S(1)} %add_add_fusion.3._), channel_id=1, source_target_pairs={{0,3},{1,2},{2,1},{3,0},{4,7},{5,6},{6,5},{7,4},{8,11},{9,10},{10,... | collective-permute-start | bytes 86024 | tf_op jit(solution)/shard_map/ppermute | solution.py:309
  17.8 4.8 %collective-permute-start.5 = (f32[56,128]{1,0:T(8,128)S(1)}, f32[56,128]{1,0:T(8,128)S(1)}, u32[]{:S(2)}, u32[]{:S(2)}) collective-permute-start(f32[56,128]{1,0:T(8,128)S(1)} %add_add_fusion.3._), channel_id=1, source_target_pairs={{0,2},{1,3},{2,0},{3,1},{4,6},{5,7},{6,4},{7,5},{8,10},{9,11},{10,... | collective-permute-start | bytes 86024 | tf_op jit(solution)/shard_map/ppermute | solution.py:309
  17.8 4.8 %collective-permute-start.4 = (f32[56,128]{1,0:T(8,128)S(1)}, f32[56,128]{1,0:T(8,128)S(1)}, u32[]{:S(2)}, u32[]{:S(2)}) collective-permute-start(f32[56,128]{1,0:T(8,128)S(1)} %add_add_fusion.3._), channel_id=1, source_target_pairs={{0,1},{1,0},{2,3},{3,2},{4,5},{5,4},{6,7},{7,6},{8,9},{9,8},{10,11... | collective-permute-start | bytes 86024 | tf_op jit(solution)/shard_map/ppermute | solution.py:309
  22.6 3.6 %collective-permute-start.9 = (f32[56,128]{1,0:T(8,128)S(1)}, f32[56,128]{1,0:T(8,128)S(1)}, u32[]{:S(2)}, u32[]{:S(2)}) collective-permute-start(f32[56,128]{1,0:T(8,128)S(1)} %add_add_fusion.2.refs_0_), channel_id=1, source_target_pairs={{0,12},{4,8},{8,4},{12,0},{16,28},{20,24},{24,20},{28,16},{1,13},{... | collective-permute-start | bytes 86024 | tf_op jit(solution)/shard_map/ppermute | solution.py:309
  22.7 3.9 %collective-permute-start.8 = (f32[56,128]{1,0:T(8,128)S(1)}, f32[56,128]{1,0:T(8,128)S(1)}, u32[]{:S(2)}, u32[]{:S(2)}) collective-permute-start(f32[56,128]{1,0:T(8,128)S(1)} %add_add_fusion.2.refs_0_), channel_id=1, source_target_pairs={{0,8},{4,12},{8,0},{12,4},{16,24},{20,28},{24,16},{28,20},{1,9},{5... | collective-permute-start | bytes 86024 | tf_op jit(solution)/shard_map/ppermute | solution.py:309
  24.3 2.4 %collective-permute-start.7 = (f32[56,128]{1,0:T(8,128)S(1)}, f32[56,128]{1,0:T(8,128)S(1)}, u32[]{:S(2)}, u32[]{:S(2)}) collective-permute-start(f32[56,128]{1,0:T(8,128)S(1)} %add_add_fusion.2.refs_0_), channel_id=1, source_target_pairs={{0,4},{4,0},{8,12},{12,8},{16,20},{20,16},{24,28},{28,24},{1,5},{5... | collective-permute-start | bytes 86024 | tf_op jit(solution)/shard_map/ppermute | solution.py:309
  26.6 17.1 %copy-start = (f32[256,16,256]{2,1,0:T(8,128)S(1)}, f32[256,16,256]{2,1,0:T(8,128)}, u32[]{:S(2)}) copy-start(f32[256,16,256]{2,1,0:T(8,128)} %param.2) | copy-start | bytes 12582916
  31.8 1.4 %collective-permute-start.10 = (f32[144,128]{1,0:T(8,128)S(1)}, f32[144,128]{1,0:T(8,128)S(1)}, u32[]{:S(2)}, u32[]{:S(2)}) collective-permute-start(f32[144,128]{1,0:T(8,128)S(1)} %get-tuple-element.26), channel_id=1, source_target_pairs={{0,4},{4,0},{8,12},{12,8},{16,20},{20,16},{24,28},{28,24},{1,5},{5... | collective-permute-start | bytes 221192 | tf_op jit(solution)/shard_map/ppermute | solution.py:309
  33.2 6.1 %collective-permute-start.13 = (f32[72,128]{1,0:T(8,128)S(1)}, f32[72,128]{1,0:T(8,128)S(1)}, u32[]{:S(2)}, u32[]{:S(2)}) collective-permute-start(f32[72,128]{1,0:T(8,128)S(1)} %get-tuple-element.33), channel_id=1, source_target_pairs={{0,24},{4,28},{8,16},{12,20},{16,8},{20,12},{24,0},{28,4},{1,25},{... | collective-permute-start | bytes 110600 | tf_op jit(solution)/shard_map/ppermute | solution.py:309
  34.7 4.5 %collective-permute-start.11 = (f32[72,128]{1,0:T(8,128)S(1)}, f32[72,128]{1,0:T(8,128)S(1)}, u32[]{:S(2)}, u32[]{:S(2)}) collective-permute-start(f32[72,128]{1,0:T(8,128)S(1)} %get-tuple-element.33), channel_id=1, source_target_pairs={{0,8},{4,12},{8,0},{12,4},{16,24},{20,28},{24,16},{28,20},{1,9},{5... | collective-permute-start | bytes 110600 | tf_op jit(solution)/shard_map/ppermute | solution.py:309
  35.2 4.0 %collective-permute-start.12 = (f32[72,128]{1,0:T(8,128)S(1)}, f32[72,128]{1,0:T(8,128)S(1)}, u32[]{:S(2)}, u32[]{:S(2)}) collective-permute-start(f32[72,128]{1,0:T(8,128)S(1)} %get-tuple-element.34._), channel_id=1, source_target_pairs={{0,16},{4,20},{8,24},{12,28},{16,0},{20,4},{24,8},{28,12},{1,17},{... | collective-permute-start | bytes 110600 | tf_op jit(solution)/shard_map/ppermute | solution.py:309
  39.2 7.3 %collective-permute-start.16 = (f32[72,128]{1,0:T(8,128)S(1)}, f32[72,128]{1,0:T(8,128)S(1)}, u32[]{:S(2)}, u32[]{:S(2)}) collective-permute-start(f32[72,128]{1,0:T(8,128)S(1)} %add_add_fusion.1._), channel_id=1, source_target_pairs={{0,3},{1,2},{2,1},{3,0},{4,7},{5,6},{6,5},{7,4},{8,11},{9,10},{10,... | collective-permute-start | bytes 110600 | tf_op jit(solution)/shard_map/ppermute | solution.py:309
  41.8 5.0 %collective-permute-start.15 = (f32[72,128]{1,0:T(8,128)S(1)}, f32[72,128]{1,0:T(8,128)S(1)}, u32[]{:S(2)}, u32[]{:S(2)}) collective-permute-start(f32[72,128]{1,0:T(8,128)S(1)} %add_add_fusion.1._), channel_id=1, source_target_pairs={{0,2},{1,3},{2,0},{3,1},{4,6},{5,7},{6,4},{7,5},{8,10},{9,11},{10,... | collective-permute-start | bytes 110600 | tf_op jit(solution)/shard_map/ppermute | solution.py:309
  41.8 5.0 %collective-permute-start.14 = (f32[72,128]{1,0:T(8,128)S(1)}, f32[72,128]{1,0:T(8,128)S(1)}, u32[]{:S(2)}, u32[]{:S(2)}) collective-permute-start(f32[72,128]{1,0:T(8,128)S(1)} %add_add_fusion.1._), channel_id=1, source_target_pairs={{0,1},{1,0},{2,3},{3,2},{4,5},{5,4},{6,7},{7,6},{8,9},{9,8},{10,11... | collective-permute-start | bytes 110600 | tf_op jit(solution)/shard_map/ppermute | solution.py:309
  46.8 3.8 %collective-permute-start.19 = (f32[72,128]{1,0:T(8,128)S(1)}, f32[72,128]{1,0:T(8,128)S(1)}, u32[]{:S(2)}, u32[]{:S(2)}) collective-permute-start(f32[72,128]{1,0:T(8,128)S(1)} %add_add_fusion.refs_0_), channel_id=1, source_target_pairs={{0,12},{4,8},{8,4},{12,0},{16,28},{20,24},{24,20},{28,16},{1,13},{... | collective-permute-start | bytes 110600 | tf_op jit(solution)/shard_map/ppermute | solution.py:309
  46.9 4.2 %collective-permute-start.18 = (f32[72,128]{1,0:T(8,128)S(1)}, f32[72,128]{1,0:T(8,128)S(1)}, u32[]{:S(2)}, u32[]{:S(2)}) collective-permute-start(f32[72,128]{1,0:T(8,128)S(1)} %add_add_fusion.refs_0_), channel_id=1, source_target_pairs={{0,8},{4,12},{8,0},{12,4},{16,24},{20,28},{24,16},{28,20},{1,9},{5... | collective-permute-start | bytes 110600 | tf_op jit(solution)/shard_map/ppermute | solution.py:309
  48.4 2.8 %collective-permute-start.17 = (f32[72,128]{1,0:T(8,128)S(1)}, f32[72,128]{1,0:T(8,128)S(1)}, u32[]{:S(2)}, u32[]{:S(2)}) collective-permute-start(f32[72,128]{1,0:T(8,128)S(1)} %add_add_fusion.refs_0_), channel_id=1, source_target_pairs={{0,4},{4,0},{8,12},{12,8},{16,20},{20,16},{24,28},{28,24},{1,5},{5... | collective-permute-start | bytes 110600 | tf_op jit(solution)/shard_map/ppermute | solution.py:309

commit v12 on v10

--- a/solution.py
+++ b/solution.py
@@ -143,7 +143,7 @@
         )
 
     for i in range(steps):
-        copy(i).start(priority=i % 2)
+        copy(i).start()
     return copy
 
 

time: 54.8 us -> 54.5 us (level)
  no operation moved by 1% of the time
where the time goes in v12:
time: 54.5 us; the launch traced here: 54.3 us
  Pallas kernels  23.5 us (43%)
  starting transfers between devices  17.9 us (33%)
  waiting for transfers between devices  12.1 us (22%)
  between operations  0.71 us (1%)
    ppermute x16, starting transfers between devices, swap(): return lax.ppermute(value, axes, [(i, i ^ mask) for i in range(size)])  17.9 us
    ppermute x16, waiting for transfers between devices, swap(): return lax.ppermute(value, axes, [(i, i ^ mask) for i in range(size)])  12.1 us
    pallas_call x1, Pallas kernels, per_device(): pl.pallas_call(functools.partial(factor_kernel, 1.0 / (RK * total_points)...  6.44 us
    pallas_call x1, Pallas kernels, per_device(): pl.pallas_call(functools.partial(absorb_kernel, math.sqrt(rank_left * tot...  5.13 us
    pallas_call x1, Pallas kernels, per_device(): pl.pallas_call(gram_kernel, in_specs=[pl.BlockSpec(memory_space=pl.ANY)],...  3.84 us
    pallas_call x1, Pallas kernels, left_part(): pl.pallas_call(left_kernel, grid=(steps,), in_specs=[pl.BlockSpec((chunk,...  2.83 us
    pallas_call x1, Pallas kernels, relay_part(): pl.pallas_call(functools.partial(relay_kernel, points), in_specs=[pl.Bloc...  2.8 us
    pallas_call x1, Pallas kernels, right_part(): pl.pallas_call(functools.partial(right_kernel, points), grid=(steps, 2),...  2.49 us
  transfers between devices with their start and end apart: 16, of which 10 were waited for; matrix products, arithmetic and copies ran while one was open for 0% of the time, Pallas kernels for 15%

profile of v12, /device:TPU:0, one launch (start us, length us, event | category | flops | bytes accessed | tf_op | source)
XLA Modules:
  0.0 54.3 jit_solution(4285239132332227705)
XLA Ops:
  0.6 3.8 %gram_top.1 = (f32[104,128]{1,0:T(8,128)S(1)}, f32[104,128]{1,0:T(8,128)S(1)}) custom-call(f32[4096,256]{1,0:T(8,128)} %bitcast.10), custom_call_target="tpu_custom_call" | custom-call | tf_op jit(solution)/shard_map/gram_top/pallas_call | solution.py:415
  5.0 0.9 %collective-permute-done = f32[104,128]{1,0:T(8,128)S(1)} collective-permute-done((f32[104,128]{1,0:T(8,128)S(1)}, f32[104,128]{1,0:T(8,128)S(1)}, u32[]{:S(2)}, u32[]{:S(2)}) %collective-permute-start) | collective-permute-done | bytes 53280 | tf_op jit(solution)/shard_map/ppermute | solution.py:305
  5.9 3.9 %collective-permute-start.3 = (f32[104,128]{1,0:T(8,128)S(1)}, f32[104,128]{1,0:T(8,128)S(1)}, u32[]{:S(2)}, u32[]{:S(2)}) collective-permute-start(f32[104,128]{1,0:T(8,128)S(1)} %add.72), channel_id=1, source_target_pairs={{0,24},{4,28},{8,16},{12,20},{16,8},{20,12},{24,0},{28,4},{1,25},{... | collective-permute-start | bytes 159752 | tf_op jit(solution)/shard_map/ppermute | solution.py:305
  9.7 0.5 collective-permute-start.2
  10.4 1.5 %collective-permute-done.3 = f32[104,128]{1,0:T(8,128)S(1)} collective-permute-done((f32[104,128]{1,0:T(8,128)S(1)}, f32[104,128]{1,0:T(8,128)S(1)}, u32[]{:S(2)}, u32[]{:S(2)}) %collective-permute-start.3) | collective-permute-done | bytes 53280 | tf_op jit(solution)/shard_map/ppermute | solution.py:305
  11.9 2.0 %collective-permute-done.2 = f32[104,128]{1,0:T(8,128)S(1)} collective-permute-done((f32[104,128]{1,0:T(8,128)S(1)}, f32[104,128]{1,0:T(8,128)S(1)}, u32[]{:S(2)}, u32[]{:S(2)}) %collective-permute-start.2) | collective-permute-done | bytes 53280 | tf_op jit(solution)/shard_map/ppermute | solution.py:305
  13.9 0.5 collective-permute-done.1
  14.4 3.7 %collective-permute-start.6 = (f32[104,128]{1,0:T(8,128)S(1)}, f32[104,128]{1,0:T(8,128)S(1)}, u32[]{:S(2)}, u32[]{:S(2)}) collective-permute-start(f32[104,128]{1,0:T(8,128)S(1)} %add_add_fusion.3._), channel_id=1, source_target_pairs={{0,3},{1,2},{2,1},{3,0},{4,7},{5,6},{6,5},{7,4},{8,11},{9,10},{10,... | collective-permute-start | bytes 159752 | tf_op jit(solution)/shard_map/ppermute | solution.py:305
  18.1 0.8 %collective-permute-start.4 = (f32[104,128]{1,0:T(8,128)S(1)}, f32[104,128]{1,0:T(8,128)S(1)}, u32[]{:S(2)}, u32[]{:S(2)}) collective-permute-start(f32[104,128]{1,0:T(8,128)S(1)} %add_add_fusion.3._), channel_id=1, source_target_pairs={{0,1},{1,0},{2,3},{3,2},{4,5},{5,4},{6,7},{7,6},{8,9},{9,8},{10,11... | collective-permute-start | bytes 159752 | tf_op jit(solution)/shard_map/ppermute | solution.py:305
  18.9 2.8 %relay_right.1 = (bf16[16,256,256]{2,1,0:T(8,128)(2,1)S(1)}, bf16[16,256,256]{2,1,0:T(8,128)(2,1)S(1)}, f32[8,128]{1,0:T(8,128)S(1)}) custom-call(f32[4096,256]{1,0:T(8,128)} %bitcast.12, f32[104,128]{1,0:T(8,128)S(1)} %add_add_fusion.3._), custom_call_target="tpu_custom_call" | custom-call | bytes 8388608 | tf_op jit(solution)/shard_map/relay_right/pallas_call | solution.py:346
  21.7 1.4 %collective-permute-done.5 = f32[104,128]{1,0:T(8,128)S(1)} collective-permute-done((f32[104,128]{1,0:T(8,128)S(1)}, f32[104,128]{1,0:T(8,128)S(1)}, u32[]{:S(2)}, u32[]{:S(2)}) %collective-permute-start.5) | collective-permute-done | bytes 53280 | tf_op jit(solution)/shard_map/ppermute | solution.py:305
  23.2 1.2 %collective-permute-done.7.refs_1_ = f32[104,128]{1,0:T(8,128)S(1)} collective-permute-done((f32[104,128]{1,0:T(8,128)S(1)}, f32[104,128]{1,0:T(8,128)S(1)}, u32[]{:S(2)}, u32[]{:S(2)}) %collective-permute-start.7) | collective-permute-done | bytes 53280 | tf_op jit(solution)/shard_map/ppermute | solution.py:305
  24.5 5.1 %factor_absorb.1 = (f32[16,128,256]{2,1,0:T(8,128)S(1)}, f32[128,128]{1,0:T(8,128)S(1)}, f32[136,128]{1,0:T(8,128)S(1)}, f32[136,128]{1,0:T(8,128)S(1)}) custom-call(f32[104,128]{1,0:T(8,128)S(1)} %add_add_fusion.2.refs_0_, f32[104,128]{1,0:T(8,128)S(1)} %collective-permute-done.7.refs_1_, bf16[16,256,256]{2,1,0:T(8,128)(2,1)S(1)} %get-tuple-element.19.refs_2_, ...), custom_call_target="tpu_custom_call" | custom-call | tf_op jit(solution)/shard_map/factor_absorb/pallas_call | solution.py:437
  29.8 1.1 %collective-permute-done.8 = f32[136,128]{1,0:T(8,128)S(1)} collective-permute-done((f32[136,128]{1,0:T(8,128)S(1)}, f32[136,128]{1,0:T(8,128)S(1)}, u32[]{:S(2)}, u32[]{:S(2)}) %collective-permute-start.8) | collective-permute-done | bytes 69664 | tf_op jit(solution)/shard_map/ppermute | solution.py:305
  30.9 1.6 %collective-permute-start.11 = (f32[136,128]{1,0:T(8,128)S(1)}, f32[136,128]{1,0:T(8,128)S(1)}, u32[]{:S(2)}, u32[]{:S(2)}) collective-permute-start(f32[136,128]{1,0:T(8,128)S(1)} %add.82._), channel_id=1, source_target_pairs={{0,24},{4,28},{8,16},{12,20},{16,8},{20,12},{24,0},{28,4},{1,25},{... | collective-permute-start | bytes 208904 | tf_op jit(solution)/shard_map/ppermute | solution.py:305
  33.0 1.5 %collective-permute-start.9 = (f32[136,128]{1,0:T(8,128)S(1)}, f32[136,128]{1,0:T(8,128)S(1)}, u32[]{:S(2)}, u32[]{:S(2)}) collective-permute-start(f32[136,128]{1,0:T(8,128)S(1)} %add.82._), channel_id=1, source_target_pairs={{0,8},{4,12},{8,0},{12,4},{16,24},{20,28},{24,16},{28,20},{1,9},{5... | collective-permute-start | bytes 208904 | tf_op jit(solution)/shard_map/ppermute | solution.py:305
  34.5 2.5 %right_out.1 = (f32[2048,256]{1,0:T(8,128)}, f32[8,128]{1,0:T(8,128)S(1)}) custom-call(f32[16,128,256]{2,1,0:T(8,128)S(1)} %get-tuple-element.24.absorbed_ref, f32[136,128]{1,0:T(8,128)S(1)} %add.82._), custom_call_target="tpu_custom_call" | custom-call | bytes 8388608 | tf_op jit(solution)/shard_map/right_out/pallas_call | solution.py:387
  37.0 0.7 %collective-permute-done.9 = f32[136,128]{1,0:T(8,128)S(1)} collective-permute-done((f32[136,128]{1,0:T(8,128)S(1)}, f32[136,128]{1,0:T(8,128)S(1)}, u32[]{:S(2)}, u32[]{:S(2)}) %collective-permute-start.9) | collective-permute-done | bytes 69664 | tf_op jit(solution)/shard_map/ppermute | solution.py:305
  37.7 2.3 %collective-permute-start.14 = (f32[136,128]{1,0:T(8,128)S(1)}, f32[136,128]{1,0:T(8,128)S(1)}, u32[]{:S(2)}, u32[]{:S(2)}) collective-permute-start(f32[136,128]{1,0:T(8,128)S(1)} %add_add_fusion.1._), channel_id=1, source_target_pairs={{0,3},{1,2},{2,1},{3,0},{4,7},{5,6},{6,5},{7,4},{8,11},{9,10},{10,... | collective-permute-start | bytes 208904 | tf_op jit(solution)/shard_map/ppermute | solution.py:305
  40.0 2.2 %collective-permute-start.12 = (f32[136,128]{1,0:T(8,128)S(1)}, f32[136,128]{1,0:T(8,128)S(1)}, u32[]{:S(2)}, u32[]{:S(2)}) collective-permute-start(f32[136,128]{1,0:T(8,128)S(1)} %add_add_fusion.1._), channel_id=1, source_target_pairs={{0,1},{1,0},{2,3},{3,2},{4,5},{5,4},{6,7},{7,6},{8,9},{9,8},{10,11... | collective-permute-start | bytes 208904 | tf_op jit(solution)/shard_map/ppermute | solution.py:305
  42.1 2.8 %left_out.1 = (f32[4096,128]{1,0:T(8,128)}, f32[8,128]{1,0:T(8,128)S(1)}) custom-call(f32[4096,256]{1,0:T(8,128)S(1)} %bitcast.11, f32[128,128]{1,0:T(8,128)S(1)} %get-tuple-element.21.linv_ref, f32[136,128]{1,0:T(8,128)S(1)} %add_add_fusion.1._), custom_call_target="tpu_custom_call" | custom-call | bytes 8388608 | tf_op jit(solution)/shard_map/left_out/pallas_call | solution.py:365
  45.0 1.6 %collective-permute-done.13 = f32[136,128]{1,0:T(8,128)S(1)} collective-permute-done((f32[136,128]{1,0:T(8,128)S(1)}, f32[136,128]{1,0:T(8,128)S(1)}, u32[]{:S(2)}, u32[]{:S(2)}) %collective-permute-start.13) | collective-permute-done | bytes 69664 | tf_op jit(solution)/shard_map/ppermute | solution.py:305
  46.7 1.2 %collective-permute-done.15.refs_1_ = f32[136,128]{1,0:T(8,128)S(1)} collective-permute-done((f32[136,128]{1,0:T(8,128)S(1)}, f32[136,128]{1,0:T(8,128)S(1)}, u32[]{:S(2)}, u32[]{:S(2)}) %collective-permute-start.15) | collective-permute-done | bytes 69664 | tf_op jit(solution)/shard_map/ppermute | solution.py:305
  47.9 6.4 %factor_next.1 = f32[256,256]{1,0:T(8,128)} custom-call(f32[136,128]{1,0:T(8,128)S(1)} %add_add_fusion.refs_0_, f32[136,128]{1,0:T(8,128)S(1)} %collective-permute-done.15.refs_1_), custom_call_target="tpu_custom_call" | custom-call | tf_op jit(solution)/shard_map/factor_next/pallas_call | solution.py:459
  (25 shorter events, 1.6 us)
Async XLA Ops:
  4.5 1.4 %collective-permute-start = (f32[104,128]{1,0:T(8,128)S(1)}, f32[104,128]{1,0:T(8,128)S(1)}, u32[]{:S(2)}, u32[]{:S(2)}) collective-permute-start(f32[104,128]{1,0:T(8,128)S(1)} %get-tuple-element.17), channel_id=1, source_target_pairs={{0,4},{4,0},{8,12},{12,8},{16,20},{20,16},{24,28},{28,24},{1,5},{5... | collective-permute-start | bytes 159752 | tf_op jit(solution)/shard_map/ppermute | solution.py:305
  5.9 6.0 %collective-permute-start.3 = (f32[104,128]{1,0:T(8,128)S(1)}, f32[104,128]{1,0:T(8,128)S(1)}, u32[]{:S(2)}, u32[]{:S(2)}) collective-permute-start(f32[104,128]{1,0:T(8,128)S(1)} %add.72), channel_id=1, source_target_pairs={{0,24},{4,28},{8,16},{12,20},{16,8},{20,12},{24,0},{28,4},{1,25},{... | collective-permute-start | bytes 159752 | tf_op jit(solution)/shard_map/ppermute | solution.py:305
  9.7 4.1 %collective-permute-start.2 = (f32[104,128]{1,0:T(8,128)S(1)}, f32[104,128]{1,0:T(8,128)S(1)}, u32[]{:S(2)}, u32[]{:S(2)}) collective-permute-start(f32[104,128]{1,0:T(8,128)S(1)} %add.72), channel_id=1, source_target_pairs={{0,16},{4,20},{8,24},{12,28},{16,0},{20,4},{24,8},{28,12},{1,17},{... | collective-permute-start | bytes 159752 | tf_op jit(solution)/shard_map/ppermute | solution.py:305
  10.3 4.1 %collective-permute-start.1 = (f32[104,128]{1,0:T(8,128)S(1)}, f32[104,128]{1,0:T(8,128)S(1)}, u32[]{:S(2)}, u32[]{:S(2)}) collective-permute-start(f32[104,128]{1,0:T(8,128)S(1)} %add.72), channel_id=1, source_target_pairs={{0,8},{4,12},{8,0},{12,4},{16,24},{20,28},{24,16},{28,20},{1,9},{5... | collective-permute-start | bytes 159752 | tf_op jit(solution)/shard_map/ppermute | solution.py:305
  14.4 7.3 %collective-permute-start.6 = (f32[104,128]{1,0:T(8,128)S(1)}, f32[104,128]{1,0:T(8,128)S(1)}, u32[]{:S(2)}, u32[]{:S(2)}) collective-permute-start(f32[104,128]{1,0:T(8,128)S(1)} %add_add_fusion.3._), channel_id=1, source_target_pairs={{0,3},{1,2},{2,1},{3,0},{4,7},{5,6},{6,5},{7,4},{8,11},{9,10},{10,... | collective-permute-start | bytes 159752 | tf_op jit(solution)/shard_map/ppermute | solution.py:305
  18.1 5.0 %collective-permute-start.5 = (f32[104,128]{1,0:T(8,128)S(1)}, f32[104,128]{1,0:T(8,128)S(1)}, u32[]{:S(2)}, u32[]{:S(2)}) collective-permute-start(f32[104,128]{1,0:T(8,128)S(1)} %add_add_fusion.3._), channel_id=1, source_target_pairs={{0,2},{1,3},{2,0},{3,1},{4,6},{5,7},{6,4},{7,5},{8,10},{9,11},{10,... | collective-permute-start | bytes 159752 | tf_op jit(solution)/shard_map/ppermute | solution.py:305
  18.1 5.0 %collective-permute-start.4 = (f32[104,128]{1,0:T(8,128)S(1)}, f32[104,128]{1,0:T(8,128)S(1)}, u32[]{:S(2)}, u32[]{:S(2)}) collective-permute-start(f32[104,128]{1,0:T(8,128)S(1)} %add_add_fusion.3._), channel_id=1, source_target_pairs={{0,1},{1,0},{2,3},{3,2},{4,5},{5,4},{6,7},{7,6},{8,9},{9,8},{10,11... | collective-permute-start | bytes 159752 | tf_op jit(solution)/shard_map/ppermute | solution.py:305
  23.2 1.3 %collective-permute-start.7 = (f32[104,128]{1,0:T(8,128)S(1)}, f32[104,128]{1,0:T(8,128)S(1)}, u32[]{:S(2)}, u32[]{:S(2)}) collective-permute-start(f32[104,128]{1,0:T(8,128)S(1)} %add_add_fusion.2.refs_0_), channel_id=1, source_target_pairs={{0,4},{4,0},{8,12},{12,8},{16,20},{20,16},{24,28},{28,24},{1,5},{5... | collective-permute-start | bytes 159752 | tf_op jit(solution)/shard_map/ppermute | solution.py:305
  24.5 17.7 %copy-start = (f32[256,16,256]{2,1,0:T(8,128)S(1)}, f32[256,16,256]{2,1,0:T(8,128)}, u32[]{:S(2)}) copy-start(f32[256,16,256]{2,1,0:T(8,128)} %param.2) | copy-start | bytes 12582916
  29.6 1.3 %collective-permute-start.8 = (f32[136,128]{1,0:T(8,128)S(1)}, f32[136,128]{1,0:T(8,128)S(1)}, u32[]{:S(2)}, u32[]{:S(2)}) collective-permute-start(f32[136,128]{1,0:T(8,128)S(1)} %get-tuple-element.23), channel_id=1, source_target_pairs={{0,4},{4,0},{8,12},{12,8},{16,20},{20,16},{24,28},{28,24},{1,5},{5... | collective-permute-start | bytes 208904 | tf_op jit(solution)/shard_map/ppermute | solution.py:305
  30.9 6.1 %collective-permute-start.11 = (f32[136,128]{1,0:T(8,128)S(1)}, f32[136,128]{1,0:T(8,128)S(1)}, u32[]{:S(2)}, u32[]{:S(2)}) collective-permute-start(f32[136,128]{1,0:T(8,128)S(1)} %add.82._), channel_id=1, source_target_pairs={{0,24},{4,28},{8,16},{12,20},{16,8},{20,12},{24,0},{28,4},{1,25},{... | collective-permute-start | bytes 208904 | tf_op jit(solution)/shard_map/ppermute | solution.py:305
  32.5 4.5 %collective-permute-start.10 = (f32[136,128]{1,0:T(8,128)S(1)}, f32[136,128]{1,0:T(8,128)S(1)}, u32[]{:S(2)}, u32[]{:S(2)}) collective-permute-start(f32[136,128]{1,0:T(8,128)S(1)} %add.82._), channel_id=1, source_target_pairs={{0,16},{4,20},{8,24},{12,28},{16,0},{20,4},{24,8},{28,12},{1,17},{... | collective-permute-start | bytes 208904 | tf_op jit(solution)/shard_map/ppermute | solution.py:305
  33.0 4.7 %collective-permute-start.9 = (f32[136,128]{1,0:T(8,128)S(1)}, f32[136,128]{1,0:T(8,128)S(1)}, u32[]{:S(2)}, u32[]{:S(2)}) collective-permute-start(f32[136,128]{1,0:T(8,128)S(1)} %add.82._), channel_id=1, source_target_pairs={{0,8},{4,12},{8,0},{12,4},{16,24},{20,28},{24,16},{28,20},{1,9},{5... | collective-permute-start | bytes 208904 | tf_op jit(solution)/shard_map/ppermute | solution.py:305
  37.7 7.3 %collective-permute-start.14 = (f32[136,128]{1,0:T(8,128)S(1)}, f32[136,128]{1,0:T(8,128)S(1)}, u32[]{:S(2)}, u32[]{:S(2)}) collective-permute-start(f32[136,128]{1,0:T(8,128)S(1)} %add_add_fusion.1._), channel_id=1, source_target_pairs={{0,3},{1,2},{2,1},{3,0},{4,7},{5,6},{6,5},{7,4},{8,11},{9,10},{10,... | collective-permute-start | bytes 208904 | tf_op jit(solution)/shard_map/ppermute | solution.py:305
  40.0 6.6 %collective-permute-start.13 = (f32[136,128]{1,0:T(8,128)S(1)}, f32[136,128]{1,0:T(8,128)S(1)}, u32[]{:S(2)}, u32[]{:S(2)}) collective-permute-start(f32[136,128]{1,0:T(8,128)S(1)} %add_add_fusion.1._), channel_id=1, source_target_pairs={{0,2},{1,3},{2,0},{3,1},{4,6},{5,7},{6,4},{7,5},{8,10},{9,11},{10,... | collective-permute-start | bytes 208904 | tf_op jit(solution)/shard_map/ppermute | solution.py:305
  40.0 6.6 %collective-permute-start.12 = (f32[136,128]{1,0:T(8,128)S(1)}, f32[136,128]{1,0:T(8,128)S(1)}, u32[]{:S(2)}, u32[]{:S(2)}) collective-permute-start(f32[136,128]{1,0:T(8,128)S(1)} %add_add_fusion.1._), channel_id=1, source_target_pairs={{0,1},{1,0},{2,3},{3,2},{4,5},{5,4},{6,7},{7,6},{8,9},{9,8},{10,11... | collective-permute-start | bytes 208904 | tf_op jit(solution)/shard_map/ppermute | solution.py:305
  46.6 1.3 %collective-permute-start.15 = (f32[136,128]{1,0:T(8,128)S(1)}, f32[136,128]{1,0:T(8,128)S(1)}, u32[]{:S(2)}, u32[]{:S(2)}) collective-permute-start(f32[136,128]{1,0:T(8,128)S(1)} %add_add_fusion.refs_0_), channel_id=1, source_target_pairs={{0,4},{4,0},{8,12},{12,8},{16,20},{20,16},{24,28},{28,24},{1,5},{5... | collective-permute-start | bytes 208904 | tf_op jit(solution)/shard_map/ppermute | solution.py:305

commit v13 on v12

--- a/solution.py
+++ b/solution.py
@@ -410,7 +410,7 @@
     rows_right = right_core.reshape(rank_mid * points, rank_right)
     vmem = pl.BlockSpec(memory_space=pltpu.VMEM)
 
-    steps = 8
+    steps = 16
     block_rows = (RK // 2 + RK + 16) // SPREAD_ONE
     blocks = pl.pallas_call(
         gram_kernel,

time: 54.5 us -> 55.9 us (1.026)
  Pallas kernels: 23.5 us -> 25 us
    pallas_call x1, Pallas kernels: 3.84 us -> 5.25 us  [per_device(): pl.pallas_call(gram_kernel, in_specs=[pl.BlockSpec(memory_space=pl.ANY)],...]
where the time goes in v13:
time: 55.9 us; the launch traced here: 55.8 us
  Pallas kernels  25 us (45%)
  starting transfers between devices  17.9 us (32%)
  waiting for transfers between devices  12.1 us (22%)
  between operations  0.71 us (1%)
    ppermute x16, starting transfers between devices, swap(): return lax.ppermute(value, axes, [(i, i ^ mask) for i in range(size)])  17.9 us
    ppermute x16, waiting for transfers between devices, swap(): return lax.ppermute(value, axes, [(i, i ^ mask) for i in range(size)])  12.1 us
    pallas_call x1, Pallas kernels, per_device(): pl.pallas_call(functools.partial(factor_kernel, 1.0 / (RK * total_points)...  6.44 us
    pallas_call x1, Pallas kernels, per_device(): pl.pallas_call(gram_kernel, in_specs=[pl.BlockSpec(memory_space=pl.ANY)],...  5.25 us
    pallas_call x1, Pallas kernels, per_device(): pl.pallas_call(functools.partial(absorb_kernel, math.sqrt(rank_left * tot...  5.13 us
    pallas_call x1, Pallas kernels, left_part(): pl.pallas_call(left_kernel, grid=(steps,), in_specs=[pl.BlockSpec((chunk,...  2.83 us
    pallas_call x1, Pallas kernels, relay_part(): pl.pallas_call(functools.partial(relay_kernel, points), in_specs=[pl.Bloc...  2.8 us
    pallas_call x1, Pallas kernels, right_part(): pl.pallas_call(functools.partial(right_kernel, points), grid=(steps, 2),...  2.49 us
  transfers between devices with their start and end apart: 16, of which 10 were waited for; matrix products, arithmetic and copies ran while one was open for 0% of the time, Pallas kernels for 15%

profile of v13, /device:TPU:0, one launch (start us, length us, event | category | flops | bytes accessed | tf_op | source)
XLA Modules:
  0.0 55.8 jit_solution(15037278191800502632)
XLA Ops:
  0.6 5.3 %gram_top.1 = (f32[104,128]{1,0:T(8,128)S(1)}, f32[104,128]{1,0:T(8,128)S(1)}) custom-call(f32[4096,256]{1,0:T(8,128)} %bitcast.10), custom_call_target="tpu_custom_call" | custom-call | tf_op jit(solution)/shard_map/gram_top/pallas_call | solution.py:415
  6.4 0.9 %collective-permute-done = f32[104,128]{1,0:T(8,128)S(1)} collective-permute-done((f32[104,128]{1,0:T(8,128)S(1)}, f32[104,128]{1,0:T(8,128)S(1)}, u32[]{:S(2)}, u32[]{:S(2)}) %collective-permute-start) | collective-permute-done | bytes 53280 | tf_op jit(solution)/shard_map/ppermute | solution.py:305
  7.3 3.9 %collective-permute-start.3 = (f32[104,128]{1,0:T(8,128)S(1)}, f32[104,128]{1,0:T(8,128)S(1)}, u32[]{:S(2)}, u32[]{:S(2)}) collective-permute-start(f32[104,128]{1,0:T(8,128)S(1)} %add.72), channel_id=1, source_target_pairs={{0,24},{4,28},{8,16},{12,20},{16,8},{20,12},{24,0},{28,4},{1,25},{... | collective-permute-start | bytes 159752 | tf_op jit(solution)/shard_map/ppermute | solution.py:305
  11.2 0.5 collective-permute-start.2
  11.8 1.5 %collective-permute-done.3 = f32[104,128]{1,0:T(8,128)S(1)} collective-permute-done((f32[104,128]{1,0:T(8,128)S(1)}, f32[104,128]{1,0:T(8,128)S(1)}, u32[]{:S(2)}, u32[]{:S(2)}) %collective-permute-start.3) | collective-permute-done | bytes 53280 | tf_op jit(solution)/shard_map/ppermute | solution.py:305
  13.3 2.0 %collective-permute-done.2 = f32[104,128]{1,0:T(8,128)S(1)} collective-permute-done((f32[104,128]{1,0:T(8,128)S(1)}, f32[104,128]{1,0:T(8,128)S(1)}, u32[]{:S(2)}, u32[]{:S(2)}) %collective-permute-start.2) | collective-permute-done | bytes 53280 | tf_op jit(solution)/shard_map/ppermute | solution.py:305
  15.3 0.5 collective-permute-done.1
  15.8 3.7 %collective-permute-start.6 = (f32[104,128]{1,0:T(8,128)S(1)}, f32[104,128]{1,0:T(8,128)S(1)}, u32[]{:S(2)}, u32[]{:S(2)}) collective-permute-start(f32[104,128]{1,0:T(8,128)S(1)} %add_add_fusion.3._), channel_id=1, source_target_pairs={{0,3},{1,2},{2,1},{3,0},{4,7},{5,6},{6,5},{7,4},{8,11},{9,10},{10,... | collective-permute-start | bytes 159752 | tf_op jit(solution)/shard_map/ppermute | solution.py:305
  19.5 0.8 %collective-permute-start.4 = (f32[104,128]{1,0:T(8,128)S(1)}, f32[104,128]{1,0:T(8,128)S(1)}, u32[]{:S(2)}, u32[]{:S(2)}) collective-permute-start(f32[104,128]{1,0:T(8,128)S(1)} %add_add_fusion.3._), channel_id=1, source_target_pairs={{0,1},{1,0},{2,3},{3,2},{4,5},{5,4},{6,7},{7,6},{8,9},{9,8},{10,11... | collective-permute-start | bytes 159752 | tf_op jit(solution)/shard_map/ppermute | solution.py:305
  20.3 2.8 %relay_right.1 = (bf16[16,256,256]{2,1,0:T(8,128)(2,1)S(1)}, bf16[16,256,256]{2,1,0:T(8,128)(2,1)S(1)}, f32[8,128]{1,0:T(8,128)S(1)}) custom-call(f32[4096,256]{1,0:T(8,128)} %bitcast.12, f32[104,128]{1,0:T(8,128)S(1)} %add_add_fusion.3._), custom_call_target="tpu_custom_call" | custom-call | bytes 8388608 | tf_op jit(solution)/shard_map/relay_right/pallas_call | solution.py:346
  23.1 1.4 %collective-permute-done.5 = f32[104,128]{1,0:T(8,128)S(1)} collective-permute-done((f32[104,128]{1,0:T(8,128)S(1)}, f32[104,128]{1,0:T(8,128)S(1)}, u32[]{:S(2)}, u32[]{:S(2)}) %collective-permute-start.5) | collective-permute-done | bytes 53280 | tf_op jit(solution)/shard_map/ppermute | solution.py:305
  24.7 1.2 %collective-permute-done.7.refs_1_ = f32[104,128]{1,0:T(8,128)S(1)} collective-permute-done((f32[104,128]{1,0:T(8,128)S(1)}, f32[104,128]{1,0:T(8,128)S(1)}, u32[]{:S(2)}, u32[]{:S(2)}) %collective-permute-start.7) | collective-permute-done | bytes 53280 | tf_op jit(solution)/shard_map/ppermute | solution.py:305
  25.9 5.1 %factor_absorb.1 = (f32[16,128,256]{2,1,0:T(8,128)S(1)}, f32[128,128]{1,0:T(8,128)S(1)}, f32[136,128]{1,0:T(8,128)S(1)}, f32[136,128]{1,0:T(8,128)S(1)}) custom-call(f32[104,128]{1,0:T(8,128)S(1)} %add_add_fusion.2.refs_0_, f32[104,128]{1,0:T(8,128)S(1)} %collective-permute-done.7.refs_1_, bf16[16,256,256]{2,1,0:T(8,128)(2,1)S(1)} %get-tuple-element.19.refs_2_, ...), custom_call_target="tpu_custom_call" | custom-call | tf_op jit(solution)/shard_map/factor_absorb/pallas_call | solution.py:437
  31.3 1.1 %collective-permute-done.8 = f32[136,128]{1,0:T(8,128)S(1)} collective-permute-done((f32[136,128]{1,0:T(8,128)S(1)}, f32[136,128]{1,0:T(8,128)S(1)}, u32[]{:S(2)}, u32[]{:S(2)}) %collective-permute-start.8) | collective-permute-done | bytes 69664 | tf_op jit(solution)/shard_map/ppermute | solution.py:305
  32.4 1.6 %collective-permute-start.11 = (f32[136,128]{1,0:T(8,128)S(1)}, f32[136,128]{1,0:T(8,128)S(1)}, u32[]{:S(2)}, u32[]{:S(2)}) collective-permute-start(f32[136,128]{1,0:T(8,128)S(1)} %add.82._), channel_id=1, source_target_pairs={{0,24},{4,28},{8,16},{12,20},{16,8},{20,12},{24,0},{28,4},{1,25},{... | collective-permute-start | bytes 208904 | tf_op jit(solution)/shard_map/ppermute | solution.py:305
  34.4 1.5 %collective-permute-start.9 = (f32[136,128]{1,0:T(8,128)S(1)}, f32[136,128]{1,0:T(8,128)S(1)}, u32[]{:S(2)}, u32[]{:S(2)}) collective-permute-start(f32[136,128]{1,0:T(8,128)S(1)} %add.82._), channel_id=1, source_target_pairs={{0,8},{4,12},{8,0},{12,4},{16,24},{20,28},{24,16},{28,20},{1,9},{5... | collective-permute-start | bytes 208904 | tf_op jit(solution)/shard_map/ppermute | solution.py:305
  35.9 2.5 %right_out.1 = (f32[2048,256]{1,0:T(8,128)}, f32[8,128]{1,0:T(8,128)S(1)}) custom-call(f32[16,128,256]{2,1,0:T(8,128)S(1)} %get-tuple-element.24.absorbed_ref, f32[136,128]{1,0:T(8,128)S(1)} %add.82._), custom_call_target="tpu_custom_call" | custom-call | bytes 8388608 | tf_op jit(solution)/shard_map/right_out/pallas_call | solution.py:387
  38.4 0.7 %collective-permute-done.9 = f32[136,128]{1,0:T(8,128)S(1)} collective-permute-done((f32[136,128]{1,0:T(8,128)S(1)}, f32[136,128]{1,0:T(8,128)S(1)}, u32[]{:S(2)}, u32[]{:S(2)}) %collective-permute-start.9) | collective-permute-done | bytes 69664 | tf_op jit(solution)/shard_map/ppermute | solution.py:305
  39.1 2.3 %collective-permute-start.14 = (f32[136,128]{1,0:T(8,128)S(1)}, f32[136,128]{1,0:T(8,128)S(1)}, u32[]{:S(2)}, u32[]{:S(2)}) collective-permute-start(f32[136,128]{1,0:T(8,128)S(1)} %add_add_fusion.1._), channel_id=1, source_target_pairs={{0,3},{1,2},{2,1},{3,0},{4,7},{5,6},{6,5},{7,4},{8,11},{9,10},{10,... | collective-permute-start | bytes 208904 | tf_op jit(solution)/shard_map/ppermute | solution.py:305
  41.4 2.2 %collective-permute-start.12 = (f32[136,128]{1,0:T(8,128)S(1)}, f32[136,128]{1,0:T(8,128)S(1)}, u32[]{:S(2)}, u32[]{:S(2)}) collective-permute-start(f32[136,128]{1,0:T(8,128)S(1)} %add_add_fusion.1._), channel_id=1, source_target_pairs={{0,1},{1,0},{2,3},{3,2},{4,5},{5,4},{6,7},{7,6},{8,9},{9,8},{10,11... | collective-permute-start | bytes 208904 | tf_op jit(solution)/shard_map/ppermute | solution.py:305
  43.6 2.8 %left_out.1 = (f32[4096,128]{1,0:T(8,128)}, f32[8,128]{1,0:T(8,128)S(1)}) custom-call(f32[4096,256]{1,0:T(8,128)S(1)} %bitcast.11, f32[128,128]{1,0:T(8,128)S(1)} %get-tuple-element.21.linv_ref, f32[136,128]{1,0:T(8,128)S(1)} %add_add_fusion.1._), custom_call_target="tpu_custom_call" | custom-call | bytes 8388608 | tf_op jit(solution)/shard_map/left_out/pallas_call | solution.py:365
  46.4 1.6 %collective-permute-done.13 = f32[136,128]{1,0:T(8,128)S(1)} collective-permute-done((f32[136,128]{1,0:T(8,128)S(1)}, f32[136,128]{1,0:T(8,128)S(1)}, u32[]{:S(2)}, u32[]{:S(2)}) %collective-permute-start.13) | collective-permute-done | bytes 69664 | tf_op jit(solution)/shard_map/ppermute | solution.py:305
  48.1 1.2 %collective-permute-done.15.refs_1_ = f32[136,128]{1,0:T(8,128)S(1)} collective-permute-done((f32[136,128]{1,0:T(8,128)S(1)}, f32[136,128]{1,0:T(8,128)S(1)}, u32[]{:S(2)}, u32[]{:S(2)}) %collective-permute-start.15) | collective-permute-done | bytes 69664 | tf_op jit(solution)/shard_map/ppermute | solution.py:305
  49.3 6.4 %factor_next.1 = f32[256,256]{1,0:T(8,128)} custom-call(f32[136,128]{1,0:T(8,128)S(1)} %add_add_fusion.refs_0_, f32[136,128]{1,0:T(8,128)S(1)} %collective-permute-done.15.refs_1_), custom_call_target="tpu_custom_call" | custom-call | tf_op jit(solution)/shard_map/factor_next/pallas_call | solution.py:459
  (25 shorter events, 1.6 us)
Async XLA Ops:
  5.9 1.4 %collective-permute-start = (f32[104,128]{1,0:T(8,128)S(1)}, f32[104,128]{1,0:T(8,128)S(1)}, u32[]{:S(2)}, u32[]{:S(2)}) collective-permute-start(f32[104,128]{1,0:T(8,128)S(1)} %get-tuple-element.17), channel_id=1, source_target_pairs={{0,4},{4,0},{8,12},{12,8},{16,20},{20,16},{24,28},{28,24},{1,5},{5... | collective-permute-start | bytes 159752 | tf_op jit(solution)/shard_map/ppermute | solution.py:305
  7.3 6.0 %collective-permute-start.3 = (f32[104,128]{1,0:T(8,128)S(1)}, f32[104,128]{1,0:T(8,128)S(1)}, u32[]{:S(2)}, u32[]{:S(2)}) collective-permute-start(f32[104,128]{1,0:T(8,128)S(1)} %add.72), channel_id=1, source_target_pairs={{0,24},{4,28},{8,16},{12,20},{16,8},{20,12},{24,0},{28,4},{1,25},{... | collective-permute-start | bytes 159752 | tf_op jit(solution)/shard_map/ppermute | solution.py:305
  11.2 4.1 %collective-permute-start.2 = (f32[104,128]{1,0:T(8,128)S(1)}, f32[104,128]{1,0:T(8,128)S(1)}, u32[]{:S(2)}, u32[]{:S(2)}) collective-permute-start(f32[104,128]{1,0:T(8,128)S(1)} %add.72), channel_id=1, source_target_pairs={{0,16},{4,20},{8,24},{12,28},{16,0},{20,4},{24,8},{28,12},{1,17},{... | collective-permute-start | bytes 159752 | tf_op jit(solution)/shard_map/ppermute | solution.py:305
  11.7 4.1 %collective-permute-start.1 = (f32[104,128]{1,0:T(8,128)S(1)}, f32[104,128]{1,0:T(8,128)S(1)}, u32[]{:S(2)}, u32[]{:S(2)}) collective-permute-start(f32[104,128]{1,0:T(8,128)S(1)} %add.72), channel_id=1, source_target_pairs={{0,8},{4,12},{8,0},{12,4},{16,24},{20,28},{24,16},{28,20},{1,9},{5... | collective-permute-start | bytes 159752 | tf_op jit(solution)/shard_map/ppermute | solution.py:305
  15.8 7.3 %collective-permute-start.6 = (f32[104,128]{1,0:T(8,128)S(1)}, f32[104,128]{1,0:T(8,128)S(1)}, u32[]{:S(2)}, u32[]{:S(2)}) collective-permute-start(f32[104,128]{1,0:T(8,128)S(1)} %add_add_fusion.3._), channel_id=1, source_target_pairs={{0,3},{1,2},{2,1},{3,0},{4,7},{5,6},{6,5},{7,4},{8,11},{9,10},{10,... | collective-permute-start | bytes 159752 | tf_op jit(solution)/shard_map/ppermute | solution.py:305
  19.5 5.0 %collective-permute-start.5 = (f32[104,128]{1,0:T(8,128)S(1)}, f32[104,128]{1,0:T(8,128)S(1)}, u32[]{:S(2)}, u32[]{:S(2)}) collective-permute-start(f32[104,128]{1,0:T(8,128)S(1)} %add_add_fusion.3._), channel_id=1, source_target_pairs={{0,2},{1,3},{2,0},{3,1},{4,6},{5,7},{6,4},{7,5},{8,10},{9,11},{10,... | collective-permute-start | bytes 159752 | tf_op jit(solution)/shard_map/ppermute | solution.py:305
  19.5 5.0 %collective-permute-start.4 = (f32[104,128]{1,0:T(8,128)S(1)}, f32[104,128]{1,0:T(8,128)S(1)}, u32[]{:S(2)}, u32[]{:S(2)}) collective-permute-start(f32[104,128]{1,0:T(8,128)S(1)} %add_add_fusion.3._), channel_id=1, source_target_pairs={{0,1},{1,0},{2,3},{3,2},{4,5},{5,4},{6,7},{7,6},{8,9},{9,8},{10,11... | collective-permute-start | bytes 159752 | tf_op jit(solution)/shard_map/ppermute | solution.py:305
  24.6 1.3 %collective-permute-start.7 = (f32[104,128]{1,0:T(8,128)S(1)}, f32[104,128]{1,0:T(8,128)S(1)}, u32[]{:S(2)}, u32[]{:S(2)}) collective-permute-start(f32[104,128]{1,0:T(8,128)S(1)} %add_add_fusion.2.refs_0_), channel_id=1, source_target_pairs={{0,4},{4,0},{8,12},{12,8},{16,20},{20,16},{24,28},{28,24},{1,5},{5... | collective-permute-start | bytes 159752 | tf_op jit(solution)/shard_map/ppermute | solution.py:305
  25.9 17.7 %copy-start = (f32[256,16,256]{2,1,0:T(8,128)S(1)}, f32[256,16,256]{2,1,0:T(8,128)}, u32[]{:S(2)}) copy-start(f32[256,16,256]{2,1,0:T(8,128)} %param.2) | copy-start | bytes 12582916
  31.0 1.3 %collective-permute-start.8 = (f32[136,128]{1,0:T(8,128)S(1)}, f32[136,128]{1,0:T(8,128)S(1)}, u32[]{:S(2)}, u32[]{:S(2)}) collective-permute-start(f32[136,128]{1,0:T(8,128)S(1)} %get-tuple-element.23), channel_id=1, source_target_pairs={{0,4},{4,0},{8,12},{12,8},{16,20},{20,16},{24,28},{28,24},{1,5},{5... | collective-permute-start | bytes 208904 | tf_op jit(solution)/shard_map/ppermute | solution.py:305
  32.4 6.1 %collective-permute-start.11 = (f32[136,128]{1,0:T(8,128)S(1)}, f32[136,128]{1,0:T(8,128)S(1)}, u32[]{:S(2)}, u32[]{:S(2)}) collective-permute-start(f32[136,128]{1,0:T(8,128)S(1)} %add.82._), channel_id=1, source_target_pairs={{0,24},{4,28},{8,16},{12,20},{16,8},{20,12},{24,0},{28,4},{1,25},{... | collective-permute-start | bytes 208904 | tf_op jit(solution)/shard_map/ppermute | solution.py:305
  33.9 4.5 %collective-permute-start.10 = (f32[136,128]{1,0:T(8,128)S(1)}, f32[136,128]{1,0:T(8,128)S(1)}, u32[]{:S(2)}, u32[]{:S(2)}) collective-permute-start(f32[136,128]{1,0:T(8,128)S(1)} %add.82._), channel_id=1, source_target_pairs={{0,16},{4,20},{8,24},{12,28},{16,0},{20,4},{24,8},{28,12},{1,17},{... | collective-permute-start | bytes 208904 | tf_op jit(solution)/shard_map/ppermute | solution.py:305
  34.4 4.7 %collective-permute-start.9 = (f32[136,128]{1,0:T(8,128)S(1)}, f32[136,128]{1,0:T(8,128)S(1)}, u32[]{:S(2)}, u32[]{:S(2)}) collective-permute-start(f32[136,128]{1,0:T(8,128)S(1)} %add.82._), channel_id=1, source_target_pairs={{0,8},{4,12},{8,0},{12,4},{16,24},{20,28},{24,16},{28,20},{1,9},{5... | collective-permute-start | bytes 208904 | tf_op jit(solution)/shard_map/ppermute | solution.py:305
  39.1 7.3 %collective-permute-start.14 = (f32[136,128]{1,0:T(8,128)S(1)}, f32[136,128]{1,0:T(8,128)S(1)}, u32[]{:S(2)}, u32[]{:S(2)}) collective-permute-start(f32[136,128]{1,0:T(8,128)S(1)} %add_add_fusion.1._), channel_id=1, source_target_pairs={{0,3},{1,2},{2,1},{3,0},{4,7},{5,6},{6,5},{7,4},{8,11},{9,10},{10,... | collective-permute-start | bytes 208904 | tf_op jit(solution)/shard_map/ppermute | solution.py:305
  41.4 6.6 %collective-permute-start.13 = (f32[136,128]{1,0:T(8,128)S(1)}, f32[136,128]{1,0:T(8,128)S(1)}, u32[]{:S(2)}, u32[]{:S(2)}) collective-permute-start(f32[136,128]{1,0:T(8,128)S(1)} %add_add_fusion.1._), channel_id=1, source_target_pairs={{0,2},{1,3},{2,0},{3,1},{4,6},{5,7},{6,4},{7,5},{8,10},{9,11},{10,... | collective-permute-start | bytes 208904 | tf_op jit(solution)/shard_map/ppermute | solution.py:305
  41.4 6.6 %collective-permute-start.12 = (f32[136,128]{1,0:T(8,128)S(1)}, f32[136,128]{1,0:T(8,128)S(1)}, u32[]{:S(2)}, u32[]{:S(2)}) collective-permute-start(f32[136,128]{1,0:T(8,128)S(1)} %add_add_fusion.1._), channel_id=1, source_target_pairs={{0,1},{1,0},{2,3},{3,2},{4,5},{5,4},{6,7},{7,6},{8,9},{9,8},{10,11... | collective-permute-start | bytes 208904 | tf_op jit(solution)/shard_map/ppermute | solution.py:305
  48.0 1.3 %collective-permute-start.15 = (f32[136,128]{1,0:T(8,128)S(1)}, f32[136,128]{1,0:T(8,128)S(1)}, u32[]{:S(2)}, u32[]{:S(2)}) collective-permute-start(f32[136,128]{1,0:T(8,128)S(1)} %add_add_fusion.refs_0_), channel_id=1, source_target_pairs={{0,4},{4,0},{8,12},{12,8},{16,20},{20,16},{24,28},{28,24},{1,5},{5... | collective-permute-start | bytes 208904 | tf_op jit(solution)/shard_map/ppermute | solution.py:305
